TPU v7x, 32 devices: a whole 2x2x4 slice. The times are simulated.
32 devices in a mesh: ctx: 4 (over y, core), head: 4 (over z), dp: 2 (over x).
Axes of the slice: x: 2, y: 2, z: 4, core: 2. Of those that a mesh axis runs over, the one named last changes fastest.
Arguments:
- queries: bfloat16 [2048, 8192], P(('dp', 'ctx', 'head')), parts along dimension 0, may hold values from -100 to 100, as said below
- unscaled_key_rows: bfloat16 [2048, 1024], P(('dp', 'ctx', 'head')), parts along dimension 0, may hold values from -4 to 4
- unscaled_value_rows: bfloat16 [2048, 1024], P(('dp', 'ctx', 'head')), parts along dimension 0, may hold values from -12 to 12
- key_block_scale: float32 [16, 8], P('dp', 'head'), parts along dimension 0, may hold values from 0.8 to 1.6
- value_block_scale: float32 [16, 8], P('dp', 'head'), parts along dimension 0, may hold values from 0.5 to 2
- span_order: int32 [8], replicated, may hold values from 0 to 7, each once
- block_keep: int32 [8, 8], replicated, may hold values 0 or 1
Outputs:
- attended: bfloat16 [2048, 8192], P(('dp', 'ctx', 'head')), parts along dimension 0
- row_check: float32 [2048, 64], P(('dp', 'ctx', 'head')), parts along dimension 0
There are 2 independent parts, one for each index of `dp`. A program takes and returns all parts, laid end to end along the dimension named above; an argument that names none is the same for every part. Nothing has to cross between parts.
Inputs may be any that keep to these rules, and one draw needn't show every extreme that they name: `queries`: queries of one head and token.
All inputs are finite; a program needn't handle non-finite values.
Results may differ from a plain program's by a relative error of at most 0.004.
Values may be sent and summed in bfloat16 or wider, within the bound.
No kernel may reach another device: no remote copies, remote signals or barrier semaphores. Data moves between devices by JAX's collectives and lax.ppermute only.
A program may use at most 64 MiB of HBM per device.

v0:
```python
import functools
import math

import jax
import jax.numpy as jnp
from jax import lax
from jax.experimental import pallas as pl
from jax.experimental.pallas import tpu as pltpu
from jax.sharding import PartitionSpec as P

HEAD_WIDTH = 128
SPAN = 128
LOG2E = 1.4426950408889634
MASKED = -1e30


def absorb_kernel(
    order_ref, keep_ref, *refs, groups, per_step, kv_heads, kv_local, sources, ctx_size, head_size, first, last
):
    refs = list(refs)
    scale_in = [refs.pop(0) for _ in range(head_size)]
    pieces = [refs.pop(0) for _ in sources]
    q_ref = refs.pop(0)
    mixed_in, stats_in = (None, None) if first else (refs.pop(0), refs.pop(0))
    result_ref, stats_ref, scale_ref, mask_ref, x_ref, p_ref, scale_sem = refs
    step = pl.program_id(0)
    tokens = q_ref.shape[0]
    width = tokens * len(sources)
    inverse_root = 1.0 / math.sqrt(HEAD_WIDTH)
    ctx, head = lax.axis_index("ctx"), lax.axis_index("head")
    starts = [
        ((ctx ^ flip) * head_size + lax.rem(head - shift + head_size, head_size)) * tokens
        for flip, shift in sources
    ]
    spans = [start // SPAN for start in starts]

    @pl.when(step == 0)
    def _():
        copies = []
        for shift in range(head_size):
            owner = lax.rem(head - shift + head_size, head_size)
            copies.append(
                pltpu.make_async_copy(scale_in[shift], scale_ref.at[owner], scale_sem.at[shift])
            )
        for copy in copies:
            copy.start()
        own_start = (ctx * head_size + head) * tokens
        own = own_start // SPAN
        key = lax.broadcasted_iota(jnp.int32, (tokens, SPAN), 0)
        token = lax.broadcasted_iota(jnp.int32, (tokens, SPAN), 1)
        for i, (start, span) in enumerate(zip(starts, spans)):
            seen = (order_ref[span] < order_ref[own]) & (keep_ref[own, span] > 0)
            whole = jnp.where(seen, 0.0, MASKED)
            causal = jnp.where(key + (start - own_start) <= token, 0.0, MASKED)
            mask = jnp.where(own == span, causal, whole)
            mask_ref[i * tokens : (i + 1) * tokens, :] = mask.astype(jnp.bfloat16)
        for copy in copies:
            copy.wait()

    row = lax.broadcasted_iota(jnp.int32, (tokens, SPAN), 0)
    lane = lax.broadcasted_iota(jnp.int32, (tokens, SPAN), 1)
    lane_row = lax.broadcasted_iota(jnp.int32, (1, SPAN), 1)
    one_hot = jnp.where(row == lane, 1.0, 0.0).astype(jnp.bfloat16)
    if last:
        checks = stats_ref[...]
        check_lane = lax.broadcasted_iota(jnp.int32, checks.shape, 1)
    for u in range(per_step):
        g = step * per_step + u
        k_cols = pl.ds(pl.multiple_of(g * HEAD_WIDTH, HEAD_WIDTH), HEAD_WIDTH)
        q = [
            q_ref[:, (u * groups + h) * HEAD_WIDTH : (u * groups + h + 1) * HEAD_WIDTH]
            for h in range(groups)
        ]
        q = jnp.concatenate(
            [jnp.concatenate(q, axis=0), jnp.concatenate([one_hot] * groups, axis=0)], axis=1
        )
        k = jnp.concatenate([piece[:, k_cols] for piece in pieces], axis=0)
        k = jnp.concatenate([k, mask_ref[...]], axis=1)
        x_ref[u] = lax.dot_general(
            q, k, (((1,), (1,)), ((), ())), preferred_element_type=jnp.float32
        )
    for u in range(per_step):
        g = step * per_step + u
        owner, member = g // kv_local, g % kv_local
        per_tile = SPAN // tokens
        factors = []
        for tile in range(width // SPAN):
            vector = None
            for j in range(per_tile):
                value = scale_ref[owner, spans[tile * per_tile + j], member] * (inverse_root * LOG2E)
                vector = (
                    jnp.full((1, SPAN), value, jnp.float32)
                    if vector is None
                    else jnp.where(lane_row >= j * tokens, value, vector)
                )
            factors.append(vector)
        v_cols = pl.ds(pl.multiple_of((g + kv_heads) * HEAD_WIDTH, HEAD_WIDTH), HEAD_WIDTH)
        high, low = [], []
        for i, piece in enumerate(pieces):
            v = piece[:, v_cols].astype(jnp.float32) * scale_ref[owner, spans[i], kv_local + member]
            high.append(v.astype(jnp.bfloat16))
            low.append((v - high[-1].astype(jnp.float32)).astype(jnp.bfloat16))
        v = jnp.concatenate(
            [jnp.concatenate(high, axis=0), jnp.concatenate(low, axis=0)], axis=1
        )
        tops, totals, fades = [], [], []
        for h in range(groups):
            rows = slice(h * tokens, (h + 1) * tokens)
            xs = [
                x_ref[u, rows, i * SPAN : (i + 1) * SPAN] * factor
                for i, factor in enumerate(factors)
            ]
            top = xs[0]
            for x in xs[1:]:
                top = jnp.maximum(top, x)
            top = jnp.max(top, axis=1, keepdims=True)
            if not first:
                before = stats_in[u, 0, :, h : h + 1]
                top = jnp.maximum(top, before)
                fades.append(jnp.exp2(before - top))
            total = None
            for i, x in enumerate(xs):
                weight = jnp.exp2(x - top)
                p_ref[u, rows, i * SPAN : (i + 1) * SPAN] = weight.astype(jnp.bfloat16)
                total = weight if total is None else total + weight
            total = jnp.sum(total, axis=1, keepdims=True)
            if not first:
                total = total + fades[h] * stats_in[u, 1, :, h : h + 1]
            tops.append(top)
            totals.append(total)
        both = jnp.dot(p_ref[u], v, preferred_element_type=jnp.float32)
        new_top = new_total = jnp.zeros((tokens, SPAN), jnp.float32)
        for h in range(groups):
            rows = slice(h * tokens, (h + 1) * tokens)
            cols = slice((u * groups + h) * HEAD_WIDTH, (u * groups + h + 1) * HEAD_WIDTH)
            mixed = both[rows, :HEAD_WIDTH] + both[rows, HEAD_WIDTH:]
            if not first:
                mixed = mixed + fades[h] * mixed_in[:, cols]
            if last:
                mixed = mixed * (1.0 / totals[h])
                check = jnp.sum(mixed, axis=1, keepdims=True) * inverse_root
                checks = jnp.where(check_lane == g * groups + h, check, checks)
            else:
                new_top = jnp.where(lane == h, tops[h], new_top)
                new_total = jnp.where(lane == h, totals[h], new_total)
            result_ref[:, cols] = mixed.astype(result_ref.dtype)
        if not last:
            stats_ref[u, 0] = new_top
            stats_ref[u, 1] = new_total
    if last:
        stats_ref[...] = checks


def absorb(queries, chunk, scales, span_order, block_keep, state, last, kv_heads, kv_local, sizes):
    tokens, width = queries.shape
    groups = width // HEAD_WIDTH // kv_heads
    per_step = 2 if kv_heads % 2 == 0 else 1
    pieces = [block for _, _, block in chunk]
    sources = [(flip, shift) for flip, shift, _ in chunk]
    keys = tokens * len(chunk)
    first = state is None
    columns = pl.BlockSpec((tokens, per_step * groups * HEAD_WIDTH), lambda s: (0, s))
    stats = pl.BlockSpec((per_step, 2, tokens, SPAN), lambda s: (s, 0, 0, 0))
    smem = pl.BlockSpec(memory_space=pltpu.SMEM)
    in_specs = [smem, smem] + [pl.BlockSpec(memory_space=pl.ANY)] * len(scales)
    in_specs += [pl.BlockSpec(piece.shape, lambda s: (0, 0)) for piece in pieces]
    in_specs += [columns] + ([] if first else [columns, stats])
    if last:
        out_specs = [columns, pl.BlockSpec((tokens, kv_heads * groups), lambda s: (0, 0))]
        out_shape = [
            jax.ShapeDtypeStruct((tokens, width), jnp.bfloat16),
            jax.ShapeDtypeStruct((tokens, kv_heads * groups), jnp.float32),
        ]
    else:
        out_specs = [columns, stats]
        out_shape = [
            jax.ShapeDtypeStruct((tokens, width), jnp.float32),
            jax.ShapeDtypeStruct((kv_heads, 2, tokens, SPAN), jnp.float32),
        ]
    return pl.pallas_call(
        functools.partial(
            absorb_kernel,
            groups=groups,
            per_step=per_step,
            kv_heads=kv_heads,
            kv_local=kv_local,
            sources=sources,
            ctx_size=sizes[0],
            head_size=sizes[1],
            first=first,
            last=last,
        ),
        grid=(kv_heads // per_step,),
        in_specs=in_specs,
        out_specs=out_specs,
        out_shape=out_shape,
        scratch_shapes=[
            pltpu.SMEM((len(scales),) + scales[0].shape, jnp.float32),
            pltpu.VMEM((keys, SPAN), jnp.bfloat16),
            pltpu.VMEM((per_step, groups * tokens, keys), jnp.float32),
            pltpu.VMEM((per_step, groups * tokens, keys), jnp.bfloat16),
            pltpu.SemaphoreType.DMA((len(scales),)),
        ],
        compiler_params=pltpu.CompilerParams(vmem_limit_bytes=24 * 1024 * 1024),
        cost_estimate=pl.CostEstimate(
            flops=16 * tokens * width * keys,
            bytes_accessed=16 * tokens * width,
            transcendentals=tokens * width // HEAD_WIDTH * keys,
        ),
    )(span_order, block_keep, *scales, *pieces, queries, *(() if first else state))


def local(queries, keys, values, key_scale, value_scale, span_order, block_keep):
    tokens, width = queries.shape
    kv_heads = keys.shape[1] // HEAD_WIDTH
    ctx_size, head_size = lax.axis_size("ctx"), lax.axis_size("head")
    levels = ctx_size.bit_length() - 1
    batch = 2 * SPAN // tokens

    def along_head(block, distance):
        return lax.ppermute(block, "head", [(i, (i + distance) % head_size) for i in range(head_size)])

    def across_ctx(block, flip):
        return lax.ppermute(block, "ctx", [(i, i ^ flip) for i in range(ctx_size)])

    def attend(chunk, state, last):
        return absorb(
            queries,
            chunk,
            scales,
            span_order,
            block_keep,
            state,
            last,
            kv_heads,
            key_scale.shape[1],
            (ctx_size, head_size),
        )

    scale = jnp.concatenate([key_scale, value_scale], axis=1)
    block = jnp.concatenate([keys, values], axis=1)
    arrived = [(0, 0, -1, block)]
    waiting, state, scales = [(0, 0, block)], None, None
    while arrived:
        coming = []
        for flip, shift, level, block in arrived:
            if level < 0 and shift + 1 < head_size:
                coming.append((flip, shift + 1, level, along_head(block, 1)))
            for later in range(level + 1, levels):
                bit = ctx_size >> (later + 1)
                coming.append((flip ^ bit, shift, later, across_ctx(block, bit)))
        if scales is None:
            scales = [scale] + [along_head(scale, s) for s in range(1, head_size)]
        ready = len(waiting) // batch * batch
        if ready:
            state = attend(waiting[:ready], state, not coming)
            waiting = waiting[ready:]
        if coming:
            blocks = [block for _, _, _, block in coming]
            blocks, state, scales = lax.optimization_barrier((blocks, state, scales))
            coming = [(f, s, l, b) for (f, s, l, _), b in zip(coming, blocks)]
        waiting += [(f, s, b) for f, s, _, b in coming]
        arrived = coming
    attended, row_check = state
    return attended, row_check


def solution(mesh):
    rows = P(("dp", "ctx", "head"), None)
    return jax.shard_map(
        local,
        mesh=mesh,
        in_specs=(rows, rows, rows, P("dp", "head"), P("dp", "head"), P(), P()),
        out_specs=(rows, rows),
        check_vma=False,
    )
```

profile of v0, /device:TPU:0, one launch (start us, length us, event | category | flops | bytes accessed | tf_op | source)
XLA Modules:
  0.0 80.9 jit_solution(10288286877693421328)
XLA Ops:
  0.6 0.9 %constant_dynamic-update-slice_fusion.1 = bf16[64,2048]{1,0:T(8,128)(2,1)S(1)} fusion(bf16[64,1024]{1,0:T(8,128)(2,1)} %param.8), kind=kLoop, calls=%fused_computation.1 | loop fusion | bytes 262144
  1.5 0.9 %constant_dynamic-update-slice_fusion.refs_4_ = bf16[64,2048]{1,0:T(8,128)(2,1)S(1)} fusion(bf16[64,2048]{1,0:T(8,128)(2,1)S(1)} %constant_dynamic-update-slice_fusion.1, bf16[64,1024]{1,0:T(8,128)(2,1)} %param.9), kind=kLoop, calls=%fused_computation | loop fusion | bytes 262144 | tf_op jit(solution)/shard_map/concatenate | solution.py:241
  2.5 0.5 collective-permute-start.2
  3.0 2.6 %collective-permute-start.1 = (bf16[64,2048]{1,0:T(8,128)(2,1)S(1)}, bf16[64,2048]{1,0:T(8,128)(2,1)S(1)}, u32[]{:S(2)}, u32[]{:S(2)}) collective-permute-start(bf16[64,2048]{1,0:T(8,128)(2,1)S(1)} %constant_dynamic-update-slice_fusion.refs_4_), channel_id=1, source_target_pairs={{0,16},{8,24},{16,0},{24,8},{1,17},{9,25},{17,1},{25,9},{2,18},{10... | collective-permute-start | bytes 786440 | tf_op jit(solution)/shard_map/ppermute | solution.py:224
  5.6 1.6 %collective-permute-start = (bf16[64,2048]{1,0:T(8,128)(2,1)S(1)}, bf16[64,2048]{1,0:T(8,128)(2,1)S(1)}, u32[]{:S(2)}, u32[]{:S(2)}) collective-permute-start(bf16[64,2048]{1,0:T(8,128)(2,1)S(1)} %constant_dynamic-update-slice_fusion.refs_4_), channel_id=1, source_target_pairs={{0,2},{2,4},{4,6},{6,0},{1,3},{3,5},{5,7},{7,1},{8,10},{10,12},{12... | collective-permute-start | bytes 786440 | tf_op jit(solution)/shard_map/ppermute | solution.py:221
  7.2 0.8 copy.9
  7.9 0.8 copy.10
  8.7 0.1 pad_maximum_fusion.refs_0_
  8.7 2.2 %collective-permute-start.5 = (f32[8,4]{1,0:T(8,128)S(1)}, f32[8,4]{1,0:T(8,128)S(1)}, u32[]{:S(2)}, u32[]{:S(2)}) collective-permute-start(f32[8,4]{1,0:T(8,128)S(1)} %pad_maximum_fusion.refs_0_), channel_id=1, source_target_pairs={{0,6},{2,0},{4,2},{6,4},{1,7},{3,1},{5,3},{7,5},{8,14},{10,8},{12,... | collective-permute-start | bytes 392 | tf_op jit(solution)/shard_map/ppermute | solution.py:221
  11.0 0.8 collective-permute-start.4
  11.8 1.4 %collective-permute-done.5.refs_3_ = f32[8,4]{1,0:T(8,128)S(1)} collective-permute-done((f32[8,4]{1,0:T(8,128)S(1)}, f32[8,4]{1,0:T(8,128)S(1)}, u32[]{:S(2)}, u32[]{:S(2)}) %collective-permute-start.5) | collective-permute-done | bytes 160 | tf_op jit(solution)/shard_map/ppermute | solution.py:221
  13.2 1.1 %collective-permute-start.3 = (f32[8,4]{1,0:T(8,128)S(1)}, f32[8,4]{1,0:T(8,128)S(1)}, u32[]{:S(2)}, u32[]{:S(2)}) collective-permute-start(f32[8,4]{1,0:T(8,128)S(1)} %pad_maximum_fusion.refs_0_), channel_id=1, source_target_pairs={{0,2},{2,4},{4,6},{6,0},{1,3},{3,5},{5,7},{7,1},{8,10},{10,12},{12... | collective-permute-start | bytes 392 | tf_op jit(solution)/shard_map/ppermute | solution.py:221
  14.3 1.8 %collective-permute-done.4.refs_2_ = f32[8,4]{1,0:T(8,128)S(1)} collective-permute-done((f32[8,4]{1,0:T(8,128)S(1)}, f32[8,4]{1,0:T(8,128)S(1)}, u32[]{:S(2)}, u32[]{:S(2)}) %collective-permute-start.4) | collective-permute-done | bytes 160 | tf_op jit(solution)/shard_map/ppermute | solution.py:221
  16.1 3.1 %collective-permute-done.3.refs_1_ = f32[8,4]{1,0:T(8,128)S(1)} collective-permute-done((f32[8,4]{1,0:T(8,128)S(1)}, f32[8,4]{1,0:T(8,128)S(1)}, u32[]{:S(2)}, u32[]{:S(2)}) %collective-permute-start.3) | collective-permute-done | bytes 160 | tf_op jit(solution)/shard_map/ppermute | solution.py:221
  19.2 0.0 collective-permute-done.2.refs_7_
  19.2 0.0 collective-permute-done.1.refs_6_
  19.2 0.0 collective-permute-done.refs_5_
  19.2 0.1 collective-permute-start.9
  19.2 0.5 collective-permute-start.8
  19.7 0.5 collective-permute-start.7
  20.2 0.0 collective-permute-start.6
  20.3 1.2 %copy-done = bf16[64,8192]{1,0:T(8,128)(2,1)S(1)} copy-done((bf16[64,8192]{1,0:T(8,128)(2,1)S(1)}, bf16[64,8192]{1,0:T(8,128)(2,1)}, u32[]{:S(2)}) %copy-start) | copy-done | bytes 1048600
  21.5 0.7 copy-done.2
  22.2 0.7 copy-done.3
  22.8 4.6 %shard_map.86 = (f32[64,8192]{1,0:T(8,128)S(1)}, f32[8,2,64,128]{3,2,1,0:T(8,128)S(1)}) custom-call(s32[8]{0:T(128)S(1)} %copy-done.3, s32[8,8]{1,0:T(8,128)S(1)} %copy-done.2, f32[8,4]{1,0:T(8,128)S(1)} %pad_maximum_fusion.refs_0_, f32[8,4]{1,0:T(8,128)S(1)} %collective-permute-done.3.refs_1_, f32[8,4]{1,0:T(8,128)S(1)} %collective-permute-done.4.refs_2_, ...), custom_call_target="tpu_custom_call" | custom-call | flops 2147483648 | bytes 8388608 | tf_op jit(solution)/shard_map/pallas_call | solution.py:180
  27.4 0.0 collective-permute-done.9.refs_7_
  27.4 0.0 collective-permute-done.8.refs_6_
  27.4 0.6 collective-permute-done.7.refs_5_
  28.0 2.0 %collective-permute-done.6.refs_4_ = bf16[64,2048]{1,0:T(8,128)(2,1)S(1)} collective-permute-done((bf16[64,2048]{1,0:T(8,128)(2,1)S(1)}, bf16[64,2048]{1,0:T(8,128)(2,1)S(1)}, u32[]{:S(2)}, u32[]{:S(2)}) %collective-permute-start.6) | collective-permute-done | bytes 262176 | tf_op jit(solution)/shard_map/ppermute | solution.py:221
  30.1 0.0 collective-permute-start.13
  30.1 0.5 collective-permute-start.12
  30.6 1.5 %collective-permute-start.11 = (bf16[64,2048]{1,0:T(8,128)(2,1)S(1)}, bf16[64,2048]{1,0:T(8,128)(2,1)S(1)}, u32[]{:S(2)}, u32[]{:S(2)}) collective-permute-start(bf16[64,2048]{1,0:T(8,128)(2,1)S(1)} %collective-permute-done.6.refs_4_), channel_id=1, source_target_pairs={{0,16},{8,24},{16,0},{24,8},{1,17},{9,25},{17,1},{25,9},{2,18},{10... | collective-permute-start | bytes 786440 | tf_op jit(solution)/shard_map/ppermute | solution.py:224
  32.1 0.0 collective-permute-start.10
  32.1 13.3 %shard_map.87 = (f32[64,8192]{1,0:T(8,128)S(1)}, f32[8,2,64,128]{3,2,1,0:T(8,128)S(1)}) custom-call(s32[8]{0:T(128)S(1)} %copy-done.3, s32[8,8]{1,0:T(8,128)S(1)} %copy-done.2, f32[8,4]{1,0:T(8,128)S(1)} %pad_maximum_fusion.refs_0_, f32[8,4]{1,0:T(8,128)S(1)} %collective-permute-done.3.refs_1_, f32[8,4]{1,0:T(8,128)S(1)} %collective-permute-done.4.refs_2_, ...), custom_call_target="tpu_custom_call" | custom-call | flops 2147483648 | bytes 8388608 | tf_op jit(solution)/shard_map/pallas_call | solution.py:180
  45.4 0.0 collective-permute-done.13.refs_7_
  45.4 0.0 collective-permute-done.12.refs_6_
  45.5 0.0 collective-permute-done.11.refs_5_
  45.5 0.0 collective-permute-done.10.refs_4_
  45.5 0.1 collective-permute-start.16
  45.6 0.5 collective-permute-start.15
  46.1 0.5 collective-permute-start.14
  46.6 13.3 %shard_map.88 = (f32[64,8192]{1,0:T(8,128)S(1)}, f32[8,2,64,128]{3,2,1,0:T(8,128)S(1)}) custom-call(s32[8]{0:T(128)S(1)} %copy-done.3, s32[8,8]{1,0:T(8,128)S(1)} %copy-done.2, f32[8,4]{1,0:T(8,128)S(1)} %pad_maximum_fusion.refs_0_, f32[8,4]{1,0:T(8,128)S(1)} %collective-permute-done.3.refs_1_, f32[8,4]{1,0:T(8,128)S(1)} %collective-permute-done.4.refs_2_, ...), custom_call_target="tpu_custom_call" | custom-call | flops 2147483648 | bytes 8388608 | tf_op jit(solution)/shard_map/pallas_call | solution.py:180
  59.9 0.0 collective-permute-done.16.refs_6_
  59.9 0.0 collective-permute-done.15.refs_5_
  59.9 0.0 collective-permute-done.14.refs_4_
  59.9 0.1 collective-permute-start.17
  60.0 1.5 %collective-permute-done.17.refs_7_ = bf16[64,2048]{1,0:T(8,128)(2,1)S(1)} collective-permute-done((bf16[64,2048]{1,0:T(8,128)(2,1)S(1)}, bf16[64,2048]{1,0:T(8,128)(2,1)S(1)}, u32[]{:S(2)}, u32[]{:S(2)}) %collective-permute-start.17) | collective-permute-done | bytes 262176 | tf_op jit(solution)/shard_map/ppermute | solution.py:224
  61.5 19.3 %shard_map.89 = (bf16[64,8192]{1,0:T(8,128)(2,1)}, f32[64,64]{1,0:T(8,128)}) custom-call(s32[8]{0:T(128)S(1)} %copy-done.3, s32[8,8]{1,0:T(8,128)S(1)} %copy-done.2, f32[8,4]{1,0:T(8,128)S(1)} %pad_maximum_fusion.refs_0_, f32[8,4]{1,0:T(8,128)S(1)} %collective-permute-done.3.refs_1_, f32[8,4]{1,0:T(8,128)S(1)} %collective-permute-done.4.refs_2_, ...), custom_call_target="tpu_custom_call" | custom-call | flops 2147483648 | bytes 8388608 | tf_op jit(solution)/shard_map/pallas_call | solution.py:180
  (5 shorter events, 0.0 us)
Async XLA Ops:
  2.5 16.7 %collective-permute-start.2 = (bf16[64,2048]{1,0:T(8,128)(2,1)S(1)}, bf16[64,2048]{1,0:T(8,128)(2,1)S(1)}, u32[]{:S(2)}, u32[]{:S(2)}) collective-permute-start(bf16[64,2048]{1,0:T(8,128)(2,1)S(1)} %constant_dynamic-update-slice_fusion.refs_4_), channel_id=1, source_target_pairs={{0,8},{8,0},{16,24},{24,16},{1,9},{9,1},{17,25},{25,17},{2,10},{10... | collective-permute-start | bytes 786440 | tf_op jit(solution)/shard_map/ppermute | solution.py:224
  3.0 16.2 %collective-permute-start.1 = (bf16[64,2048]{1,0:T(8,128)(2,1)S(1)}, bf16[64,2048]{1,0:T(8,128)(2,1)S(1)}, u32[]{:S(2)}, u32[]{:S(2)}) collective-permute-start(bf16[64,2048]{1,0:T(8,128)(2,1)S(1)} %constant_dynamic-update-slice_fusion.refs_4_), channel_id=1, source_target_pairs={{0,16},{8,24},{16,0},{24,8},{1,17},{9,25},{17,1},{25,9},{2,18},{10... | collective-permute-start | bytes 786440 | tf_op jit(solution)/shard_map/ppermute | solution.py:224
  5.6 13.6 %collective-permute-start = (bf16[64,2048]{1,0:T(8,128)(2,1)S(1)}, bf16[64,2048]{1,0:T(8,128)(2,1)S(1)}, u32[]{:S(2)}, u32[]{:S(2)}) collective-permute-start(bf16[64,2048]{1,0:T(8,128)(2,1)S(1)} %constant_dynamic-update-slice_fusion.refs_4_), channel_id=1, source_target_pairs={{0,2},{2,4},{4,6},{6,0},{1,3},{3,5},{5,7},{7,1},{8,10},{10,12},{12... | collective-permute-start | bytes 786440 | tf_op jit(solution)/shard_map/ppermute | solution.py:221
  8.7 4.4 %collective-permute-start.5 = (f32[8,4]{1,0:T(8,128)S(1)}, f32[8,4]{1,0:T(8,128)S(1)}, u32[]{:S(2)}, u32[]{:S(2)}) collective-permute-start(f32[8,4]{1,0:T(8,128)S(1)} %pad_maximum_fusion.refs_0_), channel_id=1, source_target_pairs={{0,6},{2,0},{4,2},{6,4},{1,7},{3,1},{5,3},{7,5},{8,14},{10,8},{12,... | collective-permute-start | bytes 392 | tf_op jit(solution)/shard_map/ppermute | solution.py:221
  11.0 5.1 %collective-permute-start.4 = (f32[8,4]{1,0:T(8,128)S(1)}, f32[8,4]{1,0:T(8,128)S(1)}, u32[]{:S(2)}, u32[]{:S(2)}) collective-permute-start(f32[8,4]{1,0:T(8,128)S(1)} %pad_maximum_fusion.refs_0_), channel_id=1, source_target_pairs={{0,4},{2,6},{4,0},{6,2},{1,5},{3,7},{5,1},{7,3},{8,12},{10,14},{12... | collective-permute-start | bytes 392 | tf_op jit(solution)/shard_map/ppermute | solution.py:221
  13.2 6.0 %collective-permute-start.3 = (f32[8,4]{1,0:T(8,128)S(1)}, f32[8,4]{1,0:T(8,128)S(1)}, u32[]{:S(2)}, u32[]{:S(2)}) collective-permute-start(f32[8,4]{1,0:T(8,128)S(1)} %pad_maximum_fusion.refs_0_), channel_id=1, source_target_pairs={{0,2},{2,4},{4,6},{6,0},{1,3},{3,5},{5,7},{7,1},{8,10},{10,12},{12... | collective-permute-start | bytes 392 | tf_op jit(solution)/shard_map/ppermute | solution.py:221
  19.2 8.2 %collective-permute-start.9 = (bf16[64,2048]{1,0:T(8,128)(2,1)S(1)}, bf16[64,2048]{1,0:T(8,128)(2,1)S(1)}, u32[]{:S(2)}, u32[]{:S(2)}) collective-permute-start(bf16[64,2048]{1,0:T(8,128)(2,1)S(1)} %collective-permute-done.1.refs_6_), channel_id=1, source_target_pairs={{0,8},{8,0},{16,24},{24,16},{1,9},{9,1},{17,25},{25,17},{2,10},{10... | collective-permute-start | bytes 786440 | tf_op jit(solution)/shard_map/ppermute | solution.py:224
  19.2 8.2 %collective-permute-start.8 = (bf16[64,2048]{1,0:T(8,128)(2,1)S(1)}, bf16[64,2048]{1,0:T(8,128)(2,1)S(1)}, u32[]{:S(2)}, u32[]{:S(2)}) collective-permute-start(bf16[64,2048]{1,0:T(8,128)(2,1)S(1)} %collective-permute-done.refs_5_), channel_id=1, source_target_pairs={{0,8},{8,0},{16,24},{24,16},{1,9},{9,1},{17,25},{25,17},{2,10},{10... | collective-permute-start | bytes 786440 | tf_op jit(solution)/shard_map/ppermute | solution.py:224
  19.7 8.3 %collective-permute-start.7 = (bf16[64,2048]{1,0:T(8,128)(2,1)S(1)}, bf16[64,2048]{1,0:T(8,128)(2,1)S(1)}, u32[]{:S(2)}, u32[]{:S(2)}) collective-permute-start(bf16[64,2048]{1,0:T(8,128)(2,1)S(1)} %collective-permute-done.refs_5_), channel_id=1, source_target_pairs={{0,16},{8,24},{16,0},{24,8},{1,17},{9,25},{17,1},{25,9},{2,18},{10... | collective-permute-start | bytes 786440 | tf_op jit(solution)/shard_map/ppermute | solution.py:224
  20.2 9.8 %collective-permute-start.6 = (bf16[64,2048]{1,0:T(8,128)(2,1)S(1)}, bf16[64,2048]{1,0:T(8,128)(2,1)S(1)}, u32[]{:S(2)}, u32[]{:S(2)}) collective-permute-start(bf16[64,2048]{1,0:T(8,128)(2,1)S(1)} %collective-permute-done.refs_5_), channel_id=1, source_target_pairs={{0,2},{2,4},{4,6},{6,0},{1,3},{3,5},{5,7},{7,1},{8,10},{10,12},{12... | collective-permute-start | bytes 786440 | tf_op jit(solution)/shard_map/ppermute | solution.py:221
  20.3 1.2 %copy-start = (bf16[64,8192]{1,0:T(8,128)(2,1)S(1)}, bf16[64,8192]{1,0:T(8,128)(2,1)}, u32[]{:S(2)}) copy-start(bf16[64,8192]{1,0:T(8,128)(2,1)} %refs_8_.7) | copy-start | bytes 3145732
  21.5 0.7 copy-start.2
  22.2 0.7 copy-start.3
  22.8 9.3 %copy-start.1 = (bf16[64,8192]{1,0:T(8,128)(2,1)S(1)}, bf16[64,8192]{1,0:T(8,128)(2,1)}, u32[]{:S(2)}) copy-start(bf16[64,8192]{1,0:T(8,128)(2,1)} %refs_8_.7) | copy-start | bytes 3145732
  30.1 15.4 %collective-permute-start.13 = (bf16[64,2048]{1,0:T(8,128)(2,1)S(1)}, bf16[64,2048]{1,0:T(8,128)(2,1)S(1)}, u32[]{:S(2)}, u32[]{:S(2)}) collective-permute-start(bf16[64,2048]{1,0:T(8,128)(2,1)S(1)} %collective-permute-done.7.refs_5_), channel_id=1, source_target_pairs={{0,8},{8,0},{16,24},{24,16},{1,9},{9,1},{17,25},{25,17},{2,10},{10... | collective-permute-start | bytes 786440 | tf_op jit(solution)/shard_map/ppermute | solution.py:224
  30.1 15.4 %collective-permute-start.12 = (bf16[64,2048]{1,0:T(8,128)(2,1)S(1)}, bf16[64,2048]{1,0:T(8,128)(2,1)S(1)}, u32[]{:S(2)}, u32[]{:S(2)}) collective-permute-start(bf16[64,2048]{1,0:T(8,128)(2,1)S(1)} %collective-permute-done.6.refs_4_), channel_id=1, source_target_pairs={{0,8},{8,0},{16,24},{24,16},{1,9},{9,1},{17,25},{25,17},{2,10},{10... | collective-permute-start | bytes 786440 | tf_op jit(solution)/shard_map/ppermute | solution.py:224
  30.6 14.9 %collective-permute-start.11 = (bf16[64,2048]{1,0:T(8,128)(2,1)S(1)}, bf16[64,2048]{1,0:T(8,128)(2,1)S(1)}, u32[]{:S(2)}, u32[]{:S(2)}) collective-permute-start(bf16[64,2048]{1,0:T(8,128)(2,1)S(1)} %collective-permute-done.6.refs_4_), channel_id=1, source_target_pairs={{0,16},{8,24},{16,0},{24,8},{1,17},{9,25},{17,1},{25,9},{2,18},{10... | collective-permute-start | bytes 786440 | tf_op jit(solution)/shard_map/ppermute | solution.py:224
  32.1 13.4 %collective-permute-start.10 = (bf16[64,2048]{1,0:T(8,128)(2,1)S(1)}, bf16[64,2048]{1,0:T(8,128)(2,1)S(1)}, u32[]{:S(2)}, u32[]{:S(2)}) collective-permute-start(bf16[64,2048]{1,0:T(8,128)(2,1)S(1)} %collective-permute-done.6.refs_4_), channel_id=1, source_target_pairs={{0,2},{2,4},{4,6},{6,0},{1,3},{3,5},{5,7},{7,1},{8,10},{10,12},{12... | collective-permute-start | bytes 786440 | tf_op jit(solution)/shard_map/ppermute | solution.py:221
  45.5 14.4 %collective-permute-start.16 = (bf16[64,2048]{1,0:T(8,128)(2,1)S(1)}, bf16[64,2048]{1,0:T(8,128)(2,1)S(1)}, u32[]{:S(2)}, u32[]{:S(2)}) collective-permute-start(bf16[64,2048]{1,0:T(8,128)(2,1)S(1)} %collective-permute-done.11.refs_5_), channel_id=1, source_target_pairs={{0,8},{8,0},{16,24},{24,16},{1,9},{9,1},{17,25},{25,17},{2,10},{10... | collective-permute-start | bytes 786440 | tf_op jit(solution)/shard_map/ppermute | solution.py:224
  45.6 14.4 %collective-permute-start.15 = (bf16[64,2048]{1,0:T(8,128)(2,1)S(1)}, bf16[64,2048]{1,0:T(8,128)(2,1)S(1)}, u32[]{:S(2)}, u32[]{:S(2)}) collective-permute-start(bf16[64,2048]{1,0:T(8,128)(2,1)S(1)} %collective-permute-done.10.refs_4_), channel_id=1, source_target_pairs={{0,8},{8,0},{16,24},{24,16},{1,9},{9,1},{17,25},{25,17},{2,10},{10... | collective-permute-start | bytes 786440 | tf_op jit(solution)/shard_map/ppermute | solution.py:224
  46.1 13.9 %collective-permute-start.14 = (bf16[64,2048]{1,0:T(8,128)(2,1)S(1)}, bf16[64,2048]{1,0:T(8,128)(2,1)S(1)}, u32[]{:S(2)}, u32[]{:S(2)}) collective-permute-start(bf16[64,2048]{1,0:T(8,128)(2,1)S(1)} %collective-permute-done.10.refs_4_), channel_id=1, source_target_pairs={{0,16},{8,24},{16,0},{24,8},{1,17},{9,25},{17,1},{25,9},{2,18},{10... | collective-permute-start | bytes 786440 | tf_op jit(solution)/shard_map/ppermute | solution.py:224
  59.9 1.6 %collective-permute-start.17 = (bf16[64,2048]{1,0:T(8,128)(2,1)S(1)}, bf16[64,2048]{1,0:T(8,128)(2,1)S(1)}, u32[]{:S(2)}, u32[]{:S(2)}) collective-permute-start(bf16[64,2048]{1,0:T(8,128)(2,1)S(1)} %collective-permute-done.14.refs_4_), channel_id=1, source_target_pairs={{0,8},{8,0},{16,24},{24,16},{1,9},{9,1},{17,25},{25,17},{2,10},{10... | collective-permute-start | bytes 786440 | tf_op jit(solution)/shard_map/ppermute | solution.py:224
where the time goes:
time: 81.1 us; the launch traced here: 80.9 us
  Pallas kernels  50.6 us (62%)
  starting transfers between devices  13.1 us (16%)
  waiting for transfers between devices  10.5 us (13%)
  local copies, waits for them, and re-layouts  5.9 us (7%)
    pallas_call x4, Pallas kernels, absorb(): pl.pallas_call(functools.partial(absorb_kernel, groups=groups, per_step=p...  50.6 us
    ppermute x6, waiting for transfers between devices, along_head(): lax.ppermute(block, 'head', [(i, (i + distance) % head_size) for i in ran...  8.32 us
    ppermute x12, starting transfers between devices, across_ctx(): return lax.ppermute(block, 'ctx', [(i, i ^ flip) for i in range(ctx_size)])  7.36 us
    ppermute x6, starting transfers between devices, along_head(): lax.ppermute(block, 'head', [(i, (i + distance) % head_size) for i in ran...  5.7 us
    unnamed x11, local copies, waits for them, and re-layouts  4.99 us
    ppermute x12, waiting for transfers between devices, across_ctx(): return lax.ppermute(block, 'ctx', [(i, i ^ flip) for i in range(ctx_size)])  2.16 us
  transfers between devices with their start and end apart: 18, of which 6 were waited for; matrix products, arithmetic and copies ran while one was open for 2% of the time, Pallas kernels for 39%

commit v1 on v0

v1 whole, which is shorter than its diff:
```python
import functools
import math

import jax
import jax.numpy as jnp
from jax import lax
from jax.experimental import pallas as pl
from jax.experimental.pallas import tpu as pltpu
from jax.sharding import PartitionSpec as P

HEAD_WIDTH = 128
SPAN = 128
LOG2E = 1.4426950408889634
MASKED = -1e30


def pack_kernel(k_ref, v_ref, key_scale_ref, value_scale_ref, block_ref, scale_ref, sems):
    tokens = k_ref.shape[0]
    copies = [
        pltpu.make_async_copy(k_ref, block_ref.at[pl.ds(0, tokens), :], sems.at[0]),
        pltpu.make_async_copy(v_ref, block_ref.at[pl.ds(tokens, tokens), :], sems.at[1]),
        pltpu.make_async_copy(key_scale_ref, scale_ref.at[0], sems.at[2]),
        pltpu.make_async_copy(value_scale_ref, scale_ref.at[1], sems.at[3]),
    ]
    for copy in copies:
        copy.start()
    for copy in copies:
        copy.wait()


def pack(keys, values, key_scale, value_scale):
    tokens, width = keys.shape
    anywhere = pl.BlockSpec(memory_space=pl.ANY)
    return pl.pallas_call(
        pack_kernel,
        in_specs=[anywhere] * 4,
        out_specs=[anywhere] * 2,
        out_shape=[
            jax.ShapeDtypeStruct((2 * tokens, width), keys.dtype),
            jax.ShapeDtypeStruct((2,) + key_scale.shape, key_scale.dtype),
        ],
        scratch_shapes=[pltpu.SemaphoreType.DMA((4,))],
        compiler_params=pltpu.CompilerParams(vmem_limit_bytes=56 * 1024 * 1024),
    )(keys, values, key_scale, value_scale)


def absorb_kernel(
    order_ref, keep_ref, *refs, groups, per_step, kv_local, sources, ctx_size, head_size, first, last
):
    refs = list(refs)
    scale_in = [refs.pop(0) for _ in range(head_size)]
    pieces = [refs.pop(0) for _ in sources]
    q_ref = refs.pop(0)
    mixed_in, stats_in = (None, None) if first else (refs.pop(0), refs.pop(0))
    result_ref, stats_ref, scale_ref, mask_ref, x_ref, p_ref, check_ref, scale_sem = refs
    step = pl.program_id(0)
    tokens = q_ref.shape[0]
    inverse_root = 1.0 / math.sqrt(HEAD_WIDTH)
    ctx, head = lax.axis_index("ctx"), lax.axis_index("head")
    starts = [
        ((ctx ^ flip) * head_size + lax.rem(head - shift + head_size, head_size)) * tokens
        for flip, shift in sources
    ]
    spans = [start // SPAN for start in starts]

    @pl.when(step == 0)
    def _():
        copies = []
        for shift in range(head_size):
            owner = lax.rem(head - shift + head_size, head_size)
            copies.append(
                pltpu.make_async_copy(scale_in[shift], scale_ref.at[owner], scale_sem.at[shift])
            )
        for copy in copies:
            copy.start()
        own_start = (ctx * head_size + head) * tokens
        own = own_start // SPAN
        key = lax.broadcasted_iota(jnp.int32, (tokens, SPAN), 0)
        token = lax.broadcasted_iota(jnp.int32, (tokens, SPAN), 1)
        for i, (start, span) in enumerate(zip(starts, spans)):
            seen = (order_ref[span] < order_ref[own]) & (keep_ref[own, span] > 0)
            whole = jnp.where(seen, 0.0, MASKED)
            causal = jnp.where(key + (start - own_start) <= token, 0.0, MASKED)
            mask = jnp.where(own == span, causal, whole)
            mask_ref[i * tokens : (i + 1) * tokens, :] = mask.astype(jnp.bfloat16)
        for copy in copies:
            copy.wait()

    row = lax.broadcasted_iota(jnp.int32, (tokens, SPAN), 0)
    lane = lax.broadcasted_iota(jnp.int32, (tokens, SPAN), 1)
    one_hot = jnp.where(row == lane, 1.0, 0.0).astype(jnp.bfloat16)
    for u in range(per_step):
        g = step * per_step + u
        cols = pl.ds(pl.multiple_of(g * HEAD_WIDTH, HEAD_WIDTH), HEAD_WIDTH)
        q = [
            q_ref[:, (u * groups + h) * HEAD_WIDTH : (u * groups + h + 1) * HEAD_WIDTH]
            for h in range(groups)
        ]
        q = jnp.concatenate(
            [jnp.concatenate(q, axis=0), jnp.concatenate([one_hot] * groups, axis=0)], axis=1
        )
        k = jnp.concatenate([piece[:tokens, cols] for piece in pieces], axis=0)
        k = jnp.concatenate([k, mask_ref[...]], axis=1)
        x_ref[u] = lax.dot_general(
            k, q, (((1,), (1,)), ((), ())), preferred_element_type=jnp.float32
        )
    for u in range(per_step):
        g = step * per_step + u
        owner, member = g // kv_local, g % kv_local
        factors = [scale_ref[owner, 0, span, member] * (inverse_root * LOG2E) for span in spans]
        cols = pl.ds(pl.multiple_of(g * HEAD_WIDTH, HEAD_WIDTH), HEAD_WIDTH)
        high, low = [], []
        for i, piece in enumerate(pieces):
            v = piece[tokens:, cols].astype(jnp.float32) * scale_ref[owner, 1, spans[i], member]
            high.append(v.astype(jnp.bfloat16))
            low.append((v - high[-1].astype(jnp.float32)).astype(jnp.bfloat16))
        v = jnp.concatenate(
            [jnp.concatenate(high, axis=0), jnp.concatenate(low, axis=0)], axis=1
        )
        tops, totals, fades = [], [], []
        for tile in range(groups * tokens // SPAN):
            lanes = slice(tile * SPAN, (tile + 1) * SPAN)
            top = None
            for i, factor in enumerate(factors):
                x = x_ref[u, i * tokens : (i + 1) * tokens, lanes]
                highest = jnp.max(x.reshape(tokens // 8, 8, SPAN), axis=0) * factor
                top = highest if top is None else jnp.maximum(top, highest)
            top = jnp.max(top, axis=0, keepdims=True)
            if not first:
                before = stats_in[u, 0:1, lanes]
                top = jnp.maximum(top, before)
                fades.append(jnp.exp2(before - top))
            total = None
            for i, factor in enumerate(factors):
                keys = slice(i * tokens, (i + 1) * tokens)
                weight = jnp.exp2(x_ref[u, keys, lanes] * factor - top)
                p_ref[u, keys, lanes] = weight.astype(jnp.bfloat16)
                part = jnp.sum(weight.reshape(tokens // 8, 8, SPAN), axis=0)
                total = part if total is None else total + part
            total = jnp.sum(total, axis=0, keepdims=True)
            if not first:
                total = total + fades[tile] * stats_in[u, 1:2, lanes]
            tops.append(top)
            totals.append(total)
        both = lax.dot_general(
            v, p_ref[u], (((0,), (0,)), ((), ())), preferred_element_type=jnp.float32
        )
        for tile in range(groups * tokens // SPAN):
            lanes = slice(tile * SPAN, (tile + 1) * SPAN)
            mixed = both[:HEAD_WIDTH, lanes] + both[HEAD_WIDTH:, lanes]
            if not first:
                mixed = mixed + fades[tile] * mixed_in[u, :, lanes]
            if not last:
                result_ref[u, :, lanes] = mixed
                stats_ref[u, 0:1, lanes] = tops[tile]
                stats_ref[u, 1:2, lanes] = totals[tile]
                continue
            mixed = mixed * (1.0 / totals[tile])
            check = jnp.sum(mixed, axis=0, keepdims=True) * inverse_root
            mixed = jnp.transpose(mixed).astype(result_ref.dtype)
            for j in range(SPAN // tokens):
                h = tile * (SPAN // tokens) + j
                at = (u * groups + h) * HEAD_WIDTH
                result_ref[:, at : at + HEAD_WIDTH] = mixed[j * tokens : (j + 1) * tokens]
                check_ref[pl.ds(g * groups + h, 1), :] = check[:, j * tokens : (j + 1) * tokens]
    if last:

        @pl.when(step == pl.num_programs(0) - 1)
        def _():
            stats_ref[...] = jnp.transpose(check_ref[...])


def absorb(queries, chunk, scales, span_order, block_keep, state, last, kv_heads, kv_local, sizes):
    tokens, width = queries.shape
    groups = width // HEAD_WIDTH // kv_heads
    per_step = 2 if kv_heads % 2 == 0 else 1
    pieces = [block for _, _, block in chunk]
    sources = [(flip, shift) for flip, shift, _ in chunk]
    keys = tokens * len(chunk)
    first = state is None
    rows = groups * tokens
    columns = pl.BlockSpec((tokens, per_step * groups * HEAD_WIDTH), lambda s: (0, s))
    mixed = pl.BlockSpec((per_step, HEAD_WIDTH, rows), lambda s: (s, 0, 0))
    stats = pl.BlockSpec((per_step, 2, rows), lambda s: (s, 0, 0))
    smem = pl.BlockSpec(memory_space=pltpu.SMEM)
    in_specs = [smem, smem] + [pl.BlockSpec(memory_space=pl.ANY)] * len(scales)
    in_specs += [pl.BlockSpec(piece.shape, lambda s: (0, 0)) for piece in pieces]
    in_specs += [columns] + ([] if first else [mixed, stats])
    if last:
        out_specs = [columns, pl.BlockSpec((tokens, kv_heads * groups), lambda s: (0, 0))]
        out_shape = [
            jax.ShapeDtypeStruct((tokens, width), jnp.bfloat16),
            jax.ShapeDtypeStruct((tokens, kv_heads * groups), jnp.float32),
        ]
    else:
        out_specs = [mixed, stats]
        out_shape = [
            jax.ShapeDtypeStruct((kv_heads, HEAD_WIDTH, rows), jnp.float32),
            jax.ShapeDtypeStruct((kv_heads, 2, rows), jnp.float32),
        ]
    return pl.pallas_call(
        functools.partial(
            absorb_kernel,
            groups=groups,
            per_step=per_step,
            kv_local=kv_local,
            sources=sources,
            ctx_size=sizes[0],
            head_size=sizes[1],
            first=first,
            last=last,
        ),
        grid=(kv_heads // per_step,),
        in_specs=in_specs,
        out_specs=out_specs,
        out_shape=out_shape,
        scratch_shapes=[
            pltpu.SMEM((len(scales),) + scales[0].shape, jnp.float32),
            pltpu.VMEM((keys, SPAN), jnp.bfloat16),
            pltpu.VMEM((per_step, keys, rows), jnp.float32),
            pltpu.VMEM((per_step, keys, rows), jnp.bfloat16),
            pltpu.VMEM((kv_heads * groups, tokens), jnp.float32),
            pltpu.SemaphoreType.DMA((len(scales),)),
        ],
        compiler_params=pltpu.CompilerParams(vmem_limit_bytes=32 * 1024 * 1024),
        cost_estimate=pl.CostEstimate(
            flops=16 * tokens * width * keys,
            bytes_accessed=16 * tokens * width,
            transcendentals=tokens * width // HEAD_WIDTH * keys,
        ),
    )(span_order, block_keep, *scales, *pieces, queries, *(() if first else state))


def local(queries, keys, values, key_scale, value_scale, span_order, block_keep):
    tokens, width = queries.shape
    kv_heads = keys.shape[1] // HEAD_WIDTH
    ctx_size, head_size = lax.axis_size("ctx"), lax.axis_size("head")
    levels = ctx_size.bit_length() - 1
    batch = 2 * SPAN // tokens

    def along_head(block, distance):
        return lax.ppermute(block, "head", [(i, (i + distance) % head_size) for i in range(head_size)])

    def across_ctx(block, flip):
        return lax.ppermute(block, "ctx", [(i, i ^ flip) for i in range(ctx_size)])

    def attend(chunk, state, last):
        return absorb(
            queries,
            chunk,
            scales,
            span_order,
            block_keep,
            state,
            last,
            kv_heads,
            key_scale.shape[1],
            (ctx_size, head_size),
        )

    block, scale = pack(keys, values, key_scale, value_scale)
    arrived = [(0, 0, -1, block)]
    waiting, state, scales = [(0, 0, block)], None, [scale]
    while arrived:
        coming = []
        for flip, shift, level, block in arrived:
            if level < 0 and shift + 1 < head_size:
                coming.append((flip, shift + 1, level, along_head(block, 1)))
            for later in range(level + 1, levels):
                bit = ctx_size >> (later + 1)
                coming.append((flip ^ bit, shift, later, across_ctx(block, bit)))
        complete = len(scales) == head_size
        for shift in range(len(scales), min(head_size, len(scales) + head_size // 2)):
            scales = scales + [along_head(scale, shift)]
        ready = len(waiting) // batch * batch if complete else 0
        if ready:
            state = attend(waiting[:ready], state, not coming)
            waiting = waiting[ready:]
        if coming:
            blocks = [block for _, _, _, block in coming]
            blocks, state, scales = lax.optimization_barrier((blocks, state, scales))
            coming = [(f, s, l, b) for (f, s, l, _), b in zip(coming, blocks)]
        waiting += [(f, s, b) for f, s, _, b in coming]
        arrived = coming
    attended, row_check = state
    return attended, row_check


def solution(mesh):
    rows = P(("dp", "ctx", "head"), None)
    return jax.shard_map(
        local,
        mesh=mesh,
        in_specs=(rows, rows, rows, P("dp", "head"), P("dp", "head"), P(), P()),
        out_specs=(rows, rows),
        check_vma=False,
    )
```

time: 81.1 us -> 68 us (0.84)
  Pallas kernels: 50.6 us -> 27.9 us
  waiting for transfers between devices: 10.5 us -> 17 us
  starting transfers between devices: 13.1 us -> 15.2 us
  local copies, waits for them, and re-layouts: 5.9 us -> 6.91 us
    pallas_call x4 -> x3, Pallas kernels: 50.6 us -> 18.6 us  [absorb(): pl.pallas_call(functools.partial(absorb_kernel, groups=groups, per_step=p...]
    pallas_call x0 -> x1, Pallas kernels: none -> 9.32 us  [pack(): pl.pallas_call(pack_kernel, in_specs=[anywhere] * 4, out_specs=[anywhere]...]
    ppermute x12, waiting for transfers between devices: 2.16 us -> 5.91 us  [across_ctx(): return lax.ppermute(block, 'ctx', [(i, i ^ flip) for i in range(ctx_size)])]
    ppermute x6, waiting for transfers between devices: 8.32 us -> 11 us  [along_head(): lax.ppermute(block, 'head', [(i, (i + distance) % head_size) for i in ran...]
    ppermute x6, starting transfers between devices: 5.7 us -> 8.21 us  [along_head(): lax.ppermute(block, 'head', [(i, (i + distance) % head_size) for i in ran...]
    unnamed x11 -> x20, local copies, waits for them, and re-layouts: 4.99 us -> 6.91 us
    concatenate x1 -> x0, local copies, waits for them, and re-layouts: 0.92 us -> none  [local(): block = jnp.concatenate([keys, values], axis=1)]
  transfers between devices with their start and end apart: 18 -> 18, of which waited for: 6 -> 6; matrix products, arithmetic and copies ran while one was open for 2% -> 0% of each run, Pallas kernels for 39% -> 18%
where the time goes in v1:
time: 68 us; the launch traced here: 67.7 us
  Pallas kernels  27.9 us (41%)
  waiting for transfers between devices  17 us (25%)
  starting transfers between devices  15.2 us (22%)
  local copies, waits for them, and re-layouts  6.91 us (10%)
  between operations  0.75 us (1%)
    pallas_call x3, Pallas kernels, absorb(): pl.pallas_call(functools.partial(absorb_kernel, groups=groups, per_step=p...  18.6 us
    ppermute x6, waiting for transfers between devices, along_head(): lax.ppermute(block, 'head', [(i, (i + distance) % head_size) for i in ran...  11 us
    pallas_call x1, Pallas kernels, pack(): pl.pallas_call(pack_kernel, in_specs=[anywhere] * 4, out_specs=[anywhere]...  9.32 us
    ppermute x6, starting transfers between devices, along_head(): lax.ppermute(block, 'head', [(i, (i + distance) % head_size) for i in ran...  8.21 us
    ppermute x12, starting transfers between devices, across_ctx(): return lax.ppermute(block, 'ctx', [(i, i ^ flip) for i in range(ctx_size)])  7.02 us
    unnamed x20, local copies, waits for them, and re-layouts  6.91 us
    ppermute x12, waiting for transfers between devices, across_ctx(): return lax.ppermute(block, 'ctx', [(i, i ^ flip) for i in range(ctx_size)])  5.91 us
  transfers between devices with their start and end apart: 18, of which 6 were waited for; matrix products, arithmetic and copies ran while one was open for 0% of the time, Pallas kernels for 18%

profile of v1, /device:TPU:0, one launch (start us, length us, event | category | flops | bytes accessed | tf_op | source)
XLA Modules:
  0.0 67.7 jit_solution(15682804845807665742)
XLA Ops:
  0.6 1.3 %copy.9.key_scale_ref = f32[8,2]{1,0:T(8,128)} copy(f32[8,2]{0,1:T(2,128)} %param.10) | data formatting | bytes 128 | tf_op args[3]
  2.0 1.3 %copy.10.value_scale_ref = f32[8,2]{1,0:T(8,128)} copy(f32[8,2]{0,1:T(2,128)} %param.11) | data formatting | bytes 128 | tf_op args[4]
  3.3 9.3 %shard_map.86 = (bf16[128,1024]{1,0:T(8,128)(2,1)}, f32[2,8,2]{2,1,0:T(8,128)}) custom-call(bf16[64,1024]{1,0:T(8,128)(2,1)} %k_ref.1, bf16[64,1024]{1,0:T(8,128)(2,1)} %v_ref.1, f32[8,2]{1,0:T(8,128)} %copy.9.key_scale_ref, f32[8,2]{1,0:T(8,128)} %copy.10.value_scale_ref), custom_call_target="tpu_custom_call" | custom-call | tf_op jit(solution)/shard_map/pallas_call | solution.py:34
  12.6 0.5 collective-permute-start.2
  13.2 2.6 %collective-permute-start.1 = (bf16[128,1024]{1,0:T(8,128)(2,1)}, bf16[128,1024]{1,0:T(8,128)(2,1)S(1)}, u32[]{:S(2)}, u32[]{:S(2)}) collective-permute-start(bf16[128,1024]{1,0:T(8,128)(2,1)} %get-tuple-element.48.refs_4_), channel_id=1, source_target_pairs={{0,16},{8,24},{16,0},{24,8},{1,17},{9,25},{17,1},{25,9},{2,18},{10... | collective-permute-start | bytes 786440 | tf_op jit(solution)/shard_map/ppermute | solution.py:245
  15.8 1.6 %collective-permute-start = (bf16[128,1024]{1,0:T(8,128)(2,1)}, bf16[128,1024]{1,0:T(8,128)(2,1)S(1)}, u32[]{:S(2)}, u32[]{:S(2)}) collective-permute-start(bf16[128,1024]{1,0:T(8,128)(2,1)} %get-tuple-element.48.refs_4_), channel_id=1, source_target_pairs={{0,2},{2,4},{4,6},{6,0},{1,3},{3,5},{5,7},{7,1},{8,10},{10,12},{12... | collective-permute-start | bytes 786440 | tf_op jit(solution)/shard_map/ppermute | solution.py:242
  17.3 2.6 %collective-permute-start.4 = (f32[2,8,2]{2,1,0:T(8,128)}, f32[2,8,2]{2,1,0:T(8,128)S(1)}, u32[]{:S(2)}, u32[]{:S(2)}) collective-permute-start(f32[2,8,2]{2,1,0:T(8,128)} %get-tuple-element.85.refs_0_), channel_id=1, source_target_pairs={{0,4},{2,6},{4,0},{6,2},{1,5},{3,7},{5,1},{7,3},{8,12},{10,14},{12... | collective-permute-start | bytes 392 | tf_op jit(solution)/shard_map/ppermute | solution.py:242
  19.9 0.2 collective-permute-start.3
  20.2 6.6 %collective-permute-done.4.refs_2_ = f32[2,8,2]{2,1,0:T(8,128)S(1)} collective-permute-done((f32[2,8,2]{2,1,0:T(8,128)}, f32[2,8,2]{2,1,0:T(8,128)S(1)}, u32[]{:S(2)}, u32[]{:S(2)}) %collective-permute-start.4) | collective-permute-done | bytes 160 | tf_op jit(solution)/shard_map/ppermute | solution.py:242
  26.8 0.0 collective-permute-done.3.refs_1_
  26.8 0.0 collective-permute-done.2.refs_7_
  26.8 0.0 collective-permute-done.1.refs_6_
  26.8 0.0 collective-permute-done.refs_5_
  26.8 0.1 collective-permute-start.8
  26.9 0.5 collective-permute-start.7
  27.4 0.5 collective-permute-start.6
  27.9 0.4 collective-permute-start.5
  28.3 3.4 %collective-permute-start.9 = (f32[2,8,2]{2,1,0:T(8,128)}, f32[2,8,2]{2,1,0:T(8,128)S(1)}, u32[]{:S(2)}, u32[]{:S(2)}) collective-permute-start(f32[2,8,2]{2,1,0:T(8,128)} %get-tuple-element.85.refs_0_), channel_id=1, source_target_pairs={{0,6},{2,0},{4,2},{6,4},{1,7},{3,1},{5,3},{7,5},{8,14},{10,8},{12,... | collective-permute-start | bytes 392 | tf_op jit(solution)/shard_map/ppermute | solution.py:242
  31.7 2.3 %collective-permute-done.9.refs_3_ = f32[2,8,2]{2,1,0:T(8,128)S(1)} collective-permute-done((f32[2,8,2]{2,1,0:T(8,128)}, f32[2,8,2]{2,1,0:T(8,128)S(1)}, u32[]{:S(2)}, u32[]{:S(2)}) %collective-permute-start.9) | collective-permute-done | bytes 160 | tf_op jit(solution)/shard_map/ppermute | solution.py:242
  34.0 0.0 collective-permute-done.8.refs_11_
  34.0 0.0 collective-permute-done.7.refs_10_
  34.0 1.7 %collective-permute-done.6.refs_9_ = bf16[128,1024]{1,0:T(8,128)(2,1)S(1)} collective-permute-done((bf16[128,1024]{1,0:T(8,128)(2,1)S(1)}, bf16[128,1024]{1,0:T(8,128)(2,1)S(1)}, u32[]{:S(2)}, u32[]{:S(2)}) %collective-permute-start.6) | collective-permute-done | bytes 262176 | tf_op jit(solution)/shard_map/ppermute | solution.py:245
  35.7 2.1 %collective-permute-done.5.refs_8_ = bf16[128,1024]{1,0:T(8,128)(2,1)S(1)} collective-permute-done((bf16[128,1024]{1,0:T(8,128)(2,1)S(1)}, bf16[128,1024]{1,0:T(8,128)(2,1)S(1)}, u32[]{:S(2)}, u32[]{:S(2)}) %collective-permute-start.5) | collective-permute-done | bytes 262176 | tf_op jit(solution)/shard_map/ppermute | solution.py:242
  37.8 0.0 collective-permute-start.12
  37.8 1.5 %collective-permute-start.11 = (bf16[128,1024]{1,0:T(8,128)(2,1)S(1)}, bf16[128,1024]{1,0:T(8,128)(2,1)S(1)}, u32[]{:S(2)}, u32[]{:S(2)}) collective-permute-start(bf16[128,1024]{1,0:T(8,128)(2,1)S(1)} %collective-permute-done.5.refs_8_), channel_id=1, source_target_pairs={{0,16},{8,24},{16,0},{24,8},{1,17},{9,25},{17,1},{25,9},{2,18},{10... | collective-permute-start | bytes 786440 | tf_op jit(solution)/shard_map/ppermute | solution.py:245
  39.3 0.0 collective-permute-start.10
  39.3 0.2 collective-permute-start.13
  39.6 1.2 %copy-done = bf16[64,8192]{1,0:T(8,128)(2,1)S(1)} copy-done((bf16[64,8192]{1,0:T(8,128)(2,1)S(1)}, bf16[64,8192]{1,0:T(8,128)(2,1)}, u32[]{:S(2)}) %copy-start) | copy-done | bytes 1048600
  40.8 0.9 %copy-done.2 = bf16[128,1024]{1,0:T(8,128)(2,1)S(1)} copy-done((bf16[128,1024]{1,0:T(8,128)(2,1)S(1)}, bf16[128,1024]{1,0:T(8,128)(2,1)}, u32[]{:S(2)}) %copy-start.2) | copy-done | bytes 262168
  41.7 0.7 %copy-done.3 = f32[2,8,2]{2,1,0:T(8,128)S(1)} copy-done((f32[2,8,2]{2,1,0:T(8,128)S(1)}, f32[2,8,2]{2,1,0:T(8,128)}, u32[]{:S(2)}) %copy-start.3) | copy-done | bytes 152
  42.4 0.7 %copy-done.5 = s32[8,8]{1,0:T(8,128)S(1)} copy-done((s32[8,8]{1,0:T(8,128)S(1)}, s32[8,8]{1,0:T(8,128)}, u32[]{:S(2)}) %copy-start.5) | copy-done | bytes 280
  43.1 0.7 copy-done.7
  43.8 6.9 %shard_map.87 = (f32[8,128,512]{2,1,0:T(8,128)S(1)}, f32[8,2,512]{2,1,0:T(2,128)S(1)}) custom-call(s32[8]{0:T(128)S(1)} %copy-done.7, s32[8,8]{1,0:T(8,128)S(1)} %copy-done.5, f32[2,8,2]{2,1,0:T(8,128)S(1)} %copy-done.3, f32[2,8,2]{2,1,0:T(8,128)S(1)} %collective-permute-done.3.refs_1_, f32[2,8,2]{2,1,0:T(8,128)S(1)} %collective-permute-done.4.refs_2_, ...), custom_call_target="tpu_custom_call" | custom-call | flops 4294967296 | bytes 8388608 | tf_op jit(solution)/shard_map/pallas_call | solution.py:201
  50.7 0.0 collective-permute-done.13.refs_7_
  50.7 0.0 collective-permute-done.12.refs_6_
  50.8 0.0 collective-permute-done.11.refs_5_
  50.8 0.0 collective-permute-done.10.refs_4_
  50.8 0.3 collective-permute-start.16
  51.1 0.2 collective-permute-start.15
  51.3 0.5 collective-permute-start.14
  51.9 0.0 copy-done.1
  51.9 5.3 %shard_map.88 = (f32[8,128,512]{2,1,0:T(8,128)S(1)}, f32[8,2,512]{2,1,0:T(2,128)S(1)}) custom-call(s32[8]{0:T(128)S(1)} %copy-done.8, s32[8,8]{1,0:T(8,128)S(1)} %copy-done.6, f32[2,8,2]{2,1,0:T(8,128)S(1)} %copy-done.4, f32[2,8,2]{2,1,0:T(8,128)S(1)} %collective-permute-done.3.refs_1_, f32[2,8,2]{2,1,0:T(8,128)S(1)} %collective-permute-done.4.refs_2_, ...), custom_call_target="tpu_custom_call" | custom-call | flops 2147483648 | bytes 8388608 | tf_op jit(solution)/shard_map/pallas_call | solution.py:201
  57.1 0.0 collective-permute-done.16.refs_6_
  57.1 0.0 collective-permute-done.15.refs_5_
  57.2 2.7 %collective-permute-done.14.refs_4_ = bf16[128,1024]{1,0:T(8,128)(2,1)S(1)} collective-permute-done((bf16[128,1024]{1,0:T(8,128)(2,1)S(1)}, bf16[128,1024]{1,0:T(8,128)(2,1)S(1)}, u32[]{:S(2)}, u32[]{:S(2)}) %collective-permute-start.14) | collective-permute-done | bytes 262176 | tf_op jit(solution)/shard_map/ppermute | solution.py:245
  59.8 0.0 collective-permute-start.17
  59.8 1.5 %collective-permute-done.17.refs_7_ = bf16[128,1024]{1,0:T(8,128)(2,1)S(1)} collective-permute-done((bf16[128,1024]{1,0:T(8,128)(2,1)S(1)}, bf16[128,1024]{1,0:T(8,128)(2,1)S(1)}, u32[]{:S(2)}, u32[]{:S(2)}) %collective-permute-start.17) | collective-permute-done | bytes 262176 | tf_op jit(solution)/shard_map/ppermute | solution.py:245
  61.4 6.4 %shard_map.89 = (bf16[64,8192]{1,0:T(8,128)(2,1)}, f32[64,64]{1,0:T(8,128)}) custom-call(s32[8]{0:T(128)S(1)} %copy-done.8, s32[8,8]{1,0:T(8,128)S(1)} %copy-done.6, f32[2,8,2]{2,1,0:T(8,128)S(1)} %copy-done.4, f32[2,8,2]{2,1,0:T(8,128)S(1)} %collective-permute-done.3.refs_1_, f32[2,8,2]{2,1,0:T(8,128)S(1)} %collective-permute-done.4.refs_2_, ...), custom_call_target="tpu_custom_call" | custom-call | flops 2147483648 | bytes 8388608 | tf_op jit(solution)/shard_map/pallas_call | solution.py:201
  (12 shorter events, 0.0 us)
Async XLA Ops:
  3.3 48.5 %copy-start.6 = (s32[8,8]{1,0:T(8,128)S(1)}, s32[8,8]{1,0:T(8,128)}, u32[]{:S(2)}) copy-start(s32[8,8]{1,0:T(8,128)} %keep_ref.5) | copy-start | bytes 772
  12.6 14.1 %collective-permute-start.2 = (bf16[128,1024]{1,0:T(8,128)(2,1)}, bf16[128,1024]{1,0:T(8,128)(2,1)S(1)}, u32[]{:S(2)}, u32[]{:S(2)}) collective-permute-start(bf16[128,1024]{1,0:T(8,128)(2,1)} %get-tuple-element.48.refs_4_), channel_id=1, source_target_pairs={{0,8},{8,0},{16,24},{24,16},{1,9},{9,1},{17,25},{25,17},{2,10},{10... | collective-permute-start | bytes 786440 | tf_op jit(solution)/shard_map/ppermute | solution.py:245
  13.2 13.6 %collective-permute-start.1 = (bf16[128,1024]{1,0:T(8,128)(2,1)}, bf16[128,1024]{1,0:T(8,128)(2,1)S(1)}, u32[]{:S(2)}, u32[]{:S(2)}) collective-permute-start(bf16[128,1024]{1,0:T(8,128)(2,1)} %get-tuple-element.48.refs_4_), channel_id=1, source_target_pairs={{0,16},{8,24},{16,0},{24,8},{1,17},{9,25},{17,1},{25,9},{2,18},{10... | collective-permute-start | bytes 786440 | tf_op jit(solution)/shard_map/ppermute | solution.py:245
  15.8 11.0 %collective-permute-start = (bf16[128,1024]{1,0:T(8,128)(2,1)}, bf16[128,1024]{1,0:T(8,128)(2,1)S(1)}, u32[]{:S(2)}, u32[]{:S(2)}) collective-permute-start(bf16[128,1024]{1,0:T(8,128)(2,1)} %get-tuple-element.48.refs_4_), channel_id=1, source_target_pairs={{0,2},{2,4},{4,6},{6,0},{1,3},{3,5},{5,7},{7,1},{8,10},{10,12},{12... | collective-permute-start | bytes 786440 | tf_op jit(solution)/shard_map/ppermute | solution.py:242
  17.3 34.5 %copy-start.8 = (s32[8]{0:T(128)S(1)}, s32[8]{0:T(128)}, u32[]{:S(2)}) copy-start(s32[8]{0:T(128)} %order_ref.5) | copy-start | bytes 100
  17.3 9.4 %collective-permute-start.4 = (f32[2,8,2]{2,1,0:T(8,128)}, f32[2,8,2]{2,1,0:T(8,128)S(1)}, u32[]{:S(2)}, u32[]{:S(2)}) collective-permute-start(f32[2,8,2]{2,1,0:T(8,128)} %get-tuple-element.85.refs_0_), channel_id=1, source_target_pairs={{0,4},{2,6},{4,0},{6,2},{1,5},{3,7},{5,1},{7,3},{8,12},{10,14},{12... | collective-permute-start | bytes 392 | tf_op jit(solution)/shard_map/ppermute | solution.py:242
  19.9 6.8 %collective-permute-start.3 = (f32[2,8,2]{2,1,0:T(8,128)}, f32[2,8,2]{2,1,0:T(8,128)S(1)}, u32[]{:S(2)}, u32[]{:S(2)}) collective-permute-start(f32[2,8,2]{2,1,0:T(8,128)} %get-tuple-element.85.refs_0_), channel_id=1, source_target_pairs={{0,2},{2,4},{4,6},{6,0},{1,3},{3,5},{5,7},{7,1},{8,10},{10,12},{12... | collective-permute-start | bytes 392 | tf_op jit(solution)/shard_map/ppermute | solution.py:242
  26.8 7.2 %collective-permute-start.8 = (bf16[128,1024]{1,0:T(8,128)(2,1)S(1)}, bf16[128,1024]{1,0:T(8,128)(2,1)S(1)}, u32[]{:S(2)}, u32[]{:S(2)}) collective-permute-start(bf16[128,1024]{1,0:T(8,128)(2,1)S(1)} %collective-permute-done.1.refs_6_), channel_id=1, source_target_pairs={{0,8},{8,0},{16,24},{24,16},{1,9},{9,1},{17,25},{25,17},{2,10},{10... | collective-permute-start | bytes 786440 | tf_op jit(solution)/shard_map/ppermute | solution.py:245
  26.9 7.1 %collective-permute-start.7 = (bf16[128,1024]{1,0:T(8,128)(2,1)S(1)}, bf16[128,1024]{1,0:T(8,128)(2,1)S(1)}, u32[]{:S(2)}, u32[]{:S(2)}) collective-permute-start(bf16[128,1024]{1,0:T(8,128)(2,1)S(1)} %collective-permute-done.refs_5_), channel_id=1, source_target_pairs={{0,8},{8,0},{16,24},{24,16},{1,9},{9,1},{17,25},{25,17},{2,10},{10... | collective-permute-start | bytes 786440 | tf_op jit(solution)/shard_map/ppermute | solution.py:245
  27.4 8.3 %collective-permute-start.6 = (bf16[128,1024]{1,0:T(8,128)(2,1)S(1)}, bf16[128,1024]{1,0:T(8,128)(2,1)S(1)}, u32[]{:S(2)}, u32[]{:S(2)}) collective-permute-start(bf16[128,1024]{1,0:T(8,128)(2,1)S(1)} %collective-permute-done.refs_5_), channel_id=1, source_target_pairs={{0,16},{8,24},{16,0},{24,8},{1,17},{9,25},{17,1},{25,9},{2,18},{10... | collective-permute-start | bytes 786440 | tf_op jit(solution)/shard_map/ppermute | solution.py:245
  27.9 9.9 %collective-permute-start.5 = (bf16[128,1024]{1,0:T(8,128)(2,1)S(1)}, bf16[128,1024]{1,0:T(8,128)(2,1)S(1)}, u32[]{:S(2)}, u32[]{:S(2)}) collective-permute-start(bf16[128,1024]{1,0:T(8,128)(2,1)S(1)} %collective-permute-done.refs_5_), channel_id=1, source_target_pairs={{0,2},{2,4},{4,6},{6,0},{1,3},{3,5},{5,7},{7,1},{8,10},{10,12},{12... | collective-permute-start | bytes 786440 | tf_op jit(solution)/shard_map/ppermute | solution.py:242
  28.3 5.7 %collective-permute-start.9 = (f32[2,8,2]{2,1,0:T(8,128)}, f32[2,8,2]{2,1,0:T(8,128)S(1)}, u32[]{:S(2)}, u32[]{:S(2)}) collective-permute-start(f32[2,8,2]{2,1,0:T(8,128)} %get-tuple-element.85.refs_0_), channel_id=1, source_target_pairs={{0,6},{2,0},{4,2},{6,4},{1,7},{3,1},{5,3},{7,5},{8,14},{10,8},{12,... | collective-permute-start | bytes 392 | tf_op jit(solution)/shard_map/ppermute | solution.py:242
  37.8 12.9 %collective-permute-start.12 = (bf16[128,1024]{1,0:T(8,128)(2,1)S(1)}, bf16[128,1024]{1,0:T(8,128)(2,1)S(1)}, u32[]{:S(2)}, u32[]{:S(2)}) collective-permute-start(bf16[128,1024]{1,0:T(8,128)(2,1)S(1)} %collective-permute-done.5.refs_8_), channel_id=1, source_target_pairs={{0,8},{8,0},{16,24},{24,16},{1,9},{9,1},{17,25},{25,17},{2,10},{10... | collective-permute-start | bytes 786440 | tf_op jit(solution)/shard_map/ppermute | solution.py:245
  37.8 13.0 %collective-permute-start.11 = (bf16[128,1024]{1,0:T(8,128)(2,1)S(1)}, bf16[128,1024]{1,0:T(8,128)(2,1)S(1)}, u32[]{:S(2)}, u32[]{:S(2)}) collective-permute-start(bf16[128,1024]{1,0:T(8,128)(2,1)S(1)} %collective-permute-done.5.refs_8_), channel_id=1, source_target_pairs={{0,16},{8,24},{16,0},{24,8},{1,17},{9,25},{17,1},{25,9},{2,18},{10... | collective-permute-start | bytes 786440 | tf_op jit(solution)/shard_map/ppermute | solution.py:245
  39.3 11.4 %collective-permute-start.10 = (bf16[128,1024]{1,0:T(8,128)(2,1)S(1)}, bf16[128,1024]{1,0:T(8,128)(2,1)S(1)}, u32[]{:S(2)}, u32[]{:S(2)}) collective-permute-start(bf16[128,1024]{1,0:T(8,128)(2,1)S(1)} %collective-permute-done.5.refs_8_), channel_id=1, source_target_pairs={{0,2},{2,4},{4,6},{6,0},{1,3},{3,5},{5,7},{7,1},{8,10},{10,12},{12... | collective-permute-start | bytes 786440 | tf_op jit(solution)/shard_map/ppermute | solution.py:242
  39.3 11.4 %collective-permute-start.13 = (bf16[128,1024]{1,0:T(8,128)(2,1)S(1)}, bf16[128,1024]{1,0:T(8,128)(2,1)S(1)}, u32[]{:S(2)}, u32[]{:S(2)}) collective-permute-start(bf16[128,1024]{1,0:T(8,128)(2,1)S(1)} %collective-permute-done.6.refs_9_), channel_id=1, source_target_pairs={{0,8},{8,0},{16,24},{24,16},{1,9},{9,1},{17,25},{25,17},{2,10},{10... | collective-permute-start | bytes 786440 | tf_op jit(solution)/shard_map/ppermute | solution.py:245
  39.6 1.2 %copy-start = (bf16[64,8192]{1,0:T(8,128)(2,1)S(1)}, bf16[64,8192]{1,0:T(8,128)(2,1)}, u32[]{:S(2)}) copy-start(bf16[64,8192]{1,0:T(8,128)(2,1)} %refs_8_.3) | copy-start | bytes 3145732
  40.8 0.9 %copy-start.2 = (bf16[128,1024]{1,0:T(8,128)(2,1)S(1)}, bf16[128,1024]{1,0:T(8,128)(2,1)}, u32[]{:S(2)}) copy-start(bf16[128,1024]{1,0:T(8,128)(2,1)} %get-tuple-element.48.refs_4_) | copy-start | bytes 786436
  41.7 0.7 %copy-start.3 = (f32[2,8,2]{2,1,0:T(8,128)S(1)}, f32[2,8,2]{2,1,0:T(8,128)}, u32[]{:S(2)}) copy-start(f32[2,8,2]{2,1,0:T(8,128)} %get-tuple-element.85.refs_0_) | copy-start | bytes 388
  42.4 0.7 %copy-start.5 = (s32[8,8]{1,0:T(8,128)S(1)}, s32[8,8]{1,0:T(8,128)}, u32[]{:S(2)}) copy-start(s32[8,8]{1,0:T(8,128)} %keep_ref.5) | copy-start | bytes 772
  43.1 0.7 copy-start.7
  43.8 8.1 %copy-start.1 = (bf16[64,8192]{1,0:T(8,128)(2,1)S(1)}, bf16[64,8192]{1,0:T(8,128)(2,1)}, u32[]{:S(2)}) copy-start(bf16[64,8192]{1,0:T(8,128)(2,1)} %refs_8_.3) | copy-start | bytes 3145732
  43.8 8.1 %copy-start.4 = (f32[2,8,2]{2,1,0:T(8,128)S(1)}, f32[2,8,2]{2,1,0:T(8,128)}, u32[]{:S(2)}) copy-start(f32[2,8,2]{2,1,0:T(8,128)} %get-tuple-element.85.refs_0_) | copy-start | bytes 388
  50.8 6.4 %collective-permute-start.16 = (bf16[128,1024]{1,0:T(8,128)(2,1)S(1)}, bf16[128,1024]{1,0:T(8,128)(2,1)S(1)}, u32[]{:S(2)}, u32[]{:S(2)}) collective-permute-start(bf16[128,1024]{1,0:T(8,128)(2,1)S(1)} %collective-permute-done.11.refs_5_), channel_id=1, source_target_pairs={{0,8},{8,0},{16,24},{24,16},{1,9},{9,1},{17,25},{25,17},{2,10},{10... | collective-permute-start | bytes 786440 | tf_op jit(solution)/shard_map/ppermute | solution.py:245
  51.1 6.0 %collective-permute-start.15 = (bf16[128,1024]{1,0:T(8,128)(2,1)S(1)}, bf16[128,1024]{1,0:T(8,128)(2,1)S(1)}, u32[]{:S(2)}, u32[]{:S(2)}) collective-permute-start(bf16[128,1024]{1,0:T(8,128)(2,1)S(1)} %collective-permute-done.10.refs_4_), channel_id=1, source_target_pairs={{0,8},{8,0},{16,24},{24,16},{1,9},{9,1},{17,25},{25,17},{2,10},{10... | collective-permute-start | bytes 786440 | tf_op jit(solution)/shard_map/ppermute | solution.py:245
  51.3 8.5 %collective-permute-start.14 = (bf16[128,1024]{1,0:T(8,128)(2,1)S(1)}, bf16[128,1024]{1,0:T(8,128)(2,1)S(1)}, u32[]{:S(2)}, u32[]{:S(2)}) collective-permute-start(bf16[128,1024]{1,0:T(8,128)(2,1)S(1)} %collective-permute-done.10.refs_4_), channel_id=1, source_target_pairs={{0,16},{8,24},{16,0},{24,8},{1,17},{9,25},{17,1},{25,9},{2,18},{10... | collective-permute-start | bytes 786440 | tf_op jit(solution)/shard_map/ppermute | solution.py:245
  59.8 1.5 %collective-permute-start.17 = (bf16[128,1024]{1,0:T(8,128)(2,1)S(1)}, bf16[128,1024]{1,0:T(8,128)(2,1)S(1)}, u32[]{:S(2)}, u32[]{:S(2)}) collective-permute-start(bf16[128,1024]{1,0:T(8,128)(2,1)S(1)} %collective-permute-done.14.refs_4_), channel_id=1, source_target_pairs={{0,8},{8,0},{16,24},{24,16},{1,9},{9,1},{17,25},{25,17},{2,10},{10... | collective-permute-start | bytes 786440 | tf_op jit(solution)/shard_map/ppermute | solution.py:245

commit v2 on v1

v2 whole, which is shorter than its diff:
```python
import functools
import math

import jax
import jax.numpy as jnp
from jax import lax
from jax.experimental import pallas as pl
from jax.experimental.pallas import tpu as pltpu
from jax.sharding import PartitionSpec as P

HEAD_WIDTH = 128
SPAN = 128
LOG2E = 1.4426950408889634
MASKED = -1e30


def prepare_kernel(order_ref, keep_ref, *refs, groups, per_step, kv_local, sources, ctx_size, head_size):
    refs = list(refs)
    scale_in = [refs.pop(0) for _ in range(head_size)]
    q_ref, qa_ref, mask_ref, key_scale_ref, value_scale_ref, scale_ref, scale_sem = refs
    step = pl.program_id(0)
    tokens = q_ref.shape[0]
    inverse_root = 1.0 / math.sqrt(HEAD_WIDTH)
    ctx, head = lax.axis_index("ctx"), lax.axis_index("head")
    starts = [
        ((ctx ^ flip) * head_size + lax.rem(head - shift + head_size, head_size)) * tokens
        for flip, shift in sources
    ]
    spans = [start // SPAN for start in starts]
    row = lax.broadcasted_iota(jnp.int32, (tokens, SPAN), 0)
    lane = lax.broadcasted_iota(jnp.int32, (tokens, SPAN), 1)

    @pl.when(step == 0)
    def _():
        copies = []
        for shift in range(head_size):
            owner = lax.rem(head - shift + head_size, head_size)
            copies.append(
                pltpu.make_async_copy(scale_in[shift], scale_ref.at[owner], scale_sem.at[shift])
            )
        for copy in copies:
            copy.start()
        own_start = (ctx * head_size + head) * tokens
        own = own_start // SPAN
        for i, (start, span) in enumerate(zip(starts, spans)):
            seen = (order_ref[span] < order_ref[own]) & (keep_ref[own, span] > 0)
            whole = jnp.where(seen, 0.0, MASKED)
            causal = jnp.where(row + (start - own_start) <= lane, 0.0, MASKED)
            mask = jnp.where(own == span, causal, whole)
            mask_ref[i * tokens : (i + 1) * tokens, :] = mask.astype(jnp.bfloat16)
        for copy in copies:
            copy.wait()

    one_hot = jnp.where(row == lane, 1.0, 0.0).astype(jnp.bfloat16)
    for u in range(per_step):
        g = step * per_step + u
        owner, member = g // kv_local, g % kv_local
        for h in range(groups):
            at = (u * groups + h) * HEAD_WIDTH
            qa_ref[u, h * tokens : (h + 1) * tokens, :HEAD_WIDTH] = q_ref[:, at : at + HEAD_WIDTH]
            qa_ref[u, h * tokens : (h + 1) * tokens, HEAD_WIDTH:] = one_hot
        for i, span in enumerate(spans):
            factor = scale_ref[owner, member, span] * (inverse_root * LOG2E)
            key_scale_ref[u, i : i + 1, :] = jnp.full((1, SPAN), factor, jnp.float32)
            factor = scale_ref[owner, kv_local + member, span]
            value_scale_ref[u, i : i + 1, :] = jnp.full((1, SPAN), factor, jnp.float32)


def prepare(queries, scales, span_order, block_keep, sources, kv_heads, kv_local, sizes):
    tokens, width = queries.shape
    groups = width // HEAD_WIDTH // kv_heads
    per_step = 2 if kv_heads % 2 == 0 else 1
    rows = groups * tokens
    smem = pl.BlockSpec(memory_space=pltpu.SMEM)
    scale_rows = pl.BlockSpec((per_step, len(sources), SPAN), lambda s: (s, 0, 0))
    return pl.pallas_call(
        functools.partial(
            prepare_kernel,
            groups=groups,
            per_step=per_step,
            kv_local=kv_local,
            sources=sources,
            ctx_size=sizes[0],
            head_size=sizes[1],
        ),
        grid=(kv_heads // per_step,),
        in_specs=[smem, smem]
        + [pl.BlockSpec(memory_space=pl.ANY)] * len(scales)
        + [pl.BlockSpec((tokens, per_step * groups * HEAD_WIDTH), lambda s: (0, s))],
        out_specs=[
            pl.BlockSpec((per_step, rows, HEAD_WIDTH + SPAN), lambda s: (s, 0, 0)),
            pl.BlockSpec((tokens * len(sources), SPAN), lambda s: (0, 0)),
            scale_rows,
            scale_rows,
        ],
        out_shape=[
            jax.ShapeDtypeStruct((kv_heads, rows, HEAD_WIDTH + SPAN), jnp.bfloat16),
            jax.ShapeDtypeStruct((tokens * len(sources), SPAN), jnp.bfloat16),
            jax.ShapeDtypeStruct((kv_heads, len(sources), SPAN), jnp.float32),
            jax.ShapeDtypeStruct((kv_heads, len(sources), SPAN), jnp.float32),
        ],
        scratch_shapes=[
            pltpu.SMEM((len(scales),) + scales[0].shape, jnp.float32),
            pltpu.SemaphoreType.DMA((len(scales),)),
        ],
        compiler_params=pltpu.CompilerParams(vmem_limit_bytes=32 * 1024 * 1024),
        cost_estimate=pl.CostEstimate(
            flops=8 * tokens * width, bytes_accessed=16 * tokens * width, transcendentals=0
        ),
    )(span_order, block_keep, *scales, queries)


def absorb_kernel(*refs, groups, tokens, per_step, begin, count, first, last):
    refs = list(refs)
    pieces = [refs.pop(0) for _ in range(count)]
    qa_ref, mask_ref, key_scale_ref, value_scale_ref = [refs.pop(0) for _ in range(4)]
    mixed_in, stats_in = (None, None) if first else (refs.pop(0), refs.pop(0))
    result_ref, stats_ref, x_ref, p_ref, check_ref = refs
    step = pl.program_id(0)
    inverse_root = 1.0 / math.sqrt(HEAD_WIDTH)
    for u in range(per_step):
        g = step * per_step + u
        cols = pl.ds(pl.multiple_of(g * HEAD_WIDTH, HEAD_WIDTH), HEAD_WIDTH)
        k = jnp.concatenate([piece[:tokens, cols] for piece in pieces], axis=0)
        k = jnp.concatenate([k, mask_ref[begin * tokens : (begin + count) * tokens, :]], axis=1)
        x_ref[u] = lax.dot_general(
            k, qa_ref[u], (((1,), (1,)), ((), ())), preferred_element_type=jnp.float32
        )
    for u in range(per_step):
        g = step * per_step + u
        cols = pl.ds(pl.multiple_of(g * HEAD_WIDTH, HEAD_WIDTH), HEAD_WIDTH)
        factors = [key_scale_ref[u, begin + i : begin + i + 1, :] for i in range(count)]
        high, low = [], []
        for i, piece in enumerate(pieces):
            factor = value_scale_ref[u, begin + i : begin + i + 1, :]
            v = piece[tokens:, cols].astype(jnp.float32) * factor
            high.append(v.astype(jnp.bfloat16))
            low.append((v - high[-1].astype(jnp.float32)).astype(jnp.bfloat16))
        v = jnp.concatenate(
            [jnp.concatenate(high, axis=0), jnp.concatenate(low, axis=0)], axis=1
        )
        tops, totals, fades = [], [], []
        for tile in range(groups * tokens // SPAN):
            lanes = slice(tile * SPAN, (tile + 1) * SPAN)
            top = None
            for i, factor in enumerate(factors):
                x = x_ref[u, i * tokens : (i + 1) * tokens, lanes]
                highest = jnp.max(x.reshape(tokens // 8, 8, SPAN), axis=0) * factor
                top = highest if top is None else jnp.maximum(top, highest)
            top = jnp.max(top, axis=0, keepdims=True)
            if not first:
                before = stats_in[u, 0:1, lanes]
                top = jnp.maximum(top, before)
                fades.append(jnp.exp2(before - top))
            total = None
            for i, factor in enumerate(factors):
                keys = slice(i * tokens, (i + 1) * tokens)
                weight = jnp.exp2(x_ref[u, keys, lanes] * factor - top)
                p_ref[u, keys, lanes] = weight.astype(jnp.bfloat16)
                part = jnp.sum(weight.reshape(tokens // 8, 8, SPAN), axis=0)
                total = part if total is None else total + part
            total = jnp.sum(total, axis=0, keepdims=True)
            if not first:
                total = total + fades[tile] * stats_in[u, 1:2, lanes]
            tops.append(top)
            totals.append(total)
        both = lax.dot_general(
            v, p_ref[u], (((0,), (0,)), ((), ())), preferred_element_type=jnp.float32
        )
        for tile in range(groups * tokens // SPAN):
            lanes = slice(tile * SPAN, (tile + 1) * SPAN)
            mixed = both[:HEAD_WIDTH, lanes] + both[HEAD_WIDTH:, lanes]
            if not first:
                mixed = mixed + fades[tile] * mixed_in[u, :, lanes]
            if not last:
                result_ref[u, :, lanes] = mixed
                stats_ref[u, 0:1, lanes] = tops[tile]
                stats_ref[u, 1:2, lanes] = totals[tile]
                continue
            mixed = mixed * (1.0 / totals[tile])
            check = jnp.sum(mixed, axis=0, keepdims=True) * inverse_root
            mixed = jnp.transpose(mixed).astype(result_ref.dtype)
            for j in range(SPAN // tokens):
                h = tile * (SPAN // tokens) + j
                at = (u * groups + h) * HEAD_WIDTH
                result_ref[:, at : at + HEAD_WIDTH] = mixed[j * tokens : (j + 1) * tokens]
                check_ref[pl.ds(g * groups + h, 1), :] = check[:, j * tokens : (j + 1) * tokens]
    if last:

        @pl.when(step == pl.num_programs(0) - 1)
        def _():
            stats_ref[...] = jnp.transpose(check_ref[...])


def absorb(prepared, pieces, begin, state, last, tokens):
    kv_heads, rows, depth = prepared[0].shape
    groups = rows // tokens
    count = len(pieces)
    per_step = 2 if kv_heads % 2 == 0 else 1
    keys = tokens * count
    width = kv_heads * groups * HEAD_WIDTH
    first = state is None
    mixed = pl.BlockSpec((per_step, HEAD_WIDTH, rows), lambda s: (s, 0, 0))
    stats = pl.BlockSpec((per_step, 2, rows), lambda s: (s, 0, 0))
    scale_rows = pl.BlockSpec((per_step,) + prepared[2].shape[1:], lambda s: (s, 0, 0))
    in_specs = [pl.BlockSpec(piece.shape, lambda s: (0, 0)) for piece in pieces]
    in_specs += [
        pl.BlockSpec((per_step, rows, depth), lambda s: (s, 0, 0)),
        pl.BlockSpec(prepared[1].shape, lambda s: (0, 0)),
        scale_rows,
        scale_rows,
    ]
    in_specs += [] if first else [mixed, stats]
    if last:
        out_specs = [
            pl.BlockSpec((tokens, per_step * groups * HEAD_WIDTH), lambda s: (0, s)),
            pl.BlockSpec((tokens, kv_heads * groups), lambda s: (0, 0)),
        ]
        out_shape = [
            jax.ShapeDtypeStruct((tokens, width), jnp.bfloat16),
            jax.ShapeDtypeStruct((tokens, kv_heads * groups), jnp.float32),
        ]
    else:
        out_specs = [mixed, stats]
        out_shape = [
            jax.ShapeDtypeStruct((kv_heads, HEAD_WIDTH, rows), jnp.float32),
            jax.ShapeDtypeStruct((kv_heads, 2, rows), jnp.float32),
        ]
    return pl.pallas_call(
        functools.partial(
            absorb_kernel,
            groups=groups,
            tokens=tokens,
            per_step=per_step,
            begin=begin,
            count=count,
            first=first,
            last=last,
        ),
        grid=(kv_heads // per_step,),
        in_specs=in_specs,
        out_specs=out_specs,
        out_shape=out_shape,
        scratch_shapes=[
            pltpu.VMEM((per_step, keys, rows), jnp.float32),
            pltpu.VMEM((per_step, keys, rows), jnp.bfloat16),
            pltpu.VMEM((kv_heads * groups, tokens), jnp.float32),
        ],
        compiler_params=pltpu.CompilerParams(vmem_limit_bytes=32 * 1024 * 1024),
        cost_estimate=pl.CostEstimate(
            flops=16 * tokens * width * keys,
            bytes_accessed=16 * tokens * width,
            transcendentals=tokens * width // HEAD_WIDTH * keys,
        ),
    )(*pieces, *prepared, *(() if first else state))


def local(queries, keys, values, key_scale, value_scale, span_order, block_keep):
    tokens = queries.shape[0]
    kv_heads = keys.shape[1] // HEAD_WIDTH
    ctx_size, head_size = lax.axis_size("ctx"), lax.axis_size("head")
    levels = ctx_size.bit_length() - 1
    batch = 2 * SPAN // tokens

    def along_head(block, distance):
        return lax.ppermute(block, "head", [(i, (i + distance) % head_size) for i in range(head_size)])

    def across_ctx(block, flip):
        return lax.ppermute(block, "ctx", [(i, i ^ flip) for i in range(ctx_size)])

    plan, arrived = [[(0, 0, -1)]], [(0, 0, -1)]
    while arrived:
        coming = []
        for index, (flip, shift, level) in enumerate(arrived):
            if level < 0 and shift + 1 < head_size:
                coming.append((flip, shift + 1, level, index, 0))
            for later in range(level + 1, levels):
                bit = ctx_size >> (later + 1)
                coming.append((flip ^ bit, shift, later, index, bit))
        if coming:
            plan.append(coming)
        arrived = [source[:3] for source in coming]
    sources = [source[:2] for phase in plan for source in phase]

    scale = jnp.concatenate([jnp.transpose(key_scale), jnp.transpose(value_scale)], axis=0)
    scales = [scale] + [along_head(scale, shift) for shift in range(1, head_size)]
    block = jnp.concatenate([keys, values], axis=0)
    block, scales = lax.optimization_barrier((block, scales))
    arrived, pieces, done = [block], [block], 0
    prepared, state = None, None
    for phase, routes in enumerate(plan[1:]):
        coming = [
            across_ctx(arrived[index], bit) if bit else along_head(arrived[index], 1)
            for _, _, _, index, bit in routes
        ]
        if phase == 0:
            prepared = prepare(
                queries,
                scales,
                span_order,
                block_keep,
                sources,
                kv_heads,
                key_scale.shape[1],
                (ctx_size, head_size),
            )
        elif phase > 1:
            ready = (len(pieces) - done) // batch * batch
            if ready:
                state = absorb(prepared, pieces[done : done + ready], done, state, False, tokens)
                done += ready
        arrived, prepared, state = lax.optimization_barrier((coming, prepared, state))
        pieces = pieces + list(arrived)
    return tuple(absorb(prepared, pieces[done:], done, state, True, tokens))


def solution(mesh):
    rows = P(("dp", "ctx", "head"), None)
    return jax.shard_map(
        local,
        mesh=mesh,
        in_specs=(rows, rows, rows, P("dp", "head"), P("dp", "head"), P(), P()),
        out_specs=(rows, rows),
        check_vma=False,
    )
```

time: 68 us -> 60.9 us (0.90)
  Pallas kernels: 27.9 us -> 15.1 us
  waiting for transfers between devices: 17 us -> 29.2 us
  local copies, waits for them, and re-layouts: 6.91 us -> 2.57 us
  starting transfers between devices: 15.2 us -> 11.4 us
  other arithmetic: 0 us -> 1.69 us
    pallas_call x4, Pallas kernels: 27.9 us -> 15.1 us  [the longest x3 12.5 us: absorb(): pl.pallas_call(functools.partial(absorb_kernel, groups=groups, tokens=tok...]
    ppermute x12, waiting for transfers between devices: 5.91 us -> 17.7 us  [across_ctx(): return lax.ppermute(block, 'ctx', [(i, i ^ flip) for i in range(ctx_size)])]
    unnamed x20 -> x6, local copies, waits for them, and re-layouts: 6.91 us -> 2.57 us
    ppermute x6, starting transfers between devices: 8.21 us -> 6.07 us  [along_head(): lax.ppermute(block, 'head', [(i, (i + distance) % head_size) for i in ran...]
    ppermute x12, starting transfers between devices: 7.02 us -> 5.31 us  [across_ctx(): return lax.ppermute(block, 'ctx', [(i, i ^ flip) for i in range(ctx_size)])]
    concatenate x0 -> x2, other arithmetic: none -> 1.69 us  [the longest x1 0.99 us: local(): block = jnp.concatenate([keys, values], axis=0)]
  transfers between devices with their start and end apart: 18 -> 18, of which waited for: 6 -> 12; matrix products, arithmetic and copies ran while one was open for 0% -> 2% of each run, Pallas kernels for 18% -> 18%
where the time goes in v2:
time: 60.9 us; the launch traced here: 60.7 us
  waiting for transfers between devices  29.2 us (48%)
  Pallas kernels  15.1 us (25%)
  starting transfers between devices  11.4 us (19%)
  local copies, waits for them, and re-layouts  2.57 us (4%)
  other arithmetic  1.69 us (3%)
  between operations  0.72 us (1%)
    ppermute x12, waiting for transfers between devices, across_ctx(): return lax.ppermute(block, 'ctx', [(i, i ^ flip) for i in range(ctx_size)])  17.7 us
    pallas_call x3, Pallas kernels, absorb(): pl.pallas_call(functools.partial(absorb_kernel, groups=groups, tokens=tok...  12.5 us
    ppermute x6, waiting for transfers between devices, along_head(): lax.ppermute(block, 'head', [(i, (i + distance) % head_size) for i in ran...  11.5 us
    ppermute x6, starting transfers between devices, along_head(): lax.ppermute(block, 'head', [(i, (i + distance) % head_size) for i in ran...  6.07 us
    ppermute x12, starting transfers between devices, across_ctx(): return lax.ppermute(block, 'ctx', [(i, i ^ flip) for i in range(ctx_size)])  5.31 us
    pallas_call x1, Pallas kernels, prepare(): pl.pallas_call(functools.partial(prepare_kernel, groups=groups, per_step=...  2.65 us
    unnamed x6, local copies, waits for them, and re-layouts  2.57 us
  transfers between devices with their start and end apart: 18, of which 12 were waited for; matrix products, arithmetic and copies ran while one was open for 2% of the time, Pallas kernels for 18%

profile of v2, /device:TPU:0, one launch (start us, length us, event | category | flops | bytes accessed | tf_op | source)
XLA Modules:
  0.0 60.7 jit_solution(4432980463565292594)
XLA Ops:
  0.6 0.7 %pad_maximum_fusion.1.refs_0_ = f32[4,8]{1,0:T(4,128)S(1)} fusion(f32[2,8]{1,0:T(2,128)} %bitcast.2, f32[2,8]{1,0:T(2,128)} %bitcast.3), kind=kLoop, calls=%fused_computation.1 | loop fusion | flops 32 | bytes 256 | tf_op jit(solution)/shard_map/concatenate | solution.py:285
  1.3 5.0 %collective-permute-start.2 = (f32[4,8]{1,0:T(4,128)S(1)}, f32[4,8]{1,0:T(4,128)S(1)}, u32[]{:S(2)}, u32[]{:S(2)}) collective-permute-start(f32[4,8]{1,0:T(4,128)S(1)} %pad_maximum_fusion.1.refs_0_), channel_id=1, source_target_pairs={{0,6},{2,0},{4,2},{6,4},{1,7},{3,1},{5,3},{7,5},{8,14},{10,8},{12,... | collective-permute-start | bytes 392 | tf_op jit(solution)/shard_map/ppermute | solution.py:266
  6.4 0.0 collective-permute-start.1
  6.4 1.0 %collective-permute-start = (f32[4,8]{1,0:T(4,128)S(1)}, f32[4,8]{1,0:T(4,128)S(1)}, u32[]{:S(2)}, u32[]{:S(2)}) collective-permute-start(f32[4,8]{1,0:T(4,128)S(1)} %pad_maximum_fusion.1.refs_0_), channel_id=1, source_target_pairs={{0,2},{2,4},{4,6},{6,0},{1,3},{3,5},{5,7},{7,1},{8,10},{10,12},{12... | collective-permute-start | bytes 392 | tf_op jit(solution)/shard_map/ppermute | solution.py:266
  7.4 1.0 %pad_maximum_fusion.refs_0_ = bf16[128,1024]{1,0:T(8,128)(2,1)S(1)} fusion(bf16[64,1024]{1,0:T(8,128)(2,1)} %param.9, bf16[64,1024]{1,0:T(8,128)(2,1)} %param.8), kind=kLoop, calls=%fused_computation | loop fusion | flops 524288 | bytes 524288 | tf_op jit(solution)/shard_map/concatenate | solution.py:287
  8.4 0.0 collective-permute-done.2.refs_3_
  8.4 2.5 %collective-permute-done.1.refs_2_ = f32[4,8]{1,0:T(4,128)S(1)} collective-permute-done((f32[4,8]{1,0:T(4,128)S(1)}, f32[4,8]{1,0:T(4,128)S(1)}, u32[]{:S(2)}, u32[]{:S(2)}) %collective-permute-start.1) | collective-permute-done | bytes 160 | tf_op jit(solution)/shard_map/ppermute | solution.py:266
  10.9 0.9 %collective-permute-done.refs_1_ = f32[4,8]{1,0:T(4,128)S(1)} collective-permute-done((f32[4,8]{1,0:T(4,128)S(1)}, f32[4,8]{1,0:T(4,128)S(1)}, u32[]{:S(2)}, u32[]{:S(2)}) %collective-permute-start) | collective-permute-done | bytes 160 | tf_op jit(solution)/shard_map/ppermute | solution.py:266
  11.8 0.0 collective-permute-start.5
  11.8 1.5 %collective-permute-start.4 = (bf16[128,1024]{1,0:T(8,128)(2,1)S(1)}, bf16[128,1024]{1,0:T(8,128)(2,1)S(1)}, u32[]{:S(2)}, u32[]{:S(2)}) collective-permute-start(bf16[128,1024]{1,0:T(8,128)(2,1)S(1)} %pad_maximum_fusion.refs_0_), channel_id=1, source_target_pairs={{0,16},{8,24},{16,0},{24,8},{1,17},{9,25},{17,1},{25,9},{2,18},{10... | collective-permute-start | bytes 786440 | tf_op jit(solution)/shard_map/ppermute | solution.py:269
  13.3 0.0 collective-permute-start.3
  13.3 0.0 copy-start
  13.3 1.2 %copy-done = bf16[64,8192]{1,0:T(8,128)(2,1)S(1)} copy-done((bf16[64,8192]{1,0:T(8,128)(2,1)S(1)}, bf16[64,8192]{1,0:T(8,128)(2,1)}, u32[]{:S(2)}) %copy-start) | copy-done | bytes 1048600
  14.5 0.0 copy-start.1
  14.5 0.7 %copy-done.1 = s32[8,8]{1,0:T(8,128)S(1)} copy-done((s32[8,8]{1,0:T(8,128)S(1)}, s32[8,8]{1,0:T(8,128)}, u32[]{:S(2)}) %copy-start.1) | copy-done | bytes 280
  15.2 0.0 copy-start.2
  15.2 0.7 %copy-done.2 = s32[8]{0:T(128)S(1)} copy-done((s32[8]{0:T(128)S(1)}, s32[8]{0:T(128)}, u32[]{:S(2)}) %copy-start.2) | copy-done | bytes 56
  15.9 2.7 %shard_map.86 = (bf16[8,512,256]{2,1,0:T(8,128)(2,1)S(1)}, bf16[1024,128]{1,0:T(8,128)(2,1)S(1)}, f32[8,16,128]{2,1,0:T(8,128)S(1)}, f32[8,16,128]{2,1,0:T(8,128)S(1)}) custom-call(s32[8]{0:T(128)S(1)} %copy-done.2, s32[8,8]{1,0:T(8,128)S(1)} %copy-done.1, f32[4,8]{1,0:T(4,128)S(1)} %pad_maximum_fusion.1.refs_0_, f32[4,8]{1,0:T(4,128)S(1)} %collective-permute-done.refs_1_, ...), custom_call_target="tpu_custom_call" | custom-call | flops 4194304 | bytes 8388608 | tf_op jit(solution)/shard_map/pallas_call | solution.py:76
  18.5 0.0 collective-permute-done.5.refs_3_
  18.5 2.0 %collective-permute-done.4.refs_2_ = bf16[128,1024]{1,0:T(8,128)(2,1)S(1)} collective-permute-done((bf16[128,1024]{1,0:T(8,128)(2,1)S(1)}, bf16[128,1024]{1,0:T(8,128)(2,1)S(1)}, u32[]{:S(2)}, u32[]{:S(2)}) %collective-permute-start.4) | collective-permute-done | bytes 262176 | tf_op jit(solution)/shard_map/ppermute | solution.py:269
  20.5 3.0 %collective-permute-done.3.refs_1_ = bf16[128,1024]{1,0:T(8,128)(2,1)S(1)} collective-permute-done((bf16[128,1024]{1,0:T(8,128)(2,1)S(1)}, bf16[128,1024]{1,0:T(8,128)(2,1)S(1)}, u32[]{:S(2)}, u32[]{:S(2)}) %collective-permute-start.3) | collective-permute-done | bytes 262176 | tf_op jit(solution)/shard_map/ppermute | solution.py:266
  23.5 0.0 collective-permute-start.9
  23.5 0.5 collective-permute-start.8
  24.0 0.5 collective-permute-start.7
  24.5 0.0 collective-permute-start.6
  24.6 0.5 collective-permute-done.9.refs_7_
  25.1 0.4 collective-permute-done.8.refs_6_
  25.4 6.8 %collective-permute-done.7.refs_5_ = bf16[128,1024]{1,0:T(8,128)(2,1)S(1)} collective-permute-done((bf16[128,1024]{1,0:T(8,128)(2,1)S(1)}, bf16[128,1024]{1,0:T(8,128)(2,1)S(1)}, u32[]{:S(2)}, u32[]{:S(2)}) %collective-permute-start.7) | collective-permute-done | bytes 262176 | tf_op jit(solution)/shard_map/ppermute | solution.py:269
  32.3 2.0 %collective-permute-done.6.refs_4_ = bf16[128,1024]{1,0:T(8,128)(2,1)S(1)} collective-permute-done((bf16[128,1024]{1,0:T(8,128)(2,1)S(1)}, bf16[128,1024]{1,0:T(8,128)(2,1)S(1)}, u32[]{:S(2)}, u32[]{:S(2)}) %collective-permute-start.6) | collective-permute-done | bytes 262176 | tf_op jit(solution)/shard_map/ppermute | solution.py:266
  34.3 0.0 collective-permute-start.12
  34.3 1.5 %collective-permute-start.11 = (bf16[128,1024]{1,0:T(8,128)(2,1)S(1)}, bf16[128,1024]{1,0:T(8,128)(2,1)S(1)}, u32[]{:S(2)}, u32[]{:S(2)}) collective-permute-start(bf16[128,1024]{1,0:T(8,128)(2,1)S(1)} %collective-permute-done.6.refs_4_), channel_id=1, source_target_pairs={{0,16},{8,24},{16,0},{24,8},{1,17},{9,25},{17,1},{25,9},{2,18},{10... | collective-permute-start | bytes 786440 | tf_op jit(solution)/shard_map/ppermute | solution.py:269
  35.8 0.0 collective-permute-start.10
  35.8 0.2 collective-permute-start.13
  36.0 4.9 %shard_map.87 = (f32[8,128,512]{2,1,0:T(8,128)S(1)}, f32[8,2,512]{2,1,0:T(2,128)S(1)}) custom-call(bf16[128,1024]{1,0:T(8,128)(2,1)S(1)} %pad_maximum_fusion.refs_0_, bf16[128,1024]{1,0:T(8,128)(2,1)S(1)} %collective-permute-done.3.refs_1_, bf16[128,1024]{1,0:T(8,128)(2,1)S(1)} %collective-permute-done.4.refs_2_, ...), custom_call_target="tpu_custom_call" | custom-call | flops 4294967296 | bytes 8388608 | tf_op jit(solution)/shard_map/pallas_call | solution.py:229
  41.0 0.0 collective-permute-done.13.refs_3_
  41.0 0.0 collective-permute-done.12.refs_2_
  41.0 2.0 %collective-permute-done.11.refs_1_ = bf16[128,1024]{1,0:T(8,128)(2,1)S(1)} collective-permute-done((bf16[128,1024]{1,0:T(8,128)(2,1)S(1)}, bf16[128,1024]{1,0:T(8,128)(2,1)S(1)}, u32[]{:S(2)}, u32[]{:S(2)}) %collective-permute-start.11) | collective-permute-done | bytes 262176 | tf_op jit(solution)/shard_map/ppermute | solution.py:269
  43.0 3.0 %collective-permute-done.10.refs_0_ = bf16[128,1024]{1,0:T(8,128)(2,1)S(1)} collective-permute-done((bf16[128,1024]{1,0:T(8,128)(2,1)S(1)}, bf16[128,1024]{1,0:T(8,128)(2,1)S(1)}, u32[]{:S(2)}, u32[]{:S(2)}) %collective-permute-start.10) | collective-permute-done | bytes 262176 | tf_op jit(solution)/shard_map/ppermute | solution.py:266
  46.0 0.0 collective-permute-start.16
  46.0 0.5 collective-permute-start.15
  46.6 0.5 collective-permute-start.14
  47.1 3.2 %shard_map.88 = (f32[8,128,512]{2,1,0:T(8,128)S(1)}, f32[8,2,512]{2,1,0:T(2,128)S(1)}) custom-call(bf16[128,1024]{1,0:T(8,128)(2,1)S(1)} %collective-permute-done.10.refs_0_, bf16[128,1024]{1,0:T(8,128)(2,1)S(1)} %collective-permute-done.11.refs_1_, bf16[128,1024]{1,0:T(8,128)(2,1)S(1)} %collective-permute-done.12.refs_2_, ...), custom_call_target="tpu_custom_call" | custom-call | flops 2147483648 | bytes 8388608 | tf_op jit(solution)/shard_map/pallas_call | solution.py:229
  50.3 0.0 collective-permute-done.16.refs_2_
  50.3 0.0 collective-permute-done.15.refs_1_
  50.3 4.5 %collective-permute-done.14.refs_0_ = bf16[128,1024]{1,0:T(8,128)(2,1)S(1)} collective-permute-done((bf16[128,1024]{1,0:T(8,128)(2,1)S(1)}, bf16[128,1024]{1,0:T(8,128)(2,1)S(1)}, u32[]{:S(2)}, u32[]{:S(2)}) %collective-permute-start.14) | collective-permute-done | bytes 262176 | tf_op jit(solution)/shard_map/ppermute | solution.py:269
  54.8 0.0 collective-permute-start.17
  54.8 1.5 %collective-permute-done.17.refs_3_ = bf16[128,1024]{1,0:T(8,128)(2,1)S(1)} collective-permute-done((bf16[128,1024]{1,0:T(8,128)(2,1)S(1)}, bf16[128,1024]{1,0:T(8,128)(2,1)S(1)}, u32[]{:S(2)}, u32[]{:S(2)}) %collective-permute-start.17) | collective-permute-done | bytes 262176 | tf_op jit(solution)/shard_map/ppermute | solution.py:269
  56.3 4.4 %shard_map.89 = (bf16[64,8192]{1,0:T(8,128)(2,1)}, f32[64,64]{1,0:T(8,128)}) custom-call(bf16[128,1024]{1,0:T(8,128)(2,1)S(1)} %collective-permute-done.14.refs_0_, bf16[128,1024]{1,0:T(8,128)(2,1)S(1)} %collective-permute-done.15.refs_1_, bf16[128,1024]{1,0:T(8,128)(2,1)S(1)} %collective-permute-done.16.refs_2_, ...), custom_call_target="tpu_custom_call" | custom-call | flops 2147483648 | bytes 8388608 | tf_op jit(solution)/shard_map/pallas_call | solution.py:229
Async XLA Ops:
  1.3 7.1 %collective-permute-start.2 = (f32[4,8]{1,0:T(4,128)S(1)}, f32[4,8]{1,0:T(4,128)S(1)}, u32[]{:S(2)}, u32[]{:S(2)}) collective-permute-start(f32[4,8]{1,0:T(4,128)S(1)} %pad_maximum_fusion.1.refs_0_), channel_id=1, source_target_pairs={{0,6},{2,0},{4,2},{6,4},{1,7},{3,1},{5,3},{7,5},{8,14},{10,8},{12,... | collective-permute-start | bytes 392 | tf_op jit(solution)/shard_map/ppermute | solution.py:266
  6.4 4.5 %collective-permute-start.1 = (f32[4,8]{1,0:T(4,128)S(1)}, f32[4,8]{1,0:T(4,128)S(1)}, u32[]{:S(2)}, u32[]{:S(2)}) collective-permute-start(f32[4,8]{1,0:T(4,128)S(1)} %pad_maximum_fusion.1.refs_0_), channel_id=1, source_target_pairs={{0,4},{2,6},{4,0},{6,2},{1,5},{3,7},{5,1},{7,3},{8,12},{10,14},{12... | collective-permute-start | bytes 392 | tf_op jit(solution)/shard_map/ppermute | solution.py:266
  6.4 5.4 %collective-permute-start = (f32[4,8]{1,0:T(4,128)S(1)}, f32[4,8]{1,0:T(4,128)S(1)}, u32[]{:S(2)}, u32[]{:S(2)}) collective-permute-start(f32[4,8]{1,0:T(4,128)S(1)} %pad_maximum_fusion.1.refs_0_), channel_id=1, source_target_pairs={{0,2},{2,4},{4,6},{6,0},{1,3},{3,5},{5,7},{7,1},{8,10},{10,12},{12... | collective-permute-start | bytes 392 | tf_op jit(solution)/shard_map/ppermute | solution.py:266
  11.8 6.8 %collective-permute-start.5 = (bf16[128,1024]{1,0:T(8,128)(2,1)S(1)}, bf16[128,1024]{1,0:T(8,128)(2,1)S(1)}, u32[]{:S(2)}, u32[]{:S(2)}) collective-permute-start(bf16[128,1024]{1,0:T(8,128)(2,1)S(1)} %pad_maximum_fusion.refs_0_), channel_id=1, source_target_pairs={{0,8},{8,0},{16,24},{24,16},{1,9},{9,1},{17,25},{25,17},{2,10},{10... | collective-permute-start | bytes 786440 | tf_op jit(solution)/shard_map/ppermute | solution.py:269
  11.8 8.7 %collective-permute-start.4 = (bf16[128,1024]{1,0:T(8,128)(2,1)S(1)}, bf16[128,1024]{1,0:T(8,128)(2,1)S(1)}, u32[]{:S(2)}, u32[]{:S(2)}) collective-permute-start(bf16[128,1024]{1,0:T(8,128)(2,1)S(1)} %pad_maximum_fusion.refs_0_), channel_id=1, source_target_pairs={{0,16},{8,24},{16,0},{24,8},{1,17},{9,25},{17,1},{25,9},{2,18},{10... | collective-permute-start | bytes 786440 | tf_op jit(solution)/shard_map/ppermute | solution.py:269
  13.3 10.2 %collective-permute-start.3 = (bf16[128,1024]{1,0:T(8,128)(2,1)S(1)}, bf16[128,1024]{1,0:T(8,128)(2,1)S(1)}, u32[]{:S(2)}, u32[]{:S(2)}) collective-permute-start(bf16[128,1024]{1,0:T(8,128)(2,1)S(1)} %pad_maximum_fusion.refs_0_), channel_id=1, source_target_pairs={{0,2},{2,4},{4,6},{6,0},{1,3},{3,5},{5,7},{7,1},{8,10},{10,12},{12... | collective-permute-start | bytes 786440 | tf_op jit(solution)/shard_map/ppermute | solution.py:266
  13.3 1.2 %copy-start = (bf16[64,8192]{1,0:T(8,128)(2,1)S(1)}, bf16[64,8192]{1,0:T(8,128)(2,1)}, u32[]{:S(2)}) copy-start(bf16[64,8192]{1,0:T(8,128)(2,1)} %refs_4_.1) | copy-start | bytes 3145732
  14.5 0.7 %copy-start.1 = (s32[8,8]{1,0:T(8,128)S(1)}, s32[8,8]{1,0:T(8,128)}, u32[]{:S(2)}) copy-start(s32[8,8]{1,0:T(8,128)} %keep_ref.1) | copy-start | bytes 772
  15.2 0.7 %copy-start.2 = (s32[8]{0:T(128)S(1)}, s32[8]{0:T(128)}, u32[]{:S(2)}) copy-start(s32[8]{0:T(128)} %order_ref.1) | copy-start | bytes 100
  23.5 1.5 %collective-permute-start.9 = (bf16[128,1024]{1,0:T(8,128)(2,1)S(1)}, bf16[128,1024]{1,0:T(8,128)(2,1)S(1)}, u32[]{:S(2)}, u32[]{:S(2)}) collective-permute-start(bf16[128,1024]{1,0:T(8,128)(2,1)S(1)} %collective-permute-done.4.refs_2_), channel_id=1, source_target_pairs={{0,8},{8,0},{16,24},{24,16},{1,9},{9,1},{17,25},{25,17},{2,10},{10... | collective-permute-start | bytes 786440 | tf_op jit(solution)/shard_map/ppermute | solution.py:269
  23.5 1.9 %collective-permute-start.8 = (bf16[128,1024]{1,0:T(8,128)(2,1)S(1)}, bf16[128,1024]{1,0:T(8,128)(2,1)S(1)}, u32[]{:S(2)}, u32[]{:S(2)}) collective-permute-start(bf16[128,1024]{1,0:T(8,128)(2,1)S(1)} %collective-permute-done.3.refs_1_), channel_id=1, source_target_pairs={{0,8},{8,0},{16,24},{24,16},{1,9},{9,1},{17,25},{25,17},{2,10},{10... | collective-permute-start | bytes 786440 | tf_op jit(solution)/shard_map/ppermute | solution.py:269
  24.0 8.2 %collective-permute-start.7 = (bf16[128,1024]{1,0:T(8,128)(2,1)S(1)}, bf16[128,1024]{1,0:T(8,128)(2,1)S(1)}, u32[]{:S(2)}, u32[]{:S(2)}) collective-permute-start(bf16[128,1024]{1,0:T(8,128)(2,1)S(1)} %collective-permute-done.3.refs_1_), channel_id=1, source_target_pairs={{0,16},{8,24},{16,0},{24,8},{1,17},{9,25},{17,1},{25,9},{2,18},{10... | collective-permute-start | bytes 786440 | tf_op jit(solution)/shard_map/ppermute | solution.py:269
  24.5 9.7 %collective-permute-start.6 = (bf16[128,1024]{1,0:T(8,128)(2,1)S(1)}, bf16[128,1024]{1,0:T(8,128)(2,1)S(1)}, u32[]{:S(2)}, u32[]{:S(2)}) collective-permute-start(bf16[128,1024]{1,0:T(8,128)(2,1)S(1)} %collective-permute-done.3.refs_1_), channel_id=1, source_target_pairs={{0,2},{2,4},{4,6},{6,0},{1,3},{3,5},{5,7},{7,1},{8,10},{10,12},{12... | collective-permute-start | bytes 786440 | tf_op jit(solution)/shard_map/ppermute | solution.py:266
  34.3 6.7 %collective-permute-start.12 = (bf16[128,1024]{1,0:T(8,128)(2,1)S(1)}, bf16[128,1024]{1,0:T(8,128)(2,1)S(1)}, u32[]{:S(2)}, u32[]{:S(2)}) collective-permute-start(bf16[128,1024]{1,0:T(8,128)(2,1)S(1)} %collective-permute-done.6.refs_4_), channel_id=1, source_target_pairs={{0,8},{8,0},{16,24},{24,16},{1,9},{9,1},{17,25},{25,17},{2,10},{10... | collective-permute-start | bytes 786440 | tf_op jit(solution)/shard_map/ppermute | solution.py:269
  34.3 8.7 %collective-permute-start.11 = (bf16[128,1024]{1,0:T(8,128)(2,1)S(1)}, bf16[128,1024]{1,0:T(8,128)(2,1)S(1)}, u32[]{:S(2)}, u32[]{:S(2)}) collective-permute-start(bf16[128,1024]{1,0:T(8,128)(2,1)S(1)} %collective-permute-done.6.refs_4_), channel_id=1, source_target_pairs={{0,16},{8,24},{16,0},{24,8},{1,17},{9,25},{17,1},{25,9},{2,18},{10... | collective-permute-start | bytes 786440 | tf_op jit(solution)/shard_map/ppermute | solution.py:269
  35.8 10.2 %collective-permute-start.10 = (bf16[128,1024]{1,0:T(8,128)(2,1)S(1)}, bf16[128,1024]{1,0:T(8,128)(2,1)S(1)}, u32[]{:S(2)}, u32[]{:S(2)}) collective-permute-start(bf16[128,1024]{1,0:T(8,128)(2,1)S(1)} %collective-permute-done.6.refs_4_), channel_id=1, source_target_pairs={{0,2},{2,4},{4,6},{6,0},{1,3},{3,5},{5,7},{7,1},{8,10},{10,12},{12... | collective-permute-start | bytes 786440 | tf_op jit(solution)/shard_map/ppermute | solution.py:266
  35.8 5.2 %collective-permute-start.13 = (bf16[128,1024]{1,0:T(8,128)(2,1)S(1)}, bf16[128,1024]{1,0:T(8,128)(2,1)S(1)}, u32[]{:S(2)}, u32[]{:S(2)}) collective-permute-start(bf16[128,1024]{1,0:T(8,128)(2,1)S(1)} %collective-permute-done.7.refs_5_), channel_id=1, source_target_pairs={{0,8},{8,0},{16,24},{24,16},{1,9},{9,1},{17,25},{25,17},{2,10},{10... | collective-permute-start | bytes 786440 | tf_op jit(solution)/shard_map/ppermute | solution.py:269
  46.0 4.2 %collective-permute-start.16 = (bf16[128,1024]{1,0:T(8,128)(2,1)S(1)}, bf16[128,1024]{1,0:T(8,128)(2,1)S(1)}, u32[]{:S(2)}, u32[]{:S(2)}) collective-permute-start(bf16[128,1024]{1,0:T(8,128)(2,1)S(1)} %collective-permute-done.11.refs_1_), channel_id=1, source_target_pairs={{0,8},{8,0},{16,24},{24,16},{1,9},{9,1},{17,25},{25,17},{2,10},{10... | collective-permute-start | bytes 786440 | tf_op jit(solution)/shard_map/ppermute | solution.py:269
  46.0 4.2 %collective-permute-start.15 = (bf16[128,1024]{1,0:T(8,128)(2,1)S(1)}, bf16[128,1024]{1,0:T(8,128)(2,1)S(1)}, u32[]{:S(2)}, u32[]{:S(2)}) collective-permute-start(bf16[128,1024]{1,0:T(8,128)(2,1)S(1)} %collective-permute-done.10.refs_0_), channel_id=1, source_target_pairs={{0,8},{8,0},{16,24},{24,16},{1,9},{9,1},{17,25},{25,17},{2,10},{10... | collective-permute-start | bytes 786440 | tf_op jit(solution)/shard_map/ppermute | solution.py:269
  46.6 8.2 %collective-permute-start.14 = (bf16[128,1024]{1,0:T(8,128)(2,1)S(1)}, bf16[128,1024]{1,0:T(8,128)(2,1)S(1)}, u32[]{:S(2)}, u32[]{:S(2)}) collective-permute-start(bf16[128,1024]{1,0:T(8,128)(2,1)S(1)} %collective-permute-done.10.refs_0_), channel_id=1, source_target_pairs={{0,16},{8,24},{16,0},{24,8},{1,17},{9,25},{17,1},{25,9},{2,18},{10... | collective-permute-start | bytes 786440 | tf_op jit(solution)/shard_map/ppermute | solution.py:269
  54.8 1.5 %collective-permute-start.17 = (bf16[128,1024]{1,0:T(8,128)(2,1)S(1)}, bf16[128,1024]{1,0:T(8,128)(2,1)S(1)}, u32[]{:S(2)}, u32[]{:S(2)}) collective-permute-start(bf16[128,1024]{1,0:T(8,128)(2,1)S(1)} %collective-permute-done.14.refs_0_), channel_id=1, source_target_pairs={{0,8},{8,0},{16,24},{24,16},{1,9},{9,1},{17,25},{25,17},{2,10},{10... | collective-permute-start | bytes 786440 | tf_op jit(solution)/shard_map/ppermute | solution.py:269

commit v3 on v2

--- a/solution.py
+++ b/solution.py
@@ -110,11 +110,12 @@
     )(span_order, block_keep, *scales, queries)
 
 
-def absorb_kernel(*refs, groups, tokens, per_step, begin, count, first, last):
+def absorb_kernel(*refs, groups, tokens, per_step, begin, count, first, last, head_step, merge):
     refs = list(refs)
     pieces = [refs.pop(0) for _ in range(count)]
     qa_ref, mask_ref, key_scale_ref, value_scale_ref = [refs.pop(0) for _ in range(4)]
     mixed_in, stats_in = (None, None) if first else (refs.pop(0), refs.pop(0))
+    checks_in = (refs.pop(0), refs.pop(0))[1] if merge else None
     result_ref, stats_ref, x_ref, p_ref, check_ref = refs
     step = pl.program_id(0)
     inverse_root = 1.0 / math.sqrt(HEAD_WIDTH)
@@ -184,37 +185,48 @@
                 h = tile * (SPAN // tokens) + j
                 at = (u * groups + h) * HEAD_WIDTH
                 result_ref[:, at : at + HEAD_WIDTH] = mixed[j * tokens : (j + 1) * tokens]
-                check_ref[pl.ds(g * groups + h, 1), :] = check[:, j * tokens : (j + 1) * tokens]
+                check_ref[pl.ds((head_step * per_step + g) * groups + h, 1), :] = check[:, j * tokens : (j + 1) * tokens]
     if last:
 
         @pl.when(step == pl.num_programs(0) - 1)
         def _():
-            stats_ref[...] = jnp.transpose(check_ref[...])
-
-
-def absorb(prepared, pieces, begin, state, last, tokens):
+            lane = lax.broadcasted_iota(jnp.int32, stats_ref.shape, 1)
+            checks = jnp.transpose(check_ref[...])
+            if merge:
+                checks = jnp.where(lane < head_step * per_step * groups, checks_in[...], checks)
+            stats_ref[...] = checks
+
+
+def absorb(prepared, pieces, begin, state, tokens, stream, streams, last, before):
     kv_heads, rows, depth = prepared[0].shape
     groups = rows // tokens
     count = len(pieces)
-    per_step = 2 if kv_heads % 2 == 0 else 1
+    own_heads = kv_heads // streams
+    per_step = 2 if own_heads % 2 == 0 else 1
+    head_step = stream * own_heads // per_step
     keys = tokens * count
     width = kv_heads * groups * HEAD_WIDTH
-    first = state is None
+    first, merge = state is None, before is not None
     mixed = pl.BlockSpec((per_step, HEAD_WIDTH, rows), lambda s: (s, 0, 0))
     stats = pl.BlockSpec((per_step, 2, rows), lambda s: (s, 0, 0))
-    scale_rows = pl.BlockSpec((per_step,) + prepared[2].shape[1:], lambda s: (s, 0, 0))
+    scale_rows = pl.BlockSpec((per_step,) + prepared[2].shape[1:], lambda s: (s + head_step, 0, 0))
+    checks = pl.BlockSpec((tokens, kv_heads * groups), lambda s: (0, 0))
     in_specs = [pl.BlockSpec(piece.shape, lambda s: (0, 0)) for piece in pieces]
     in_specs += [
-        pl.BlockSpec((per_step, rows, depth), lambda s: (s, 0, 0)),
+        pl.BlockSpec((per_step, rows, depth), lambda s: (s + head_step, 0, 0)),
         pl.BlockSpec(prepared[1].shape, lambda s: (0, 0)),
         scale_rows,
         scale_rows,
     ]
     in_specs += [] if first else [mixed, stats]
+    aliases = {}
+    if merge:
+        aliases = {len(in_specs): 0}
+        in_specs += [pl.BlockSpec(memory_space=pl.ANY), checks]
     if last:
         out_specs = [
-            pl.BlockSpec((tokens, per_step * groups * HEAD_WIDTH), lambda s: (0, s)),
-            pl.BlockSpec((tokens, kv_heads * groups), lambda s: (0, 0)),
+            pl.BlockSpec((tokens, per_step * groups * HEAD_WIDTH), lambda s: (0, s + head_step)),
+            checks,
         ]
         out_shape = [
             jax.ShapeDtypeStruct((tokens, width), jnp.bfloat16),
@@ -223,8 +235,8 @@
     else:
         out_specs = [mixed, stats]
         out_shape = [
-            jax.ShapeDtypeStruct((kv_heads, HEAD_WIDTH, rows), jnp.float32),
-            jax.ShapeDtypeStruct((kv_heads, 2, rows), jnp.float32),
+            jax.ShapeDtypeStruct((own_heads, HEAD_WIDTH, rows), jnp.float32),
+            jax.ShapeDtypeStruct((own_heads, 2, rows), jnp.float32),
         ]
     return pl.pallas_call(
         functools.partial(
@@ -236,11 +248,14 @@
             count=count,
             first=first,
             last=last,
+            head_step=head_step,
+            merge=merge,
         ),
-        grid=(kv_heads // per_step,),
+        grid=(own_heads // per_step,),
         in_specs=in_specs,
         out_specs=out_specs,
         out_shape=out_shape,
+        input_output_aliases=aliases,
         scratch_shapes=[
             pltpu.VMEM((per_step, keys, rows), jnp.float32),
             pltpu.VMEM((per_step, keys, rows), jnp.bfloat16),
@@ -248,11 +263,11 @@
         ],
         compiler_params=pltpu.CompilerParams(vmem_limit_bytes=32 * 1024 * 1024),
         cost_estimate=pl.CostEstimate(
-            flops=16 * tokens * width * keys,
-            bytes_accessed=16 * tokens * width,
-            transcendentals=tokens * width // HEAD_WIDTH * keys,
+            flops=16 * tokens * width * keys // streams,
+            bytes_accessed=16 * tokens * width // streams,
+            transcendentals=tokens * width // HEAD_WIDTH * keys // streams,
         ),
-    )(*pieces, *prepared, *(() if first else state))
+    )(*pieces, *prepared, *(() if first else state), *(before if merge else ()))
 
 
 def local(queries, keys, values, key_scale, value_scale, span_order, block_keep):
@@ -284,34 +299,44 @@
 
     scale = jnp.concatenate([jnp.transpose(key_scale), jnp.transpose(value_scale)], axis=0)
     scales = [scale] + [along_head(scale, shift) for shift in range(1, head_size)]
-    block = jnp.concatenate([keys, values], axis=0)
-    block, scales = lax.optimization_barrier((block, scales))
-    arrived, pieces, done = [block], [block], 0
-    prepared, state = None, None
+    streams = 2 if kv_heads % 2 == 0 else 1
+    part = keys.shape[1] // streams
+    cuts = [slice(i * part, (i + 1) * part) for i in range(streams)]
+    blocks = [jnp.concatenate([keys[:, cut], values[:, cut]], axis=0) for cut in cuts]
+    blocks, scales = lax.optimization_barrier((blocks, scales))
+    arrived = [[block] for block in blocks]
+    pieces = [[block] for block in blocks]
+    done, state = [0] * streams, [None] * streams
+    prepared, result = None, None
     for phase, routes in enumerate(plan[1:]):
-        coming = [
-            across_ctx(arrived[index], bit) if bit else along_head(arrived[index], 1)
-            for _, _, _, index, bit in routes
-        ]
-        if phase == 0:
-            prepared = prepare(
-                queries,
-                scales,
-                span_order,
-                block_keep,
-                sources,
-                kv_heads,
-                key_scale.shape[1],
-                (ctx_size, head_size),
-            )
-        elif phase > 1:
-            ready = (len(pieces) - done) // batch * batch
-            if ready:
-                state = absorb(prepared, pieces[done : done + ready], done, state, False, tokens)
-                done += ready
-        arrived, prepared, state = lax.optimization_barrier((coming, prepared, state))
-        pieces = pieces + list(arrived)
-    return tuple(absorb(prepared, pieces[done:], done, state, True, tokens))
+        for i in range(streams):
+            coming = [
+                across_ctx(arrived[i][index], bit) if bit else along_head(arrived[i][index], 1)
+                for _, _, _, index, bit in routes
+            ]
+            if phase == 0 and i == 0:
+                prepared = prepare(
+                    queries,
+                    scales,
+                    span_order,
+                    block_keep,
+                    sources,
+                    kv_heads,
+                    key_scale.shape[1],
+                    (ctx_size, head_size),
+                )
+            elif phase > 1:
+                ready = (len(pieces[i]) - done[i]) // batch * batch
+                if ready:
+                    now = pieces[i][done[i] : done[i] + ready]
+                    state[i] = absorb(prepared, now, done[i], state[i], tokens, i, streams, False, None)
+                    done[i] += ready
+            arrived[i], prepared, state[i] = lax.optimization_barrier((coming, prepared, state[i]))
+            pieces[i] = pieces[i] + list(arrived[i])
+    for i in range(streams):
+        now = pieces[i][done[i] :]
+        result = absorb(prepared, now, done[i], state[i], tokens, i, streams, True, result)
+    return tuple(result)
 
 
 def solution(mesh):

time: 60.9 us -> 59.3 us (0.974)
  waiting for transfers between devices: 29.2 us -> 12.6 us
  starting transfers between devices: 11.4 us -> 24.6 us
  local copies, waits for them, and re-layouts: 2.57 us -> 4.33 us
  other arithmetic: 1.69 us -> 0.72 us
  Pallas kernels: 15.1 us -> 15.9 us
    ppermute x12 -> x24, waiting for transfers between devices: 17.7 us -> 4.56 us  [across_ctx(): return lax.ppermute(block, 'ctx', [(i, i ^ flip) for i in range(ctx_size)])]
    ppermute x12 -> x24, starting transfers between devices: 5.31 us -> 12.3 us  [across_ctx(): return lax.ppermute(block, 'ctx', [(i, i ^ flip) for i in range(ctx_size)])]
    ppermute x6 -> x9, starting transfers between devices: 6.07 us -> 12.3 us  [along_head(): lax.ppermute(block, 'head', [(i, (i + distance) % head_size) for i in ran...]
    ppermute x6 -> x9, waiting for transfers between devices: 11.5 us -> 8.04 us  [along_head(): lax.ppermute(block, 'head', [(i, (i + distance) % head_size) for i in ran...]
    slice x0 -> x2, local copies, waits for them, and re-layouts: none -> 1.77 us  [the longest x1 0.89 us: local(): values[:, cut]]
    concatenate x1, other arithmetic: 0.99 us -> 0.02 us  [local(): jnp.concatenate([keys[:, cut], values[:, cut]], axis=0)]
    pallas_call x3 -> x6, Pallas kernels: 12.5 us -> 13.3 us  [absorb(): pl.pallas_call(functools.partial(absorb_kernel, groups=groups, tokens=tok...]
  transfers between devices with their start and end apart: 18 -> 33, of which waited for: 12 -> 9; matrix products, arithmetic and copies ran while one was open for 2% -> 3% of each run, Pallas kernels for 18% -> 18%
where the time goes in v3:
time: 59.3 us; the launch traced here: 59 us
  starting transfers between devices  24.6 us (41%)
  Pallas kernels  15.9 us (27%)
  waiting for transfers between devices  12.6 us (21%)
  local copies, waits for them, and re-layouts  4.33 us (7%)
  between operations  0.81 us (1%)
  other arithmetic  0.72 us (1%)
    pallas_call x6, Pallas kernels, absorb(): pl.pallas_call(functools.partial(absorb_kernel, groups=groups, tokens=tok...  13.3 us
    ppermute x24, starting transfers between devices, across_ctx(): return lax.ppermute(block, 'ctx', [(i, i ^ flip) for i in range(ctx_size)])  12.3 us
    ppermute x9, starting transfers between devices, along_head(): lax.ppermute(block, 'head', [(i, (i + distance) % head_size) for i in ran...  12.3 us
    ppermute x9, waiting for transfers between devices, along_head(): lax.ppermute(block, 'head', [(i, (i + distance) % head_size) for i in ran...  8.04 us
    ppermute x24, waiting for transfers between devices, across_ctx(): return lax.ppermute(block, 'ctx', [(i, i ^ flip) for i in range(ctx_size)])  4.56 us
    pallas_call x1, Pallas kernels, prepare(): pl.pallas_call(functools.partial(prepare_kernel, groups=groups, per_step=...  2.65 us
    unnamed x6, local copies, waits for them, and re-layouts  2.57 us
  transfers between devices with their start and end apart: 33, of which 9 were waited for; matrix products, arithmetic and copies ran while one was open for 3% of the time, Pallas kernels for 18%

profile of v3, /device:TPU:0, one launch (start us, length us, event | category | flops | bytes accessed | tf_op | source)
XLA Modules:
  0.0 59.0 jit_solution(15828435159589765727)
XLA Ops:
  0.6 0.7 %pad_maximum_fusion.2.refs_0_ = f32[4,8]{1,0:T(4,128)S(1)} fusion(f32[2,8]{1,0:T(2,128)} %bitcast.2, f32[2,8]{1,0:T(2,128)} %bitcast.3), kind=kLoop, calls=%fused_computation.2 | loop fusion | flops 32 | bytes 256 | tf_op jit(solution)/shard_map/concatenate | solution.py:300
  1.3 3.0 %collective-permute-start = (f32[4,8]{1,0:T(4,128)S(1)}, f32[4,8]{1,0:T(4,128)S(1)}, u32[]{:S(2)}, u32[]{:S(2)}) collective-permute-start(f32[4,8]{1,0:T(4,128)S(1)} %pad_maximum_fusion.2.refs_0_), channel_id=1, source_target_pairs={{0,2},{2,4},{4,6},{6,0},{1,3},{3,5},{5,7},{7,1},{8,10},{10,12},{12... | collective-permute-start | bytes 392 | tf_op jit(solution)/shard_map/ppermute | solution.py:281
  4.4 2.6 %collective-permute-start.1 = (f32[4,8]{1,0:T(4,128)S(1)}, f32[4,8]{1,0:T(4,128)S(1)}, u32[]{:S(2)}, u32[]{:S(2)}) collective-permute-start(f32[4,8]{1,0:T(4,128)S(1)} %pad_maximum_fusion.2.refs_0_), channel_id=1, source_target_pairs={{0,4},{2,6},{4,0},{6,2},{1,5},{3,7},{5,1},{7,3},{8,12},{10,14},{12... | collective-permute-start | bytes 392 | tf_op jit(solution)/shard_map/ppermute | solution.py:281
  6.9 1.3 %collective-permute-start.2 = (f32[4,8]{1,0:T(4,128)S(1)}, f32[4,8]{1,0:T(4,128)S(1)}, u32[]{:S(2)}, u32[]{:S(2)}) collective-permute-start(f32[4,8]{1,0:T(4,128)S(1)} %pad_maximum_fusion.2.refs_0_), channel_id=1, source_target_pairs={{0,6},{2,0},{4,2},{6,4},{1,7},{3,1},{5,3},{7,5},{8,14},{10,8},{12,... | collective-permute-start | bytes 392 | tf_op jit(solution)/shard_map/ppermute | solution.py:281
  8.3 0.9 %fusion = (bf16[64,512]{1,0:T(8,128)(2,1)S(1)}, bf16[64,512]{1,0:T(8,128)(2,1)S(1)}) fusion(bf16[64,1024]{1,0:T(8,128)(2,1)} %param.8), kind=kLoop, calls=%fused_computation.3 | loop fusion | bytes 262144 | tf_op jit(solution)/shard_map/slice | solution.py:305
  9.2 0.9 %fusion.1 = (bf16[64,512]{1,0:T(8,128)(2,1)S(1)}, bf16[64,512]{1,0:T(8,128)(2,1)S(1)}) fusion(bf16[64,1024]{1,0:T(8,128)(2,1)} %param.9), kind=kLoop, calls=%fused_computation.4 | loop fusion | bytes 262144 | tf_op jit(solution)/shard_map/slice | solution.py:305
  10.1 0.0 collective-permute-done.refs_1_
  10.1 0.4 collective-permute-done.2.refs_3_
  10.5 0.3 collective-permute-start.6
  10.9 1.5 %collective-permute-start.7 = (bf16[128,512]{1,0:T(8,128)(2,1)S(1)}, bf16[128,512]{1,0:T(8,128)(2,1)S(1)}, u32[]{:S(2)}, u32[]{:S(2)}) collective-permute-start(bf16[128,512]{1,0:T(8,128)(2,1)S(1)} %get-tuple-element.105.refs_0_), channel_id=1, source_target_pairs={{0,16},{8,24},{16,0},{24,8},{1,17},{9,25},{17,1},{25,9},{2,18},{10... | collective-permute-start | bytes 393224 | tf_op jit(solution)/shard_map/ppermute | solution.py:284
  12.4 1.1 %collective-permute-start.3 = (bf16[128,512]{1,0:T(8,128)(2,1)S(1)}, bf16[128,512]{1,0:T(8,128)(2,1)S(1)}, u32[]{:S(2)}, u32[]{:S(2)}) collective-permute-start(bf16[128,512]{1,0:T(8,128)(2,1)S(1)} %get-tuple-element.104.refs_0_), channel_id=1, source_target_pairs={{0,2},{2,4},{4,6},{6,0},{1,3},{3,5},{5,7},{7,1},{8,10},{10,12},{12... | collective-permute-start | bytes 393224 | tf_op jit(solution)/shard_map/ppermute | solution.py:281
  13.5 0.5 collective-permute-start.4
  14.0 1.2 %copy-done = bf16[64,8192]{1,0:T(8,128)(2,1)S(1)} copy-done((bf16[64,8192]{1,0:T(8,128)(2,1)S(1)}, bf16[64,8192]{1,0:T(8,128)(2,1)}, u32[]{:S(2)}) %copy-start) | copy-done | bytes 1048600
  15.3 0.7 %copy-done.1 = s32[8,8]{1,0:T(8,128)S(1)} copy-done((s32[8,8]{1,0:T(8,128)S(1)}, s32[8,8]{1,0:T(8,128)}, u32[]{:S(2)}) %copy-start.1) | copy-done | bytes 280
  15.9 0.7 %copy-done.2 = s32[8]{0:T(128)S(1)} copy-done((s32[8]{0:T(128)S(1)}, s32[8]{0:T(128)}, u32[]{:S(2)}) %copy-start.2) | copy-done | bytes 56
  16.6 2.7 %shard_map.86 = (bf16[8,512,256]{2,1,0:T(8,128)(2,1)S(1)}, bf16[1024,128]{1,0:T(8,128)(2,1)S(1)}, f32[8,16,128]{2,1,0:T(8,128)S(1)}, f32[8,16,128]{2,1,0:T(8,128)S(1)}) custom-call(s32[8]{0:T(128)S(1)} %copy-done.2, s32[8,8]{1,0:T(8,128)S(1)} %copy-done.1, f32[4,8]{1,0:T(4,128)S(1)} %pad_maximum_fusion.2.refs_0_, f32[4,8]{1,0:T(4,128)S(1)} %collective-permute-done.refs_1_, ...), custom_call_target="tpu_custom_call" | custom-call | flops 4194304 | bytes 8388608 | tf_op jit(solution)/shard_map/pallas_call | solution.py:76
  19.3 0.1 collective-permute-start.5
  19.4 3.0 %collective-permute-start.13 = (bf16[128,512]{1,0:T(8,128)(2,1)S(1)}, bf16[128,512]{1,0:T(8,128)(2,1)S(1)}, u32[]{:S(2)}, u32[]{:S(2)}) collective-permute-start(bf16[128,512]{1,0:T(8,128)(2,1)S(1)} %collective-permute-done.6.refs_1_), channel_id=1, source_target_pairs={{0,2},{2,4},{4,6},{6,0},{1,3},{3,5},{5,7},{7,1},{8,10},{10,12},{12... | collective-permute-start | bytes 393224 | tf_op jit(solution)/shard_map/ppermute | solution.py:281
  22.3 1.5 %collective-permute-start.14 = (bf16[128,512]{1,0:T(8,128)(2,1)S(1)}, bf16[128,512]{1,0:T(8,128)(2,1)S(1)}, u32[]{:S(2)}, u32[]{:S(2)}) collective-permute-start(bf16[128,512]{1,0:T(8,128)(2,1)S(1)} %collective-permute-done.6.refs_1_), channel_id=1, source_target_pairs={{0,16},{8,24},{16,0},{24,8},{1,17},{9,25},{17,1},{25,9},{2,18},{10... | collective-permute-start | bytes 393224 | tf_op jit(solution)/shard_map/ppermute | solution.py:284
  23.9 0.5 collective-permute-start.16
  24.4 0.5 collective-permute-start.10
  24.9 2.2 %collective-permute-done.13.refs_4_ = bf16[128,512]{1,0:T(8,128)(2,1)S(1)} collective-permute-done((bf16[128,512]{1,0:T(8,128)(2,1)S(1)}, bf16[128,512]{1,0:T(8,128)(2,1)S(1)}, u32[]{:S(2)}, u32[]{:S(2)}) %collective-permute-start.13) | collective-permute-done | bytes 131104 | tf_op jit(solution)/shard_map/ppermute | solution.py:281
  27.1 1.6 %collective-permute-done.14.refs_5_ = bf16[128,512]{1,0:T(8,128)(2,1)S(1)} collective-permute-done((bf16[128,512]{1,0:T(8,128)(2,1)S(1)}, bf16[128,512]{1,0:T(8,128)(2,1)S(1)}, u32[]{:S(2)}, u32[]{:S(2)}) %collective-permute-start.14) | collective-permute-done | bytes 131104 | tf_op jit(solution)/shard_map/ppermute | solution.py:284
  28.7 0.6 collective-permute-start.9
  29.3 0.3 collective-permute-start.21
  29.6 1.1 %collective-permute-done.10.refs_5_ = bf16[128,512]{1,0:T(8,128)(2,1)S(1)} collective-permute-done((bf16[128,512]{1,0:T(8,128)(2,1)S(1)}, bf16[128,512]{1,0:T(8,128)(2,1)S(1)}, u32[]{:S(2)}, u32[]{:S(2)}) %collective-permute-start.10) | collective-permute-done | bytes 131104 | tf_op jit(solution)/shard_map/ppermute | solution.py:284
  30.7 1.5 %collective-permute-start.22 = (bf16[128,512]{1,0:T(8,128)(2,1)S(1)}, bf16[128,512]{1,0:T(8,128)(2,1)S(1)}, u32[]{:S(2)}, u32[]{:S(2)}) collective-permute-start(bf16[128,512]{1,0:T(8,128)(2,1)S(1)} %collective-permute-done.13.refs_4_), channel_id=1, source_target_pairs={{0,16},{8,24},{16,0},{24,8},{1,17},{9,25},{17,1},{25,9},{2,18},{10... | collective-permute-start | bytes 393224 | tf_op jit(solution)/shard_map/ppermute | solution.py:284
  32.2 4.5 %collective-permute-done.9.refs_4_ = bf16[128,512]{1,0:T(8,128)(2,1)S(1)} collective-permute-done((bf16[128,512]{1,0:T(8,128)(2,1)S(1)}, bf16[128,512]{1,0:T(8,128)(2,1)S(1)}, u32[]{:S(2)}, u32[]{:S(2)}) %collective-permute-start.9) | collective-permute-done | bytes 131104 | tf_op jit(solution)/shard_map/ppermute | solution.py:281
  36.8 1.5 %collective-permute-start.18 = (bf16[128,512]{1,0:T(8,128)(2,1)S(1)}, bf16[128,512]{1,0:T(8,128)(2,1)S(1)}, u32[]{:S(2)}, u32[]{:S(2)}) collective-permute-start(bf16[128,512]{1,0:T(8,128)(2,1)S(1)} %collective-permute-done.9.refs_4_), channel_id=1, source_target_pairs={{0,16},{8,24},{16,0},{24,8},{1,17},{9,25},{17,1},{25,9},{2,18},{10... | collective-permute-start | bytes 393224 | tf_op jit(solution)/shard_map/ppermute | solution.py:284
  38.3 0.9 %collective-permute-done.21.refs_0_ = bf16[128,512]{1,0:T(8,128)(2,1)S(1)} collective-permute-done((bf16[128,512]{1,0:T(8,128)(2,1)S(1)}, bf16[128,512]{1,0:T(8,128)(2,1)S(1)}, u32[]{:S(2)}, u32[]{:S(2)}) %collective-permute-start.21) | collective-permute-done | bytes 131104 | tf_op jit(solution)/shard_map/ppermute | solution.py:281
  39.2 2.4 %shard_map.87 = (f32[4,128,512]{2,1,0:T(8,128)S(1)}, f32[4,2,512]{2,1,0:T(2,128)S(1)}) custom-call(bf16[128,512]{1,0:T(8,128)(2,1)S(1)} %get-tuple-element.105.refs_0_, bf16[128,512]{1,0:T(8,128)(2,1)S(1)} %collective-permute-done.6.refs_1_, bf16[128,512]{1,0:T(8,128)(2,1)S(1)} %collective-permute-done.7.refs_2_, ...), custom_call_target="tpu_custom_call" | custom-call | flops 2147483648 | bytes 4194304 | tf_op jit(solution)/shard_map/pallas_call | solution.py:241
  41.7 0.6 collective-permute-start.19
  42.2 0.1 collective-permute-start.20
  42.3 1.5 %collective-permute-start.28 = (bf16[128,512]{1,0:T(8,128)(2,1)S(1)}, bf16[128,512]{1,0:T(8,128)(2,1)S(1)}, u32[]{:S(2)}, u32[]{:S(2)}) collective-permute-start(bf16[128,512]{1,0:T(8,128)(2,1)S(1)} %collective-permute-done.21.refs_0_), channel_id=1, source_target_pairs={{0,16},{8,24},{16,0},{24,8},{1,17},{9,25},{17,1},{25,9},{2,18},{10... | collective-permute-start | bytes 393224 | tf_op jit(solution)/shard_map/ppermute | solution.py:284
  43.9 0.2 collective-permute-start.29
  44.0 0.4 collective-permute-start.30
  44.4 2.4 %shard_map.88 = (f32[4,128,512]{2,1,0:T(8,128)S(1)}, f32[4,2,512]{2,1,0:T(2,128)S(1)}) custom-call(bf16[128,512]{1,0:T(8,128)(2,1)S(1)} %get-tuple-element.104.refs_0_, bf16[128,512]{1,0:T(8,128)(2,1)S(1)} %collective-permute-done.3.refs_1_, bf16[128,512]{1,0:T(8,128)(2,1)S(1)} %collective-permute-done.4.refs_2_, ...), custom_call_target="tpu_custom_call" | custom-call | flops 2147483648 | bytes 4194304 | tf_op jit(solution)/shard_map/pallas_call | solution.py:241
  46.8 1.3 %collective-permute-start.25 = (bf16[128,512]{1,0:T(8,128)(2,1)S(1)}, bf16[128,512]{1,0:T(8,128)(2,1)S(1)}, u32[]{:S(2)}, u32[]{:S(2)}) collective-permute-start(bf16[128,512]{1,0:T(8,128)(2,1)S(1)} %collective-permute-done.17.refs_0_), channel_id=1, source_target_pairs={{0,16},{8,24},{16,0},{24,8},{1,17},{9,25},{17,1},{25,9},{2,18},{10... | collective-permute-start | bytes 393224 | tf_op jit(solution)/shard_map/ppermute | solution.py:284
  48.1 0.1 collective-permute-done.28.refs_0_
  48.2 0.5 collective-permute-start.27
  48.6 1.6 %shard_map.89 = (f32[4,128,512]{2,1,0:T(8,128)S(1)}, f32[4,2,512]{2,1,0:T(2,128)S(1)}) custom-call(bf16[128,512]{1,0:T(8,128)(2,1)S(1)} %collective-permute-done.21.refs_0_, bf16[128,512]{1,0:T(8,128)(2,1)S(1)} %collective-permute-done.22.refs_1_, bf16[128,512]{1,0:T(8,128)(2,1)S(1)} %collective-permute-done.23.refs_2_, ...), custom_call_target="tpu_custom_call" | custom-call | flops 1073741824 | bytes 4194304 | tf_op jit(solution)/shard_map/pallas_call | solution.py:241
  50.3 0.1 collective-permute-start.32
  50.4 1.6 %shard_map.90 = (f32[4,128,512]{2,1,0:T(8,128)S(1)}, f32[4,2,512]{2,1,0:T(2,128)S(1)}) custom-call(bf16[128,512]{1,0:T(8,128)(2,1)S(1)} %collective-permute-done.17.refs_0_, bf16[128,512]{1,0:T(8,128)(2,1)S(1)} %collective-permute-done.18.refs_1_, bf16[128,512]{1,0:T(8,128)(2,1)S(1)} %collective-permute-done.19.refs_2_, ...), custom_call_target="tpu_custom_call" | custom-call | flops 1073741824 | bytes 4194304 | tf_op jit(solution)/shard_map/pallas_call | solution.py:241
  52.0 0.5 collective-permute-done.25.refs_0_
  52.5 0.1 collective-permute-start.31
  52.6 1.3 %collective-permute-done.31.refs_3_ = bf16[128,512]{1,0:T(8,128)(2,1)S(1)} collective-permute-done((bf16[128,512]{1,0:T(8,128)(2,1)S(1)}, bf16[128,512]{1,0:T(8,128)(2,1)S(1)}, u32[]{:S(2)}, u32[]{:S(2)}) %collective-permute-start.31) | collective-permute-done | bytes 131104 | tf_op jit(solution)/shard_map/ppermute | solution.py:284
  53.8 2.6 %shard_map.91 = (bf16[64,8192]{1,0:T(8,128)(2,1)}, f32[64,64]{1,0:T(8,128)S(1)}) custom-call(bf16[128,512]{1,0:T(8,128)(2,1)S(1)} %collective-permute-done.28.refs_0_, bf16[128,512]{1,0:T(8,128)(2,1)S(1)} %collective-permute-done.29.refs_1_, bf16[128,512]{1,0:T(8,128)(2,1)S(1)} %collective-permute-done.30.refs_2_, ...), custom_call_target="tpu_custom_call" | custom-call | flops 1073741824 | bytes 4194304 | tf_op jit(solution)/shard_map/pallas_call | solution.py:241
  56.4 2.6 %shard_map.92 = (bf16[64,8192]{1,0:T(8,128)(2,1)}, f32[64,64]{1,0:T(8,128)}) custom-call(bf16[128,512]{1,0:T(8,128)(2,1)S(1)} %collective-permute-done.25.refs_0_, bf16[128,512]{1,0:T(8,128)(2,1)S(1)} %collective-permute-done.26.refs_1_, bf16[128,512]{1,0:T(8,128)(2,1)S(1)} %collective-permute-done.27.refs_2_, ...), custom_call_target="tpu_custom_call", output_to_operand_aliasing={{0}: (10, {})} | custom-call | flops 1073741824 | bytes 4194304 | tf_op jit(solution)/shard_map/pallas_call | solution.py:241
  (35 shorter events, 0.1 us)
Async XLA Ops:
  1.3 8.8 %collective-permute-start = (f32[4,8]{1,0:T(4,128)S(1)}, f32[4,8]{1,0:T(4,128)S(1)}, u32[]{:S(2)}, u32[]{:S(2)}) collective-permute-start(f32[4,8]{1,0:T(4,128)S(1)} %pad_maximum_fusion.2.refs_0_), channel_id=1, source_target_pairs={{0,2},{2,4},{4,6},{6,0},{1,3},{3,5},{5,7},{7,1},{8,10},{10,12},{12... | collective-permute-start | bytes 392 | tf_op jit(solution)/shard_map/ppermute | solution.py:281
  4.4 5.8 %collective-permute-start.1 = (f32[4,8]{1,0:T(4,128)S(1)}, f32[4,8]{1,0:T(4,128)S(1)}, u32[]{:S(2)}, u32[]{:S(2)}) collective-permute-start(f32[4,8]{1,0:T(4,128)S(1)} %pad_maximum_fusion.2.refs_0_), channel_id=1, source_target_pairs={{0,4},{2,6},{4,0},{6,2},{1,5},{3,7},{5,1},{7,3},{8,12},{10,14},{12... | collective-permute-start | bytes 392 | tf_op jit(solution)/shard_map/ppermute | solution.py:281
  6.9 3.6 %collective-permute-start.2 = (f32[4,8]{1,0:T(4,128)S(1)}, f32[4,8]{1,0:T(4,128)S(1)}, u32[]{:S(2)}, u32[]{:S(2)}) collective-permute-start(f32[4,8]{1,0:T(4,128)S(1)} %pad_maximum_fusion.2.refs_0_), channel_id=1, source_target_pairs={{0,6},{2,0},{4,2},{6,4},{1,7},{3,1},{5,3},{7,5},{8,14},{10,8},{12,... | collective-permute-start | bytes 392 | tf_op jit(solution)/shard_map/ppermute | solution.py:281
  10.5 8.7 %collective-permute-start.6 = (bf16[128,512]{1,0:T(8,128)(2,1)S(1)}, bf16[128,512]{1,0:T(8,128)(2,1)S(1)}, u32[]{:S(2)}, u32[]{:S(2)}) collective-permute-start(bf16[128,512]{1,0:T(8,128)(2,1)S(1)} %get-tuple-element.105.refs_0_), channel_id=1, source_target_pairs={{0,2},{2,4},{4,6},{6,0},{1,3},{3,5},{5,7},{7,1},{8,10},{10,12},{12... | collective-permute-start | bytes 393224 | tf_op jit(solution)/shard_map/ppermute | solution.py:281
  10.9 8.5 %collective-permute-start.7 = (bf16[128,512]{1,0:T(8,128)(2,1)S(1)}, bf16[128,512]{1,0:T(8,128)(2,1)S(1)}, u32[]{:S(2)}, u32[]{:S(2)}) collective-permute-start(bf16[128,512]{1,0:T(8,128)(2,1)S(1)} %get-tuple-element.105.refs_0_), channel_id=1, source_target_pairs={{0,16},{8,24},{16,0},{24,8},{1,17},{9,25},{17,1},{25,9},{2,18},{10... | collective-permute-start | bytes 393224 | tf_op jit(solution)/shard_map/ppermute | solution.py:284
  12.4 7.0 %collective-permute-start.8 = (bf16[128,512]{1,0:T(8,128)(2,1)S(1)}, bf16[128,512]{1,0:T(8,128)(2,1)S(1)}, u32[]{:S(2)}, u32[]{:S(2)}) collective-permute-start(bf16[128,512]{1,0:T(8,128)(2,1)S(1)} %get-tuple-element.105.refs_0_), channel_id=1, source_target_pairs={{0,8},{8,0},{16,24},{24,16},{1,9},{9,1},{17,25},{25,17},{2,10},{10... | collective-permute-start | bytes 393224 | tf_op jit(solution)/shard_map/ppermute | solution.py:284
  12.4 11.5 %collective-permute-start.3 = (bf16[128,512]{1,0:T(8,128)(2,1)S(1)}, bf16[128,512]{1,0:T(8,128)(2,1)S(1)}, u32[]{:S(2)}, u32[]{:S(2)}) collective-permute-start(bf16[128,512]{1,0:T(8,128)(2,1)S(1)} %get-tuple-element.104.refs_0_), channel_id=1, source_target_pairs={{0,2},{2,4},{4,6},{6,0},{1,3},{3,5},{5,7},{7,1},{8,10},{10,12},{12... | collective-permute-start | bytes 393224 | tf_op jit(solution)/shard_map/ppermute | solution.py:281
  13.5 10.3 %collective-permute-start.4 = (bf16[128,512]{1,0:T(8,128)(2,1)S(1)}, bf16[128,512]{1,0:T(8,128)(2,1)S(1)}, u32[]{:S(2)}, u32[]{:S(2)}) collective-permute-start(bf16[128,512]{1,0:T(8,128)(2,1)S(1)} %get-tuple-element.104.refs_0_), channel_id=1, source_target_pairs={{0,16},{8,24},{16,0},{24,8},{1,17},{9,25},{17,1},{25,9},{2,18},{10... | collective-permute-start | bytes 393224 | tf_op jit(solution)/shard_map/ppermute | solution.py:284
  14.0 1.2 %copy-start = (bf16[64,8192]{1,0:T(8,128)(2,1)S(1)}, bf16[64,8192]{1,0:T(8,128)(2,1)}, u32[]{:S(2)}) copy-start(bf16[64,8192]{1,0:T(8,128)(2,1)} %refs_4_.1) | copy-start | bytes 3145732
  15.3 0.7 %copy-start.1 = (s32[8,8]{1,0:T(8,128)S(1)}, s32[8,8]{1,0:T(8,128)}, u32[]{:S(2)}) copy-start(s32[8,8]{1,0:T(8,128)} %keep_ref.1) | copy-start | bytes 772
  15.9 0.7 %copy-start.2 = (s32[8]{0:T(128)S(1)}, s32[8]{0:T(128)}, u32[]{:S(2)}) copy-start(s32[8]{0:T(128)} %order_ref.1) | copy-start | bytes 100
  19.3 5.1 %collective-permute-start.5 = (bf16[128,512]{1,0:T(8,128)(2,1)S(1)}, bf16[128,512]{1,0:T(8,128)(2,1)S(1)}, u32[]{:S(2)}, u32[]{:S(2)}) collective-permute-start(bf16[128,512]{1,0:T(8,128)(2,1)S(1)} %get-tuple-element.104.refs_0_), channel_id=1, source_target_pairs={{0,8},{8,0},{16,24},{24,16},{1,9},{9,1},{17,25},{25,17},{2,10},{10... | collective-permute-start | bytes 393224 | tf_op jit(solution)/shard_map/ppermute | solution.py:284
  19.4 7.7 %collective-permute-start.13 = (bf16[128,512]{1,0:T(8,128)(2,1)S(1)}, bf16[128,512]{1,0:T(8,128)(2,1)S(1)}, u32[]{:S(2)}, u32[]{:S(2)}) collective-permute-start(bf16[128,512]{1,0:T(8,128)(2,1)S(1)} %collective-permute-done.6.refs_1_), channel_id=1, source_target_pairs={{0,2},{2,4},{4,6},{6,0},{1,3},{3,5},{5,7},{7,1},{8,10},{10,12},{12... | collective-permute-start | bytes 393224 | tf_op jit(solution)/shard_map/ppermute | solution.py:281
  22.3 6.3 %collective-permute-start.14 = (bf16[128,512]{1,0:T(8,128)(2,1)S(1)}, bf16[128,512]{1,0:T(8,128)(2,1)S(1)}, u32[]{:S(2)}, u32[]{:S(2)}) collective-permute-start(bf16[128,512]{1,0:T(8,128)(2,1)S(1)} %collective-permute-done.6.refs_1_), channel_id=1, source_target_pairs={{0,16},{8,24},{16,0},{24,8},{1,17},{9,25},{17,1},{25,9},{2,18},{10... | collective-permute-start | bytes 393224 | tf_op jit(solution)/shard_map/ppermute | solution.py:284
  23.9 4.8 %collective-permute-start.15 = (bf16[128,512]{1,0:T(8,128)(2,1)S(1)}, bf16[128,512]{1,0:T(8,128)(2,1)S(1)}, u32[]{:S(2)}, u32[]{:S(2)}) collective-permute-start(bf16[128,512]{1,0:T(8,128)(2,1)S(1)} %collective-permute-done.6.refs_1_), channel_id=1, source_target_pairs={{0,8},{8,0},{16,24},{24,16},{1,9},{9,1},{17,25},{25,17},{2,10},{10... | collective-permute-start | bytes 393224 | tf_op jit(solution)/shard_map/ppermute | solution.py:284
  23.9 5.4 %collective-permute-start.16 = (bf16[128,512]{1,0:T(8,128)(2,1)S(1)}, bf16[128,512]{1,0:T(8,128)(2,1)S(1)}, u32[]{:S(2)}, u32[]{:S(2)}) collective-permute-start(bf16[128,512]{1,0:T(8,128)(2,1)S(1)} %collective-permute-done.7.refs_2_), channel_id=1, source_target_pairs={{0,8},{8,0},{16,24},{24,16},{1,9},{9,1},{17,25},{25,17},{2,10},{10... | collective-permute-start | bytes 393224 | tf_op jit(solution)/shard_map/ppermute | solution.py:284
  24.4 6.3 %collective-permute-start.10 = (bf16[128,512]{1,0:T(8,128)(2,1)S(1)}, bf16[128,512]{1,0:T(8,128)(2,1)S(1)}, u32[]{:S(2)}, u32[]{:S(2)}) collective-permute-start(bf16[128,512]{1,0:T(8,128)(2,1)S(1)} %collective-permute-done.3.refs_1_), channel_id=1, source_target_pairs={{0,16},{8,24},{16,0},{24,8},{1,17},{9,25},{17,1},{25,9},{2,18},{10... | collective-permute-start | bytes 393224 | tf_op jit(solution)/shard_map/ppermute | solution.py:284
  27.1 5.2 %collective-permute-start.11 = (bf16[128,512]{1,0:T(8,128)(2,1)S(1)}, bf16[128,512]{1,0:T(8,128)(2,1)S(1)}, u32[]{:S(2)}, u32[]{:S(2)}) collective-permute-start(bf16[128,512]{1,0:T(8,128)(2,1)S(1)} %collective-permute-done.3.refs_1_), channel_id=1, source_target_pairs={{0,8},{8,0},{16,24},{24,16},{1,9},{9,1},{17,25},{25,17},{2,10},{10... | collective-permute-start | bytes 393224 | tf_op jit(solution)/shard_map/ppermute | solution.py:284
  28.7 3.6 %collective-permute-start.12 = (bf16[128,512]{1,0:T(8,128)(2,1)S(1)}, bf16[128,512]{1,0:T(8,128)(2,1)S(1)}, u32[]{:S(2)}, u32[]{:S(2)}) collective-permute-start(bf16[128,512]{1,0:T(8,128)(2,1)S(1)} %collective-permute-done.4.refs_2_), channel_id=1, source_target_pairs={{0,8},{8,0},{16,24},{24,16},{1,9},{9,1},{17,25},{25,17},{2,10},{10... | collective-permute-start | bytes 393224 | tf_op jit(solution)/shard_map/ppermute | solution.py:284
  28.7 8.1 %collective-permute-start.9 = (bf16[128,512]{1,0:T(8,128)(2,1)S(1)}, bf16[128,512]{1,0:T(8,128)(2,1)S(1)}, u32[]{:S(2)}, u32[]{:S(2)}) collective-permute-start(bf16[128,512]{1,0:T(8,128)(2,1)S(1)} %collective-permute-done.3.refs_1_), channel_id=1, source_target_pairs={{0,2},{2,4},{4,6},{6,0},{1,3},{3,5},{5,7},{7,1},{8,10},{10,12},{12... | collective-permute-start | bytes 393224 | tf_op jit(solution)/shard_map/ppermute | solution.py:281
  29.3 9.9 %collective-permute-start.21 = (bf16[128,512]{1,0:T(8,128)(2,1)S(1)}, bf16[128,512]{1,0:T(8,128)(2,1)S(1)}, u32[]{:S(2)}, u32[]{:S(2)}) collective-permute-start(bf16[128,512]{1,0:T(8,128)(2,1)S(1)} %collective-permute-done.13.refs_4_), channel_id=1, source_target_pairs={{0,2},{2,4},{4,6},{6,0},{1,3},{3,5},{5,7},{7,1},{8,10},{10,12},{12... | collective-permute-start | bytes 393224 | tf_op jit(solution)/shard_map/ppermute | solution.py:281
  30.7 11.0 %collective-permute-start.22 = (bf16[128,512]{1,0:T(8,128)(2,1)S(1)}, bf16[128,512]{1,0:T(8,128)(2,1)S(1)}, u32[]{:S(2)}, u32[]{:S(2)}) collective-permute-start(bf16[128,512]{1,0:T(8,128)(2,1)S(1)} %collective-permute-done.13.refs_4_), channel_id=1, source_target_pairs={{0,16},{8,24},{16,0},{24,8},{1,17},{9,25},{17,1},{25,9},{2,18},{10... | collective-permute-start | bytes 393224 | tf_op jit(solution)/shard_map/ppermute | solution.py:284
  32.2 10.0 %collective-permute-start.23 = (bf16[128,512]{1,0:T(8,128)(2,1)S(1)}, bf16[128,512]{1,0:T(8,128)(2,1)S(1)}, u32[]{:S(2)}, u32[]{:S(2)}) collective-permute-start(bf16[128,512]{1,0:T(8,128)(2,1)S(1)} %collective-permute-done.13.refs_4_), channel_id=1, source_target_pairs={{0,8},{8,0},{16,24},{24,16},{1,9},{9,1},{17,25},{25,17},{2,10},{10... | collective-permute-start | bytes 393224 | tf_op jit(solution)/shard_map/ppermute | solution.py:284
  36.8 7.1 %collective-permute-start.17 = (bf16[128,512]{1,0:T(8,128)(2,1)S(1)}, bf16[128,512]{1,0:T(8,128)(2,1)S(1)}, u32[]{:S(2)}, u32[]{:S(2)}) collective-permute-start(bf16[128,512]{1,0:T(8,128)(2,1)S(1)} %collective-permute-done.9.refs_4_), channel_id=1, source_target_pairs={{0,2},{2,4},{4,6},{6,0},{1,3},{3,5},{5,7},{7,1},{8,10},{10,12},{12... | collective-permute-start | bytes 393224 | tf_op jit(solution)/shard_map/ppermute | solution.py:281
  36.8 7.2 %collective-permute-start.18 = (bf16[128,512]{1,0:T(8,128)(2,1)S(1)}, bf16[128,512]{1,0:T(8,128)(2,1)S(1)}, u32[]{:S(2)}, u32[]{:S(2)}) collective-permute-start(bf16[128,512]{1,0:T(8,128)(2,1)S(1)} %collective-permute-done.9.refs_4_), channel_id=1, source_target_pairs={{0,16},{8,24},{16,0},{24,8},{1,17},{9,25},{17,1},{25,9},{2,18},{10... | collective-permute-start | bytes 393224 | tf_op jit(solution)/shard_map/ppermute | solution.py:284
  39.2 3.1 %collective-permute-start.24 = (bf16[128,512]{1,0:T(8,128)(2,1)S(1)}, bf16[128,512]{1,0:T(8,128)(2,1)S(1)}, u32[]{:S(2)}, u32[]{:S(2)}) collective-permute-start(bf16[128,512]{1,0:T(8,128)(2,1)S(1)} %collective-permute-done.14.refs_5_), channel_id=1, source_target_pairs={{0,8},{8,0},{16,24},{24,16},{1,9},{9,1},{17,25},{25,17},{2,10},{10... | collective-permute-start | bytes 393224 | tf_op jit(solution)/shard_map/ppermute | solution.py:284
  41.7 5.2 %collective-permute-start.19 = (bf16[128,512]{1,0:T(8,128)(2,1)S(1)}, bf16[128,512]{1,0:T(8,128)(2,1)S(1)}, u32[]{:S(2)}, u32[]{:S(2)}) collective-permute-start(bf16[128,512]{1,0:T(8,128)(2,1)S(1)} %collective-permute-done.9.refs_4_), channel_id=1, source_target_pairs={{0,8},{8,0},{16,24},{24,16},{1,9},{9,1},{17,25},{25,17},{2,10},{10... | collective-permute-start | bytes 393224 | tf_op jit(solution)/shard_map/ppermute | solution.py:284
  42.2 4.6 %collective-permute-start.20 = (bf16[128,512]{1,0:T(8,128)(2,1)S(1)}, bf16[128,512]{1,0:T(8,128)(2,1)S(1)}, u32[]{:S(2)}, u32[]{:S(2)}) collective-permute-start(bf16[128,512]{1,0:T(8,128)(2,1)S(1)} %collective-permute-done.10.refs_5_), channel_id=1, source_target_pairs={{0,8},{8,0},{16,24},{24,16},{1,9},{9,1},{17,25},{25,17},{2,10},{10... | collective-permute-start | bytes 393224 | tf_op jit(solution)/shard_map/ppermute | solution.py:284
  42.3 5.8 %collective-permute-start.28 = (bf16[128,512]{1,0:T(8,128)(2,1)S(1)}, bf16[128,512]{1,0:T(8,128)(2,1)S(1)}, u32[]{:S(2)}, u32[]{:S(2)}) collective-permute-start(bf16[128,512]{1,0:T(8,128)(2,1)S(1)} %collective-permute-done.21.refs_0_), channel_id=1, source_target_pairs={{0,16},{8,24},{16,0},{24,8},{1,17},{9,25},{17,1},{25,9},{2,18},{10... | collective-permute-start | bytes 393224 | tf_op jit(solution)/shard_map/ppermute | solution.py:284
  43.9 6.4 %collective-permute-start.29 = (bf16[128,512]{1,0:T(8,128)(2,1)S(1)}, bf16[128,512]{1,0:T(8,128)(2,1)S(1)}, u32[]{:S(2)}, u32[]{:S(2)}) collective-permute-start(bf16[128,512]{1,0:T(8,128)(2,1)S(1)} %collective-permute-done.21.refs_0_), channel_id=1, source_target_pairs={{0,8},{8,0},{16,24},{24,16},{1,9},{9,1},{17,25},{25,17},{2,10},{10... | collective-permute-start | bytes 393224 | tf_op jit(solution)/shard_map/ppermute | solution.py:284
  44.0 6.2 %collective-permute-start.30 = (bf16[128,512]{1,0:T(8,128)(2,1)S(1)}, bf16[128,512]{1,0:T(8,128)(2,1)S(1)}, u32[]{:S(2)}, u32[]{:S(2)}) collective-permute-start(bf16[128,512]{1,0:T(8,128)(2,1)S(1)} %collective-permute-done.22.refs_1_), channel_id=1, source_target_pairs={{0,8},{8,0},{16,24},{24,16},{1,9},{9,1},{17,25},{25,17},{2,10},{10... | collective-permute-start | bytes 393224 | tf_op jit(solution)/shard_map/ppermute | solution.py:284
  46.8 5.6 %collective-permute-start.25 = (bf16[128,512]{1,0:T(8,128)(2,1)S(1)}, bf16[128,512]{1,0:T(8,128)(2,1)S(1)}, u32[]{:S(2)}, u32[]{:S(2)}) collective-permute-start(bf16[128,512]{1,0:T(8,128)(2,1)S(1)} %collective-permute-done.17.refs_0_), channel_id=1, source_target_pairs={{0,16},{8,24},{16,0},{24,8},{1,17},{9,25},{17,1},{25,9},{2,18},{10... | collective-permute-start | bytes 393224 | tf_op jit(solution)/shard_map/ppermute | solution.py:284
  48.1 4.4 %collective-permute-start.26 = (bf16[128,512]{1,0:T(8,128)(2,1)S(1)}, bf16[128,512]{1,0:T(8,128)(2,1)S(1)}, u32[]{:S(2)}, u32[]{:S(2)}) collective-permute-start(bf16[128,512]{1,0:T(8,128)(2,1)S(1)} %collective-permute-done.17.refs_0_), channel_id=1, source_target_pairs={{0,8},{8,0},{16,24},{24,16},{1,9},{9,1},{17,25},{25,17},{2,10},{10... | collective-permute-start | bytes 393224 | tf_op jit(solution)/shard_map/ppermute | solution.py:284
  48.2 4.3 %collective-permute-start.27 = (bf16[128,512]{1,0:T(8,128)(2,1)S(1)}, bf16[128,512]{1,0:T(8,128)(2,1)S(1)}, u32[]{:S(2)}, u32[]{:S(2)}) collective-permute-start(bf16[128,512]{1,0:T(8,128)(2,1)S(1)} %collective-permute-done.18.refs_1_), channel_id=1, source_target_pairs={{0,8},{8,0},{16,24},{24,16},{1,9},{9,1},{17,25},{25,17},{2,10},{10... | collective-permute-start | bytes 393224 | tf_op jit(solution)/shard_map/ppermute | solution.py:284
  50.3 2.3 %collective-permute-start.32 = (bf16[128,512]{1,0:T(8,128)(2,1)S(1)}, bf16[128,512]{1,0:T(8,128)(2,1)S(1)}, u32[]{:S(2)}, u32[]{:S(2)}) collective-permute-start(bf16[128,512]{1,0:T(8,128)(2,1)S(1)} %collective-permute-done.28.refs_0_), channel_id=1, source_target_pairs={{0,8},{8,0},{16,24},{24,16},{1,9},{9,1},{17,25},{25,17},{2,10},{10... | collective-permute-start | bytes 393224 | tf_op jit(solution)/shard_map/ppermute | solution.py:284
  52.5 1.4 %collective-permute-start.31 = (bf16[128,512]{1,0:T(8,128)(2,1)S(1)}, bf16[128,512]{1,0:T(8,128)(2,1)S(1)}, u32[]{:S(2)}, u32[]{:S(2)}) collective-permute-start(bf16[128,512]{1,0:T(8,128)(2,1)S(1)} %collective-permute-done.25.refs_0_), channel_id=1, source_target_pairs={{0,8},{8,0},{16,24},{24,16},{1,9},{9,1},{17,25},{25,17},{2,10},{10... | collective-permute-start | bytes 393224 | tf_op jit(solution)/shard_map/ppermute | solution.py:284

commit v4 on v2

v4 whole, which is shorter than its diff:
```python
import functools
import math

import jax
import jax.numpy as jnp
from jax import lax
from jax.experimental import pallas as pl
from jax.experimental.pallas import tpu as pltpu
from jax.sharding import PartitionSpec as P

HEAD_WIDTH = 128
SPAN = 128
LOG2E = 1.4426950408889634
MASKED = -1e30


def source_start(distance, flip, tokens, ctx_size, head_size):
    ctx, head = lax.axis_index("ctx"), lax.axis_index("head")
    size = ctx_size // 2 * head_size
    row = ctx // 2
    place = row * head_size + jnp.where(row % 2 == 0, head, head_size - 1 - head)
    place = lax.rem(place - distance + size, size)
    row, column = place // head_size, place % head_size
    column = jnp.where(row % 2 == 0, column, head_size - 1 - column)
    return ((2 * row + (ctx % 2) ^ flip) * head_size + column) * tokens


def prepare_kernel(order_ref, keep_ref, q_ref, qa_ref, mask_ref, *, groups, per_step, sources, ctx_size, head_size):
    step = pl.program_id(0)
    tokens = q_ref.shape[0]
    row = lax.broadcasted_iota(jnp.int32, (tokens, SPAN), 0)
    lane = lax.broadcasted_iota(jnp.int32, (tokens, SPAN), 1)

    @pl.when(step == 0)
    def _():
        own_start = source_start(0, 0, tokens, ctx_size, head_size)
        own = own_start // SPAN
        for i, source in enumerate(sources):
            start = source_start(*source, tokens, ctx_size, head_size)
            span = start // SPAN
            seen = (order_ref[span] < order_ref[own]) & (keep_ref[own, span] > 0)
            whole = jnp.where(seen, 0.0, MASKED)
            causal = jnp.where(row + (start - own_start) <= lane, 0.0, MASKED)
            mask = jnp.where(own == span, causal, whole)
            mask_ref[i * tokens : (i + 1) * tokens, :] = mask.astype(jnp.bfloat16)

    one_hot = jnp.where(row == lane, 1.0, 0.0).astype(jnp.bfloat16)
    for u in range(per_step):
        for h in range(groups):
            at = (u * groups + h) * HEAD_WIDTH
            qa_ref[u, h * tokens : (h + 1) * tokens, :HEAD_WIDTH] = q_ref[:, at : at + HEAD_WIDTH]
            qa_ref[u, h * tokens : (h + 1) * tokens, HEAD_WIDTH:] = one_hot


def prepare(queries, span_order, block_keep, sources, kv_heads, sizes):
    tokens, width = queries.shape
    groups = width // HEAD_WIDTH // kv_heads
    per_step = 2 if kv_heads % 2 == 0 else 1
    rows = groups * tokens
    smem = pl.BlockSpec(memory_space=pltpu.SMEM)
    return pl.pallas_call(
        functools.partial(
            prepare_kernel,
            groups=groups,
            per_step=per_step,
            sources=sources,
            ctx_size=sizes[0],
            head_size=sizes[1],
        ),
        grid=(kv_heads // per_step,),
        in_specs=[smem, smem, pl.BlockSpec((tokens, per_step * groups * HEAD_WIDTH), lambda s: (0, s))],
        out_specs=[
            pl.BlockSpec((per_step, rows, HEAD_WIDTH + SPAN), lambda s: (s, 0, 0)),
            pl.BlockSpec((tokens * len(sources), SPAN), lambda s: (0, 0)),
        ],
        out_shape=[
            jax.ShapeDtypeStruct((kv_heads, rows, HEAD_WIDTH + SPAN), jnp.bfloat16),
            jax.ShapeDtypeStruct((tokens * len(sources), SPAN), jnp.bfloat16),
        ],
        compiler_params=pltpu.CompilerParams(vmem_limit_bytes=32 * 1024 * 1024),
        cost_estimate=pl.CostEstimate(
            flops=8 * tokens * width, bytes_accessed=16 * tokens * width, transcendentals=0
        ),
    )(span_order, block_keep, queries)


def scale_rows_kernel(*refs, tokens, kv_local, sources, ctx_size, head_size):
    scale_in = refs[:head_size]
    key_scale_ref, value_scale_ref, scale_ref, scale_sem = refs[head_size:]
    inverse_root = 1.0 / math.sqrt(HEAD_WIDTH)
    head = lax.axis_index("head")
    copies = []
    for shift in range(head_size):
        owner = lax.rem(head - shift + head_size, head_size)
        copies.append(
            pltpu.make_async_copy(scale_in[shift], scale_ref.at[owner], scale_sem.at[shift])
        )
    for copy in copies:
        copy.start()
    spans = [
        source_start(*source, tokens, ctx_size, head_size) // SPAN for source in sources
    ]
    for copy in copies:
        copy.wait()
    for g in range(head_size * kv_local):
        owner, member = g // kv_local, g % kv_local
        for i, span in enumerate(spans):
            factor = scale_ref[owner, member, span] * (inverse_root * LOG2E)
            key_scale_ref[g, i : i + 1, :] = jnp.full((1, SPAN), factor, jnp.float32)
            factor = scale_ref[owner, kv_local + member, span]
            value_scale_ref[g, i : i + 1, :] = jnp.full((1, SPAN), factor, jnp.float32)


def scale_rows(scales, sources, tokens, sizes):
    kv_local = scales[0].shape[0] // 2
    shape = (sizes[1] * kv_local, len(sources), SPAN)
    return pl.pallas_call(
        functools.partial(
            scale_rows_kernel,
            tokens=tokens,
            kv_local=kv_local,
            sources=sources,
            ctx_size=sizes[0],
            head_size=sizes[1],
        ),
        in_specs=[pl.BlockSpec(memory_space=pl.ANY)] * len(scales),
        out_specs=[pl.BlockSpec(memory_space=pltpu.VMEM)] * 2,
        out_shape=[jax.ShapeDtypeStruct(shape, jnp.float32)] * 2,
        scratch_shapes=[
            pltpu.SMEM((len(scales),) + scales[0].shape, jnp.float32),
            pltpu.SemaphoreType.DMA((len(scales),)),
        ],
        compiler_params=pltpu.CompilerParams(vmem_limit_bytes=32 * 1024 * 1024),
        cost_estimate=pl.CostEstimate(
            flops=10**8, bytes_accessed=10**6, transcendentals=0
        ),
    )(*scales)


def absorb_kernel(*refs, groups, tokens, per_step, begin, count, first, last):
    refs = list(refs)
    pieces = [(refs.pop(0), refs.pop(0)) for _ in range(count)]
    qa_ref, mask_ref, key_scale_ref, value_scale_ref = [refs.pop(0) for _ in range(4)]
    mixed_in, stats_in = (None, None) if first else (refs.pop(0), refs.pop(0))
    result_ref, stats_ref, x_ref, p_ref, check_ref = refs
    step = pl.program_id(0)
    inverse_root = 1.0 / math.sqrt(HEAD_WIDTH)
    for u in range(per_step):
        g = step * per_step + u
        cols = pl.ds(pl.multiple_of(g * HEAD_WIDTH, HEAD_WIDTH), HEAD_WIDTH)
        k = jnp.concatenate([key_ref[:, cols] for key_ref, _ in pieces], axis=0)
        k = jnp.concatenate([k, mask_ref[begin * tokens : (begin + count) * tokens, :]], axis=1)
        x_ref[u] = lax.dot_general(
            k, qa_ref[u], (((1,), (1,)), ((), ())), preferred_element_type=jnp.float32
        )
    for u in range(per_step):
        g = step * per_step + u
        cols = pl.ds(pl.multiple_of(g * HEAD_WIDTH, HEAD_WIDTH), HEAD_WIDTH)
        factors = [key_scale_ref[u, begin + i : begin + i + 1, :] for i in range(count)]
        high, low = [], []
        for i, (_, value_ref) in enumerate(pieces):
            factor = value_scale_ref[u, begin + i : begin + i + 1, :]
            v = value_ref[:, cols].astype(jnp.float32) * factor
            high.append(v.astype(jnp.bfloat16))
            low.append((v - high[-1].astype(jnp.float32)).astype(jnp.bfloat16))
        v = jnp.concatenate(
            [jnp.concatenate(high, axis=0), jnp.concatenate(low, axis=0)], axis=1
        )
        tops, totals, fades = [], [], []
        for tile in range(groups * tokens // SPAN):
            lanes = slice(tile * SPAN, (tile + 1) * SPAN)
            top = None
            for i, factor in enumerate(factors):
                x = x_ref[u, i * tokens : (i + 1) * tokens, lanes]
                highest = jnp.max(x.reshape(tokens // 8, 8, SPAN), axis=0) * factor
                top = highest if top is None else jnp.maximum(top, highest)
            top = jnp.max(top, axis=0, keepdims=True)
            if not first:
                before = stats_in[u, 0:1, lanes]
                top = jnp.maximum(top, before)
                fades.append(jnp.exp2(before - top))
            total = None
            for i, factor in enumerate(factors):
                keys = slice(i * tokens, (i + 1) * tokens)
                weight = jnp.exp2(x_ref[u, keys, lanes] * factor - top)
                p_ref[u, keys, lanes] = weight.astype(jnp.bfloat16)
                part = jnp.sum(weight.reshape(tokens // 8, 8, SPAN), axis=0)
                total = part if total is None else total + part
            total = jnp.sum(total, axis=0, keepdims=True)
            if not first:
                total = total + fades[tile] * stats_in[u, 1:2, lanes]
            tops.append(top)
            totals.append(total)
        both = lax.dot_general(
            v, p_ref[u], (((0,), (0,)), ((), ())), preferred_element_type=jnp.float32
        )
        for tile in range(groups * tokens // SPAN):
            lanes = slice(tile * SPAN, (tile + 1) * SPAN)
            mixed = both[:HEAD_WIDTH, lanes] + both[HEAD_WIDTH:, lanes]
            if not first:
                mixed = mixed + fades[tile] * mixed_in[u, :, lanes]
            if not last:
                result_ref[u, :, lanes] = mixed
                stats_ref[u, 0:1, lanes] = tops[tile]
                stats_ref[u, 1:2, lanes] = totals[tile]
                continue
            mixed = mixed * (1.0 / totals[tile])
            check = jnp.sum(mixed, axis=0, keepdims=True) * inverse_root
            mixed = jnp.transpose(mixed).astype(result_ref.dtype)
            for j in range(SPAN // tokens):
                h = tile * (SPAN // tokens) + j
                at = (u * groups + h) * HEAD_WIDTH
                result_ref[:, at : at + HEAD_WIDTH] = mixed[j * tokens : (j + 1) * tokens]
                check_ref[pl.ds(g * groups + h, 1), :] = check[:, j * tokens : (j + 1) * tokens]
    if last:

        @pl.when(step == pl.num_programs(0) - 1)
        def _():
            stats_ref[...] = jnp.transpose(check_ref[...])


def absorb(prepared, pieces, begin, state, last, tokens):
    kv_heads, rows, depth = prepared[0].shape
    groups = rows // tokens
    count = len(pieces)
    per_step = 2 if kv_heads % 2 == 0 else 1
    keys = tokens * count
    width = kv_heads * groups * HEAD_WIDTH
    first = state is None
    mixed = pl.BlockSpec((per_step, HEAD_WIDTH, rows), lambda s: (s, 0, 0))
    stats = pl.BlockSpec((per_step, 2, rows), lambda s: (s, 0, 0))
    scale_rows = pl.BlockSpec((per_step,) + prepared[2].shape[1:], lambda s: (s, 0, 0))
    in_specs, operands = [], []
    for piece in pieces:
        joined = len(piece) == 1
        half = (tokens, piece[0].shape[1])
        in_specs.append(pl.BlockSpec(half, lambda s: (0, 0)))
        in_specs.append(pl.BlockSpec(half, lambda s: (1, 0)) if joined else in_specs[-1])
        operands += [piece[0], piece[-1]]
    in_specs += [
        pl.BlockSpec((per_step, rows, depth), lambda s: (s, 0, 0)),
        pl.BlockSpec(prepared[1].shape, lambda s: (0, 0)),
        scale_rows,
        scale_rows,
    ]
    in_specs += [] if first else [mixed, stats]
    if last:
        out_specs = [
            pl.BlockSpec((tokens, per_step * groups * HEAD_WIDTH), lambda s: (0, s)),
            pl.BlockSpec((tokens, kv_heads * groups), lambda s: (0, 0)),
        ]
        out_shape = [
            jax.ShapeDtypeStruct((tokens, width), jnp.bfloat16),
            jax.ShapeDtypeStruct((tokens, kv_heads * groups), jnp.float32),
        ]
    else:
        out_specs = [mixed, stats]
        out_shape = [
            jax.ShapeDtypeStruct((kv_heads, HEAD_WIDTH, rows), jnp.float32),
            jax.ShapeDtypeStruct((kv_heads, 2, rows), jnp.float32),
        ]
    return pl.pallas_call(
        functools.partial(
            absorb_kernel,
            groups=groups,
            tokens=tokens,
            per_step=per_step,
            begin=begin,
            count=count,
            first=first,
            last=last,
        ),
        grid=(kv_heads // per_step,),
        in_specs=in_specs,
        out_specs=out_specs,
        out_shape=out_shape,
        scratch_shapes=[
            pltpu.VMEM((per_step, keys, rows), jnp.float32),
            pltpu.VMEM((per_step, keys, rows), jnp.bfloat16),
            pltpu.VMEM((kv_heads * groups, tokens), jnp.float32),
        ],
        compiler_params=pltpu.CompilerParams(vmem_limit_bytes=32 * 1024 * 1024),
        cost_estimate=pl.CostEstimate(
            flops=16 * tokens * width * keys,
            bytes_accessed=16 * tokens * width,
            transcendentals=tokens * width // HEAD_WIDTH * keys,
        ),
    )(*operands, *prepared, *(() if first else state))


def local(queries, keys, values, key_scale, value_scale, span_order, block_keep):
    tokens = queries.shape[0]
    kv_heads = keys.shape[1] // HEAD_WIDTH
    sizes = ctx_size, head_size = lax.axis_size("ctx"), lax.axis_size("head")
    size = ctx_size // 2 * head_size
    batch = 2 * SPAN // tokens

    def device(place, core):
        row, column = place // head_size, place % head_size
        return (2 * row + core) * head_size + (column if row % 2 == 0 else head_size - 1 - column)

    def around(block, distance):
        route = [
            (device(p, core), device((p + distance) % size, core))
            for p in range(size)
            for core in range(2)
        ]
        return lax.ppermute(block, ("ctx", "head"), route)

    def to_other_core(piece):
        return [lax.ppermute(block, "ctx", [(i, i ^ 1) for i in range(ctx_size)]) for block in piece]

    def along_head(block, distance):
        return lax.ppermute(block, "head", [(i, (i + distance) % head_size) for i in range(head_size)])

    sources = [(0, 0)]
    for step in range(1, size // 2 + 2):
        if step < size // 2:
            sources += [(step, 0), (-step, 0)]
        elif step == size // 2:
            sources += [(step, 0)]
        if step == 1:
            sources += [(0, 1)]
        elif step <= size // 2:
            sources += [(step - 1, 1), (1 - step, 1)]
        else:
            sources += [(step - 1, 1)]

    block = jnp.concatenate([keys, values], axis=0)
    scale = jnp.concatenate([jnp.transpose(key_scale), jnp.transpose(value_scale)], axis=0)
    scales, pieces, done = [scale], [[block]], 0
    fresh, forward, backward = [[block]], block, block
    prepared, rows, state = None, None, None
    for step in range(1, size // 2 + 2):
        sent = []
        if step < size // 2:
            forward, backward = around(forward, 1), around(backward, -1)
            sent = [[forward], [backward]]
        elif step == size // 2:
            sent = [[around(forward[:tokens], 1), around(backward[tokens:], -1)]]
        coming = sent + [to_other_core(piece) for piece in fresh]
        complete = len(scales) == head_size
        if not complete:
            scales = scales + [along_head(scale, len(scales))]
        if step == 1:
            prepared = prepare(queries, span_order, block_keep, sources, kv_heads, sizes)
        if complete:
            if rows is None:
                rows = scale_rows(scales, sources, tokens, sizes)
            ready = (len(pieces) - done) // batch * batch
            if ready and step <= size // 2:
                now = pieces[done : done + ready]
                state = absorb((*prepared, *rows), now, done, state, False, tokens)
                done += ready
        coming, scales, prepared, rows, state = lax.optimization_barrier(
            (coming, scales, prepared, rows, state)
        )
        fresh = coming[: len(sent)]
        if step < size // 2:
            forward, backward = fresh[0][0], fresh[1][0]
        pieces = pieces + list(coming)
    return tuple(absorb((*prepared, *rows), pieces[done:], done, state, True, tokens))


def solution(mesh):
    rows = P(("dp", "ctx", "head"), None)
    return jax.shard_map(
        local,
        mesh=mesh,
        in_specs=(rows, rows, rows, P("dp", "head"), P("dp", "head"), P(), P()),
        out_specs=(rows, rows),
        check_vma=False,
    )
```

time: 60.9 us -> 49.3 us (0.81)
  waiting for transfers between devices: 29.2 us -> 14.5 us
  starting transfers between devices: 11.4 us -> 15.2 us
  local copies, waits for them, and re-layouts: 2.57 us -> 4.42 us
  Pallas kernels: 15.1 us -> 13.5 us
  other arithmetic: 1.69 us -> 0.7 us
    ppermute x12 -> x17, waiting for transfers between devices: 17.7 us -> 2.11 us  [the longest x8 1.07 us: around(): return lax.ppermute(block, ('ctx', 'head'), route)]
    ppermute x12 -> x17, starting transfers between devices: 5.31 us -> 11.5 us  [the longest x8 9.26 us: around(): return lax.ppermute(block, ('ctx', 'head'), route)]
    ppermute x6 -> x3, starting transfers between devices: 6.07 us -> 3.7 us  [along_head(): lax.ppermute(block, 'head', [(i, (i + distance) % head_size) for i in ran...]
    pallas_call x3 -> x2, Pallas kernels: 12.5 us -> 11.1 us  [absorb(): pl.pallas_call(functools.partial(absorb_kernel, groups=groups, tokens=tok...]
    pallas_call x1, Pallas kernels: 2.65 us -> 1.36 us  [prepare(): pl.pallas_call(functools.partial(prepare_kernel, groups=groups, per_step=...]
    pallas_call x0 -> x1, Pallas kernels: none -> 1.04 us  [scale_rows(): pl.pallas_call(functools.partial(scale_rows_kernel, tokens=tokens, kv_loc...]
    concatenate x1 -> x0, other arithmetic: 0.99 us -> none  [local(): block = jnp.concatenate([keys, values], axis=0)]
    ppermute x6 -> x3, waiting for transfers between devices: 11.5 us -> 12.4 us  [along_head(): lax.ppermute(block, 'head', [(i, (i + distance) % head_size) for i in ran...]
  transfers between devices with their start and end apart: 18 -> 20, of which waited for: 12 -> 6; matrix products, arithmetic and copies ran while one was open for 2% -> 1% of each run, Pallas kernels for 18% -> 19%
where the time goes in v4:
time: 49.3 us; the launch traced here: 49.1 us
  starting transfers between devices  15.2 us (31%)
  waiting for transfers between devices  14.5 us (29%)
  Pallas kernels  13.5 us (27%)
  local copies, waits for them, and re-layouts  4.42 us (9%)
  between operations  0.76 us (2%)
  other arithmetic  0.7 us (1%)
    ppermute x3, waiting for transfers between devices, along_head(): lax.ppermute(block, 'head', [(i, (i + distance) % head_size) for i in ran...  12.4 us
    pallas_call x2, Pallas kernels, absorb(): pl.pallas_call(functools.partial(absorb_kernel, groups=groups, tokens=tok...  11.1 us
    ppermute x8, starting transfers between devices, around(): return lax.ppermute(block, ('ctx', 'head'), route)  9.26 us
    ppermute x3, starting transfers between devices, along_head(): lax.ppermute(block, 'head', [(i, (i + distance) % head_size) for i in ran...  3.7 us
    unnamed x7, local copies, waits for them, and re-layouts  3.48 us
    ppermute x9, starting transfers between devices, to_other_core(): lax.ppermute(block, 'ctx', [(i, i ^ 1) for i in range(ctx_size)])  2.22 us
    pallas_call x1, Pallas kernels, prepare(): pl.pallas_call(functools.partial(prepare_kernel, groups=groups, per_step=...  1.36 us
    ppermute x8, waiting for transfers between devices, around(): return lax.ppermute(block, ('ctx', 'head'), route)  1.07 us
  transfers between devices with their start and end apart: 20, of which 6 were waited for; matrix products, arithmetic and copies ran while one was open for 1% of the time, Pallas kernels for 19%

profile of v4, /device:TPU:0, one launch (start us, length us, event | category | flops | bytes accessed | tf_op | source)
XLA Modules:
  0.0 49.1 jit_solution(5070037042988122032)
XLA Ops:
  0.6 0.9 %constant_dynamic-update-slice_fusion.1 = bf16[128,1024]{1,0:T(8,128)(2,1)S(1)} fusion(bf16[64,1024]{1,0:T(8,128)(2,1)} %param.8), kind=kLoop, calls=%fused_computation.1 | loop fusion | bytes 262144
  1.5 0.9 %constant_dynamic-update-slice_fusion.refs_0_.refs_1_ = bf16[128,1024]{1,0:T(8,128)(2,1)S(1)} fusion(bf16[128,1024]{1,0:T(8,128)(2,1)S(1)} %constant_dynamic-update-slice_fusion.1, bf16[64,1024]{1,0:T(8,128)(2,1)} %param.9), kind=kLoop, calls=%fused_computation | loop fusion | bytes 262144 | tf_op jit(solution)/shard_map/concatenate | solution.py:329
  2.5 3.1 %collective-permute-start = (bf16[128,1024]{1,0:T(8,128)(2,1)S(1)}, bf16[128,1024]{1,0:T(8,128)(2,1)S(1)}, u32[]{:S(2)}, u32[]{:S(2)}) collective-permute-start(bf16[128,1024]{1,0:T(8,128)(2,1)S(1)} %constant_dynamic-update-slice_fusion.refs_0_.refs_1_), channel_id=1, source_target_pairs={{0,2},{8,10},{2,4},{10,12},{4,6},{12,14},{6,22},{14,30},{22,20},{3... | collective-permute-start | bytes 786440 | tf_op jit(solution)/shard_map/ppermute | solution.py:308
  5.5 0.0 collective-permute-start.1
  5.6 0.0 collective-permute-start.2
  5.6 0.7 %pad_maximum_fusion.refs_0_ = f32[4,8]{1,0:T(4,128)S(1)} fusion(f32[2,8]{1,0:T(2,128)} %bitcast.2, f32[2,8]{1,0:T(2,128)} %bitcast.3), kind=kLoop, calls=%fused_computation.2 | loop fusion | flops 32 | bytes 256 | tf_op jit(solution)/shard_map/concatenate | solution.py:330
  6.3 2.0 %collective-permute-start.3 = (f32[4,8]{1,0:T(4,128)S(1)}, f32[4,8]{1,0:T(4,128)S(1)}, u32[]{:S(2)}, u32[]{:S(2)}) collective-permute-start(f32[4,8]{1,0:T(4,128)S(1)} %pad_maximum_fusion.refs_0_), channel_id=1, source_target_pairs={{0,2},{2,4},{4,6},{6,0},{1,3},{3,5},{5,7},{7,1},{8,10},{10,12},{12... | collective-permute-start | bytes 392 | tf_op jit(solution)/shard_map/ppermute | solution.py:314
  8.3 1.2 %copy-done = bf16[64,8192]{1,0:T(8,128)(2,1)S(1)} copy-done((bf16[64,8192]{1,0:T(8,128)(2,1)S(1)}, bf16[64,8192]{1,0:T(8,128)(2,1)}, u32[]{:S(2)}) %copy-start) | copy-done | bytes 1048600
  9.5 0.7 %copy-done.1 = s32[8,8]{1,0:T(8,128)S(1)} copy-done((s32[8,8]{1,0:T(8,128)S(1)}, s32[8,8]{1,0:T(8,128)}, u32[]{:S(2)}) %copy-start.1) | copy-done | bytes 280
  10.2 0.7 %copy-done.2 = s32[8]{0:T(128)S(1)} copy-done((s32[8]{0:T(128)S(1)}, s32[8]{0:T(128)}, u32[]{:S(2)}) %copy-start.2) | copy-done | bytes 56
  10.8 1.4 %shard_map.86 = (bf16[8,512,256]{2,1,0:T(8,128)(2,1)S(1)}, bf16[1024,128]{1,0:T(8,128)(2,1)S(1)}) custom-call(s32[8]{0:T(128)S(1)} %copy-done.2, s32[8,8]{1,0:T(8,128)S(1)} %copy-done.1, bf16[64,8192]{1,0:T(8,128)(2,1)S(1)} %copy-done), custom_call_target="tpu_custom_call" | custom-call | flops 4194304 | bytes 8388608 | tf_op jit(solution)/shard_map/pallas_call | solution.py:61
  12.2 3.2 %collective-permute-done.3.refs_1_ = f32[4,8]{1,0:T(4,128)S(1)} collective-permute-done((f32[4,8]{1,0:T(4,128)S(1)}, f32[4,8]{1,0:T(4,128)S(1)}, u32[]{:S(2)}, u32[]{:S(2)}) %collective-permute-start.3) | collective-permute-done | bytes 160 | tf_op jit(solution)/shard_map/ppermute | solution.py:314
  15.4 0.0 collective-permute-done.refs_2_.refs_3_
  15.4 0.0 collective-permute-done.1.refs_4_.refs_5_
  15.4 0.0 collective-permute-done.2.refs_6_.refs_7_
  15.4 0.1 collective-permute-start.4
  15.5 2.0 %collective-permute-start.5 = (bf16[128,1024]{1,0:T(8,128)(2,1)S(1)}, bf16[128,1024]{1,0:T(8,128)(2,1)S(1)}, u32[]{:S(2)}, u32[]{:S(2)}) collective-permute-start(bf16[128,1024]{1,0:T(8,128)(2,1)S(1)} %collective-permute-done.1.refs_4_.refs_5_), channel_id=1, source_target_pairs={{0,16},{8,24},{2,0},{10,8},{4,2},{12,10},{6,4},{14,12},{22,6},{30,... | collective-permute-start | bytes 786440 | tf_op jit(solution)/shard_map/ppermute | solution.py:308
  17.5 0.0 collective-permute-start.6
  17.5 0.5 %collective-permute-start.7 = (bf16[128,1024]{1,0:T(8,128)(2,1)S(1)}, bf16[128,1024]{1,0:T(8,128)(2,1)S(1)}, u32[]{:S(2)}, u32[]{:S(2)}) collective-permute-start(bf16[128,1024]{1,0:T(8,128)(2,1)S(1)} %collective-permute-done.1.refs_4_.refs_5_), channel_id=1, source_target_pairs={{0,8},{8,0},{16,24},{24,16},{1,9},{9,1},{17,25},{25,17},{2,10},{10... | collective-permute-start | bytes 786440 | tf_op jit(solution)/shard_map/ppermute | solution.py:311
  18.0 0.5 collective-permute-start.8
  18.5 4.7 %collective-permute-done.8.refs_2_ = f32[4,8]{1,0:T(4,128)S(1)} collective-permute-done((f32[4,8]{1,0:T(4,128)S(1)}, f32[4,8]{1,0:T(4,128)S(1)}, u32[]{:S(2)}, u32[]{:S(2)}) %collective-permute-start.8) | collective-permute-done | bytes 160 | tf_op jit(solution)/shard_map/ppermute | solution.py:314
  23.1 0.0 collective-permute-done.4.refs_8_.refs_9_
  23.1 0.0 collective-permute-done.5.refs_10_.refs_11_
  23.1 0.0 collective-permute-done.6.refs_12_.refs_13_
  23.1 0.0 collective-permute-done.7.refs_14_.refs_15_
  23.1 0.7 %collective-permute-start.10 = (bf16[128,1024]{1,0:T(8,128)(2,1)S(1)}, bf16[128,1024]{1,0:T(8,128)(2,1)S(1)}, u32[]{:S(2)}, u32[]{:S(2)}) collective-permute-start(bf16[128,1024]{1,0:T(8,128)(2,1)S(1)} %collective-permute-done.5.refs_10_.refs_11_), channel_id=1, source_target_pairs={{0,16},{8,24},{2,0},{10,8},{4,2},{12,10},{6,4},{14,12},{22,6},{30,... | collective-permute-start | bytes 786440 | tf_op jit(solution)/shard_map/ppermute | solution.py:308
  23.9 0.0 collective-permute-start.11
  23.9 0.5 %collective-permute-start.12 = (bf16[128,1024]{1,0:T(8,128)(2,1)S(1)}, bf16[128,1024]{1,0:T(8,128)(2,1)S(1)}, u32[]{:S(2)}, u32[]{:S(2)}) collective-permute-start(bf16[128,1024]{1,0:T(8,128)(2,1)S(1)} %collective-permute-done.5.refs_10_.refs_11_), channel_id=1, source_target_pairs={{0,8},{8,0},{16,24},{24,16},{1,9},{9,1},{17,25},{25,17},{2,10},{10... | collective-permute-start | bytes 786440 | tf_op jit(solution)/shard_map/ppermute | solution.py:311
  24.4 1.4 %collective-permute-start.9 = (bf16[128,1024]{1,0:T(8,128)(2,1)S(1)}, bf16[128,1024]{1,0:T(8,128)(2,1)S(1)}, u32[]{:S(2)}, u32[]{:S(2)}) collective-permute-start(bf16[128,1024]{1,0:T(8,128)(2,1)S(1)} %collective-permute-done.4.refs_8_.refs_9_), channel_id=1, source_target_pairs={{0,2},{8,10},{2,4},{10,12},{4,6},{12,14},{6,22},{14,30},{22,20},{3... | collective-permute-start | bytes 786440 | tf_op jit(solution)/shard_map/ppermute | solution.py:308
  25.7 1.2 %collective-permute-start.13 = (f32[4,8]{1,0:T(4,128)S(1)}, f32[4,8]{1,0:T(4,128)S(1)}, u32[]{:S(2)}, u32[]{:S(2)}) collective-permute-start(f32[4,8]{1,0:T(4,128)S(1)} %pad_maximum_fusion.refs_0_), channel_id=1, source_target_pairs={{0,6},{2,0},{4,2},{6,4},{1,7},{3,1},{5,3},{7,5},{8,14},{10,8},{12,... | collective-permute-start | bytes 392 | tf_op jit(solution)/shard_map/ppermute | solution.py:314
  26.9 4.6 %collective-permute-done.13.refs_3_ = f32[4,8]{1,0:T(4,128)S(1)} collective-permute-done((f32[4,8]{1,0:T(4,128)S(1)}, f32[4,8]{1,0:T(4,128)S(1)}, u32[]{:S(2)}, u32[]{:S(2)}) %collective-permute-start.13) | collective-permute-done | bytes 160 | tf_op jit(solution)/shard_map/ppermute | solution.py:314
  31.5 0.0 collective-permute-done.10.refs_18_.refs_19_
  31.5 0.0 collective-permute-done.11.refs_20_.refs_21_
  31.5 0.0 collective-permute-done.12.refs_22_.refs_23_
  31.5 1.1 %collective-permute-done.9.refs_16_.refs_17_ = bf16[128,1024]{1,0:T(8,128)(2,1)S(1)} collective-permute-done((bf16[128,1024]{1,0:T(8,128)(2,1)S(1)}, bf16[128,1024]{1,0:T(8,128)(2,1)S(1)}, u32[]{:S(2)}, u32[]{:S(2)}) %collective-permute-start.9) | collective-permute-done | bytes 262176 | tf_op jit(solution)/shard_map/ppermute | solution.py:308
  32.6 0.1 collective-permute-start.16
  32.7 0.6 %collective-permute-start.17 = (bf16[128,1024]{1,0:T(8,128)(2,1)S(1)}, bf16[128,1024]{1,0:T(8,128)(2,1)S(1)}, u32[]{:S(2)}, u32[]{:S(2)}) collective-permute-start(bf16[128,1024]{1,0:T(8,128)(2,1)S(1)} %collective-permute-done.10.refs_18_.refs_19_), channel_id=1, source_target_pairs={{0,8},{8,0},{16,24},{24,16},{1,9},{9,1},{17,25},{25,17},{2,10},{10... | collective-permute-start | bytes 786440 | tf_op jit(solution)/shard_map/ppermute | solution.py:311
  33.2 1.4 %collective-permute-start.14 = (bf16[64,1024]{1,0:T(8,128)(2,1)S(1)}, bf16[64,1024]{1,0:T(8,128)(2,1)S(1)}, u32[]{:S(2)}, u32[]{:S(2)}) collective-permute-start(bf16[64,1024]{1,0:T(8,128)(2,1)S(1)} %slice.6), channel_id=1, source_target_pairs={{0,2},{8,10},{2,4},{10,12},{4,6},{12,14},{6,22},{14,30},{22,20},{3... | collective-permute-start | bytes 393224 | tf_op jit(solution)/shard_map/ppermute | solution.py:308
  34.6 0.6 %collective-permute-start.15 = (bf16[64,1024]{1,0:T(8,128)(2,1)S(1)}, bf16[64,1024]{1,0:T(8,128)(2,1)S(1)}, u32[]{:S(2)}, u32[]{:S(2)}) collective-permute-start(bf16[64,1024]{1,0:T(8,128)(2,1)S(1)} %slice.7), channel_id=1, source_target_pairs={{0,16},{8,24},{2,0},{10,8},{4,2},{12,10},{6,4},{14,12},{22,6},{30,... | collective-permute-start | bytes 393224 | tf_op jit(solution)/shard_map/ppermute | solution.py:308
  35.3 1.0 %shard_map.87 = (f32[8,16,128]{2,1,0:T(8,128)S(1)}, f32[8,16,128]{2,1,0:T(8,128)S(1)}) custom-call(f32[4,8]{1,0:T(4,128)S(1)} %pad_maximum_fusion.refs_0_, f32[4,8]{1,0:T(4,128)S(1)} %collective-permute-done.3.refs_1_, f32[4,8]{1,0:T(4,128)S(1)} %collective-permute-done.8.refs_2_, f32[4,8]{1,0:T(4,128)S(1)} %collective-permute-done.13.refs_3_), custom_call_target="tpu_custom_call" | custom-call | flops 100000000 | bytes 1000000 | tf_op jit(solution)/shard_map/pallas_call | solution.py:117
  36.3 6.7 %shard_map.88 = (f32[8,128,512]{2,1,0:T(8,128)S(1)}, f32[8,2,512]{2,1,0:T(2,128)S(1)}) custom-call(bf16[128,1024]{1,0:T(8,128)(2,1)S(1)} %constant_dynamic-update-slice_fusion.refs_0_.refs_1_, bf16[128,1024]{1,0:T(8,128)(2,1)S(1)} %constant_dynamic-update-slice_fusion.refs_0_.refs_1_, bf16[128,1024]{1,0:T(8,128)(2,1)S(1)} %collective-permute-done.refs_2_.refs_3_, ...), custom_call_target="tpu_custom_call" | custom-call | flops 6442450944 | bytes 8388608 | tf_op jit(solution)/shard_map/pallas_call | solution.py:262
  43.1 0.0 collective-permute-done.14.refs_0_
  43.1 0.0 collective-permute-done.15.refs_1_
  43.1 0.1 collective-permute-start.18
  43.2 0.5 %collective-permute-start.19 = (bf16[64,1024]{1,0:T(8,128)(2,1)S(1)}, bf16[64,1024]{1,0:T(8,128)(2,1)S(1)}, u32[]{:S(2)}, u32[]{:S(2)}) collective-permute-start(bf16[64,1024]{1,0:T(8,128)(2,1)S(1)} %collective-permute-done.15.refs_1_), channel_id=1, source_target_pairs={{0,8},{8,0},{16,24},{24,16},{1,9},{9,1},{17,25},{25,17},{2,10},{10... | collective-permute-start | bytes 393224 | tf_op jit(solution)/shard_map/ppermute | solution.py:311
  43.7 0.8 %collective-permute-done.18.refs_6_ = bf16[64,1024]{1,0:T(8,128)(2,1)S(1)} collective-permute-done((bf16[64,1024]{1,0:T(8,128)(2,1)S(1)}, bf16[64,1024]{1,0:T(8,128)(2,1)S(1)}, u32[]{:S(2)}, u32[]{:S(2)}) %collective-permute-start.18) | collective-permute-done | bytes 131104 | tf_op jit(solution)/shard_map/ppermute | solution.py:311
  44.5 0.2 collective-permute-done.19.refs_7_
  44.7 4.4 %shard_map.89 = (bf16[64,8192]{1,0:T(8,128)(2,1)}, f32[64,64]{1,0:T(8,128)}) custom-call(bf16[64,1024]{1,0:T(8,128)(2,1)S(1)} %collective-permute-done.14.refs_0_, bf16[64,1024]{1,0:T(8,128)(2,1)S(1)} %collective-permute-done.15.refs_1_, bf16[128,1024]{1,0:T(8,128)(2,1)S(1)} %collective-permute-done.16.refs_2_.refs_3_, ...), custom_call_target="tpu_custom_call" | custom-call | flops 2147483648 | bytes 8388608 | tf_op jit(solution)/shard_map/pallas_call | solution.py:262
  (7 shorter events, 0.0 us)
Async XLA Ops:
  2.5 12.9 %collective-permute-start = (bf16[128,1024]{1,0:T(8,128)(2,1)S(1)}, bf16[128,1024]{1,0:T(8,128)(2,1)S(1)}, u32[]{:S(2)}, u32[]{:S(2)}) collective-permute-start(bf16[128,1024]{1,0:T(8,128)(2,1)S(1)} %constant_dynamic-update-slice_fusion.refs_0_.refs_1_), channel_id=1, source_target_pairs={{0,2},{8,10},{2,4},{10,12},{4,6},{12,14},{6,22},{14,30},{22,20},{3... | collective-permute-start | bytes 786440 | tf_op jit(solution)/shard_map/ppermute | solution.py:308
  5.5 9.8 %collective-permute-start.1 = (bf16[128,1024]{1,0:T(8,128)(2,1)S(1)}, bf16[128,1024]{1,0:T(8,128)(2,1)S(1)}, u32[]{:S(2)}, u32[]{:S(2)}) collective-permute-start(bf16[128,1024]{1,0:T(8,128)(2,1)S(1)} %constant_dynamic-update-slice_fusion.refs_0_.refs_1_), channel_id=1, source_target_pairs={{0,16},{8,24},{2,0},{10,8},{4,2},{12,10},{6,4},{14,12},{22,6},{30,... | collective-permute-start | bytes 786440 | tf_op jit(solution)/shard_map/ppermute | solution.py:308
  5.6 9.8 %collective-permute-start.2 = (bf16[128,1024]{1,0:T(8,128)(2,1)S(1)}, bf16[128,1024]{1,0:T(8,128)(2,1)S(1)}, u32[]{:S(2)}, u32[]{:S(2)}) collective-permute-start(bf16[128,1024]{1,0:T(8,128)(2,1)S(1)} %constant_dynamic-update-slice_fusion.refs_0_.refs_1_), channel_id=1, source_target_pairs={{0,8},{8,0},{16,24},{24,16},{1,9},{9,1},{17,25},{25,17},{2,10},{10... | collective-permute-start | bytes 786440 | tf_op jit(solution)/shard_map/ppermute | solution.py:311
  6.3 9.1 %collective-permute-start.3 = (f32[4,8]{1,0:T(4,128)S(1)}, f32[4,8]{1,0:T(4,128)S(1)}, u32[]{:S(2)}, u32[]{:S(2)}) collective-permute-start(f32[4,8]{1,0:T(4,128)S(1)} %pad_maximum_fusion.refs_0_), channel_id=1, source_target_pairs={{0,2},{2,4},{4,6},{6,0},{1,3},{3,5},{5,7},{7,1},{8,10},{10,12},{12... | collective-permute-start | bytes 392 | tf_op jit(solution)/shard_map/ppermute | solution.py:314
  8.3 1.2 %copy-start = (bf16[64,8192]{1,0:T(8,128)(2,1)S(1)}, bf16[64,8192]{1,0:T(8,128)(2,1)}, u32[]{:S(2)}) copy-start(bf16[64,8192]{1,0:T(8,128)(2,1)} %q_ref.1) | copy-start | bytes 3145732
  9.5 0.7 %copy-start.1 = (s32[8,8]{1,0:T(8,128)S(1)}, s32[8,8]{1,0:T(8,128)}, u32[]{:S(2)}) copy-start(s32[8,8]{1,0:T(8,128)} %keep_ref.1) | copy-start | bytes 772
  10.2 0.7 %copy-start.2 = (s32[8]{0:T(128)S(1)}, s32[8]{0:T(128)}, u32[]{:S(2)}) copy-start(s32[8]{0:T(128)} %order_ref.1) | copy-start | bytes 100
  15.4 7.7 %collective-permute-start.4 = (bf16[128,1024]{1,0:T(8,128)(2,1)S(1)}, bf16[128,1024]{1,0:T(8,128)(2,1)S(1)}, u32[]{:S(2)}, u32[]{:S(2)}) collective-permute-start(bf16[128,1024]{1,0:T(8,128)(2,1)S(1)} %collective-permute-done.refs_2_.refs_3_), channel_id=1, source_target_pairs={{0,2},{8,10},{2,4},{10,12},{4,6},{12,14},{6,22},{14,30},{22,20},{3... | collective-permute-start | bytes 786440 | tf_op jit(solution)/shard_map/ppermute | solution.py:308
  15.5 7.7 %collective-permute-start.5 = (bf16[128,1024]{1,0:T(8,128)(2,1)S(1)}, bf16[128,1024]{1,0:T(8,128)(2,1)S(1)}, u32[]{:S(2)}, u32[]{:S(2)}) collective-permute-start(bf16[128,1024]{1,0:T(8,128)(2,1)S(1)} %collective-permute-done.1.refs_4_.refs_5_), channel_id=1, source_target_pairs={{0,16},{8,24},{2,0},{10,8},{4,2},{12,10},{6,4},{14,12},{22,6},{30,... | collective-permute-start | bytes 786440 | tf_op jit(solution)/shard_map/ppermute | solution.py:308
  17.5 5.7 %collective-permute-start.6 = (bf16[128,1024]{1,0:T(8,128)(2,1)S(1)}, bf16[128,1024]{1,0:T(8,128)(2,1)S(1)}, u32[]{:S(2)}, u32[]{:S(2)}) collective-permute-start(bf16[128,1024]{1,0:T(8,128)(2,1)S(1)} %collective-permute-done.refs_2_.refs_3_), channel_id=1, source_target_pairs={{0,8},{8,0},{16,24},{24,16},{1,9},{9,1},{17,25},{25,17},{2,10},{10... | collective-permute-start | bytes 786440 | tf_op jit(solution)/shard_map/ppermute | solution.py:311
  17.5 5.7 %collective-permute-start.7 = (bf16[128,1024]{1,0:T(8,128)(2,1)S(1)}, bf16[128,1024]{1,0:T(8,128)(2,1)S(1)}, u32[]{:S(2)}, u32[]{:S(2)}) collective-permute-start(bf16[128,1024]{1,0:T(8,128)(2,1)S(1)} %collective-permute-done.1.refs_4_.refs_5_), channel_id=1, source_target_pairs={{0,8},{8,0},{16,24},{24,16},{1,9},{9,1},{17,25},{25,17},{2,10},{10... | collective-permute-start | bytes 786440 | tf_op jit(solution)/shard_map/ppermute | solution.py:311
  18.0 5.1 %collective-permute-start.8 = (f32[4,8]{1,0:T(4,128)S(1)}, f32[4,8]{1,0:T(4,128)S(1)}, u32[]{:S(2)}, u32[]{:S(2)}) collective-permute-start(f32[4,8]{1,0:T(4,128)S(1)} %pad_maximum_fusion.refs_0_), channel_id=1, source_target_pairs={{0,4},{2,6},{4,0},{6,2},{1,5},{3,7},{5,1},{7,3},{8,12},{10,14},{12... | collective-permute-start | bytes 392 | tf_op jit(solution)/shard_map/ppermute | solution.py:314
  23.1 8.4 %collective-permute-start.10 = (bf16[128,1024]{1,0:T(8,128)(2,1)S(1)}, bf16[128,1024]{1,0:T(8,128)(2,1)S(1)}, u32[]{:S(2)}, u32[]{:S(2)}) collective-permute-start(bf16[128,1024]{1,0:T(8,128)(2,1)S(1)} %collective-permute-done.5.refs_10_.refs_11_), channel_id=1, source_target_pairs={{0,16},{8,24},{2,0},{10,8},{4,2},{12,10},{6,4},{14,12},{22,6},{30,... | collective-permute-start | bytes 786440 | tf_op jit(solution)/shard_map/ppermute | solution.py:308
  23.9 7.7 %collective-permute-start.11 = (bf16[128,1024]{1,0:T(8,128)(2,1)S(1)}, bf16[128,1024]{1,0:T(8,128)(2,1)S(1)}, u32[]{:S(2)}, u32[]{:S(2)}) collective-permute-start(bf16[128,1024]{1,0:T(8,128)(2,1)S(1)} %collective-permute-done.4.refs_8_.refs_9_), channel_id=1, source_target_pairs={{0,8},{8,0},{16,24},{24,16},{1,9},{9,1},{17,25},{25,17},{2,10},{10... | collective-permute-start | bytes 786440 | tf_op jit(solution)/shard_map/ppermute | solution.py:311
  23.9 7.7 %collective-permute-start.12 = (bf16[128,1024]{1,0:T(8,128)(2,1)S(1)}, bf16[128,1024]{1,0:T(8,128)(2,1)S(1)}, u32[]{:S(2)}, u32[]{:S(2)}) collective-permute-start(bf16[128,1024]{1,0:T(8,128)(2,1)S(1)} %collective-permute-done.5.refs_10_.refs_11_), channel_id=1, source_target_pairs={{0,8},{8,0},{16,24},{24,16},{1,9},{9,1},{17,25},{25,17},{2,10},{10... | collective-permute-start | bytes 786440 | tf_op jit(solution)/shard_map/ppermute | solution.py:311
  24.4 8.2 %collective-permute-start.9 = (bf16[128,1024]{1,0:T(8,128)(2,1)S(1)}, bf16[128,1024]{1,0:T(8,128)(2,1)S(1)}, u32[]{:S(2)}, u32[]{:S(2)}) collective-permute-start(bf16[128,1024]{1,0:T(8,128)(2,1)S(1)} %collective-permute-done.4.refs_8_.refs_9_), channel_id=1, source_target_pairs={{0,2},{8,10},{2,4},{10,12},{4,6},{12,14},{6,22},{14,30},{22,20},{3... | collective-permute-start | bytes 786440 | tf_op jit(solution)/shard_map/ppermute | solution.py:308
  25.7 5.8 %collective-permute-start.13 = (f32[4,8]{1,0:T(4,128)S(1)}, f32[4,8]{1,0:T(4,128)S(1)}, u32[]{:S(2)}, u32[]{:S(2)}) collective-permute-start(f32[4,8]{1,0:T(4,128)S(1)} %pad_maximum_fusion.refs_0_), channel_id=1, source_target_pairs={{0,6},{2,0},{4,2},{6,4},{1,7},{3,1},{5,3},{7,5},{8,14},{10,8},{12,... | collective-permute-start | bytes 392 | tf_op jit(solution)/shard_map/ppermute | solution.py:314
  32.6 10.5 %collective-permute-start.16 = (bf16[128,1024]{1,0:T(8,128)(2,1)S(1)}, bf16[128,1024]{1,0:T(8,128)(2,1)S(1)}, u32[]{:S(2)}, u32[]{:S(2)}) collective-permute-start(bf16[128,1024]{1,0:T(8,128)(2,1)S(1)} %collective-permute-done.9.refs_16_.refs_17_), channel_id=1, source_target_pairs={{0,8},{8,0},{16,24},{24,16},{1,9},{9,1},{17,25},{25,17},{2,10},{10... | collective-permute-start | bytes 786440 | tf_op jit(solution)/shard_map/ppermute | solution.py:311
  32.7 10.4 %collective-permute-start.17 = (bf16[128,1024]{1,0:T(8,128)(2,1)S(1)}, bf16[128,1024]{1,0:T(8,128)(2,1)S(1)}, u32[]{:S(2)}, u32[]{:S(2)}) collective-permute-start(bf16[128,1024]{1,0:T(8,128)(2,1)S(1)} %collective-permute-done.10.refs_18_.refs_19_), channel_id=1, source_target_pairs={{0,8},{8,0},{16,24},{24,16},{1,9},{9,1},{17,25},{25,17},{2,10},{10... | collective-permute-start | bytes 786440 | tf_op jit(solution)/shard_map/ppermute | solution.py:311
  33.2 9.8 %collective-permute-start.14 = (bf16[64,1024]{1,0:T(8,128)(2,1)S(1)}, bf16[64,1024]{1,0:T(8,128)(2,1)S(1)}, u32[]{:S(2)}, u32[]{:S(2)}) collective-permute-start(bf16[64,1024]{1,0:T(8,128)(2,1)S(1)} %slice.6), channel_id=1, source_target_pairs={{0,2},{8,10},{2,4},{10,12},{4,6},{12,14},{6,22},{14,30},{22,20},{3... | collective-permute-start | bytes 393224 | tf_op jit(solution)/shard_map/ppermute | solution.py:308
  34.6 8.4 %collective-permute-start.15 = (bf16[64,1024]{1,0:T(8,128)(2,1)S(1)}, bf16[64,1024]{1,0:T(8,128)(2,1)S(1)}, u32[]{:S(2)}, u32[]{:S(2)}) collective-permute-start(bf16[64,1024]{1,0:T(8,128)(2,1)S(1)} %slice.7), channel_id=1, source_target_pairs={{0,16},{8,24},{2,0},{10,8},{4,2},{12,10},{6,4},{14,12},{22,6},{30,... | collective-permute-start | bytes 393224 | tf_op jit(solution)/shard_map/ppermute | solution.py:308
  43.1 1.4 %collective-permute-start.18 = (bf16[64,1024]{1,0:T(8,128)(2,1)S(1)}, bf16[64,1024]{1,0:T(8,128)(2,1)S(1)}, u32[]{:S(2)}, u32[]{:S(2)}) collective-permute-start(bf16[64,1024]{1,0:T(8,128)(2,1)S(1)} %collective-permute-done.14.refs_0_), channel_id=1, source_target_pairs={{0,8},{8,0},{16,24},{24,16},{1,9},{9,1},{17,25},{25,17},{2,10},{10... | collective-permute-start | bytes 393224 | tf_op jit(solution)/shard_map/ppermute | solution.py:311
  43.2 1.5 %collective-permute-start.19 = (bf16[64,1024]{1,0:T(8,128)(2,1)S(1)}, bf16[64,1024]{1,0:T(8,128)(2,1)S(1)}, u32[]{:S(2)}, u32[]{:S(2)}) collective-permute-start(bf16[64,1024]{1,0:T(8,128)(2,1)S(1)} %collective-permute-done.15.refs_1_), channel_id=1, source_target_pairs={{0,8},{8,0},{16,24},{24,16},{1,9},{9,1},{17,25},{25,17},{2,10},{10... | collective-permute-start | bytes 393224 | tf_op jit(solution)/shard_map/ppermute | solution.py:311

commit v5 on v4

--- a/solution.py
+++ b/solution.py
@@ -326,22 +326,22 @@
         else:
             sources += [(step - 1, 1)]
 
-    block = jnp.concatenate([keys, values], axis=0)
+    block = lax.optimization_barrier(jnp.concatenate([keys, values], axis=0))
     scale = jnp.concatenate([jnp.transpose(key_scale), jnp.transpose(value_scale)], axis=0)
     scales, pieces, done = [scale], [[block]], 0
     fresh, forward, backward = [[block]], block, block
     prepared, rows, state = None, None, None
     for step in range(1, size // 2 + 2):
+        crossed = [to_other_core(piece) for piece in fresh]
         sent = []
         if step < size // 2:
             forward, backward = around(forward, 1), around(backward, -1)
             sent = [[forward], [backward]]
         elif step == size // 2:
             sent = [[around(forward[:tokens], 1), around(backward[tokens:], -1)]]
-        coming = sent + [to_other_core(piece) for piece in fresh]
         complete = len(scales) == head_size
-        if not complete:
-            scales = scales + [along_head(scale, len(scales))]
+        for shift in range(len(scales), min(head_size, len(scales) + 2)):
+            scales = scales + [along_head(scale, shift)]
         if step == 1:
             prepared = prepare(queries, span_order, block_keep, sources, kv_heads, sizes)
         if complete:
@@ -352,13 +352,13 @@
                 now = pieces[done : done + ready]
                 state = absorb((*prepared, *rows), now, done, state, False, tokens)
                 done += ready
-        coming, scales, prepared, rows, state = lax.optimization_barrier(
-            (coming, scales, prepared, rows, state)
-        )
-        fresh = coming[: len(sent)]
+        crossed, sent, scales, prepared, rows, state = lax.optimization_barrier(
+            (crossed, sent, scales, prepared, rows, state)
+        )
+        fresh = sent
         if step < size // 2:
             forward, backward = fresh[0][0], fresh[1][0]
-        pieces = pieces + list(coming)
+        pieces = pieces + sent + crossed
     return tuple(absorb((*prepared, *rows), pieces[done:], done, state, True, tokens))
 
 

time: 49.3 us -> 45.9 us (0.931)
  waiting for transfers between devices: 14.5 us -> 7.97 us
  starting transfers between devices: 15.2 us -> 17.6 us
  local copies, waits for them, and re-layouts: 4.42 us -> 2.59 us
  Pallas kernels: 13.5 us -> 15 us
  other arithmetic: 0.7 us -> 1.69 us
    ppermute x3, waiting for transfers between devices: 12.4 us -> 4.34 us  [along_head(): lax.ppermute(block, 'head', [(i, (i + distance) % head_size) for i in ran...]
    ppermute x3, starting transfers between devices: 3.7 us -> 6.65 us  [along_head(): lax.ppermute(block, 'head', [(i, (i + distance) % head_size) for i in ran...]
    ppermute x8, waiting for transfers between devices: 1.07 us -> 2.58 us  [around(): return lax.ppermute(block, ('ctx', 'head'), route)]
    pallas_call x2 -> x3, Pallas kernels: 11.1 us -> 12.6 us  [absorb(): pl.pallas_call(functools.partial(absorb_kernel, groups=groups, tokens=tok...]
    concatenate x0 -> x1, other arithmetic: none -> 0.99 us  [local(): block = lax.optimization_barrier(jnp.concatenate([keys, values], axis=0))]
    concatenate x1 -> x0, local copies, waits for them, and re-layouts: 0.92 us -> none  [local(): block = jnp.concatenate([keys, values], axis=0)]
    unnamed x7 -> x6, local copies, waits for them, and re-layouts: 3.48 us -> 2.57 us
    ppermute x9, starting transfers between devices: 2.22 us -> 1.47 us  [to_other_core(): lax.ppermute(block, 'ctx', [(i, i ^ 1) for i in range(ctx_size)])]
  transfers between devices with their start and end apart: 20 -> 20, of which waited for: 6 -> 6; matrix products, arithmetic and copies ran while one was open for 1% -> 2% of each run, Pallas kernels for 19% -> 23%
where the time goes in v5:
time: 45.9 us; the launch traced here: 45.6 us
  starting transfers between devices  17.6 us (38%)
  Pallas kernels  15 us (33%)
  waiting for transfers between devices  7.97 us (17%)
  local copies, waits for them, and re-layouts  2.59 us (6%)
  other arithmetic  1.69 us (4%)
  between operations  0.78 us (2%)
    pallas_call x3, Pallas kernels, absorb(): pl.pallas_call(functools.partial(absorb_kernel, groups=groups, tokens=tok...  12.6 us
    ppermute x8, starting transfers between devices, around(): return lax.ppermute(block, ('ctx', 'head'), route)  9.52 us
    ppermute x3, starting transfers between devices, along_head(): lax.ppermute(block, 'head', [(i, (i + distance) % head_size) for i in ran...  6.65 us
    ppermute x3, waiting for transfers between devices, along_head(): lax.ppermute(block, 'head', [(i, (i + distance) % head_size) for i in ran...  4.34 us
    ppermute x8, waiting for transfers between devices, around(): return lax.ppermute(block, ('ctx', 'head'), route)  2.58 us
    unnamed x6, local copies, waits for them, and re-layouts  2.57 us
    ppermute x9, starting transfers between devices, to_other_core(): lax.ppermute(block, 'ctx', [(i, i ^ 1) for i in range(ctx_size)])  1.47 us
    pallas_call x1, Pallas kernels, prepare(): pl.pallas_call(functools.partial(prepare_kernel, groups=groups, per_step=...  1.36 us
  transfers between devices with their start and end apart: 20, of which 6 were waited for; matrix products, arithmetic and copies ran while one was open for 2% of the time, Pallas kernels for 23%

profile of v5, /device:TPU:0, one launch (start us, length us, event | category | flops | bytes accessed | tf_op | source)
XLA Modules:
  0.0 45.6 jit_solution(11998948910114433612)
XLA Ops:
  0.6 1.0 %pad_maximum_fusion.refs_0_.refs_1_ = bf16[128,1024]{1,0:T(8,128)(2,1)S(1)} fusion(bf16[64,1024]{1,0:T(8,128)(2,1)} %param.9, bf16[64,1024]{1,0:T(8,128)(2,1)} %param.8), kind=kLoop, calls=%fused_computation | loop fusion | flops 524288 | bytes 524288 | tf_op jit(solution)/shard_map/concatenate | solution.py:329
  1.6 3.0 %collective-permute-start.2 = (bf16[128,1024]{1,0:T(8,128)(2,1)S(1)}, bf16[128,1024]{1,0:T(8,128)(2,1)S(1)}, u32[]{:S(2)}, u32[]{:S(2)}) collective-permute-start(bf16[128,1024]{1,0:T(8,128)(2,1)S(1)} %pad_maximum_fusion.refs_0_.refs_1_), channel_id=1, source_target_pairs={{0,16},{8,24},{2,0},{10,8},{4,2},{12,10},{6,4},{14,12},{22,6},{30,... | collective-permute-start | bytes 786440 | tf_op jit(solution)/shard_map/ppermute | solution.py:308
  4.6 0.1 collective-permute-start.1
  4.8 0.0 collective-permute-start
  4.8 0.7 %pad_maximum_fusion.1.refs_0_ = f32[4,8]{1,0:T(4,128)S(1)} fusion(f32[2,8]{1,0:T(2,128)} %bitcast.2, f32[2,8]{1,0:T(2,128)} %bitcast.3), kind=kLoop, calls=%fused_computation.1 | loop fusion | flops 32 | bytes 256 | tf_op jit(solution)/shard_map/concatenate | solution.py:330
  5.5 3.0 %collective-permute-start.4 = (f32[4,8]{1,0:T(4,128)S(1)}, f32[4,8]{1,0:T(4,128)S(1)}, u32[]{:S(2)}, u32[]{:S(2)}) collective-permute-start(f32[4,8]{1,0:T(4,128)S(1)} %pad_maximum_fusion.1.refs_0_), channel_id=1, source_target_pairs={{0,4},{2,6},{4,0},{6,2},{1,5},{3,7},{5,1},{7,3},{8,12},{10,14},{12... | collective-permute-start | bytes 392 | tf_op jit(solution)/shard_map/ppermute | solution.py:314
  8.4 1.6 %collective-permute-start.3 = (f32[4,8]{1,0:T(4,128)S(1)}, f32[4,8]{1,0:T(4,128)S(1)}, u32[]{:S(2)}, u32[]{:S(2)}) collective-permute-start(f32[4,8]{1,0:T(4,128)S(1)} %pad_maximum_fusion.1.refs_0_), channel_id=1, source_target_pairs={{0,2},{2,4},{4,6},{6,0},{1,3},{3,5},{5,7},{7,1},{8,10},{10,12},{12... | collective-permute-start | bytes 392 | tf_op jit(solution)/shard_map/ppermute | solution.py:314
  10.0 1.2 %copy-done = bf16[64,8192]{1,0:T(8,128)(2,1)S(1)} copy-done((bf16[64,8192]{1,0:T(8,128)(2,1)S(1)}, bf16[64,8192]{1,0:T(8,128)(2,1)}, u32[]{:S(2)}) %copy-start) | copy-done | bytes 1048600
  11.2 0.7 %copy-done.1 = s32[8,8]{1,0:T(8,128)S(1)} copy-done((s32[8,8]{1,0:T(8,128)S(1)}, s32[8,8]{1,0:T(8,128)}, u32[]{:S(2)}) %copy-start.1) | copy-done | bytes 280
  11.9 0.7 %copy-done.2 = s32[8]{0:T(128)S(1)} copy-done((s32[8]{0:T(128)S(1)}, s32[8]{0:T(128)}, u32[]{:S(2)}) %copy-start.2) | copy-done | bytes 56
  12.6 1.4 %shard_map.86 = (bf16[8,512,256]{2,1,0:T(8,128)(2,1)S(1)}, bf16[1024,128]{1,0:T(8,128)(2,1)S(1)}) custom-call(s32[8]{0:T(128)S(1)} %copy-done.2, s32[8,8]{1,0:T(8,128)S(1)} %copy-done.1, bf16[64,8192]{1,0:T(8,128)(2,1)S(1)} %copy-done), custom_call_target="tpu_custom_call" | custom-call | flops 4194304 | bytes 8388608 | tf_op jit(solution)/shard_map/pallas_call | solution.py:61
  14.0 0.0 collective-permute-done.4.refs_2_
  14.0 0.0 collective-permute-done.3.refs_1_
  14.0 0.0 collective-permute-done.2.refs_4_.refs_5_
  14.0 0.0 collective-permute-done.1.refs_2_.refs_3_
  14.0 0.0 collective-permute-done.refs_6_.refs_7_
  14.0 0.1 collective-permute-start.7
  14.1 0.1 collective-permute-start.5
  14.2 2.1 %collective-permute-start.8 = (bf16[128,1024]{1,0:T(8,128)(2,1)S(1)}, bf16[128,1024]{1,0:T(8,128)(2,1)S(1)}, u32[]{:S(2)}, u32[]{:S(2)}) collective-permute-start(bf16[128,1024]{1,0:T(8,128)(2,1)S(1)} %collective-permute-done.2.refs_4_.refs_5_), channel_id=1, source_target_pairs={{0,16},{8,24},{2,0},{10,8},{4,2},{12,10},{6,4},{14,12},{22,6},{30,... | collective-permute-start | bytes 786440 | tf_op jit(solution)/shard_map/ppermute | solution.py:308
  16.3 0.2 collective-permute-start.6
  16.5 2.1 %collective-permute-start.9 = (f32[4,8]{1,0:T(4,128)S(1)}, f32[4,8]{1,0:T(4,128)S(1)}, u32[]{:S(2)}, u32[]{:S(2)}) collective-permute-start(f32[4,8]{1,0:T(4,128)S(1)} %pad_maximum_fusion.1.refs_0_), channel_id=1, source_target_pairs={{0,6},{2,0},{4,2},{6,4},{1,7},{3,1},{5,3},{7,5},{8,14},{10,8},{12,... | collective-permute-start | bytes 392 | tf_op jit(solution)/shard_map/ppermute | solution.py:314
  18.6 4.3 %collective-permute-done.9.refs_3_ = f32[4,8]{1,0:T(4,128)S(1)} collective-permute-done((f32[4,8]{1,0:T(4,128)S(1)}, f32[4,8]{1,0:T(4,128)S(1)}, u32[]{:S(2)}, u32[]{:S(2)}) %collective-permute-start.9) | collective-permute-done | bytes 160 | tf_op jit(solution)/shard_map/ppermute | solution.py:314
  22.9 0.0 collective-permute-done.7.refs_8_.refs_9_
  22.9 0.0 collective-permute-done.5.refs_12_.refs_13_
  22.9 0.0 collective-permute-done.8.refs_10_.refs_11_
  22.9 0.0 collective-permute-done.6.refs_14_.refs_15_
  22.9 1.6 %collective-permute-start.12 = (bf16[128,1024]{1,0:T(8,128)(2,1)S(1)}, bf16[128,1024]{1,0:T(8,128)(2,1)S(1)}, u32[]{:S(2)}, u32[]{:S(2)}) collective-permute-start(bf16[128,1024]{1,0:T(8,128)(2,1)S(1)} %collective-permute-done.7.refs_8_.refs_9_), channel_id=1, source_target_pairs={{0,2},{8,10},{2,4},{10,12},{4,6},{12,14},{6,22},{14,30},{22,20},{3... | collective-permute-start | bytes 786440 | tf_op jit(solution)/shard_map/ppermute | solution.py:308
  24.5 0.0 collective-permute-start.10
  24.5 0.5 %collective-permute-start.13 = (bf16[128,1024]{1,0:T(8,128)(2,1)S(1)}, bf16[128,1024]{1,0:T(8,128)(2,1)S(1)}, u32[]{:S(2)}, u32[]{:S(2)}) collective-permute-start(bf16[128,1024]{1,0:T(8,128)(2,1)S(1)} %collective-permute-done.8.refs_10_.refs_11_), channel_id=1, source_target_pairs={{0,16},{8,24},{2,0},{10,8},{4,2},{12,10},{6,4},{14,12},{22,6},{30,... | collective-permute-start | bytes 786440 | tf_op jit(solution)/shard_map/ppermute | solution.py:308
  25.0 0.2 collective-permute-start.11
  25.2 1.0 %shard_map.87 = (f32[8,16,128]{2,1,0:T(8,128)S(1)}, f32[8,16,128]{2,1,0:T(8,128)S(1)}) custom-call(f32[4,8]{1,0:T(4,128)S(1)} %pad_maximum_fusion.1.refs_0_, f32[4,8]{1,0:T(4,128)S(1)} %collective-permute-done.3.refs_1_, f32[4,8]{1,0:T(4,128)S(1)} %collective-permute-done.4.refs_2_, f32[4,8]{1,0:T(4,128)S(1)} %collective-permute-done.9.refs_3_), custom_call_target="tpu_custom_call" | custom-call | flops 100000000 | bytes 1000000 | tf_op jit(solution)/shard_map/pallas_call | solution.py:117
  26.3 5.0 %shard_map.88 = (f32[8,128,512]{2,1,0:T(8,128)S(1)}, f32[8,2,512]{2,1,0:T(2,128)S(1)}) custom-call(bf16[128,1024]{1,0:T(8,128)(2,1)S(1)} %pad_maximum_fusion.refs_0_.refs_1_, bf16[128,1024]{1,0:T(8,128)(2,1)S(1)} %pad_maximum_fusion.refs_0_.refs_1_, bf16[128,1024]{1,0:T(8,128)(2,1)S(1)} %collective-permute-done.1.refs_2_.refs_3_, ...), custom_call_target="tpu_custom_call" | custom-call | flops 4294967296 | bytes 8388608 | tf_op jit(solution)/shard_map/pallas_call | solution.py:262
  31.3 0.0 collective-permute-done.12.refs_0_.refs_1_
  31.3 0.0 collective-permute-done.10.refs_4_.refs_5_
  31.3 2.0 %collective-permute-done.13.refs_2_.refs_3_ = bf16[128,1024]{1,0:T(8,128)(2,1)S(1)} collective-permute-done((bf16[128,1024]{1,0:T(8,128)(2,1)S(1)}, bf16[128,1024]{1,0:T(8,128)(2,1)S(1)}, u32[]{:S(2)}, u32[]{:S(2)}) %collective-permute-start.13) | collective-permute-done | bytes 262176 | tf_op jit(solution)/shard_map/ppermute | solution.py:308
  33.3 0.0 collective-permute-done.11.refs_6_.refs_7_
  33.3 0.0 collective-permute-start.14
  33.3 0.5 %collective-permute-start.15 = (bf16[128,1024]{1,0:T(8,128)(2,1)S(1)}, bf16[128,1024]{1,0:T(8,128)(2,1)S(1)}, u32[]{:S(2)}, u32[]{:S(2)}) collective-permute-start(bf16[128,1024]{1,0:T(8,128)(2,1)S(1)} %collective-permute-done.13.refs_2_.refs_3_), channel_id=1, source_target_pairs={{0,8},{8,0},{16,24},{24,16},{1,9},{9,1},{17,25},{25,17},{2,10},{10... | collective-permute-start | bytes 786440 | tf_op jit(solution)/shard_map/ppermute | solution.py:311
  33.8 0.5 %collective-permute-start.17 = (bf16[64,1024]{1,0:T(8,128)(2,1)S(1)}, bf16[64,1024]{1,0:T(8,128)(2,1)S(1)}, u32[]{:S(2)}, u32[]{:S(2)}) collective-permute-start(bf16[64,1024]{1,0:T(8,128)(2,1)S(1)} %slice.7), channel_id=1, source_target_pairs={{0,16},{8,24},{2,0},{10,8},{4,2},{12,10},{6,4},{14,12},{22,6},{30,... | collective-permute-start | bytes 393224 | tf_op jit(solution)/shard_map/ppermute | solution.py:308
  34.3 1.6 %collective-permute-start.16 = (bf16[64,1024]{1,0:T(8,128)(2,1)S(1)}, bf16[64,1024]{1,0:T(8,128)(2,1)S(1)}, u32[]{:S(2)}, u32[]{:S(2)}) collective-permute-start(bf16[64,1024]{1,0:T(8,128)(2,1)S(1)} %slice.6), channel_id=1, source_target_pairs={{0,2},{8,10},{2,4},{10,12},{4,6},{12,14},{6,22},{14,30},{22,20},{3... | collective-permute-start | bytes 393224 | tf_op jit(solution)/shard_map/ppermute | solution.py:308
  35.9 3.2 %shard_map.89 = (f32[8,128,512]{2,1,0:T(8,128)S(1)}, f32[8,2,512]{2,1,0:T(2,128)S(1)}) custom-call(bf16[128,1024]{1,0:T(8,128)(2,1)S(1)} %collective-permute-done.12.refs_0_.refs_1_, bf16[128,1024]{1,0:T(8,128)(2,1)S(1)} %collective-permute-done.12.refs_0_.refs_1_, bf16[128,1024]{1,0:T(8,128)(2,1)S(1)} %collective-permute-done.13.refs_2_.refs_3_, ...), custom_call_target="tpu_custom_call" | custom-call | flops 2147483648 | bytes 8388608 | tf_op jit(solution)/shard_map/pallas_call | solution.py:262
  39.1 0.2 collective-permute-done.17.refs_1_
  39.3 0.4 collective-permute-done.16.refs_0_
  39.7 0.0 collective-permute-done.14.refs_2_.refs_3_
  39.7 0.5 %collective-permute-start.19 = (bf16[64,1024]{1,0:T(8,128)(2,1)S(1)}, bf16[64,1024]{1,0:T(8,128)(2,1)S(1)}, u32[]{:S(2)}, u32[]{:S(2)}) collective-permute-start(bf16[64,1024]{1,0:T(8,128)(2,1)S(1)} %collective-permute-done.17.refs_1_), channel_id=1, source_target_pairs={{0,8},{8,0},{16,24},{24,16},{1,9},{9,1},{17,25},{25,17},{2,10},{10... | collective-permute-start | bytes 393224 | tf_op jit(solution)/shard_map/ppermute | solution.py:311
  40.2 0.8 %collective-permute-done.18.refs_6_ = bf16[64,1024]{1,0:T(8,128)(2,1)S(1)} collective-permute-done((bf16[64,1024]{1,0:T(8,128)(2,1)S(1)}, bf16[64,1024]{1,0:T(8,128)(2,1)S(1)}, u32[]{:S(2)}, u32[]{:S(2)}) %collective-permute-start.18) | collective-permute-done | bytes 131104 | tf_op jit(solution)/shard_map/ppermute | solution.py:311
  41.1 0.2 collective-permute-done.19.refs_7_
  41.2 4.4 %shard_map.90 = (bf16[64,8192]{1,0:T(8,128)(2,1)}, f32[64,64]{1,0:T(8,128)}) custom-call(bf16[64,1024]{1,0:T(8,128)(2,1)S(1)} %collective-permute-done.16.refs_0_, bf16[64,1024]{1,0:T(8,128)(2,1)S(1)} %collective-permute-done.17.refs_1_, bf16[128,1024]{1,0:T(8,128)(2,1)S(1)} %collective-permute-done.14.refs_2_.refs_3_, ...), custom_call_target="tpu_custom_call" | custom-call | flops 2147483648 | bytes 8388608 | tf_op jit(solution)/shard_map/pallas_call | solution.py:262
  (7 shorter events, 0.0 us)
Async XLA Ops:
  1.6 12.4 %collective-permute-start.2 = (bf16[128,1024]{1,0:T(8,128)(2,1)S(1)}, bf16[128,1024]{1,0:T(8,128)(2,1)S(1)}, u32[]{:S(2)}, u32[]{:S(2)}) collective-permute-start(bf16[128,1024]{1,0:T(8,128)(2,1)S(1)} %pad_maximum_fusion.refs_0_.refs_1_), channel_id=1, source_target_pairs={{0,16},{8,24},{2,0},{10,8},{4,2},{12,10},{6,4},{14,12},{22,6},{30,... | collective-permute-start | bytes 786440 | tf_op jit(solution)/shard_map/ppermute | solution.py:308
  4.6 9.4 %collective-permute-start.1 = (bf16[128,1024]{1,0:T(8,128)(2,1)S(1)}, bf16[128,1024]{1,0:T(8,128)(2,1)S(1)}, u32[]{:S(2)}, u32[]{:S(2)}) collective-permute-start(bf16[128,1024]{1,0:T(8,128)(2,1)S(1)} %pad_maximum_fusion.refs_0_.refs_1_), channel_id=1, source_target_pairs={{0,2},{8,10},{2,4},{10,12},{4,6},{12,14},{6,22},{14,30},{22,20},{3... | collective-permute-start | bytes 786440 | tf_op jit(solution)/shard_map/ppermute | solution.py:308
  4.8 9.2 %collective-permute-start = (bf16[128,1024]{1,0:T(8,128)(2,1)S(1)}, bf16[128,1024]{1,0:T(8,128)(2,1)S(1)}, u32[]{:S(2)}, u32[]{:S(2)}) collective-permute-start(bf16[128,1024]{1,0:T(8,128)(2,1)S(1)} %pad_maximum_fusion.refs_0_.refs_1_), channel_id=1, source_target_pairs={{0,8},{8,0},{16,24},{24,16},{1,9},{9,1},{17,25},{25,17},{2,10},{10... | collective-permute-start | bytes 786440 | tf_op jit(solution)/shard_map/ppermute | solution.py:311
  5.5 8.5 %collective-permute-start.4 = (f32[4,8]{1,0:T(4,128)S(1)}, f32[4,8]{1,0:T(4,128)S(1)}, u32[]{:S(2)}, u32[]{:S(2)}) collective-permute-start(f32[4,8]{1,0:T(4,128)S(1)} %pad_maximum_fusion.1.refs_0_), channel_id=1, source_target_pairs={{0,4},{2,6},{4,0},{6,2},{1,5},{3,7},{5,1},{7,3},{8,12},{10,14},{12... | collective-permute-start | bytes 392 | tf_op jit(solution)/shard_map/ppermute | solution.py:314
  8.4 5.5 %collective-permute-start.3 = (f32[4,8]{1,0:T(4,128)S(1)}, f32[4,8]{1,0:T(4,128)S(1)}, u32[]{:S(2)}, u32[]{:S(2)}) collective-permute-start(f32[4,8]{1,0:T(4,128)S(1)} %pad_maximum_fusion.1.refs_0_), channel_id=1, source_target_pairs={{0,2},{2,4},{4,6},{6,0},{1,3},{3,5},{5,7},{7,1},{8,10},{10,12},{12... | collective-permute-start | bytes 392 | tf_op jit(solution)/shard_map/ppermute | solution.py:314
  10.0 1.2 %copy-start = (bf16[64,8192]{1,0:T(8,128)(2,1)S(1)}, bf16[64,8192]{1,0:T(8,128)(2,1)}, u32[]{:S(2)}) copy-start(bf16[64,8192]{1,0:T(8,128)(2,1)} %q_ref.1) | copy-start | bytes 3145732
  11.2 0.7 %copy-start.1 = (s32[8,8]{1,0:T(8,128)S(1)}, s32[8,8]{1,0:T(8,128)}, u32[]{:S(2)}) copy-start(s32[8,8]{1,0:T(8,128)} %keep_ref.1) | copy-start | bytes 772
  11.9 0.7 %copy-start.2 = (s32[8]{0:T(128)S(1)}, s32[8]{0:T(128)}, u32[]{:S(2)}) copy-start(s32[8]{0:T(128)} %order_ref.1) | copy-start | bytes 100
  14.0 8.9 %collective-permute-start.7 = (bf16[128,1024]{1,0:T(8,128)(2,1)S(1)}, bf16[128,1024]{1,0:T(8,128)(2,1)S(1)}, u32[]{:S(2)}, u32[]{:S(2)}) collective-permute-start(bf16[128,1024]{1,0:T(8,128)(2,1)S(1)} %collective-permute-done.1.refs_2_.refs_3_), channel_id=1, source_target_pairs={{0,2},{8,10},{2,4},{10,12},{4,6},{12,14},{6,22},{14,30},{22,20},{3... | collective-permute-start | bytes 786440 | tf_op jit(solution)/shard_map/ppermute | solution.py:308
  14.1 8.8 %collective-permute-start.5 = (bf16[128,1024]{1,0:T(8,128)(2,1)S(1)}, bf16[128,1024]{1,0:T(8,128)(2,1)S(1)}, u32[]{:S(2)}, u32[]{:S(2)}) collective-permute-start(bf16[128,1024]{1,0:T(8,128)(2,1)S(1)} %collective-permute-done.1.refs_2_.refs_3_), channel_id=1, source_target_pairs={{0,8},{8,0},{16,24},{24,16},{1,9},{9,1},{17,25},{25,17},{2,10},{10... | collective-permute-start | bytes 786440 | tf_op jit(solution)/shard_map/ppermute | solution.py:311
  14.2 8.8 %collective-permute-start.8 = (bf16[128,1024]{1,0:T(8,128)(2,1)S(1)}, bf16[128,1024]{1,0:T(8,128)(2,1)S(1)}, u32[]{:S(2)}, u32[]{:S(2)}) collective-permute-start(bf16[128,1024]{1,0:T(8,128)(2,1)S(1)} %collective-permute-done.2.refs_4_.refs_5_), channel_id=1, source_target_pairs={{0,16},{8,24},{2,0},{10,8},{4,2},{12,10},{6,4},{14,12},{22,6},{30,... | collective-permute-start | bytes 786440 | tf_op jit(solution)/shard_map/ppermute | solution.py:308
  16.3 6.6 %collective-permute-start.6 = (bf16[128,1024]{1,0:T(8,128)(2,1)S(1)}, bf16[128,1024]{1,0:T(8,128)(2,1)S(1)}, u32[]{:S(2)}, u32[]{:S(2)}) collective-permute-start(bf16[128,1024]{1,0:T(8,128)(2,1)S(1)} %collective-permute-done.2.refs_4_.refs_5_), channel_id=1, source_target_pairs={{0,8},{8,0},{16,24},{24,16},{1,9},{9,1},{17,25},{25,17},{2,10},{10... | collective-permute-start | bytes 786440 | tf_op jit(solution)/shard_map/ppermute | solution.py:311
  16.5 6.4 %collective-permute-start.9 = (f32[4,8]{1,0:T(4,128)S(1)}, f32[4,8]{1,0:T(4,128)S(1)}, u32[]{:S(2)}, u32[]{:S(2)}) collective-permute-start(f32[4,8]{1,0:T(4,128)S(1)} %pad_maximum_fusion.1.refs_0_), channel_id=1, source_target_pairs={{0,6},{2,0},{4,2},{6,4},{1,7},{3,1},{5,3},{7,5},{8,14},{10,8},{12,... | collective-permute-start | bytes 392 | tf_op jit(solution)/shard_map/ppermute | solution.py:314
  22.9 8.3 %collective-permute-start.12 = (bf16[128,1024]{1,0:T(8,128)(2,1)S(1)}, bf16[128,1024]{1,0:T(8,128)(2,1)S(1)}, u32[]{:S(2)}, u32[]{:S(2)}) collective-permute-start(bf16[128,1024]{1,0:T(8,128)(2,1)S(1)} %collective-permute-done.7.refs_8_.refs_9_), channel_id=1, source_target_pairs={{0,2},{8,10},{2,4},{10,12},{4,6},{12,14},{6,22},{14,30},{22,20},{3... | collective-permute-start | bytes 786440 | tf_op jit(solution)/shard_map/ppermute | solution.py:308
  24.5 6.7 %collective-permute-start.10 = (bf16[128,1024]{1,0:T(8,128)(2,1)S(1)}, bf16[128,1024]{1,0:T(8,128)(2,1)S(1)}, u32[]{:S(2)}, u32[]{:S(2)}) collective-permute-start(bf16[128,1024]{1,0:T(8,128)(2,1)S(1)} %collective-permute-done.7.refs_8_.refs_9_), channel_id=1, source_target_pairs={{0,8},{8,0},{16,24},{24,16},{1,9},{9,1},{17,25},{25,17},{2,10},{10... | collective-permute-start | bytes 786440 | tf_op jit(solution)/shard_map/ppermute | solution.py:311
  24.5 8.7 %collective-permute-start.13 = (bf16[128,1024]{1,0:T(8,128)(2,1)S(1)}, bf16[128,1024]{1,0:T(8,128)(2,1)S(1)}, u32[]{:S(2)}, u32[]{:S(2)}) collective-permute-start(bf16[128,1024]{1,0:T(8,128)(2,1)S(1)} %collective-permute-done.8.refs_10_.refs_11_), channel_id=1, source_target_pairs={{0,16},{8,24},{2,0},{10,8},{4,2},{12,10},{6,4},{14,12},{22,6},{30,... | collective-permute-start | bytes 786440 | tf_op jit(solution)/shard_map/ppermute | solution.py:308
  25.0 8.2 %collective-permute-start.11 = (bf16[128,1024]{1,0:T(8,128)(2,1)S(1)}, bf16[128,1024]{1,0:T(8,128)(2,1)S(1)}, u32[]{:S(2)}, u32[]{:S(2)}) collective-permute-start(bf16[128,1024]{1,0:T(8,128)(2,1)S(1)} %collective-permute-done.8.refs_10_.refs_11_), channel_id=1, source_target_pairs={{0,8},{8,0},{16,24},{24,16},{1,9},{9,1},{17,25},{25,17},{2,10},{10... | collective-permute-start | bytes 786440 | tf_op jit(solution)/shard_map/ppermute | solution.py:311
  33.3 6.4 %collective-permute-start.14 = (bf16[128,1024]{1,0:T(8,128)(2,1)S(1)}, bf16[128,1024]{1,0:T(8,128)(2,1)S(1)}, u32[]{:S(2)}, u32[]{:S(2)}) collective-permute-start(bf16[128,1024]{1,0:T(8,128)(2,1)S(1)} %collective-permute-done.12.refs_0_.refs_1_), channel_id=1, source_target_pairs={{0,8},{8,0},{16,24},{24,16},{1,9},{9,1},{17,25},{25,17},{2,10},{10... | collective-permute-start | bytes 786440 | tf_op jit(solution)/shard_map/ppermute | solution.py:311
  33.3 6.4 %collective-permute-start.15 = (bf16[128,1024]{1,0:T(8,128)(2,1)S(1)}, bf16[128,1024]{1,0:T(8,128)(2,1)S(1)}, u32[]{:S(2)}, u32[]{:S(2)}) collective-permute-start(bf16[128,1024]{1,0:T(8,128)(2,1)S(1)} %collective-permute-done.13.refs_2_.refs_3_), channel_id=1, source_target_pairs={{0,8},{8,0},{16,24},{24,16},{1,9},{9,1},{17,25},{25,17},{2,10},{10... | collective-permute-start | bytes 786440 | tf_op jit(solution)/shard_map/ppermute | solution.py:311
  33.8 5.5 %collective-permute-start.17 = (bf16[64,1024]{1,0:T(8,128)(2,1)S(1)}, bf16[64,1024]{1,0:T(8,128)(2,1)S(1)}, u32[]{:S(2)}, u32[]{:S(2)}) collective-permute-start(bf16[64,1024]{1,0:T(8,128)(2,1)S(1)} %slice.7), channel_id=1, source_target_pairs={{0,16},{8,24},{2,0},{10,8},{4,2},{12,10},{6,4},{14,12},{22,6},{30,... | collective-permute-start | bytes 393224 | tf_op jit(solution)/shard_map/ppermute | solution.py:308
  34.3 5.4 %collective-permute-start.16 = (bf16[64,1024]{1,0:T(8,128)(2,1)S(1)}, bf16[64,1024]{1,0:T(8,128)(2,1)S(1)}, u32[]{:S(2)}, u32[]{:S(2)}) collective-permute-start(bf16[64,1024]{1,0:T(8,128)(2,1)S(1)} %slice.6), channel_id=1, source_target_pairs={{0,2},{8,10},{2,4},{10,12},{4,6},{12,14},{6,22},{14,30},{22,20},{3... | collective-permute-start | bytes 393224 | tf_op jit(solution)/shard_map/ppermute | solution.py:308
  39.7 1.4 %collective-permute-start.18 = (bf16[64,1024]{1,0:T(8,128)(2,1)S(1)}, bf16[64,1024]{1,0:T(8,128)(2,1)S(1)}, u32[]{:S(2)}, u32[]{:S(2)}) collective-permute-start(bf16[64,1024]{1,0:T(8,128)(2,1)S(1)} %collective-permute-done.16.refs_0_), channel_id=1, source_target_pairs={{0,8},{8,0},{16,24},{24,16},{1,9},{9,1},{17,25},{25,17},{2,10},{10... | collective-permute-start | bytes 393224 | tf_op jit(solution)/shard_map/ppermute | solution.py:311
  39.7 1.5 %collective-permute-start.19 = (bf16[64,1024]{1,0:T(8,128)(2,1)S(1)}, bf16[64,1024]{1,0:T(8,128)(2,1)S(1)}, u32[]{:S(2)}, u32[]{:S(2)}) collective-permute-start(bf16[64,1024]{1,0:T(8,128)(2,1)S(1)} %collective-permute-done.17.refs_1_), channel_id=1, source_target_pairs={{0,8},{8,0},{16,24},{24,16},{1,9},{9,1},{17,25},{25,17},{2,10},{10... | collective-permute-start | bytes 393224 | tf_op jit(solution)/shard_map/ppermute | solution.py:311

commit v6 on v5

--- a/solution.py
+++ b/solution.py
@@ -146,8 +146,7 @@
     step = pl.program_id(0)
     inverse_root = 1.0 / math.sqrt(HEAD_WIDTH)
     for u in range(per_step):
-        g = step * per_step + u
-        cols = pl.ds(pl.multiple_of(g * HEAD_WIDTH, HEAD_WIDTH), HEAD_WIDTH)
+        cols = slice(u * HEAD_WIDTH, (u + 1) * HEAD_WIDTH)
         k = jnp.concatenate([key_ref[:, cols] for key_ref, _ in pieces], axis=0)
         k = jnp.concatenate([k, mask_ref[begin * tokens : (begin + count) * tokens, :]], axis=1)
         x_ref[u] = lax.dot_general(
@@ -155,7 +154,7 @@
         )
     for u in range(per_step):
         g = step * per_step + u
-        cols = pl.ds(pl.multiple_of(g * HEAD_WIDTH, HEAD_WIDTH), HEAD_WIDTH)
+        cols = slice(u * HEAD_WIDTH, (u + 1) * HEAD_WIDTH)
         factors = [key_scale_ref[u, begin + i : begin + i + 1, :] for i in range(count)]
         high, low = [], []
         for i, (_, value_ref) in enumerate(pieces):
@@ -206,7 +205,7 @@
                 continue
             mixed = mixed * (1.0 / totals[tile])
             check = jnp.sum(mixed, axis=0, keepdims=True) * inverse_root
-            mixed = jnp.transpose(mixed).astype(result_ref.dtype)
+            mixed = jnp.transpose(mixed.astype(result_ref.dtype))
             for j in range(SPAN // tokens):
                 h = tile * (SPAN // tokens) + j
                 at = (u * groups + h) * HEAD_WIDTH
@@ -233,9 +232,9 @@
     in_specs, operands = [], []
     for piece in pieces:
         joined = len(piece) == 1
-        half = (tokens, piece[0].shape[1])
-        in_specs.append(pl.BlockSpec(half, lambda s: (0, 0)))
-        in_specs.append(pl.BlockSpec(half, lambda s: (1, 0)) if joined else in_specs[-1])
+        half = (tokens, per_step * HEAD_WIDTH)
+        in_specs.append(pl.BlockSpec(half, lambda s: (0, s)))
+        in_specs.append(pl.BlockSpec(half, lambda s: (1, s)) if joined else in_specs[-1])
         operands += [piece[0], piece[-1]]
     in_specs += [
         pl.BlockSpec((per_step, rows, depth), lambda s: (s, 0, 0)),
@@ -342,7 +341,7 @@
         complete = len(scales) == head_size
         for shift in range(len(scales), min(head_size, len(scales) + 2)):
             scales = scales + [along_head(scale, shift)]
-        if step == 1:
+        if step == 2:
             prepared = prepare(queries, span_order, block_keep, sources, kv_heads, sizes)
         if complete:
             if rows is None:

time: 45.9 us -> 46.5 us (1.013)
  Pallas kernels: 15 us -> 16 us
  starting transfers between devices: 17.6 us -> 16.7 us
  waiting for transfers between devices: 7.97 us -> 8.54 us
    ppermute x3, starting transfers between devices: 6.65 us -> 5.44 us  [along_head(): lax.ppermute(block, 'head', [(i, (i + distance) % head_size) for i in ran...]
    pallas_call x3, Pallas kernels: 12.6 us -> 13.6 us  [absorb(): pl.pallas_call(functools.partial(absorb_kernel, groups=groups, tokens=tok...]
    ppermute x3, waiting for transfers between devices: 4.34 us -> 5.25 us  [along_head(): lax.ppermute(block, 'head', [(i, (i + distance) % head_size) for i in ran...]
  transfers between devices with their start and end apart: 20 -> 20, of which waited for: 6 -> 7; matrix products, arithmetic and copies ran while one was open for 2% -> 2% of each run, Pallas kernels for 23% -> 24%
where the time goes in v6:
time: 46.5 us; the launch traced here: 46.3 us
  starting transfers between devices  16.7 us (36%)
  Pallas kernels  16 us (34%)
  waiting for transfers between devices  8.54 us (18%)
  local copies, waits for them, and re-layouts  2.59 us (6%)
  other arithmetic  1.69 us (4%)
  between operations  0.76 us (2%)
    pallas_call x3, Pallas kernels, absorb(): pl.pallas_call(functools.partial(absorb_kernel, groups=groups, tokens=tok...  13.6 us
    ppermute x8, starting transfers between devices, around(): return lax.ppermute(block, ('ctx', 'head'), route)  9.86 us
    ppermute x3, starting transfers between devices, along_head(): lax.ppermute(block, 'head', [(i, (i + distance) % head_size) for i in ran...  5.44 us
    ppermute x3, waiting for transfers between devices, along_head(): lax.ppermute(block, 'head', [(i, (i + distance) % head_size) for i in ran...  5.25 us
    unnamed x6, local copies, waits for them, and re-layouts  2.57 us
    ppermute x8, waiting for transfers between devices, around(): return lax.ppermute(block, ('ctx', 'head'), route)  2.25 us
    ppermute x9, starting transfers between devices, to_other_core(): lax.ppermute(block, 'ctx', [(i, i ^ 1) for i in range(ctx_size)])  1.43 us
    pallas_call x1, Pallas kernels, prepare(): pl.pallas_call(functools.partial(prepare_kernel, groups=groups, per_step=...  1.36 us
  transfers between devices with their start and end apart: 20, of which 7 were waited for; matrix products, arithmetic and copies ran while one was open for 2% of the time, Pallas kernels for 24%

profile of v6, /device:TPU:0, one launch (start us, length us, event | category | flops | bytes accessed | tf_op | source)
XLA Modules:
  0.0 46.3 jit_solution(17115465273161588086)
XLA Ops:
  0.6 1.0 %pad_maximum_fusion.refs_0_.refs_1_ = bf16[128,1024]{1,0:T(8,128)(2,1)S(1)} fusion(bf16[64,1024]{1,0:T(8,128)(2,1)} %param.9, bf16[64,1024]{1,0:T(8,128)(2,1)} %param.8), kind=kLoop, calls=%fused_computation | loop fusion | flops 524288 | bytes 524288 | tf_op jit(solution)/shard_map/concatenate | solution.py:328
  1.6 3.0 %collective-permute-start.2 = (bf16[128,1024]{1,0:T(8,128)(2,1)S(1)}, bf16[128,1024]{1,0:T(8,128)(2,1)S(1)}, u32[]{:S(2)}, u32[]{:S(2)}) collective-permute-start(bf16[128,1024]{1,0:T(8,128)(2,1)S(1)} %pad_maximum_fusion.refs_0_.refs_1_), channel_id=1, source_target_pairs={{0,16},{8,24},{2,0},{10,8},{4,2},{12,10},{6,4},{14,12},{22,6},{30,... | collective-permute-start | bytes 786440 | tf_op jit(solution)/shard_map/ppermute | solution.py:307
  4.6 0.1 collective-permute-start.1
  4.8 0.0 collective-permute-start
  4.8 0.7 %pad_maximum_fusion.1.refs_0_ = f32[4,8]{1,0:T(4,128)S(1)} fusion(f32[2,8]{1,0:T(2,128)} %bitcast.2, f32[2,8]{1,0:T(2,128)} %bitcast.3), kind=kLoop, calls=%fused_computation.1 | loop fusion | flops 32 | bytes 256 | tf_op jit(solution)/shard_map/concatenate | solution.py:329
  5.5 3.0 %collective-permute-start.4 = (f32[4,8]{1,0:T(4,128)S(1)}, f32[4,8]{1,0:T(4,128)S(1)}, u32[]{:S(2)}, u32[]{:S(2)}) collective-permute-start(f32[4,8]{1,0:T(4,128)S(1)} %pad_maximum_fusion.1.refs_0_), channel_id=1, source_target_pairs={{0,4},{2,6},{4,0},{6,2},{1,5},{3,7},{5,1},{7,3},{8,12},{10,14},{12... | collective-permute-start | bytes 392 | tf_op jit(solution)/shard_map/ppermute | solution.py:313
  8.4 1.6 %collective-permute-start.3 = (f32[4,8]{1,0:T(4,128)S(1)}, f32[4,8]{1,0:T(4,128)S(1)}, u32[]{:S(2)}, u32[]{:S(2)}) collective-permute-start(f32[4,8]{1,0:T(4,128)S(1)} %pad_maximum_fusion.1.refs_0_), channel_id=1, source_target_pairs={{0,2},{2,4},{4,6},{6,0},{1,3},{3,5},{5,7},{7,1},{8,10},{10,12},{12... | collective-permute-start | bytes 392 | tf_op jit(solution)/shard_map/ppermute | solution.py:313
  10.0 2.2 %collective-permute-done.4.refs_2_ = f32[4,8]{1,0:T(4,128)S(1)} collective-permute-done((f32[4,8]{1,0:T(4,128)S(1)}, f32[4,8]{1,0:T(4,128)S(1)}, u32[]{:S(2)}, u32[]{:S(2)}) %collective-permute-start.4) | collective-permute-done | bytes 160 | tf_op jit(solution)/shard_map/ppermute | solution.py:313
  12.2 1.6 %collective-permute-done.3.refs_1_ = f32[4,8]{1,0:T(4,128)S(1)} collective-permute-done((f32[4,8]{1,0:T(4,128)S(1)}, f32[4,8]{1,0:T(4,128)S(1)}, u32[]{:S(2)}, u32[]{:S(2)}) %collective-permute-start.3) | collective-permute-done | bytes 160 | tf_op jit(solution)/shard_map/ppermute | solution.py:313
  13.8 0.0 collective-permute-done.2.refs_4_.refs_5_
  13.8 0.0 collective-permute-done.1.refs_2_.refs_3_
  13.8 0.0 collective-permute-done.refs_6_.refs_7_
  13.8 0.1 collective-permute-start.7
  13.9 0.1 collective-permute-start.5
  14.0 2.3 %collective-permute-start.8 = (bf16[128,1024]{1,0:T(8,128)(2,1)S(1)}, bf16[128,1024]{1,0:T(8,128)(2,1)S(1)}, u32[]{:S(2)}, u32[]{:S(2)}) collective-permute-start(bf16[128,1024]{1,0:T(8,128)(2,1)S(1)} %collective-permute-done.2.refs_4_.refs_5_), channel_id=1, source_target_pairs={{0,16},{8,24},{2,0},{10,8},{4,2},{12,10},{6,4},{14,12},{22,6},{30,... | collective-permute-start | bytes 786440 | tf_op jit(solution)/shard_map/ppermute | solution.py:307
  16.3 0.2 collective-permute-start.6
  16.5 0.9 %collective-permute-start.9 = (f32[4,8]{1,0:T(4,128)S(1)}, f32[4,8]{1,0:T(4,128)S(1)}, u32[]{:S(2)}, u32[]{:S(2)}) collective-permute-start(f32[4,8]{1,0:T(4,128)S(1)} %pad_maximum_fusion.1.refs_0_), channel_id=1, source_target_pairs={{0,6},{2,0},{4,2},{6,4},{1,7},{3,1},{5,3},{7,5},{8,14},{10,8},{12,... | collective-permute-start | bytes 392 | tf_op jit(solution)/shard_map/ppermute | solution.py:313
  17.4 1.2 %copy-done = bf16[64,8192]{1,0:T(8,128)(2,1)S(1)} copy-done((bf16[64,8192]{1,0:T(8,128)(2,1)S(1)}, bf16[64,8192]{1,0:T(8,128)(2,1)}, u32[]{:S(2)}) %copy-start) | copy-done | bytes 1048600
  18.6 0.7 %copy-done.1 = s32[8,8]{1,0:T(8,128)S(1)} copy-done((s32[8,8]{1,0:T(8,128)S(1)}, s32[8,8]{1,0:T(8,128)}, u32[]{:S(2)}) %copy-start.1) | copy-done | bytes 280
  19.3 0.7 %copy-done.2 = s32[8]{0:T(128)S(1)} copy-done((s32[8]{0:T(128)S(1)}, s32[8]{0:T(128)}, u32[]{:S(2)}) %copy-start.2) | copy-done | bytes 56
  19.9 1.4 %shard_map.86 = (bf16[8,512,256]{2,1,0:T(8,128)(2,1)S(1)}, bf16[1024,128]{1,0:T(8,128)(2,1)S(1)}) custom-call(s32[8]{0:T(128)S(1)} %copy-done.2, s32[8,8]{1,0:T(8,128)S(1)} %copy-done.1, bf16[64,8192]{1,0:T(8,128)(2,1)S(1)} %copy-done), custom_call_target="tpu_custom_call" | custom-call | flops 4194304 | bytes 8388608 | tf_op jit(solution)/shard_map/pallas_call | solution.py:61
  21.3 1.4 %collective-permute-done.9.refs_3_ = f32[4,8]{1,0:T(4,128)S(1)} collective-permute-done((f32[4,8]{1,0:T(4,128)S(1)}, f32[4,8]{1,0:T(4,128)S(1)}, u32[]{:S(2)}, u32[]{:S(2)}) %collective-permute-start.9) | collective-permute-done | bytes 160 | tf_op jit(solution)/shard_map/ppermute | solution.py:313
  22.7 0.0 collective-permute-done.7.refs_8_.refs_9_
  22.7 0.0 collective-permute-done.5.refs_12_.refs_13_
  22.7 0.0 collective-permute-done.8.refs_10_.refs_11_
  22.7 0.0 collective-permute-done.6.refs_14_.refs_15_
  22.8 0.8 %collective-permute-start.12 = (bf16[128,1024]{1,0:T(8,128)(2,1)S(1)}, bf16[128,1024]{1,0:T(8,128)(2,1)S(1)}, u32[]{:S(2)}, u32[]{:S(2)}) collective-permute-start(bf16[128,1024]{1,0:T(8,128)(2,1)S(1)} %collective-permute-done.7.refs_8_.refs_9_), channel_id=1, source_target_pairs={{0,2},{8,10},{2,4},{10,12},{4,6},{12,14},{6,22},{14,30},{22,20},{3... | collective-permute-start | bytes 786440 | tf_op jit(solution)/shard_map/ppermute | solution.py:307
  23.5 0.0 collective-permute-start.10
  23.5 1.5 %collective-permute-start.13 = (bf16[128,1024]{1,0:T(8,128)(2,1)S(1)}, bf16[128,1024]{1,0:T(8,128)(2,1)S(1)}, u32[]{:S(2)}, u32[]{:S(2)}) collective-permute-start(bf16[128,1024]{1,0:T(8,128)(2,1)S(1)} %collective-permute-done.8.refs_10_.refs_11_), channel_id=1, source_target_pairs={{0,16},{8,24},{2,0},{10,8},{4,2},{12,10},{6,4},{14,12},{22,6},{30,... | collective-permute-start | bytes 786440 | tf_op jit(solution)/shard_map/ppermute | solution.py:307
  25.0 0.2 collective-permute-start.11
  25.2 1.0 %shard_map.87 = (f32[8,16,128]{2,1,0:T(8,128)S(1)}, f32[8,16,128]{2,1,0:T(8,128)S(1)}) custom-call(f32[4,8]{1,0:T(4,128)S(1)} %pad_maximum_fusion.1.refs_0_, f32[4,8]{1,0:T(4,128)S(1)} %collective-permute-done.3.refs_1_, f32[4,8]{1,0:T(4,128)S(1)} %collective-permute-done.4.refs_2_, f32[4,8]{1,0:T(4,128)S(1)} %collective-permute-done.9.refs_3_), custom_call_target="tpu_custom_call" | custom-call | flops 100000000 | bytes 1000000 | tf_op jit(solution)/shard_map/pallas_call | solution.py:117
  26.2 5.4 %shard_map.88 = (f32[8,128,512]{2,1,0:T(8,128)S(1)}, f32[8,2,512]{2,1,0:T(2,128)S(1)}) custom-call(bf16[128,1024]{1,0:T(8,128)(2,1)S(1)} %pad_maximum_fusion.refs_0_.refs_1_, bf16[128,1024]{1,0:T(8,128)(2,1)S(1)} %pad_maximum_fusion.refs_0_.refs_1_, bf16[128,1024]{1,0:T(8,128)(2,1)S(1)} %collective-permute-done.1.refs_2_.refs_3_, ...), custom_call_target="tpu_custom_call" | custom-call | flops 4294967296 | bytes 8388608 | tf_op jit(solution)/shard_map/pallas_call | solution.py:261
  31.7 0.0 collective-permute-done.12.refs_0_.refs_1_
  31.7 0.0 collective-permute-done.10.refs_4_.refs_5_
  31.7 0.6 %collective-permute-done.13.refs_2_.refs_3_ = bf16[128,1024]{1,0:T(8,128)(2,1)S(1)} collective-permute-done((bf16[128,1024]{1,0:T(8,128)(2,1)S(1)}, bf16[128,1024]{1,0:T(8,128)(2,1)S(1)}, u32[]{:S(2)}, u32[]{:S(2)}) %collective-permute-start.13) | collective-permute-done | bytes 262176 | tf_op jit(solution)/shard_map/ppermute | solution.py:307
  32.2 0.0 collective-permute-done.11.refs_6_.refs_7_
  32.3 0.0 collective-permute-start.14
  32.3 0.5 %collective-permute-start.15 = (bf16[128,1024]{1,0:T(8,128)(2,1)S(1)}, bf16[128,1024]{1,0:T(8,128)(2,1)S(1)}, u32[]{:S(2)}, u32[]{:S(2)}) collective-permute-start(bf16[128,1024]{1,0:T(8,128)(2,1)S(1)} %collective-permute-done.13.refs_2_.refs_3_), channel_id=1, source_target_pairs={{0,8},{8,0},{16,24},{24,16},{1,9},{9,1},{17,25},{25,17},{2,10},{10... | collective-permute-start | bytes 786440 | tf_op jit(solution)/shard_map/ppermute | solution.py:310
  32.8 1.6 %collective-permute-start.17 = (bf16[64,1024]{1,0:T(8,128)(2,1)S(1)}, bf16[64,1024]{1,0:T(8,128)(2,1)S(1)}, u32[]{:S(2)}, u32[]{:S(2)}) collective-permute-start(bf16[64,1024]{1,0:T(8,128)(2,1)S(1)} %slice.7), channel_id=1, source_target_pairs={{0,16},{8,24},{2,0},{10,8},{4,2},{12,10},{6,4},{14,12},{22,6},{30,... | collective-permute-start | bytes 393224 | tf_op jit(solution)/shard_map/ppermute | solution.py:307
  34.4 0.5 %collective-permute-start.16 = (bf16[64,1024]{1,0:T(8,128)(2,1)S(1)}, bf16[64,1024]{1,0:T(8,128)(2,1)S(1)}, u32[]{:S(2)}, u32[]{:S(2)}) collective-permute-start(bf16[64,1024]{1,0:T(8,128)(2,1)S(1)} %slice.6), channel_id=1, source_target_pairs={{0,2},{8,10},{2,4},{10,12},{4,6},{12,14},{6,22},{14,30},{22,20},{3... | collective-permute-start | bytes 393224 | tf_op jit(solution)/shard_map/ppermute | solution.py:307
  34.9 3.4 %shard_map.89 = (f32[8,128,512]{2,1,0:T(8,128)S(1)}, f32[8,2,512]{2,1,0:T(2,128)S(1)}) custom-call(bf16[128,1024]{1,0:T(8,128)(2,1)S(1)} %collective-permute-done.12.refs_0_.refs_1_, bf16[128,1024]{1,0:T(8,128)(2,1)S(1)} %collective-permute-done.12.refs_0_.refs_1_, bf16[128,1024]{1,0:T(8,128)(2,1)S(1)} %collective-permute-done.13.refs_2_.refs_3_, ...), custom_call_target="tpu_custom_call" | custom-call | flops 2147483648 | bytes 8388608 | tf_op jit(solution)/shard_map/pallas_call | solution.py:261
  38.3 0.0 collective-permute-done.17.refs_1_
  38.3 1.7 %collective-permute-done.16.refs_0_ = bf16[64,1024]{1,0:T(8,128)(2,1)S(1)} collective-permute-done((bf16[64,1024]{1,0:T(8,128)(2,1)S(1)}, bf16[64,1024]{1,0:T(8,128)(2,1)S(1)}, u32[]{:S(2)}, u32[]{:S(2)}) %collective-permute-start.16) | collective-permute-done | bytes 131104 | tf_op jit(solution)/shard_map/ppermute | solution.py:307
  40.0 0.0 collective-permute-done.14.refs_2_.refs_3_
  40.0 0.5 %collective-permute-start.19 = (bf16[64,1024]{1,0:T(8,128)(2,1)S(1)}, bf16[64,1024]{1,0:T(8,128)(2,1)S(1)}, u32[]{:S(2)}, u32[]{:S(2)}) collective-permute-start(bf16[64,1024]{1,0:T(8,128)(2,1)S(1)} %collective-permute-done.17.refs_1_), channel_id=1, source_target_pairs={{0,8},{8,0},{16,24},{24,16},{1,9},{9,1},{17,25},{25,17},{2,10},{10... | collective-permute-start | bytes 393224 | tf_op jit(solution)/shard_map/ppermute | solution.py:310
  40.5 0.8 %collective-permute-done.18.refs_6_ = bf16[64,1024]{1,0:T(8,128)(2,1)S(1)} collective-permute-done((bf16[64,1024]{1,0:T(8,128)(2,1)S(1)}, bf16[64,1024]{1,0:T(8,128)(2,1)S(1)}, u32[]{:S(2)}, u32[]{:S(2)}) %collective-permute-start.18) | collective-permute-done | bytes 131104 | tf_op jit(solution)/shard_map/ppermute | solution.py:310
  41.4 0.2 collective-permute-done.19.refs_7_
  41.6 4.7 %shard_map.90 = (bf16[64,8192]{1,0:T(8,128)(2,1)}, f32[64,64]{1,0:T(8,128)}) custom-call(bf16[64,1024]{1,0:T(8,128)(2,1)S(1)} %collective-permute-done.16.refs_0_, bf16[64,1024]{1,0:T(8,128)(2,1)S(1)} %collective-permute-done.17.refs_1_, bf16[128,1024]{1,0:T(8,128)(2,1)S(1)} %collective-permute-done.14.refs_2_.refs_3_, ...), custom_call_target="tpu_custom_call" | custom-call | flops 2147483648 | bytes 8388608 | tf_op jit(solution)/shard_map/pallas_call | solution.py:261
  (7 shorter events, 0.0 us)
Async XLA Ops:
  1.6 12.2 %collective-permute-start.2 = (bf16[128,1024]{1,0:T(8,128)(2,1)S(1)}, bf16[128,1024]{1,0:T(8,128)(2,1)S(1)}, u32[]{:S(2)}, u32[]{:S(2)}) collective-permute-start(bf16[128,1024]{1,0:T(8,128)(2,1)S(1)} %pad_maximum_fusion.refs_0_.refs_1_), channel_id=1, source_target_pairs={{0,16},{8,24},{2,0},{10,8},{4,2},{12,10},{6,4},{14,12},{22,6},{30,... | collective-permute-start | bytes 786440 | tf_op jit(solution)/shard_map/ppermute | solution.py:307
  4.6 9.2 %collective-permute-start.1 = (bf16[128,1024]{1,0:T(8,128)(2,1)S(1)}, bf16[128,1024]{1,0:T(8,128)(2,1)S(1)}, u32[]{:S(2)}, u32[]{:S(2)}) collective-permute-start(bf16[128,1024]{1,0:T(8,128)(2,1)S(1)} %pad_maximum_fusion.refs_0_.refs_1_), channel_id=1, source_target_pairs={{0,2},{8,10},{2,4},{10,12},{4,6},{12,14},{6,22},{14,30},{22,20},{3... | collective-permute-start | bytes 786440 | tf_op jit(solution)/shard_map/ppermute | solution.py:307
  4.8 9.1 %collective-permute-start = (bf16[128,1024]{1,0:T(8,128)(2,1)S(1)}, bf16[128,1024]{1,0:T(8,128)(2,1)S(1)}, u32[]{:S(2)}, u32[]{:S(2)}) collective-permute-start(bf16[128,1024]{1,0:T(8,128)(2,1)S(1)} %pad_maximum_fusion.refs_0_.refs_1_), channel_id=1, source_target_pairs={{0,8},{8,0},{16,24},{24,16},{1,9},{9,1},{17,25},{25,17},{2,10},{10... | collective-permute-start | bytes 786440 | tf_op jit(solution)/shard_map/ppermute | solution.py:310
  5.5 6.8 %collective-permute-start.4 = (f32[4,8]{1,0:T(4,128)S(1)}, f32[4,8]{1,0:T(4,128)S(1)}, u32[]{:S(2)}, u32[]{:S(2)}) collective-permute-start(f32[4,8]{1,0:T(4,128)S(1)} %pad_maximum_fusion.1.refs_0_), channel_id=1, source_target_pairs={{0,4},{2,6},{4,0},{6,2},{1,5},{3,7},{5,1},{7,3},{8,12},{10,14},{12... | collective-permute-start | bytes 392 | tf_op jit(solution)/shard_map/ppermute | solution.py:313
  8.4 5.4 %collective-permute-start.3 = (f32[4,8]{1,0:T(4,128)S(1)}, f32[4,8]{1,0:T(4,128)S(1)}, u32[]{:S(2)}, u32[]{:S(2)}) collective-permute-start(f32[4,8]{1,0:T(4,128)S(1)} %pad_maximum_fusion.1.refs_0_), channel_id=1, source_target_pairs={{0,2},{2,4},{4,6},{6,0},{1,3},{3,5},{5,7},{7,1},{8,10},{10,12},{12... | collective-permute-start | bytes 392 | tf_op jit(solution)/shard_map/ppermute | solution.py:313
  13.8 8.9 %collective-permute-start.7 = (bf16[128,1024]{1,0:T(8,128)(2,1)S(1)}, bf16[128,1024]{1,0:T(8,128)(2,1)S(1)}, u32[]{:S(2)}, u32[]{:S(2)}) collective-permute-start(bf16[128,1024]{1,0:T(8,128)(2,1)S(1)} %collective-permute-done.1.refs_2_.refs_3_), channel_id=1, source_target_pairs={{0,2},{8,10},{2,4},{10,12},{4,6},{12,14},{6,22},{14,30},{22,20},{3... | collective-permute-start | bytes 786440 | tf_op jit(solution)/shard_map/ppermute | solution.py:307
  13.9 8.8 %collective-permute-start.5 = (bf16[128,1024]{1,0:T(8,128)(2,1)S(1)}, bf16[128,1024]{1,0:T(8,128)(2,1)S(1)}, u32[]{:S(2)}, u32[]{:S(2)}) collective-permute-start(bf16[128,1024]{1,0:T(8,128)(2,1)S(1)} %collective-permute-done.1.refs_2_.refs_3_), channel_id=1, source_target_pairs={{0,8},{8,0},{16,24},{24,16},{1,9},{9,1},{17,25},{25,17},{2,10},{10... | collective-permute-start | bytes 786440 | tf_op jit(solution)/shard_map/ppermute | solution.py:310
  14.0 8.8 %collective-permute-start.8 = (bf16[128,1024]{1,0:T(8,128)(2,1)S(1)}, bf16[128,1024]{1,0:T(8,128)(2,1)S(1)}, u32[]{:S(2)}, u32[]{:S(2)}) collective-permute-start(bf16[128,1024]{1,0:T(8,128)(2,1)S(1)} %collective-permute-done.2.refs_4_.refs_5_), channel_id=1, source_target_pairs={{0,16},{8,24},{2,0},{10,8},{4,2},{12,10},{6,4},{14,12},{22,6},{30,... | collective-permute-start | bytes 786440 | tf_op jit(solution)/shard_map/ppermute | solution.py:307
  16.3 6.4 %collective-permute-start.6 = (bf16[128,1024]{1,0:T(8,128)(2,1)S(1)}, bf16[128,1024]{1,0:T(8,128)(2,1)S(1)}, u32[]{:S(2)}, u32[]{:S(2)}) collective-permute-start(bf16[128,1024]{1,0:T(8,128)(2,1)S(1)} %collective-permute-done.2.refs_4_.refs_5_), channel_id=1, source_target_pairs={{0,8},{8,0},{16,24},{24,16},{1,9},{9,1},{17,25},{25,17},{2,10},{10... | collective-permute-start | bytes 786440 | tf_op jit(solution)/shard_map/ppermute | solution.py:310
  16.5 6.3 %collective-permute-start.9 = (f32[4,8]{1,0:T(4,128)S(1)}, f32[4,8]{1,0:T(4,128)S(1)}, u32[]{:S(2)}, u32[]{:S(2)}) collective-permute-start(f32[4,8]{1,0:T(4,128)S(1)} %pad_maximum_fusion.1.refs_0_), channel_id=1, source_target_pairs={{0,6},{2,0},{4,2},{6,4},{1,7},{3,1},{5,3},{7,5},{8,14},{10,8},{12,... | collective-permute-start | bytes 392 | tf_op jit(solution)/shard_map/ppermute | solution.py:313
  17.4 1.2 %copy-start = (bf16[64,8192]{1,0:T(8,128)(2,1)S(1)}, bf16[64,8192]{1,0:T(8,128)(2,1)}, u32[]{:S(2)}) copy-start(bf16[64,8192]{1,0:T(8,128)(2,1)} %q_ref.1) | copy-start | bytes 3145732
  18.6 0.7 %copy-start.1 = (s32[8,8]{1,0:T(8,128)S(1)}, s32[8,8]{1,0:T(8,128)}, u32[]{:S(2)}) copy-start(s32[8,8]{1,0:T(8,128)} %keep_ref.1) | copy-start | bytes 772
  19.3 0.7 %copy-start.2 = (s32[8]{0:T(128)S(1)}, s32[8]{0:T(128)}, u32[]{:S(2)}) copy-start(s32[8]{0:T(128)} %order_ref.1) | copy-start | bytes 100
  22.8 8.9 %collective-permute-start.12 = (bf16[128,1024]{1,0:T(8,128)(2,1)S(1)}, bf16[128,1024]{1,0:T(8,128)(2,1)S(1)}, u32[]{:S(2)}, u32[]{:S(2)}) collective-permute-start(bf16[128,1024]{1,0:T(8,128)(2,1)S(1)} %collective-permute-done.7.refs_8_.refs_9_), channel_id=1, source_target_pairs={{0,2},{8,10},{2,4},{10,12},{4,6},{12,14},{6,22},{14,30},{22,20},{3... | collective-permute-start | bytes 786440 | tf_op jit(solution)/shard_map/ppermute | solution.py:307
  23.5 8.1 %collective-permute-start.10 = (bf16[128,1024]{1,0:T(8,128)(2,1)S(1)}, bf16[128,1024]{1,0:T(8,128)(2,1)S(1)}, u32[]{:S(2)}, u32[]{:S(2)}) collective-permute-start(bf16[128,1024]{1,0:T(8,128)(2,1)S(1)} %collective-permute-done.7.refs_8_.refs_9_), channel_id=1, source_target_pairs={{0,8},{8,0},{16,24},{24,16},{1,9},{9,1},{17,25},{25,17},{2,10},{10... | collective-permute-start | bytes 786440 | tf_op jit(solution)/shard_map/ppermute | solution.py:310
  23.5 8.7 %collective-permute-start.13 = (bf16[128,1024]{1,0:T(8,128)(2,1)S(1)}, bf16[128,1024]{1,0:T(8,128)(2,1)S(1)}, u32[]{:S(2)}, u32[]{:S(2)}) collective-permute-start(bf16[128,1024]{1,0:T(8,128)(2,1)S(1)} %collective-permute-done.8.refs_10_.refs_11_), channel_id=1, source_target_pairs={{0,16},{8,24},{2,0},{10,8},{4,2},{12,10},{6,4},{14,12},{22,6},{30,... | collective-permute-start | bytes 786440 | tf_op jit(solution)/shard_map/ppermute | solution.py:307
  25.0 7.2 %collective-permute-start.11 = (bf16[128,1024]{1,0:T(8,128)(2,1)S(1)}, bf16[128,1024]{1,0:T(8,128)(2,1)S(1)}, u32[]{:S(2)}, u32[]{:S(2)}) collective-permute-start(bf16[128,1024]{1,0:T(8,128)(2,1)S(1)} %collective-permute-done.8.refs_10_.refs_11_), channel_id=1, source_target_pairs={{0,8},{8,0},{16,24},{24,16},{1,9},{9,1},{17,25},{25,17},{2,10},{10... | collective-permute-start | bytes 786440 | tf_op jit(solution)/shard_map/ppermute | solution.py:310
  32.3 7.8 %collective-permute-start.14 = (bf16[128,1024]{1,0:T(8,128)(2,1)S(1)}, bf16[128,1024]{1,0:T(8,128)(2,1)S(1)}, u32[]{:S(2)}, u32[]{:S(2)}) collective-permute-start(bf16[128,1024]{1,0:T(8,128)(2,1)S(1)} %collective-permute-done.12.refs_0_.refs_1_), channel_id=1, source_target_pairs={{0,8},{8,0},{16,24},{24,16},{1,9},{9,1},{17,25},{25,17},{2,10},{10... | collective-permute-start | bytes 786440 | tf_op jit(solution)/shard_map/ppermute | solution.py:310
  32.3 7.8 %collective-permute-start.15 = (bf16[128,1024]{1,0:T(8,128)(2,1)S(1)}, bf16[128,1024]{1,0:T(8,128)(2,1)S(1)}, u32[]{:S(2)}, u32[]{:S(2)}) collective-permute-start(bf16[128,1024]{1,0:T(8,128)(2,1)S(1)} %collective-permute-done.13.refs_2_.refs_3_), channel_id=1, source_target_pairs={{0,8},{8,0},{16,24},{24,16},{1,9},{9,1},{17,25},{25,17},{2,10},{10... | collective-permute-start | bytes 786440 | tf_op jit(solution)/shard_map/ppermute | solution.py:310
  32.8 5.5 %collective-permute-start.17 = (bf16[64,1024]{1,0:T(8,128)(2,1)S(1)}, bf16[64,1024]{1,0:T(8,128)(2,1)S(1)}, u32[]{:S(2)}, u32[]{:S(2)}) collective-permute-start(bf16[64,1024]{1,0:T(8,128)(2,1)S(1)} %slice.7), channel_id=1, source_target_pairs={{0,16},{8,24},{2,0},{10,8},{4,2},{12,10},{6,4},{14,12},{22,6},{30,... | collective-permute-start | bytes 393224 | tf_op jit(solution)/shard_map/ppermute | solution.py:307
  34.4 5.6 %collective-permute-start.16 = (bf16[64,1024]{1,0:T(8,128)(2,1)S(1)}, bf16[64,1024]{1,0:T(8,128)(2,1)S(1)}, u32[]{:S(2)}, u32[]{:S(2)}) collective-permute-start(bf16[64,1024]{1,0:T(8,128)(2,1)S(1)} %slice.6), channel_id=1, source_target_pairs={{0,2},{8,10},{2,4},{10,12},{4,6},{12,14},{6,22},{14,30},{22,20},{3... | collective-permute-start | bytes 393224 | tf_op jit(solution)/shard_map/ppermute | solution.py:307
  40.0 1.4 %collective-permute-start.18 = (bf16[64,1024]{1,0:T(8,128)(2,1)S(1)}, bf16[64,1024]{1,0:T(8,128)(2,1)S(1)}, u32[]{:S(2)}, u32[]{:S(2)}) collective-permute-start(bf16[64,1024]{1,0:T(8,128)(2,1)S(1)} %collective-permute-done.16.refs_0_), channel_id=1, source_target_pairs={{0,8},{8,0},{16,24},{24,16},{1,9},{9,1},{17,25},{25,17},{2,10},{10... | collective-permute-start | bytes 393224 | tf_op jit(solution)/shard_map/ppermute | solution.py:310
  40.0 1.5 %collective-permute-start.19 = (bf16[64,1024]{1,0:T(8,128)(2,1)S(1)}, bf16[64,1024]{1,0:T(8,128)(2,1)S(1)}, u32[]{:S(2)}, u32[]{:S(2)}) collective-permute-start(bf16[64,1024]{1,0:T(8,128)(2,1)S(1)} %collective-permute-done.17.refs_1_), channel_id=1, source_target_pairs={{0,8},{8,0},{16,24},{24,16},{1,9},{9,1},{17,25},{25,17},{2,10},{10... | collective-permute-start | bytes 393224 | tf_op jit(solution)/shard_map/ppermute | solution.py:310

commit v7 on v5

--- a/solution.py
+++ b/solution.py
@@ -44,12 +44,10 @@
             mask = jnp.where(own == span, causal, whole)
             mask_ref[i * tokens : (i + 1) * tokens, :] = mask.astype(jnp.bfloat16)
 
-    one_hot = jnp.where(row == lane, 1.0, 0.0).astype(jnp.bfloat16)
     for u in range(per_step):
         for h in range(groups):
             at = (u * groups + h) * HEAD_WIDTH
-            qa_ref[u, h * tokens : (h + 1) * tokens, :HEAD_WIDTH] = q_ref[:, at : at + HEAD_WIDTH]
-            qa_ref[u, h * tokens : (h + 1) * tokens, HEAD_WIDTH:] = one_hot
+            qa_ref[u, h * tokens : (h + 1) * tokens, :] = q_ref[:, at : at + HEAD_WIDTH]
 
 
 def prepare(queries, span_order, block_keep, sources, kv_heads, sizes):
@@ -70,11 +68,11 @@
         grid=(kv_heads // per_step,),
         in_specs=[smem, smem, pl.BlockSpec((tokens, per_step * groups * HEAD_WIDTH), lambda s: (0, s))],
         out_specs=[
-            pl.BlockSpec((per_step, rows, HEAD_WIDTH + SPAN), lambda s: (s, 0, 0)),
+            pl.BlockSpec((per_step, rows, HEAD_WIDTH), lambda s: (s, 0, 0)),
             pl.BlockSpec((tokens * len(sources), SPAN), lambda s: (0, 0)),
         ],
         out_shape=[
-            jax.ShapeDtypeStruct((kv_heads, rows, HEAD_WIDTH + SPAN), jnp.bfloat16),
+            jax.ShapeDtypeStruct((kv_heads, rows, HEAD_WIDTH), jnp.bfloat16),
             jax.ShapeDtypeStruct((tokens * len(sources), SPAN), jnp.bfloat16),
         ],
         compiler_params=pltpu.CompilerParams(vmem_limit_bytes=32 * 1024 * 1024),
@@ -84,17 +82,18 @@
     )(span_order, block_keep, queries)
 
 
-def scale_rows_kernel(*refs, tokens, kv_local, sources, ctx_size, head_size):
-    scale_in = refs[:head_size]
-    key_scale_ref, value_scale_ref, scale_ref, scale_sem = refs[head_size:]
+def scale_rows_kernel(*refs, owners, tokens, kv_local, sources, ctx_size, head_size):
+    scale_in = refs[: len(owners)]
+    key_scale_ref, value_scale_ref, scale_ref, scale_sem = refs[len(owners) :]
     inverse_root = 1.0 / math.sqrt(HEAD_WIDTH)
     head = lax.axis_index("head")
-    copies = []
-    for shift in range(head_size):
-        owner = lax.rem(head - shift + head_size, head_size)
-        copies.append(
-            pltpu.make_async_copy(scale_in[shift], scale_ref.at[owner], scale_sem.at[shift])
-        )
+    copies, flip = [], 0
+    for ref, count in zip(scale_in, owners):
+        for i in range(count):
+            copies.append(
+                pltpu.make_async_copy(ref.at[i], scale_ref.at[head ^ flip], scale_sem.at[flip])
+            )
+            flip += 1
     for copy in copies:
         copy.start()
     spans = [
@@ -112,11 +111,12 @@
 
 
 def scale_rows(scales, sources, tokens, sizes):
-    kv_local = scales[0].shape[0] // 2
+    kv_local = scales[0].shape[1] // 2
     shape = (sizes[1] * kv_local, len(sources), SPAN)
     return pl.pallas_call(
         functools.partial(
             scale_rows_kernel,
+            owners=[scale.shape[0] for scale in scales],
             tokens=tokens,
             kv_local=kv_local,
             sources=sources,
@@ -127,8 +127,8 @@
         out_specs=[pl.BlockSpec(memory_space=pltpu.VMEM)] * 2,
         out_shape=[jax.ShapeDtypeStruct(shape, jnp.float32)] * 2,
         scratch_shapes=[
-            pltpu.SMEM((len(scales),) + scales[0].shape, jnp.float32),
-            pltpu.SemaphoreType.DMA((len(scales),)),
+            pltpu.SMEM((sizes[1],) + scales[0].shape[1:], jnp.float32),
+            pltpu.SemaphoreType.DMA((sizes[1],)),
         ],
         compiler_params=pltpu.CompilerParams(vmem_limit_bytes=32 * 1024 * 1024),
         cost_estimate=pl.CostEstimate(
@@ -145,13 +145,20 @@
     result_ref, stats_ref, x_ref, p_ref, check_ref = refs
     step = pl.program_id(0)
     inverse_root = 1.0 / math.sqrt(HEAD_WIDTH)
+    row = lax.broadcasted_iota(jnp.int32, (tokens, SPAN), 0)
+    lane = lax.broadcasted_iota(jnp.int32, (tokens, SPAN), 1)
+    one_hot = jnp.where(row == lane, 1.0, 0.0).astype(jnp.bfloat16)
+    one_hot = jnp.concatenate([one_hot] * groups, axis=0)
     for u in range(per_step):
         g = step * per_step + u
         cols = pl.ds(pl.multiple_of(g * HEAD_WIDTH, HEAD_WIDTH), HEAD_WIDTH)
         k = jnp.concatenate([key_ref[:, cols] for key_ref, _ in pieces], axis=0)
         k = jnp.concatenate([k, mask_ref[begin * tokens : (begin + count) * tokens, :]], axis=1)
         x_ref[u] = lax.dot_general(
-            k, qa_ref[u], (((1,), (1,)), ((), ())), preferred_element_type=jnp.float32
+            k,
+            jnp.concatenate([qa_ref[u], one_hot], axis=1),
+            (((1,), (1,)), ((), ())),
+            preferred_element_type=jnp.float32,
         )
     for u in range(per_step):
         g = step * per_step + u
@@ -310,25 +317,25 @@
     def to_other_core(piece):
         return [lax.ppermute(block, "ctx", [(i, i ^ 1) for i in range(ctx_size)]) for block in piece]
 
-    def along_head(block, distance):
-        return lax.ppermute(block, "head", [(i, (i + distance) % head_size) for i in range(head_size)])
+    def swap_heads(block, flip):
+        return lax.ppermute(block, "head", [(i, i ^ flip) for i in range(head_size)])
 
     sources = [(0, 0)]
     for step in range(1, size // 2 + 2):
         if step < size // 2:
             sources += [(step, 0), (-step, 0)]
         elif step == size // 2:
-            sources += [(step, 0)]
+            sources += [(step - 1, 1), (1 - step, 1), (step, 0)]
         if step == 1:
             sources += [(0, 1)]
-        elif step <= size // 2:
+        elif step < size // 2:
             sources += [(step - 1, 1), (1 - step, 1)]
-        else:
+        elif step > size // 2:
             sources += [(step - 1, 1)]
 
     block = lax.optimization_barrier(jnp.concatenate([keys, values], axis=0))
     scale = jnp.concatenate([jnp.transpose(key_scale), jnp.transpose(value_scale)], axis=0)
-    scales, pieces, done = [scale], [[block]], 0
+    scales, pieces, done = [scale[None]], [[block]], 0
     fresh, forward, backward = [[block]], block, block
     prepared, rows, state = None, None, None
     for step in range(1, size // 2 + 2):
@@ -339,26 +346,30 @@
             sent = [[forward], [backward]]
         elif step == size // 2:
             sent = [[around(forward[:tokens], 1), around(backward[tokens:], -1)]]
-        complete = len(scales) == head_size
-        for shift in range(len(scales), min(head_size, len(scales) + 2)):
-            scales = scales + [along_head(scale, shift)]
-        if step == 1:
+        held = sum(scale.shape[0] for scale in scales)
+        complete = held == head_size
+        if not complete:
+            scales = scales + [swap_heads(jnp.concatenate(scales, axis=0), held)]
+        if step == 2:
             prepared = prepare(queries, span_order, block_keep, sources, kv_heads, sizes)
         if complete:
             if rows is None:
                 rows = scale_rows(scales, sources, tokens, sizes)
-            ready = (len(pieces) - done) // batch * batch
-            if ready and step <= size // 2:
-                now = pieces[done : done + ready]
+            ready = (len(pieces) - done) // batch * batch if step < size // 2 else 0
+            now = pieces[done : done + ready]
+            if step == size // 2:
+                now = pieces[done:] + crossed
+                ready = len(now)
+            if ready:
                 state = absorb((*prepared, *rows), now, done, state, False, tokens)
                 done += ready
-        crossed, sent, scales, prepared, rows, state = lax.optimization_barrier(
-            (crossed, sent, scales, prepared, rows, state)
+        sent, crossed, scales, prepared, rows, state = lax.optimization_barrier(
+            (sent, crossed, scales, prepared, rows, state)
         )
         fresh = sent
         if step < size // 2:
             forward, backward = fresh[0][0], fresh[1][0]
-        pieces = pieces + sent + crossed
+        pieces = pieces + (sent + crossed if step < size // 2 else crossed + sent)
     return tuple(absorb((*prepared, *rows), pieces[done:], done, state, True, tokens))
 
 

time: 45.9 us -> 43.8 us (0.954)
  starting transfers between devices: 17.6 us -> 16 us
  waiting for transfers between devices: 7.97 us -> 7.38 us
    ppermute x3 -> x2, starting transfers between devices: 6.65 us -> 4.61 us  [swap_heads(): lax.ppermute(block, 'head', [(i, i ^ flip) for i in range(head_size)])]
    ppermute x8, waiting for transfers between devices: 2.58 us -> 0.93 us  [around(): return lax.ppermute(block, ('ctx', 'head'), route)]
    ppermute x3 -> x2, waiting for transfers between devices: 4.34 us -> 5.41 us  [swap_heads(): lax.ppermute(block, 'head', [(i, i ^ flip) for i in range(head_size)])]
    broadcast_in_dim x0 -> x1, other arithmetic: none -> 0.7 us  [local(): scales, pieces, done = ([scale[None]], [[block]], 0)]
    concatenate x1, other arithmetic: 0.7 us -> 0.01 us  [local(): scales = scales + [swap_heads(jnp.concatenate(scales, axis=0), held)]]
    ppermute x9, starting transfers between devices: 1.47 us -> 2.1 us  [to_other_core(): lax.ppermute(block, 'ctx', [(i, i ^ 1) for i in range(ctx_size)])]
  transfers between devices with their start and end apart: 20 -> 19, of which waited for: 6 -> 6; matrix products, arithmetic and copies ran while one was open for 2% -> 2% of each run, Pallas kernels for 23% -> 27%
where the time goes in v7:
time: 43.8 us; the launch traced here: 43.5 us
  starting transfers between devices  16 us (37%)
  Pallas kernels  15.2 us (35%)
  waiting for transfers between devices  7.38 us (17%)
  local copies, waits for them, and re-layouts  2.59 us (6%)
  other arithmetic  1.7 us (4%)
  between operations  0.76 us (2%)
    pallas_call x3, Pallas kernels, absorb(): pl.pallas_call(functools.partial(absorb_kernel, groups=groups, tokens=tok...  12.9 us
    ppermute x8, starting transfers between devices, around(): return lax.ppermute(block, ('ctx', 'head'), route)  9.25 us
    ppermute x2, waiting for transfers between devices, swap_heads(): lax.ppermute(block, 'head', [(i, i ^ flip) for i in range(head_size)])  5.41 us
    ppermute x2, starting transfers between devices, swap_heads(): lax.ppermute(block, 'head', [(i, i ^ flip) for i in range(head_size)])  4.61 us
    unnamed x6, local copies, waits for them, and re-layouts  2.57 us
    ppermute x9, starting transfers between devices, to_other_core(): lax.ppermute(block, 'ctx', [(i, i ^ 1) for i in range(ctx_size)])  2.1 us
    pallas_call x1, Pallas kernels, prepare(): pl.pallas_call(functools.partial(prepare_kernel, groups=groups, per_step=...  1.26 us
    ppermute x9, waiting for transfers between devices, to_other_core(): lax.ppermute(block, 'ctx', [(i, i ^ 1) for i in range(ctx_size)])  1.04 us
  transfers between devices with their start and end apart: 19, of which 6 were waited for; matrix products, arithmetic and copies ran while one was open for 2% of the time, Pallas kernels for 27%

profile of v7, /device:TPU:0, one launch (start us, length us, event | category | flops | bytes accessed | tf_op | source)
XLA Modules:
  0.0 43.5 jit_solution(13503489558363873583)
XLA Ops:
  0.6 1.0 %pad_maximum_fusion.refs_0_.refs_1_ = bf16[128,1024]{1,0:T(8,128)(2,1)S(1)} fusion(bf16[64,1024]{1,0:T(8,128)(2,1)} %param.9, bf16[64,1024]{1,0:T(8,128)(2,1)} %param.8), kind=kLoop, calls=%fused_computation | loop fusion | flops 524288 | bytes 524288 | tf_op jit(solution)/shard_map/concatenate | solution.py:336
  1.6 3.1 %collective-permute-start = (bf16[128,1024]{1,0:T(8,128)(2,1)S(1)}, bf16[128,1024]{1,0:T(8,128)(2,1)S(1)}, u32[]{:S(2)}, u32[]{:S(2)}) collective-permute-start(bf16[128,1024]{1,0:T(8,128)(2,1)S(1)} %pad_maximum_fusion.refs_0_.refs_1_), channel_id=1, source_target_pairs={{0,2},{8,10},{2,4},{10,12},{4,6},{12,14},{6,22},{14,30},{22,20},{3... | collective-permute-start | bytes 786440 | tf_op jit(solution)/shard_map/ppermute | solution.py:315
  4.7 0.0 collective-permute-start.1
  4.7 0.0 collective-permute-start.2
  4.7 0.7 %maximum_bitcast_fusion.refs_0_ = f32[1,4,8]{2,1,0:T(4,128)S(1)} fusion(f32[2,8]{1,0:T(2,128)} %bitcast.4, f32[2,8]{1,0:T(2,128)} %bitcast.5), kind=kLoop, calls=%fused_computation.2 | loop fusion | flops 32 | bytes 256 | tf_op jit(solution)/shard_map/broadcast_in_dim | solution.py:338
  5.4 2.0 %collective-permute-start.3 = (f32[1,4,8]{2,1,0:T(4,128)S(1)}, f32[1,4,8]{2,1,0:T(4,128)S(1)}, u32[]{:S(2)}, u32[]{:S(2)}) collective-permute-start(f32[1,4,8]{2,1,0:T(4,128)S(1)} %maximum_bitcast_fusion.refs_0_), channel_id=1, source_target_pairs={{0,2},{2,0},{4,6},{6,4},{1,3},{3,1},{5,7},{7,5},{8,10},{10,8},{12,... | collective-permute-start | bytes 392 | tf_op jit(solution)/shard_map/ppermute | solution.py:321
  7.4 5.1 %collective-permute-done.3.refs_1_ = f32[1,4,8]{2,1,0:T(4,128)S(1)} collective-permute-done((f32[1,4,8]{2,1,0:T(4,128)S(1)}, f32[1,4,8]{2,1,0:T(4,128)S(1)}, u32[]{:S(2)}, u32[]{:S(2)}) %collective-permute-start.3) | collective-permute-done | bytes 160 | tf_op jit(solution)/shard_map/ppermute | solution.py:321
  12.5 0.0 collective-permute-done.refs_2_.refs_3_
  12.5 0.0 collective-permute-done.1.refs_4_.refs_5_
  12.5 0.0 collective-permute-done.2.refs_6_.refs_7_
  12.5 1.5 %collective-permute-start.4 = (bf16[128,1024]{1,0:T(8,128)(2,1)S(1)}, bf16[128,1024]{1,0:T(8,128)(2,1)S(1)}, u32[]{:S(2)}, u32[]{:S(2)}) collective-permute-start(bf16[128,1024]{1,0:T(8,128)(2,1)S(1)} %collective-permute-done.refs_2_.refs_3_), channel_id=1, source_target_pairs={{0,2},{8,10},{2,4},{10,12},{4,6},{12,14},{6,22},{14,30},{22,20},{3... | collective-permute-start | bytes 786440 | tf_op jit(solution)/shard_map/ppermute | solution.py:315
  14.0 0.6 %collective-permute-start.5 = (bf16[128,1024]{1,0:T(8,128)(2,1)S(1)}, bf16[128,1024]{1,0:T(8,128)(2,1)S(1)}, u32[]{:S(2)}, u32[]{:S(2)}) collective-permute-start(bf16[128,1024]{1,0:T(8,128)(2,1)S(1)} %collective-permute-done.1.refs_4_.refs_5_), channel_id=1, source_target_pairs={{0,16},{8,24},{2,0},{10,8},{4,2},{12,10},{6,4},{14,12},{22,6},{30,... | collective-permute-start | bytes 786440 | tf_op jit(solution)/shard_map/ppermute | solution.py:315
  14.6 0.0 collective-permute-start.6
  14.6 0.5 %collective-permute-start.7 = (bf16[128,1024]{1,0:T(8,128)(2,1)S(1)}, bf16[128,1024]{1,0:T(8,128)(2,1)S(1)}, u32[]{:S(2)}, u32[]{:S(2)}) collective-permute-start(bf16[128,1024]{1,0:T(8,128)(2,1)S(1)} %collective-permute-done.1.refs_4_.refs_5_), channel_id=1, source_target_pairs={{0,8},{8,0},{16,24},{24,16},{1,9},{9,1},{17,25},{25,17},{2,10},{10... | collective-permute-start | bytes 786440 | tf_op jit(solution)/shard_map/ppermute | solution.py:318
  15.1 2.6 %collective-permute-start.8 = (f32[2,4,8]{2,1,0:T(4,128)S(1)}, f32[2,4,8]{2,1,0:T(4,128)S(1)}, u32[]{:S(2)}, u32[]{:S(2)}) collective-permute-start(f32[2,4,8]{2,1,0:T(4,128)S(1)} %pad_maximum_fusion.1), channel_id=1, source_target_pairs={{0,4},{2,6},{4,0},{6,2},{1,5},{3,7},{5,1},{7,3},{8,12},{10,14},{12... | collective-permute-start | bytes 776 | tf_op jit(solution)/shard_map/ppermute | solution.py:321
  17.7 1.2 %copy-done = bf16[64,8192]{1,0:T(8,128)(2,1)S(1)} copy-done((bf16[64,8192]{1,0:T(8,128)(2,1)S(1)}, bf16[64,8192]{1,0:T(8,128)(2,1)}, u32[]{:S(2)}) %copy-start) | copy-done | bytes 1048600
  18.9 0.7 %copy-done.1 = s32[8,8]{1,0:T(8,128)S(1)} copy-done((s32[8,8]{1,0:T(8,128)S(1)}, s32[8,8]{1,0:T(8,128)}, u32[]{:S(2)}) %copy-start.1) | copy-done | bytes 280
  19.6 0.7 %copy-done.2 = s32[8]{0:T(128)S(1)} copy-done((s32[8]{0:T(128)S(1)}, s32[8]{0:T(128)}, u32[]{:S(2)}) %copy-start.2) | copy-done | bytes 56
  20.3 1.3 %shard_map.86 = (bf16[8,512,128]{2,1,0:T(8,128)(2,1)S(1)}, bf16[1024,128]{1,0:T(8,128)(2,1)S(1)}) custom-call(s32[8]{0:T(128)S(1)} %copy-done.2, s32[8,8]{1,0:T(8,128)S(1)} %copy-done.1, bf16[64,8192]{1,0:T(8,128)(2,1)S(1)} %copy-done), custom_call_target="tpu_custom_call" | custom-call | flops 4194304 | bytes 8388608 | tf_op jit(solution)/shard_map/pallas_call | solution.py:59
  21.5 0.3 collective-permute-done.8.refs_2_
  21.9 0.0 collective-permute-done.4.refs_8_.refs_9_
  21.9 0.0 collective-permute-done.5.refs_10_.refs_11_
  21.9 0.0 collective-permute-done.6.refs_12_.refs_13_
  21.9 0.0 collective-permute-done.7.refs_14_.refs_15_
  21.9 0.1 collective-permute-start.10
  22.0 0.1 collective-permute-start.12
  22.0 0.5 %collective-permute-start.11 = (bf16[128,1024]{1,0:T(8,128)(2,1)S(1)}, bf16[128,1024]{1,0:T(8,128)(2,1)S(1)}, u32[]{:S(2)}, u32[]{:S(2)}) collective-permute-start(bf16[128,1024]{1,0:T(8,128)(2,1)S(1)} %collective-permute-done.4.refs_8_.refs_9_), channel_id=1, source_target_pairs={{0,8},{8,0},{16,24},{24,16},{1,9},{9,1},{17,25},{25,17},{2,10},{10... | collective-permute-start | bytes 786440 | tf_op jit(solution)/shard_map/ppermute | solution.py:318
  22.5 1.9 %collective-permute-start.9 = (bf16[128,1024]{1,0:T(8,128)(2,1)S(1)}, bf16[128,1024]{1,0:T(8,128)(2,1)S(1)}, u32[]{:S(2)}, u32[]{:S(2)}) collective-permute-start(bf16[128,1024]{1,0:T(8,128)(2,1)S(1)} %collective-permute-done.4.refs_8_.refs_9_), channel_id=1, source_target_pairs={{0,2},{8,10},{2,4},{10,12},{4,6},{12,14},{6,22},{14,30},{22,20},{3... | collective-permute-start | bytes 786440 | tf_op jit(solution)/shard_map/ppermute | solution.py:315
  24.5 1.0 %shard_map.87 = (f32[8,16,128]{2,1,0:T(8,128)S(1)}, f32[8,16,128]{2,1,0:T(8,128)S(1)}) custom-call(f32[1,4,8]{2,1,0:T(4,128)S(1)} %maximum_bitcast_fusion.refs_0_, f32[1,4,8]{2,1,0:T(4,128)S(1)} %collective-permute-done.3.refs_1_, f32[2,4,8]{2,1,0:T(4,128)S(1)} %collective-permute-done.8.refs_2_), custom_call_target="tpu_custom_call" | custom-call | flops 100000000 | bytes 1000000 | tf_op jit(solution)/shard_map/pallas_call | solution.py:116
  25.5 4.9 %shard_map.88 = (f32[8,128,512]{2,1,0:T(8,128)S(1)}, f32[8,2,512]{2,1,0:T(2,128)S(1)}) custom-call(bf16[128,1024]{1,0:T(8,128)(2,1)S(1)} %pad_maximum_fusion.refs_0_.refs_1_, bf16[128,1024]{1,0:T(8,128)(2,1)S(1)} %pad_maximum_fusion.refs_0_.refs_1_, bf16[128,1024]{1,0:T(8,128)(2,1)S(1)} %collective-permute-done.refs_2_.refs_3_, ...), custom_call_target="tpu_custom_call" | custom-call | flops 4294967296 | bytes 8388608 | tf_op jit(solution)/shard_map/pallas_call | solution.py:269
  30.4 0.0 collective-permute-done.10.refs_2_.refs_3_
  30.5 0.0 collective-permute-done.11.refs_4_.refs_5_
  30.5 0.0 collective-permute-done.12.refs_6_.refs_7_
  30.5 0.3 collective-permute-done.9.refs_0_.refs_1_
  30.8 0.0 collective-permute-start.15
  30.8 0.5 %collective-permute-start.16 = (bf16[128,1024]{1,0:T(8,128)(2,1)S(1)}, bf16[128,1024]{1,0:T(8,128)(2,1)S(1)}, u32[]{:S(2)}, u32[]{:S(2)}) collective-permute-start(bf16[128,1024]{1,0:T(8,128)(2,1)S(1)} %collective-permute-done.10.refs_2_.refs_3_), channel_id=1, source_target_pairs={{0,8},{8,0},{16,24},{24,16},{1,9},{9,1},{17,25},{25,17},{2,10},{10... | collective-permute-start | bytes 786440 | tf_op jit(solution)/shard_map/ppermute | solution.py:318
  31.4 1.9 %collective-permute-start.13 = (bf16[64,1024]{1,0:T(8,128)(2,1)S(1)}, bf16[64,1024]{1,0:T(8,128)(2,1)S(1)}, u32[]{:S(2)}, u32[]{:S(2)}) collective-permute-start(bf16[64,1024]{1,0:T(8,128)(2,1)S(1)} %slice.6), channel_id=1, source_target_pairs={{0,2},{8,10},{2,4},{10,12},{4,6},{12,14},{6,22},{14,30},{22,20},{3... | collective-permute-start | bytes 393224 | tf_op jit(solution)/shard_map/ppermute | solution.py:315
  33.3 0.2 collective-permute-start.14
  33.4 0.0 collective-permute-done.15.refs_8_.refs_9_
  33.4 0.0 collective-permute-done.16.refs_10_.refs_11_
  33.5 4.4 %shard_map.89 = (f32[8,128,512]{2,1,0:T(8,128)S(1)}, f32[8,2,512]{2,1,0:T(2,128)S(1)}) custom-call(bf16[128,1024]{1,0:T(8,128)(2,1)S(1)} %collective-permute-done.9.refs_0_.refs_1_, bf16[128,1024]{1,0:T(8,128)(2,1)S(1)} %collective-permute-done.9.refs_0_.refs_1_, bf16[128,1024]{1,0:T(8,128)(2,1)S(1)} %collective-permute-done.10.refs_2_.refs_3_, ...), custom_call_target="tpu_custom_call" | custom-call | flops 3221225472 | bytes 8388608 | tf_op jit(solution)/shard_map/pallas_call | solution.py:269
  37.8 0.0 collective-permute-done.13.refs_0_
  37.9 0.6 %collective-permute-done.14.refs_1_ = bf16[64,1024]{1,0:T(8,128)(2,1)S(1)} collective-permute-done((bf16[64,1024]{1,0:T(8,128)(2,1)S(1)}, bf16[64,1024]{1,0:T(8,128)(2,1)S(1)}, u32[]{:S(2)}, u32[]{:S(2)}) %collective-permute-start.14) | collective-permute-done | bytes 131104 | tf_op jit(solution)/shard_map/ppermute | solution.py:315
  38.4 0.0 collective-permute-start.17
  38.4 0.5 %collective-permute-start.18 = (bf16[64,1024]{1,0:T(8,128)(2,1)S(1)}, bf16[64,1024]{1,0:T(8,128)(2,1)S(1)}, u32[]{:S(2)}, u32[]{:S(2)}) collective-permute-start(bf16[64,1024]{1,0:T(8,128)(2,1)S(1)} %collective-permute-done.14.refs_1_), channel_id=1, source_target_pairs={{0,8},{8,0},{16,24},{24,16},{1,9},{9,1},{17,25},{25,17},{2,10},{10... | collective-permute-start | bytes 393224 | tf_op jit(solution)/shard_map/ppermute | solution.py:318
  38.9 0.8 %collective-permute-done.17.refs_2_ = bf16[64,1024]{1,0:T(8,128)(2,1)S(1)} collective-permute-done((bf16[64,1024]{1,0:T(8,128)(2,1)S(1)}, bf16[64,1024]{1,0:T(8,128)(2,1)S(1)}, u32[]{:S(2)}, u32[]{:S(2)}) %collective-permute-start.17) | collective-permute-done | bytes 131104 | tf_op jit(solution)/shard_map/ppermute | solution.py:318
  39.8 0.2 collective-permute-done.18.refs_3_
  40.0 3.6 %shard_map.90 = (bf16[64,8192]{1,0:T(8,128)(2,1)}, f32[64,64]{1,0:T(8,128)}) custom-call(bf16[64,1024]{1,0:T(8,128)(2,1)S(1)} %collective-permute-done.13.refs_0_, bf16[64,1024]{1,0:T(8,128)(2,1)S(1)} %collective-permute-done.14.refs_1_, bf16[64,1024]{1,0:T(8,128)(2,1)S(1)} %collective-permute-done.17.refs_2_, ...), custom_call_target="tpu_custom_call" | custom-call | flops 1073741824 | bytes 8388608 | tf_op jit(solution)/shard_map/pallas_call | solution.py:269
  (6 shorter events, 0.0 us)
Async XLA Ops:
  1.6 10.9 %collective-permute-start = (bf16[128,1024]{1,0:T(8,128)(2,1)S(1)}, bf16[128,1024]{1,0:T(8,128)(2,1)S(1)}, u32[]{:S(2)}, u32[]{:S(2)}) collective-permute-start(bf16[128,1024]{1,0:T(8,128)(2,1)S(1)} %pad_maximum_fusion.refs_0_.refs_1_), channel_id=1, source_target_pairs={{0,2},{8,10},{2,4},{10,12},{4,6},{12,14},{6,22},{14,30},{22,20},{3... | collective-permute-start | bytes 786440 | tf_op jit(solution)/shard_map/ppermute | solution.py:315
  4.7 7.8 %collective-permute-start.1 = (bf16[128,1024]{1,0:T(8,128)(2,1)S(1)}, bf16[128,1024]{1,0:T(8,128)(2,1)S(1)}, u32[]{:S(2)}, u32[]{:S(2)}) collective-permute-start(bf16[128,1024]{1,0:T(8,128)(2,1)S(1)} %pad_maximum_fusion.refs_0_.refs_1_), channel_id=1, source_target_pairs={{0,16},{8,24},{2,0},{10,8},{4,2},{12,10},{6,4},{14,12},{22,6},{30,... | collective-permute-start | bytes 786440 | tf_op jit(solution)/shard_map/ppermute | solution.py:315
  4.7 7.8 %collective-permute-start.2 = (bf16[128,1024]{1,0:T(8,128)(2,1)S(1)}, bf16[128,1024]{1,0:T(8,128)(2,1)S(1)}, u32[]{:S(2)}, u32[]{:S(2)}) collective-permute-start(bf16[128,1024]{1,0:T(8,128)(2,1)S(1)} %pad_maximum_fusion.refs_0_.refs_1_), channel_id=1, source_target_pairs={{0,8},{8,0},{16,24},{24,16},{1,9},{9,1},{17,25},{25,17},{2,10},{10... | collective-permute-start | bytes 786440 | tf_op jit(solution)/shard_map/ppermute | solution.py:318
  5.4 7.1 %collective-permute-start.3 = (f32[1,4,8]{2,1,0:T(4,128)S(1)}, f32[1,4,8]{2,1,0:T(4,128)S(1)}, u32[]{:S(2)}, u32[]{:S(2)}) collective-permute-start(f32[1,4,8]{2,1,0:T(4,128)S(1)} %maximum_bitcast_fusion.refs_0_), channel_id=1, source_target_pairs={{0,2},{2,0},{4,6},{6,4},{1,3},{3,1},{5,7},{7,5},{8,10},{10,8},{12,... | collective-permute-start | bytes 392 | tf_op jit(solution)/shard_map/ppermute | solution.py:321
  12.5 9.4 %collective-permute-start.4 = (bf16[128,1024]{1,0:T(8,128)(2,1)S(1)}, bf16[128,1024]{1,0:T(8,128)(2,1)S(1)}, u32[]{:S(2)}, u32[]{:S(2)}) collective-permute-start(bf16[128,1024]{1,0:T(8,128)(2,1)S(1)} %collective-permute-done.refs_2_.refs_3_), channel_id=1, source_target_pairs={{0,2},{8,10},{2,4},{10,12},{4,6},{12,14},{6,22},{14,30},{22,20},{3... | collective-permute-start | bytes 786440 | tf_op jit(solution)/shard_map/ppermute | solution.py:315
  14.0 7.8 %collective-permute-start.5 = (bf16[128,1024]{1,0:T(8,128)(2,1)S(1)}, bf16[128,1024]{1,0:T(8,128)(2,1)S(1)}, u32[]{:S(2)}, u32[]{:S(2)}) collective-permute-start(bf16[128,1024]{1,0:T(8,128)(2,1)S(1)} %collective-permute-done.1.refs_4_.refs_5_), channel_id=1, source_target_pairs={{0,16},{8,24},{2,0},{10,8},{4,2},{12,10},{6,4},{14,12},{22,6},{30,... | collective-permute-start | bytes 786440 | tf_op jit(solution)/shard_map/ppermute | solution.py:315
  14.6 7.3 %collective-permute-start.6 = (bf16[128,1024]{1,0:T(8,128)(2,1)S(1)}, bf16[128,1024]{1,0:T(8,128)(2,1)S(1)}, u32[]{:S(2)}, u32[]{:S(2)}) collective-permute-start(bf16[128,1024]{1,0:T(8,128)(2,1)S(1)} %collective-permute-done.refs_2_.refs_3_), channel_id=1, source_target_pairs={{0,8},{8,0},{16,24},{24,16},{1,9},{9,1},{17,25},{25,17},{2,10},{10... | collective-permute-start | bytes 786440 | tf_op jit(solution)/shard_map/ppermute | solution.py:318
  14.6 7.3 %collective-permute-start.7 = (bf16[128,1024]{1,0:T(8,128)(2,1)S(1)}, bf16[128,1024]{1,0:T(8,128)(2,1)S(1)}, u32[]{:S(2)}, u32[]{:S(2)}) collective-permute-start(bf16[128,1024]{1,0:T(8,128)(2,1)S(1)} %collective-permute-done.1.refs_4_.refs_5_), channel_id=1, source_target_pairs={{0,8},{8,0},{16,24},{24,16},{1,9},{9,1},{17,25},{25,17},{2,10},{10... | collective-permute-start | bytes 786440 | tf_op jit(solution)/shard_map/ppermute | solution.py:318
  15.1 6.8 %collective-permute-start.8 = (f32[2,4,8]{2,1,0:T(4,128)S(1)}, f32[2,4,8]{2,1,0:T(4,128)S(1)}, u32[]{:S(2)}, u32[]{:S(2)}) collective-permute-start(f32[2,4,8]{2,1,0:T(4,128)S(1)} %pad_maximum_fusion.1), channel_id=1, source_target_pairs={{0,4},{2,6},{4,0},{6,2},{1,5},{3,7},{5,1},{7,3},{8,12},{10,14},{12... | collective-permute-start | bytes 776 | tf_op jit(solution)/shard_map/ppermute | solution.py:321
  17.7 1.2 %copy-start = (bf16[64,8192]{1,0:T(8,128)(2,1)S(1)}, bf16[64,8192]{1,0:T(8,128)(2,1)}, u32[]{:S(2)}) copy-start(bf16[64,8192]{1,0:T(8,128)(2,1)} %q_ref.1) | copy-start | bytes 3145732
  18.9 0.7 %copy-start.1 = (s32[8,8]{1,0:T(8,128)S(1)}, s32[8,8]{1,0:T(8,128)}, u32[]{:S(2)}) copy-start(s32[8,8]{1,0:T(8,128)} %keep_ref.1) | copy-start | bytes 772
  19.6 0.7 %copy-start.2 = (s32[8]{0:T(128)S(1)}, s32[8]{0:T(128)}, u32[]{:S(2)}) copy-start(s32[8]{0:T(128)} %order_ref.1) | copy-start | bytes 100
  21.9 8.6 %collective-permute-start.10 = (bf16[128,1024]{1,0:T(8,128)(2,1)S(1)}, bf16[128,1024]{1,0:T(8,128)(2,1)S(1)}, u32[]{:S(2)}, u32[]{:S(2)}) collective-permute-start(bf16[128,1024]{1,0:T(8,128)(2,1)S(1)} %collective-permute-done.5.refs_10_.refs_11_), channel_id=1, source_target_pairs={{0,16},{8,24},{2,0},{10,8},{4,2},{12,10},{6,4},{14,12},{22,6},{30,... | collective-permute-start | bytes 786440 | tf_op jit(solution)/shard_map/ppermute | solution.py:315
  22.0 8.5 %collective-permute-start.12 = (bf16[128,1024]{1,0:T(8,128)(2,1)S(1)}, bf16[128,1024]{1,0:T(8,128)(2,1)S(1)}, u32[]{:S(2)}, u32[]{:S(2)}) collective-permute-start(bf16[128,1024]{1,0:T(8,128)(2,1)S(1)} %collective-permute-done.5.refs_10_.refs_11_), channel_id=1, source_target_pairs={{0,8},{8,0},{16,24},{24,16},{1,9},{9,1},{17,25},{25,17},{2,10},{10... | collective-permute-start | bytes 786440 | tf_op jit(solution)/shard_map/ppermute | solution.py:318
  22.0 8.4 %collective-permute-start.11 = (bf16[128,1024]{1,0:T(8,128)(2,1)S(1)}, bf16[128,1024]{1,0:T(8,128)(2,1)S(1)}, u32[]{:S(2)}, u32[]{:S(2)}) collective-permute-start(bf16[128,1024]{1,0:T(8,128)(2,1)S(1)} %collective-permute-done.4.refs_8_.refs_9_), channel_id=1, source_target_pairs={{0,8},{8,0},{16,24},{24,16},{1,9},{9,1},{17,25},{25,17},{2,10},{10... | collective-permute-start | bytes 786440 | tf_op jit(solution)/shard_map/ppermute | solution.py:318
  22.5 8.3 %collective-permute-start.9 = (bf16[128,1024]{1,0:T(8,128)(2,1)S(1)}, bf16[128,1024]{1,0:T(8,128)(2,1)S(1)}, u32[]{:S(2)}, u32[]{:S(2)}) collective-permute-start(bf16[128,1024]{1,0:T(8,128)(2,1)S(1)} %collective-permute-done.4.refs_8_.refs_9_), channel_id=1, source_target_pairs={{0,2},{8,10},{2,4},{10,12},{4,6},{12,14},{6,22},{14,30},{22,20},{3... | collective-permute-start | bytes 786440 | tf_op jit(solution)/shard_map/ppermute | solution.py:315
  30.8 2.6 %collective-permute-start.15 = (bf16[128,1024]{1,0:T(8,128)(2,1)S(1)}, bf16[128,1024]{1,0:T(8,128)(2,1)S(1)}, u32[]{:S(2)}, u32[]{:S(2)}) collective-permute-start(bf16[128,1024]{1,0:T(8,128)(2,1)S(1)} %collective-permute-done.9.refs_0_.refs_1_), channel_id=1, source_target_pairs={{0,8},{8,0},{16,24},{24,16},{1,9},{9,1},{17,25},{25,17},{2,10},{10... | collective-permute-start | bytes 786440 | tf_op jit(solution)/shard_map/ppermute | solution.py:318
  30.8 2.6 %collective-permute-start.16 = (bf16[128,1024]{1,0:T(8,128)(2,1)S(1)}, bf16[128,1024]{1,0:T(8,128)(2,1)S(1)}, u32[]{:S(2)}, u32[]{:S(2)}) collective-permute-start(bf16[128,1024]{1,0:T(8,128)(2,1)S(1)} %collective-permute-done.10.refs_2_.refs_3_), channel_id=1, source_target_pairs={{0,8},{8,0},{16,24},{24,16},{1,9},{9,1},{17,25},{25,17},{2,10},{10... | collective-permute-start | bytes 786440 | tf_op jit(solution)/shard_map/ppermute | solution.py:318
  31.4 6.5 %collective-permute-start.13 = (bf16[64,1024]{1,0:T(8,128)(2,1)S(1)}, bf16[64,1024]{1,0:T(8,128)(2,1)S(1)}, u32[]{:S(2)}, u32[]{:S(2)}) collective-permute-start(bf16[64,1024]{1,0:T(8,128)(2,1)S(1)} %slice.6), channel_id=1, source_target_pairs={{0,2},{8,10},{2,4},{10,12},{4,6},{12,14},{6,22},{14,30},{22,20},{3... | collective-permute-start | bytes 393224 | tf_op jit(solution)/shard_map/ppermute | solution.py:315
  33.3 5.1 %collective-permute-start.14 = (bf16[64,1024]{1,0:T(8,128)(2,1)S(1)}, bf16[64,1024]{1,0:T(8,128)(2,1)S(1)}, u32[]{:S(2)}, u32[]{:S(2)}) collective-permute-start(bf16[64,1024]{1,0:T(8,128)(2,1)S(1)} %slice.7), channel_id=1, source_target_pairs={{0,16},{8,24},{2,0},{10,8},{4,2},{12,10},{6,4},{14,12},{22,6},{30,... | collective-permute-start | bytes 393224 | tf_op jit(solution)/shard_map/ppermute | solution.py:315
  38.4 1.3 %collective-permute-start.17 = (bf16[64,1024]{1,0:T(8,128)(2,1)S(1)}, bf16[64,1024]{1,0:T(8,128)(2,1)S(1)}, u32[]{:S(2)}, u32[]{:S(2)}) collective-permute-start(bf16[64,1024]{1,0:T(8,128)(2,1)S(1)} %collective-permute-done.13.refs_0_), channel_id=1, source_target_pairs={{0,8},{8,0},{16,24},{24,16},{1,9},{9,1},{17,25},{25,17},{2,10},{10... | collective-permute-start | bytes 393224 | tf_op jit(solution)/shard_map/ppermute | solution.py:318
  38.4 1.5 %collective-permute-start.18 = (bf16[64,1024]{1,0:T(8,128)(2,1)S(1)}, bf16[64,1024]{1,0:T(8,128)(2,1)S(1)}, u32[]{:S(2)}, u32[]{:S(2)}) collective-permute-start(bf16[64,1024]{1,0:T(8,128)(2,1)S(1)} %collective-permute-done.14.refs_1_), channel_id=1, source_target_pairs={{0,8},{8,0},{16,24},{24,16},{1,9},{9,1},{17,25},{25,17},{2,10},{10... | collective-permute-start | bytes 393224 | tf_op jit(solution)/shard_map/ppermute | solution.py:318

commit v8 on v7

--- a/solution.py
+++ b/solution.py
@@ -137,93 +137,101 @@
     )(*scales)
 
 
-def absorb_kernel(*refs, groups, tokens, per_step, begin, count, first, last):
+def absorb_kernel(*refs, groups, tokens, per_step, begin, whole, first, last):
+    count = len(whole)
     refs = list(refs)
-    pieces = [(refs.pop(0), refs.pop(0)) for _ in range(count)]
+    pieces = []
+    for joined in whole:
+        ref = refs.pop(0)
+        if joined:
+            pieces.append((ref.at[pl.ds(0, tokens)], ref.at[pl.ds(tokens, tokens)]))
+        else:
+            pieces.append((ref, refs.pop(0)))
     qa_ref, mask_ref, key_scale_ref, value_scale_ref = [refs.pop(0) for _ in range(4)]
     mixed_in, stats_in = (None, None) if first else (refs.pop(0), refs.pop(0))
     result_ref, stats_ref, x_ref, p_ref, check_ref = refs
-    step = pl.program_id(0)
+    kv_heads = qa_ref.shape[0]
     inverse_root = 1.0 / math.sqrt(HEAD_WIDTH)
     row = lax.broadcasted_iota(jnp.int32, (tokens, SPAN), 0)
     lane = lax.broadcasted_iota(jnp.int32, (tokens, SPAN), 1)
     one_hot = jnp.where(row == lane, 1.0, 0.0).astype(jnp.bfloat16)
     one_hot = jnp.concatenate([one_hot] * groups, axis=0)
-    for u in range(per_step):
-        g = step * per_step + u
-        cols = pl.ds(pl.multiple_of(g * HEAD_WIDTH, HEAD_WIDTH), HEAD_WIDTH)
-        k = jnp.concatenate([key_ref[:, cols] for key_ref, _ in pieces], axis=0)
-        k = jnp.concatenate([k, mask_ref[begin * tokens : (begin + count) * tokens, :]], axis=1)
-        x_ref[u] = lax.dot_general(
-            k,
-            jnp.concatenate([qa_ref[u], one_hot], axis=1),
-            (((1,), (1,)), ((), ())),
-            preferred_element_type=jnp.float32,
-        )
-    for u in range(per_step):
-        g = step * per_step + u
-        cols = pl.ds(pl.multiple_of(g * HEAD_WIDTH, HEAD_WIDTH), HEAD_WIDTH)
-        factors = [key_scale_ref[u, begin + i : begin + i + 1, :] for i in range(count)]
-        high, low = [], []
-        for i, (_, value_ref) in enumerate(pieces):
-            factor = value_scale_ref[u, begin + i : begin + i + 1, :]
-            v = value_ref[:, cols].astype(jnp.float32) * factor
-            high.append(v.astype(jnp.bfloat16))
-            low.append((v - high[-1].astype(jnp.float32)).astype(jnp.bfloat16))
-        v = jnp.concatenate(
-            [jnp.concatenate(high, axis=0), jnp.concatenate(low, axis=0)], axis=1
-        )
-        tops, totals, fades = [], [], []
-        for tile in range(groups * tokens // SPAN):
-            lanes = slice(tile * SPAN, (tile + 1) * SPAN)
-            top = None
-            for i, factor in enumerate(factors):
-                x = x_ref[u, i * tokens : (i + 1) * tokens, lanes]
-                highest = jnp.max(x.reshape(tokens // 8, 8, SPAN), axis=0) * factor
-                top = highest if top is None else jnp.maximum(top, highest)
-            top = jnp.max(top, axis=0, keepdims=True)
-            if not first:
-                before = stats_in[u, 0:1, lanes]
-                top = jnp.maximum(top, before)
-                fades.append(jnp.exp2(before - top))
-            total = None
-            for i, factor in enumerate(factors):
-                keys = slice(i * tokens, (i + 1) * tokens)
-                weight = jnp.exp2(x_ref[u, keys, lanes] * factor - top)
-                p_ref[u, keys, lanes] = weight.astype(jnp.bfloat16)
-                part = jnp.sum(weight.reshape(tokens // 8, 8, SPAN), axis=0)
-                total = part if total is None else total + part
-            total = jnp.sum(total, axis=0, keepdims=True)
-            if not first:
-                total = total + fades[tile] * stats_in[u, 1:2, lanes]
-            tops.append(top)
-            totals.append(total)
-        both = lax.dot_general(
-            v, p_ref[u], (((0,), (0,)), ((), ())), preferred_element_type=jnp.float32
-        )
-        for tile in range(groups * tokens // SPAN):
-            lanes = slice(tile * SPAN, (tile + 1) * SPAN)
-            mixed = both[:HEAD_WIDTH, lanes] + both[HEAD_WIDTH:, lanes]
-            if not first:
-                mixed = mixed + fades[tile] * mixed_in[u, :, lanes]
-            if not last:
-                result_ref[u, :, lanes] = mixed
-                stats_ref[u, 0:1, lanes] = tops[tile]
-                stats_ref[u, 1:2, lanes] = totals[tile]
-                continue
-            mixed = mixed * (1.0 / totals[tile])
-            check = jnp.sum(mixed, axis=0, keepdims=True) * inverse_root
-            mixed = jnp.transpose(mixed).astype(result_ref.dtype)
-            for j in range(SPAN // tokens):
-                h = tile * (SPAN // tokens) + j
-                at = (u * groups + h) * HEAD_WIDTH
-                result_ref[:, at : at + HEAD_WIDTH] = mixed[j * tokens : (j + 1) * tokens]
-                check_ref[pl.ds(g * groups + h, 1), :] = check[:, j * tokens : (j + 1) * tokens]
+
+    @pl.loop(0, kv_heads // per_step)
+    def _(step):
+        for u in range(per_step):
+            g = step * per_step + u
+            cols = pl.ds(pl.multiple_of(g * HEAD_WIDTH, HEAD_WIDTH), HEAD_WIDTH)
+            k = jnp.concatenate([key_ref[:, cols] for key_ref, _ in pieces], axis=0)
+            k = jnp.concatenate([k, mask_ref[begin * tokens : (begin + count) * tokens, :]], axis=1)
+            x_ref[u] = lax.dot_general(
+                k,
+                jnp.concatenate([qa_ref[g], one_hot], axis=1),
+                (((1,), (1,)), ((), ())),
+                preferred_element_type=jnp.float32,
+            )
+        for u in range(per_step):
+            g = step * per_step + u
+            cols = pl.ds(pl.multiple_of(g * HEAD_WIDTH, HEAD_WIDTH), HEAD_WIDTH)
+            factors = [key_scale_ref[g, begin + i : begin + i + 1, :] for i in range(count)]
+            high, low = [], []
+            for i, (_, value_ref) in enumerate(pieces):
+                factor = value_scale_ref[g, begin + i : begin + i + 1, :]
+                v = value_ref[:, cols].astype(jnp.float32) * factor
+                high.append(v.astype(jnp.bfloat16))
+                low.append((v - high[-1].astype(jnp.float32)).astype(jnp.bfloat16))
+            v = jnp.concatenate(
+                [jnp.concatenate(high, axis=0), jnp.concatenate(low, axis=0)], axis=1
+            )
+            tops, totals, fades = [], [], []
+            for tile in range(groups * tokens // SPAN):
+                lanes = slice(tile * SPAN, (tile + 1) * SPAN)
+                top = None
+                for i, factor in enumerate(factors):
+                    x = x_ref[u, i * tokens : (i + 1) * tokens, lanes]
+                    highest = jnp.max(x.reshape(tokens // 8, 8, SPAN), axis=0) * factor
+                    top = highest if top is None else jnp.maximum(top, highest)
+                top = jnp.max(top, axis=0, keepdims=True)
+                if not first:
+                    before = stats_in[g, 0:1, lanes]
+                    top = jnp.maximum(top, before)
+                    fades.append(jnp.exp2(before - top))
+                total = None
+                for i, factor in enumerate(factors):
+                    keys = slice(i * tokens, (i + 1) * tokens)
+                    weight = jnp.exp2(x_ref[u, keys, lanes] * factor - top)
+                    p_ref[u, keys, lanes] = weight.astype(jnp.bfloat16)
+                    part = jnp.sum(weight.reshape(tokens // 8, 8, SPAN), axis=0)
+                    total = part if total is None else total + part
+                total = jnp.sum(total, axis=0, keepdims=True)
+                if not first:
+                    total = total + fades[tile] * stats_in[g, 1:2, lanes]
+                tops.append(top)
+                totals.append(total)
+            both = lax.dot_general(
+                v, p_ref[u], (((0,), (0,)), ((), ())), preferred_element_type=jnp.float32
+            )
+            for tile in range(groups * tokens // SPAN):
+                lanes = slice(tile * SPAN, (tile + 1) * SPAN)
+                mixed = both[:HEAD_WIDTH, lanes] + both[HEAD_WIDTH:, lanes]
+                if not first:
+                    mixed = mixed + fades[tile] * mixed_in[g, :, lanes]
+                if not last:
+                    result_ref[g, :, lanes] = mixed
+                    stats_ref[g, 0:1, lanes] = tops[tile]
+                    stats_ref[g, 1:2, lanes] = totals[tile]
+                    continue
+                mixed = mixed * (1.0 / totals[tile])
+                check = jnp.sum(mixed, axis=0, keepdims=True) * inverse_root
+                mixed = jnp.transpose(mixed).astype(result_ref.dtype)
+                for j in range(SPAN // tokens):
+                    h = tile * (SPAN // tokens) + j
+                    at = pl.multiple_of((g * groups + h) * HEAD_WIDTH, HEAD_WIDTH)
+                    result_ref[:, pl.ds(at, HEAD_WIDTH)] = mixed[j * tokens : (j + 1) * tokens]
+                    check_ref[pl.ds(g * groups + h, 1), :] = check[:, j * tokens : (j + 1) * tokens]
+
     if last:
-
-        @pl.when(step == pl.num_programs(0) - 1)
-        def _():
-            stats_ref[...] = jnp.transpose(check_ref[...])
+        stats_ref[...] = jnp.transpose(check_ref[...])
 
 
 def absorb(prepared, pieces, begin, state, last, tokens):
@@ -234,34 +242,16 @@
     keys = tokens * count
     width = kv_heads * groups * HEAD_WIDTH
     first = state is None
-    mixed = pl.BlockSpec((per_step, HEAD_WIDTH, rows), lambda s: (s, 0, 0))
-    stats = pl.BlockSpec((per_step, 2, rows), lambda s: (s, 0, 0))
-    scale_rows = pl.BlockSpec((per_step,) + prepared[2].shape[1:], lambda s: (s, 0, 0))
-    in_specs, operands = [], []
-    for piece in pieces:
-        joined = len(piece) == 1
-        half = (tokens, piece[0].shape[1])
-        in_specs.append(pl.BlockSpec(half, lambda s: (0, 0)))
-        in_specs.append(pl.BlockSpec(half, lambda s: (1, 0)) if joined else in_specs[-1])
-        operands += [piece[0], piece[-1]]
-    in_specs += [
-        pl.BlockSpec((per_step, rows, depth), lambda s: (s, 0, 0)),
-        pl.BlockSpec(prepared[1].shape, lambda s: (0, 0)),
-        scale_rows,
-        scale_rows,
-    ]
-    in_specs += [] if first else [mixed, stats]
+    whole = [len(piece) == 1 for piece in pieces]
+    operands = [block for piece in pieces for block in piece]
+    vmem = pl.BlockSpec(memory_space=pltpu.VMEM)
+    operands += [*prepared, *(() if first else state)]
     if last:
-        out_specs = [
-            pl.BlockSpec((tokens, per_step * groups * HEAD_WIDTH), lambda s: (0, s)),
-            pl.BlockSpec((tokens, kv_heads * groups), lambda s: (0, 0)),
-        ]
         out_shape = [
             jax.ShapeDtypeStruct((tokens, width), jnp.bfloat16),
             jax.ShapeDtypeStruct((tokens, kv_heads * groups), jnp.float32),
         ]
     else:
-        out_specs = [mixed, stats]
         out_shape = [
             jax.ShapeDtypeStruct((kv_heads, HEAD_WIDTH, rows), jnp.float32),
             jax.ShapeDtypeStruct((kv_heads, 2, rows), jnp.float32),
@@ -273,13 +263,12 @@
             tokens=tokens,
             per_step=per_step,
             begin=begin,
-            count=count,
+            whole=whole,
             first=first,
             last=last,
         ),
-        grid=(kv_heads // per_step,),
-        in_specs=in_specs,
-        out_specs=out_specs,
+        in_specs=[vmem] * len(operands),
+        out_specs=[vmem] * 2,
         out_shape=out_shape,
         scratch_shapes=[
             pltpu.VMEM((per_step, keys, rows), jnp.float32),
@@ -292,7 +281,7 @@
             bytes_accessed=16 * tokens * width,
             transcendentals=tokens * width // HEAD_WIDTH * keys,
         ),
-    )(*operands, *prepared, *(() if first else state))
+    )(*operands)
 
 
 def local(queries, keys, values, key_scale, value_scale, span_order, block_keep):

time: 43.8 us -> 43.9 us (level)
  transfers between devices with their start and end apart: 19 -> 19, of which waited for: 6 -> 6; matrix products, arithmetic and copies ran while one was open for 2% -> 2% of each run, Pallas kernels for 27% -> 26%
where the time goes in v8:
time: 43.9 us; the launch traced here: 43.7 us
  starting transfers between devices  16 us (36%)
  Pallas kernels  15.2 us (35%)
  waiting for transfers between devices  7.48 us (17%)
  local copies, waits for them, and re-layouts  2.59 us (6%)
  other arithmetic  1.7 us (4%)
  between operations  0.76 us (2%)
    pallas_call x3, Pallas kernels, absorb(): pl.pallas_call(functools.partial(absorb_kernel, groups=groups, tokens=tok...  12.9 us
    ppermute x8, starting transfers between devices, around(): return lax.ppermute(block, ('ctx', 'head'), route)  9.25 us
    ppermute x2, waiting for transfers between devices, swap_heads(): lax.ppermute(block, 'head', [(i, i ^ flip) for i in range(head_size)])  5.41 us
    ppermute x2, starting transfers between devices, swap_heads(): lax.ppermute(block, 'head', [(i, i ^ flip) for i in range(head_size)])  4.61 us
    unnamed x6, local copies, waits for them, and re-layouts  2.57 us
    ppermute x9, starting transfers between devices, to_other_core(): lax.ppermute(block, 'ctx', [(i, i ^ 1) for i in range(ctx_size)])  2.1 us
    pallas_call x1, Pallas kernels, prepare(): pl.pallas_call(functools.partial(prepare_kernel, groups=groups, per_step=...  1.26 us
    ppermute x9, waiting for transfers between devices, to_other_core(): lax.ppermute(block, 'ctx', [(i, i ^ 1) for i in range(ctx_size)])  1.04 us
  transfers between devices with their start and end apart: 19, of which 6 were waited for; matrix products, arithmetic and copies ran while one was open for 2% of the time, Pallas kernels for 26%

profile of v8, /device:TPU:0, one launch (start us, length us, event | category | flops | bytes accessed | tf_op | source)
XLA Modules:
  0.0 43.7 jit_solution(2342763554885120555)
XLA Ops:
  0.6 1.0 %pad_maximum_fusion.refs_0_ = bf16[128,1024]{1,0:T(8,128)(2,1)S(1)} fusion(bf16[64,1024]{1,0:T(8,128)(2,1)} %param.9, bf16[64,1024]{1,0:T(8,128)(2,1)} %param.8), kind=kLoop, calls=%fused_computation | loop fusion | flops 524288 | bytes 524288 | tf_op jit(solution)/shard_map/concatenate | solution.py:325
  1.6 3.1 %collective-permute-start = (bf16[128,1024]{1,0:T(8,128)(2,1)S(1)}, bf16[128,1024]{1,0:T(8,128)(2,1)S(1)}, u32[]{:S(2)}, u32[]{:S(2)}) collective-permute-start(bf16[128,1024]{1,0:T(8,128)(2,1)S(1)} %pad_maximum_fusion.refs_0_), channel_id=1, source_target_pairs={{0,2},{8,10},{2,4},{10,12},{4,6},{12,14},{6,22},{14,30},{22,20},{3... | collective-permute-start | bytes 786440 | tf_op jit(solution)/shard_map/ppermute | solution.py:304
  4.7 0.0 collective-permute-start.1
  4.7 0.0 collective-permute-start.2
  4.7 0.7 %maximum_bitcast_fusion.refs_0_ = f32[1,4,8]{2,1,0:T(4,128)S(1)} fusion(f32[2,8]{1,0:T(2,128)} %bitcast.4, f32[2,8]{1,0:T(2,128)} %bitcast.5), kind=kLoop, calls=%fused_computation.2 | loop fusion | flops 32 | bytes 256 | tf_op jit(solution)/shard_map/broadcast_in_dim | solution.py:327
  5.4 2.0 %collective-permute-start.3 = (f32[1,4,8]{2,1,0:T(4,128)S(1)}, f32[1,4,8]{2,1,0:T(4,128)S(1)}, u32[]{:S(2)}, u32[]{:S(2)}) collective-permute-start(f32[1,4,8]{2,1,0:T(4,128)S(1)} %maximum_bitcast_fusion.refs_0_), channel_id=1, source_target_pairs={{0,2},{2,0},{4,6},{6,4},{1,3},{3,1},{5,7},{7,5},{8,10},{10,8},{12,... | collective-permute-start | bytes 392 | tf_op jit(solution)/shard_map/ppermute | solution.py:310
  7.4 5.1 %collective-permute-done.3.refs_1_ = f32[1,4,8]{2,1,0:T(4,128)S(1)} collective-permute-done((f32[1,4,8]{2,1,0:T(4,128)S(1)}, f32[1,4,8]{2,1,0:T(4,128)S(1)}, u32[]{:S(2)}, u32[]{:S(2)}) %collective-permute-start.3) | collective-permute-done | bytes 160 | tf_op jit(solution)/shard_map/ppermute | solution.py:310
  12.5 0.0 collective-permute-done.refs_1_
  12.5 0.0 collective-permute-done.1.refs_2_
  12.5 0.0 collective-permute-done.2.refs_3_
  12.5 1.5 %collective-permute-start.4 = (bf16[128,1024]{1,0:T(8,128)(2,1)S(1)}, bf16[128,1024]{1,0:T(8,128)(2,1)S(1)}, u32[]{:S(2)}, u32[]{:S(2)}) collective-permute-start(bf16[128,1024]{1,0:T(8,128)(2,1)S(1)} %collective-permute-done.refs_1_), channel_id=1, source_target_pairs={{0,2},{8,10},{2,4},{10,12},{4,6},{12,14},{6,22},{14,30},{22,20},{3... | collective-permute-start | bytes 786440 | tf_op jit(solution)/shard_map/ppermute | solution.py:304
  14.0 0.6 %collective-permute-start.5 = (bf16[128,1024]{1,0:T(8,128)(2,1)S(1)}, bf16[128,1024]{1,0:T(8,128)(2,1)S(1)}, u32[]{:S(2)}, u32[]{:S(2)}) collective-permute-start(bf16[128,1024]{1,0:T(8,128)(2,1)S(1)} %collective-permute-done.1.refs_2_), channel_id=1, source_target_pairs={{0,16},{8,24},{2,0},{10,8},{4,2},{12,10},{6,4},{14,12},{22,6},{30,... | collective-permute-start | bytes 786440 | tf_op jit(solution)/shard_map/ppermute | solution.py:304
  14.6 0.0 collective-permute-start.6
  14.6 0.5 %collective-permute-start.7 = (bf16[128,1024]{1,0:T(8,128)(2,1)S(1)}, bf16[128,1024]{1,0:T(8,128)(2,1)S(1)}, u32[]{:S(2)}, u32[]{:S(2)}) collective-permute-start(bf16[128,1024]{1,0:T(8,128)(2,1)S(1)} %collective-permute-done.1.refs_2_), channel_id=1, source_target_pairs={{0,8},{8,0},{16,24},{24,16},{1,9},{9,1},{17,25},{25,17},{2,10},{10... | collective-permute-start | bytes 786440 | tf_op jit(solution)/shard_map/ppermute | solution.py:307
  15.1 2.6 %collective-permute-start.8 = (f32[2,4,8]{2,1,0:T(4,128)S(1)}, f32[2,4,8]{2,1,0:T(4,128)S(1)}, u32[]{:S(2)}, u32[]{:S(2)}) collective-permute-start(f32[2,4,8]{2,1,0:T(4,128)S(1)} %pad_maximum_fusion.1), channel_id=1, source_target_pairs={{0,4},{2,6},{4,0},{6,2},{1,5},{3,7},{5,1},{7,3},{8,12},{10,14},{12... | collective-permute-start | bytes 776 | tf_op jit(solution)/shard_map/ppermute | solution.py:310
  17.7 1.2 %copy-done = bf16[64,8192]{1,0:T(8,128)(2,1)S(1)} copy-done((bf16[64,8192]{1,0:T(8,128)(2,1)S(1)}, bf16[64,8192]{1,0:T(8,128)(2,1)}, u32[]{:S(2)}) %copy-start) | copy-done | bytes 1048600
  18.9 0.7 %copy-done.1 = s32[8,8]{1,0:T(8,128)S(1)} copy-done((s32[8,8]{1,0:T(8,128)S(1)}, s32[8,8]{1,0:T(8,128)}, u32[]{:S(2)}) %copy-start.1) | copy-done | bytes 280
  19.6 0.7 %copy-done.2 = s32[8]{0:T(128)S(1)} copy-done((s32[8]{0:T(128)S(1)}, s32[8]{0:T(128)}, u32[]{:S(2)}) %copy-start.2) | copy-done | bytes 56
  20.3 1.3 %shard_map.86 = (bf16[8,512,128]{2,1,0:T(8,128)(2,1)S(1)}, bf16[1024,128]{1,0:T(8,128)(2,1)S(1)}) custom-call(s32[8]{0:T(128)S(1)} %copy-done.2, s32[8,8]{1,0:T(8,128)S(1)} %copy-done.1, bf16[64,8192]{1,0:T(8,128)(2,1)S(1)} %copy-done), custom_call_target="tpu_custom_call" | custom-call | flops 4194304 | bytes 8388608 | tf_op jit(solution)/shard_map/pallas_call | solution.py:59
  21.5 0.3 collective-permute-done.8.refs_2_
  21.9 0.0 collective-permute-done.4.refs_4_
  21.9 0.0 collective-permute-done.5.refs_5_
  21.9 0.0 collective-permute-done.6.refs_6_
  21.9 0.0 collective-permute-done.7.refs_7_
  21.9 0.1 collective-permute-start.10
  22.0 0.1 collective-permute-start.12
  22.0 0.5 %collective-permute-start.11 = (bf16[128,1024]{1,0:T(8,128)(2,1)S(1)}, bf16[128,1024]{1,0:T(8,128)(2,1)S(1)}, u32[]{:S(2)}, u32[]{:S(2)}) collective-permute-start(bf16[128,1024]{1,0:T(8,128)(2,1)S(1)} %collective-permute-done.4.refs_4_), channel_id=1, source_target_pairs={{0,8},{8,0},{16,24},{24,16},{1,9},{9,1},{17,25},{25,17},{2,10},{10... | collective-permute-start | bytes 786440 | tf_op jit(solution)/shard_map/ppermute | solution.py:307
  22.5 1.9 %collective-permute-start.9 = (bf16[128,1024]{1,0:T(8,128)(2,1)S(1)}, bf16[128,1024]{1,0:T(8,128)(2,1)S(1)}, u32[]{:S(2)}, u32[]{:S(2)}) collective-permute-start(bf16[128,1024]{1,0:T(8,128)(2,1)S(1)} %collective-permute-done.4.refs_4_), channel_id=1, source_target_pairs={{0,2},{8,10},{2,4},{10,12},{4,6},{12,14},{6,22},{14,30},{22,20},{3... | collective-permute-start | bytes 786440 | tf_op jit(solution)/shard_map/ppermute | solution.py:304
  24.5 1.0 %shard_map.87 = (f32[8,16,128]{2,1,0:T(8,128)S(1)}, f32[8,16,128]{2,1,0:T(8,128)S(1)}) custom-call(f32[1,4,8]{2,1,0:T(4,128)S(1)} %maximum_bitcast_fusion.refs_0_, f32[1,4,8]{2,1,0:T(4,128)S(1)} %collective-permute-done.3.refs_1_, f32[2,4,8]{2,1,0:T(4,128)S(1)} %collective-permute-done.8.refs_2_), custom_call_target="tpu_custom_call" | custom-call | flops 100000000 | bytes 1000000 | tf_op jit(solution)/shard_map/pallas_call | solution.py:116
  25.5 4.9 %shard_map.88 = (f32[8,128,512]{2,1,0:T(8,128)S(1)}, f32[8,2,512]{2,1,0:T(2,128)S(1)}) custom-call(bf16[128,1024]{1,0:T(8,128)(2,1)S(1)} %pad_maximum_fusion.refs_0_, bf16[128,1024]{1,0:T(8,128)(2,1)S(1)} %collective-permute-done.refs_1_, bf16[128,1024]{1,0:T(8,128)(2,1)S(1)} %collective-permute-done.1.refs_2_, ...), custom_call_target="tpu_custom_call" | custom-call | flops 4294967296 | bytes 8388608 | tf_op jit(solution)/shard_map/pallas_call | solution.py:259
  30.4 0.0 collective-permute-done.10.refs_1_
  30.4 0.0 collective-permute-done.11.refs_2_
  30.4 0.0 collective-permute-done.12.refs_3_
  30.4 0.4 collective-permute-done.9.refs_0_
  30.8 0.0 collective-permute-start.15
  30.8 0.5 %collective-permute-start.16 = (bf16[128,1024]{1,0:T(8,128)(2,1)S(1)}, bf16[128,1024]{1,0:T(8,128)(2,1)S(1)}, u32[]{:S(2)}, u32[]{:S(2)}) collective-permute-start(bf16[128,1024]{1,0:T(8,128)(2,1)S(1)} %collective-permute-done.10.refs_1_), channel_id=1, source_target_pairs={{0,8},{8,0},{16,24},{24,16},{1,9},{9,1},{17,25},{25,17},{2,10},{10... | collective-permute-start | bytes 786440 | tf_op jit(solution)/shard_map/ppermute | solution.py:307
  31.4 1.9 %collective-permute-start.13 = (bf16[64,1024]{1,0:T(8,128)(2,1)S(1)}, bf16[64,1024]{1,0:T(8,128)(2,1)S(1)}, u32[]{:S(2)}, u32[]{:S(2)}) collective-permute-start(bf16[64,1024]{1,0:T(8,128)(2,1)S(1)} %slice.6), channel_id=1, source_target_pairs={{0,2},{8,10},{2,4},{10,12},{4,6},{12,14},{6,22},{14,30},{22,20},{3... | collective-permute-start | bytes 393224 | tf_op jit(solution)/shard_map/ppermute | solution.py:304
  33.3 0.2 collective-permute-start.14
  33.4 0.0 collective-permute-done.15.refs_4_
  33.4 0.0 collective-permute-done.16.refs_5_
  33.5 4.3 %shard_map.89 = (f32[8,128,512]{2,1,0:T(8,128)S(1)}, f32[8,2,512]{2,1,0:T(2,128)S(1)}) custom-call(bf16[128,1024]{1,0:T(8,128)(2,1)S(1)} %collective-permute-done.9.refs_0_, bf16[128,1024]{1,0:T(8,128)(2,1)S(1)} %collective-permute-done.10.refs_1_, bf16[128,1024]{1,0:T(8,128)(2,1)S(1)} %collective-permute-done.11.refs_2_, ...), custom_call_target="tpu_custom_call" | custom-call | flops 3221225472 | bytes 8388608 | tf_op jit(solution)/shard_map/pallas_call | solution.py:259
  37.8 0.0 collective-permute-done.13.refs_0_
  37.8 0.6 %collective-permute-done.14.refs_1_ = bf16[64,1024]{1,0:T(8,128)(2,1)S(1)} collective-permute-done((bf16[64,1024]{1,0:T(8,128)(2,1)S(1)}, bf16[64,1024]{1,0:T(8,128)(2,1)S(1)}, u32[]{:S(2)}, u32[]{:S(2)}) %collective-permute-start.14) | collective-permute-done | bytes 131104 | tf_op jit(solution)/shard_map/ppermute | solution.py:304
  38.4 0.0 collective-permute-start.17
  38.4 0.5 %collective-permute-start.18 = (bf16[64,1024]{1,0:T(8,128)(2,1)S(1)}, bf16[64,1024]{1,0:T(8,128)(2,1)S(1)}, u32[]{:S(2)}, u32[]{:S(2)}) collective-permute-start(bf16[64,1024]{1,0:T(8,128)(2,1)S(1)} %collective-permute-done.14.refs_1_), channel_id=1, source_target_pairs={{0,8},{8,0},{16,24},{24,16},{1,9},{9,1},{17,25},{25,17},{2,10},{10... | collective-permute-start | bytes 393224 | tf_op jit(solution)/shard_map/ppermute | solution.py:307
  38.9 0.8 %collective-permute-done.17.refs_2_ = bf16[64,1024]{1,0:T(8,128)(2,1)S(1)} collective-permute-done((bf16[64,1024]{1,0:T(8,128)(2,1)S(1)}, bf16[64,1024]{1,0:T(8,128)(2,1)S(1)}, u32[]{:S(2)}, u32[]{:S(2)}) %collective-permute-start.17) | collective-permute-done | bytes 131104 | tf_op jit(solution)/shard_map/ppermute | solution.py:307
  39.8 0.2 collective-permute-done.18.refs_3_
  40.0 3.8 %shard_map.90 = (bf16[64,8192]{1,0:T(8,128)(2,1)}, f32[64,64]{1,0:T(8,128)}) custom-call(bf16[64,1024]{1,0:T(8,128)(2,1)S(1)} %collective-permute-done.13.refs_0_, bf16[64,1024]{1,0:T(8,128)(2,1)S(1)} %collective-permute-done.14.refs_1_, bf16[64,1024]{1,0:T(8,128)(2,1)S(1)} %collective-permute-done.17.refs_2_, ...), custom_call_target="tpu_custom_call" | custom-call | flops 1073741824 | bytes 8388608 | tf_op jit(solution)/shard_map/pallas_call | solution.py:259
  (6 shorter events, 0.0 us)
Async XLA Ops:
  1.6 10.9 %collective-permute-start = (bf16[128,1024]{1,0:T(8,128)(2,1)S(1)}, bf16[128,1024]{1,0:T(8,128)(2,1)S(1)}, u32[]{:S(2)}, u32[]{:S(2)}) collective-permute-start(bf16[128,1024]{1,0:T(8,128)(2,1)S(1)} %pad_maximum_fusion.refs_0_), channel_id=1, source_target_pairs={{0,2},{8,10},{2,4},{10,12},{4,6},{12,14},{6,22},{14,30},{22,20},{3... | collective-permute-start | bytes 786440 | tf_op jit(solution)/shard_map/ppermute | solution.py:304
  4.7 7.8 %collective-permute-start.1 = (bf16[128,1024]{1,0:T(8,128)(2,1)S(1)}, bf16[128,1024]{1,0:T(8,128)(2,1)S(1)}, u32[]{:S(2)}, u32[]{:S(2)}) collective-permute-start(bf16[128,1024]{1,0:T(8,128)(2,1)S(1)} %pad_maximum_fusion.refs_0_), channel_id=1, source_target_pairs={{0,16},{8,24},{2,0},{10,8},{4,2},{12,10},{6,4},{14,12},{22,6},{30,... | collective-permute-start | bytes 786440 | tf_op jit(solution)/shard_map/ppermute | solution.py:304
  4.7 7.8 %collective-permute-start.2 = (bf16[128,1024]{1,0:T(8,128)(2,1)S(1)}, bf16[128,1024]{1,0:T(8,128)(2,1)S(1)}, u32[]{:S(2)}, u32[]{:S(2)}) collective-permute-start(bf16[128,1024]{1,0:T(8,128)(2,1)S(1)} %pad_maximum_fusion.refs_0_), channel_id=1, source_target_pairs={{0,8},{8,0},{16,24},{24,16},{1,9},{9,1},{17,25},{25,17},{2,10},{10... | collective-permute-start | bytes 786440 | tf_op jit(solution)/shard_map/ppermute | solution.py:307
  5.4 7.1 %collective-permute-start.3 = (f32[1,4,8]{2,1,0:T(4,128)S(1)}, f32[1,4,8]{2,1,0:T(4,128)S(1)}, u32[]{:S(2)}, u32[]{:S(2)}) collective-permute-start(f32[1,4,8]{2,1,0:T(4,128)S(1)} %maximum_bitcast_fusion.refs_0_), channel_id=1, source_target_pairs={{0,2},{2,0},{4,6},{6,4},{1,3},{3,1},{5,7},{7,5},{8,10},{10,8},{12,... | collective-permute-start | bytes 392 | tf_op jit(solution)/shard_map/ppermute | solution.py:310
  12.5 9.4 %collective-permute-start.4 = (bf16[128,1024]{1,0:T(8,128)(2,1)S(1)}, bf16[128,1024]{1,0:T(8,128)(2,1)S(1)}, u32[]{:S(2)}, u32[]{:S(2)}) collective-permute-start(bf16[128,1024]{1,0:T(8,128)(2,1)S(1)} %collective-permute-done.refs_1_), channel_id=1, source_target_pairs={{0,2},{8,10},{2,4},{10,12},{4,6},{12,14},{6,22},{14,30},{22,20},{3... | collective-permute-start | bytes 786440 | tf_op jit(solution)/shard_map/ppermute | solution.py:304
  14.0 7.8 %collective-permute-start.5 = (bf16[128,1024]{1,0:T(8,128)(2,1)S(1)}, bf16[128,1024]{1,0:T(8,128)(2,1)S(1)}, u32[]{:S(2)}, u32[]{:S(2)}) collective-permute-start(bf16[128,1024]{1,0:T(8,128)(2,1)S(1)} %collective-permute-done.1.refs_2_), channel_id=1, source_target_pairs={{0,16},{8,24},{2,0},{10,8},{4,2},{12,10},{6,4},{14,12},{22,6},{30,... | collective-permute-start | bytes 786440 | tf_op jit(solution)/shard_map/ppermute | solution.py:304
  14.6 7.3 %collective-permute-start.6 = (bf16[128,1024]{1,0:T(8,128)(2,1)S(1)}, bf16[128,1024]{1,0:T(8,128)(2,1)S(1)}, u32[]{:S(2)}, u32[]{:S(2)}) collective-permute-start(bf16[128,1024]{1,0:T(8,128)(2,1)S(1)} %collective-permute-done.refs_1_), channel_id=1, source_target_pairs={{0,8},{8,0},{16,24},{24,16},{1,9},{9,1},{17,25},{25,17},{2,10},{10... | collective-permute-start | bytes 786440 | tf_op jit(solution)/shard_map/ppermute | solution.py:307
  14.6 7.3 %collective-permute-start.7 = (bf16[128,1024]{1,0:T(8,128)(2,1)S(1)}, bf16[128,1024]{1,0:T(8,128)(2,1)S(1)}, u32[]{:S(2)}, u32[]{:S(2)}) collective-permute-start(bf16[128,1024]{1,0:T(8,128)(2,1)S(1)} %collective-permute-done.1.refs_2_), channel_id=1, source_target_pairs={{0,8},{8,0},{16,24},{24,16},{1,9},{9,1},{17,25},{25,17},{2,10},{10... | collective-permute-start | bytes 786440 | tf_op jit(solution)/shard_map/ppermute | solution.py:307
  15.1 6.8 %collective-permute-start.8 = (f32[2,4,8]{2,1,0:T(4,128)S(1)}, f32[2,4,8]{2,1,0:T(4,128)S(1)}, u32[]{:S(2)}, u32[]{:S(2)}) collective-permute-start(f32[2,4,8]{2,1,0:T(4,128)S(1)} %pad_maximum_fusion.1), channel_id=1, source_target_pairs={{0,4},{2,6},{4,0},{6,2},{1,5},{3,7},{5,1},{7,3},{8,12},{10,14},{12... | collective-permute-start | bytes 776 | tf_op jit(solution)/shard_map/ppermute | solution.py:310
  17.7 1.2 %copy-start = (bf16[64,8192]{1,0:T(8,128)(2,1)S(1)}, bf16[64,8192]{1,0:T(8,128)(2,1)}, u32[]{:S(2)}) copy-start(bf16[64,8192]{1,0:T(8,128)(2,1)} %q_ref.1) | copy-start | bytes 3145732
  18.9 0.7 %copy-start.1 = (s32[8,8]{1,0:T(8,128)S(1)}, s32[8,8]{1,0:T(8,128)}, u32[]{:S(2)}) copy-start(s32[8,8]{1,0:T(8,128)} %keep_ref.1) | copy-start | bytes 772
  19.6 0.7 %copy-start.2 = (s32[8]{0:T(128)S(1)}, s32[8]{0:T(128)}, u32[]{:S(2)}) copy-start(s32[8]{0:T(128)} %order_ref.1) | copy-start | bytes 100
  21.9 8.5 %collective-permute-start.10 = (bf16[128,1024]{1,0:T(8,128)(2,1)S(1)}, bf16[128,1024]{1,0:T(8,128)(2,1)S(1)}, u32[]{:S(2)}, u32[]{:S(2)}) collective-permute-start(bf16[128,1024]{1,0:T(8,128)(2,1)S(1)} %collective-permute-done.5.refs_5_), channel_id=1, source_target_pairs={{0,16},{8,24},{2,0},{10,8},{4,2},{12,10},{6,4},{14,12},{22,6},{30,... | collective-permute-start | bytes 786440 | tf_op jit(solution)/shard_map/ppermute | solution.py:304
  22.0 8.5 %collective-permute-start.12 = (bf16[128,1024]{1,0:T(8,128)(2,1)S(1)}, bf16[128,1024]{1,0:T(8,128)(2,1)S(1)}, u32[]{:S(2)}, u32[]{:S(2)}) collective-permute-start(bf16[128,1024]{1,0:T(8,128)(2,1)S(1)} %collective-permute-done.5.refs_5_), channel_id=1, source_target_pairs={{0,8},{8,0},{16,24},{24,16},{1,9},{9,1},{17,25},{25,17},{2,10},{10... | collective-permute-start | bytes 786440 | tf_op jit(solution)/shard_map/ppermute | solution.py:307
  22.0 8.4 %collective-permute-start.11 = (bf16[128,1024]{1,0:T(8,128)(2,1)S(1)}, bf16[128,1024]{1,0:T(8,128)(2,1)S(1)}, u32[]{:S(2)}, u32[]{:S(2)}) collective-permute-start(bf16[128,1024]{1,0:T(8,128)(2,1)S(1)} %collective-permute-done.4.refs_4_), channel_id=1, source_target_pairs={{0,8},{8,0},{16,24},{24,16},{1,9},{9,1},{17,25},{25,17},{2,10},{10... | collective-permute-start | bytes 786440 | tf_op jit(solution)/shard_map/ppermute | solution.py:307
  22.5 8.3 %collective-permute-start.9 = (bf16[128,1024]{1,0:T(8,128)(2,1)S(1)}, bf16[128,1024]{1,0:T(8,128)(2,1)S(1)}, u32[]{:S(2)}, u32[]{:S(2)}) collective-permute-start(bf16[128,1024]{1,0:T(8,128)(2,1)S(1)} %collective-permute-done.4.refs_4_), channel_id=1, source_target_pairs={{0,2},{8,10},{2,4},{10,12},{4,6},{12,14},{6,22},{14,30},{22,20},{3... | collective-permute-start | bytes 786440 | tf_op jit(solution)/shard_map/ppermute | solution.py:304
  30.8 2.6 %collective-permute-start.15 = (bf16[128,1024]{1,0:T(8,128)(2,1)S(1)}, bf16[128,1024]{1,0:T(8,128)(2,1)S(1)}, u32[]{:S(2)}, u32[]{:S(2)}) collective-permute-start(bf16[128,1024]{1,0:T(8,128)(2,1)S(1)} %collective-permute-done.9.refs_0_), channel_id=1, source_target_pairs={{0,8},{8,0},{16,24},{24,16},{1,9},{9,1},{17,25},{25,17},{2,10},{10... | collective-permute-start | bytes 786440 | tf_op jit(solution)/shard_map/ppermute | solution.py:307
  30.8 2.6 %collective-permute-start.16 = (bf16[128,1024]{1,0:T(8,128)(2,1)S(1)}, bf16[128,1024]{1,0:T(8,128)(2,1)S(1)}, u32[]{:S(2)}, u32[]{:S(2)}) collective-permute-start(bf16[128,1024]{1,0:T(8,128)(2,1)S(1)} %collective-permute-done.10.refs_1_), channel_id=1, source_target_pairs={{0,8},{8,0},{16,24},{24,16},{1,9},{9,1},{17,25},{25,17},{2,10},{10... | collective-permute-start | bytes 786440 | tf_op jit(solution)/shard_map/ppermute | solution.py:307
  31.4 6.4 %collective-permute-start.13 = (bf16[64,1024]{1,0:T(8,128)(2,1)S(1)}, bf16[64,1024]{1,0:T(8,128)(2,1)S(1)}, u32[]{:S(2)}, u32[]{:S(2)}) collective-permute-start(bf16[64,1024]{1,0:T(8,128)(2,1)S(1)} %slice.6), channel_id=1, source_target_pairs={{0,2},{8,10},{2,4},{10,12},{4,6},{12,14},{6,22},{14,30},{22,20},{3... | collective-permute-start | bytes 393224 | tf_op jit(solution)/shard_map/ppermute | solution.py:304
  33.3 5.1 %collective-permute-start.14 = (bf16[64,1024]{1,0:T(8,128)(2,1)S(1)}, bf16[64,1024]{1,0:T(8,128)(2,1)S(1)}, u32[]{:S(2)}, u32[]{:S(2)}) collective-permute-start(bf16[64,1024]{1,0:T(8,128)(2,1)S(1)} %slice.7), channel_id=1, source_target_pairs={{0,16},{8,24},{2,0},{10,8},{4,2},{12,10},{6,4},{14,12},{22,6},{30,... | collective-permute-start | bytes 393224 | tf_op jit(solution)/shard_map/ppermute | solution.py:304
  38.4 1.3 %collective-permute-start.17 = (bf16[64,1024]{1,0:T(8,128)(2,1)S(1)}, bf16[64,1024]{1,0:T(8,128)(2,1)S(1)}, u32[]{:S(2)}, u32[]{:S(2)}) collective-permute-start(bf16[64,1024]{1,0:T(8,128)(2,1)S(1)} %collective-permute-done.13.refs_0_), channel_id=1, source_target_pairs={{0,8},{8,0},{16,24},{24,16},{1,9},{9,1},{17,25},{25,17},{2,10},{10... | collective-permute-start | bytes 393224 | tf_op jit(solution)/shard_map/ppermute | solution.py:307
  38.4 1.5 %collective-permute-start.18 = (bf16[64,1024]{1,0:T(8,128)(2,1)S(1)}, bf16[64,1024]{1,0:T(8,128)(2,1)S(1)}, u32[]{:S(2)}, u32[]{:S(2)}) collective-permute-start(bf16[64,1024]{1,0:T(8,128)(2,1)S(1)} %collective-permute-done.14.refs_1_), channel_id=1, source_target_pairs={{0,8},{8,0},{16,24},{24,16},{1,9},{9,1},{17,25},{25,17},{2,10},{10... | collective-permute-start | bytes 393224 | tf_op jit(solution)/shard_map/ppermute | solution.py:307

commit v9 on v7

--- a/solution.py
+++ b/solution.py
@@ -25,7 +25,7 @@
     return ((2 * row + (ctx % 2) ^ flip) * head_size + column) * tokens
 
 
-def prepare_kernel(order_ref, keep_ref, q_ref, qa_ref, mask_ref, *, groups, per_step, sources, ctx_size, head_size):
+def prepare_kernel(order_ref, keep_ref, q_ref, qa_ref, hot_ref, mask_ref, *, groups, per_step, sources, ctx_size, head_size):
     step = pl.program_id(0)
     tokens = q_ref.shape[0]
     row = lax.broadcasted_iota(jnp.int32, (tokens, SPAN), 0)
@@ -43,11 +43,17 @@
             causal = jnp.where(row + (start - own_start) <= lane, 0.0, MASKED)
             mask = jnp.where(own == span, causal, whole)
             mask_ref[i * tokens : (i + 1) * tokens, :] = mask.astype(jnp.bfloat16)
+        row_all = lax.broadcasted_iota(jnp.int32, hot_ref.shape, 0)
+        lane_all = lax.broadcasted_iota(jnp.int32, hot_ref.shape, 1)
+        hot = jnp.where(row_all == lane_all % tokens, 1.0, 0.0)
+        hot_ref[...] = hot.astype(jnp.bfloat16)
 
     for u in range(per_step):
-        for h in range(groups):
-            at = (u * groups + h) * HEAD_WIDTH
-            qa_ref[u, h * tokens : (h + 1) * tokens, :] = q_ref[:, at : at + HEAD_WIDTH]
+        heads = [
+            q_ref[:, (u * groups + h) * HEAD_WIDTH : (u * groups + h + 1) * HEAD_WIDTH]
+            for h in range(groups)
+        ]
+        qa_ref[u] = jnp.transpose(jnp.concatenate(heads, axis=0))
 
 
 def prepare(queries, span_order, block_keep, sources, kv_heads, sizes):
@@ -68,11 +74,13 @@
         grid=(kv_heads // per_step,),
         in_specs=[smem, smem, pl.BlockSpec((tokens, per_step * groups * HEAD_WIDTH), lambda s: (0, s))],
         out_specs=[
-            pl.BlockSpec((per_step, rows, HEAD_WIDTH), lambda s: (s, 0, 0)),
+            pl.BlockSpec((per_step, HEAD_WIDTH, rows), lambda s: (s, 0, 0)),
+            pl.BlockSpec((SPAN, rows), lambda s: (0, 0)),
             pl.BlockSpec((tokens * len(sources), SPAN), lambda s: (0, 0)),
         ],
         out_shape=[
-            jax.ShapeDtypeStruct((kv_heads, rows, HEAD_WIDTH), jnp.bfloat16),
+            jax.ShapeDtypeStruct((kv_heads, HEAD_WIDTH, rows), jnp.bfloat16),
+            jax.ShapeDtypeStruct((SPAN, rows), jnp.bfloat16),
             jax.ShapeDtypeStruct((tokens * len(sources), SPAN), jnp.bfloat16),
         ],
         compiler_params=pltpu.CompilerParams(vmem_limit_bytes=32 * 1024 * 1024),
@@ -101,18 +109,27 @@
     ]
     for copy in copies:
         copy.wait()
+    lane = lax.broadcasted_iota(jnp.int32, (1, SPAN), 1)
     for g in range(head_size * kv_local):
         owner, member = g // kv_local, g % kv_local
         for i, span in enumerate(spans):
             factor = scale_ref[owner, member, span] * (inverse_root * LOG2E)
             key_scale_ref[g, i : i + 1, :] = jnp.full((1, SPAN), factor, jnp.float32)
-            factor = scale_ref[owner, kv_local + member, span]
-            value_scale_ref[g, i : i + 1, :] = jnp.full((1, SPAN), factor, jnp.float32)
+        per_tile = SPAN // tokens
+        for tile in range(len(sources) // per_tile):
+            row = None
+            for i in range(per_tile):
+                factor = scale_ref[owner, kv_local + member, spans[tile * per_tile + i]]
+                if row is None:
+                    row = jnp.full((1, SPAN), factor, jnp.float32)
+                else:
+                    row = jnp.where(lane >= i * tokens, factor, row)
+            value_scale_ref[g, :, tile * SPAN : (tile + 1) * SPAN] = row
 
 
 def scale_rows(scales, sources, tokens, sizes):
     kv_local = scales[0].shape[1] // 2
-    shape = (sizes[1] * kv_local, len(sources), SPAN)
+    kv_heads = sizes[1] * kv_local
     return pl.pallas_call(
         functools.partial(
             scale_rows_kernel,
@@ -125,7 +142,10 @@
         ),
         in_specs=[pl.BlockSpec(memory_space=pl.ANY)] * len(scales),
         out_specs=[pl.BlockSpec(memory_space=pltpu.VMEM)] * 2,
-        out_shape=[jax.ShapeDtypeStruct(shape, jnp.float32)] * 2,
+        out_shape=[
+            jax.ShapeDtypeStruct((kv_heads, len(sources), SPAN), jnp.float32),
+            jax.ShapeDtypeStruct((kv_heads, 1, len(sources) * tokens), jnp.float32),
+        ],
         scratch_shapes=[
             pltpu.SMEM((sizes[1],) + scales[0].shape[1:], jnp.float32),
             pltpu.SemaphoreType.DMA((sizes[1],)),
@@ -140,39 +160,31 @@
 def absorb_kernel(*refs, groups, tokens, per_step, begin, count, first, last):
     refs = list(refs)
     pieces = [(refs.pop(0), refs.pop(0)) for _ in range(count)]
-    qa_ref, mask_ref, key_scale_ref, value_scale_ref = [refs.pop(0) for _ in range(4)]
+    qa_ref, hot_ref, mask_ref, key_scale_ref, value_scale_ref = [refs.pop(0) for _ in range(5)]
     mixed_in, stats_in = (None, None) if first else (refs.pop(0), refs.pop(0))
     result_ref, stats_ref, x_ref, p_ref, check_ref = refs
     step = pl.program_id(0)
     inverse_root = 1.0 / math.sqrt(HEAD_WIDTH)
-    row = lax.broadcasted_iota(jnp.int32, (tokens, SPAN), 0)
-    lane = lax.broadcasted_iota(jnp.int32, (tokens, SPAN), 1)
-    one_hot = jnp.where(row == lane, 1.0, 0.0).astype(jnp.bfloat16)
-    one_hot = jnp.concatenate([one_hot] * groups, axis=0)
     for u in range(per_step):
         g = step * per_step + u
         cols = pl.ds(pl.multiple_of(g * HEAD_WIDTH, HEAD_WIDTH), HEAD_WIDTH)
         k = jnp.concatenate([key_ref[:, cols] for key_ref, _ in pieces], axis=0)
         k = jnp.concatenate([k, mask_ref[begin * tokens : (begin + count) * tokens, :]], axis=1)
-        x_ref[u] = lax.dot_general(
+        x_ref[u] = jnp.dot(
             k,
-            jnp.concatenate([qa_ref[u], one_hot], axis=1),
-            (((1,), (1,)), ((), ())),
+            jnp.concatenate([qa_ref[u], hot_ref[...]], axis=0),
             preferred_element_type=jnp.float32,
         )
     for u in range(per_step):
         g = step * per_step + u
         cols = pl.ds(pl.multiple_of(g * HEAD_WIDTH, HEAD_WIDTH), HEAD_WIDTH)
         factors = [key_scale_ref[u, begin + i : begin + i + 1, :] for i in range(count)]
-        high, low = [], []
-        for i, (_, value_ref) in enumerate(pieces):
-            factor = value_scale_ref[u, begin + i : begin + i + 1, :]
-            v = value_ref[:, cols].astype(jnp.float32) * factor
-            high.append(v.astype(jnp.bfloat16))
-            low.append((v - high[-1].astype(jnp.float32)).astype(jnp.bfloat16))
-        v = jnp.concatenate(
-            [jnp.concatenate(high, axis=0), jnp.concatenate(low, axis=0)], axis=1
-        )
+        v = jnp.concatenate([value_ref[:, cols] for _, value_ref in pieces], axis=0)
+        v = jnp.transpose(v).astype(jnp.float32)
+        v = v * value_scale_ref[u, :, begin * tokens : (begin + count) * tokens]
+        high = v.astype(jnp.bfloat16)
+        low = (v - high.astype(jnp.float32)).astype(jnp.bfloat16)
+        v = jnp.concatenate([high, low], axis=0)
         tops, totals, fades = [], [], []
         for tile in range(groups * tokens // SPAN):
             lanes = slice(tile * SPAN, (tile + 1) * SPAN)
@@ -198,9 +210,7 @@
                 total = total + fades[tile] * stats_in[u, 1:2, lanes]
             tops.append(top)
             totals.append(total)
-        both = lax.dot_general(
-            v, p_ref[u], (((0,), (0,)), ((), ())), preferred_element_type=jnp.float32
-        )
+        both = jnp.dot(v, p_ref[u], preferred_element_type=jnp.float32)
         for tile in range(groups * tokens // SPAN):
             lanes = slice(tile * SPAN, (tile + 1) * SPAN)
             mixed = both[:HEAD_WIDTH, lanes] + both[HEAD_WIDTH:, lanes]
@@ -227,7 +237,7 @@
 
 
 def absorb(prepared, pieces, begin, state, last, tokens):
-    kv_heads, rows, depth = prepared[0].shape
+    kv_heads, _, rows = prepared[0].shape
     groups = rows // tokens
     count = len(pieces)
     per_step = 2 if kv_heads % 2 == 0 else 1
@@ -236,7 +246,6 @@
     first = state is None
     mixed = pl.BlockSpec((per_step, HEAD_WIDTH, rows), lambda s: (s, 0, 0))
     stats = pl.BlockSpec((per_step, 2, rows), lambda s: (s, 0, 0))
-    scale_rows = pl.BlockSpec((per_step,) + prepared[2].shape[1:], lambda s: (s, 0, 0))
     in_specs, operands = [], []
     for piece in pieces:
         joined = len(piece) == 1
@@ -245,10 +254,11 @@
         in_specs.append(pl.BlockSpec(half, lambda s: (1, 0)) if joined else in_specs[-1])
         operands += [piece[0], piece[-1]]
     in_specs += [
-        pl.BlockSpec((per_step, rows, depth), lambda s: (s, 0, 0)),
+        pl.BlockSpec((per_step,) + prepared[0].shape[1:], lambda s: (s, 0, 0)),
         pl.BlockSpec(prepared[1].shape, lambda s: (0, 0)),
-        scale_rows,
-        scale_rows,
+        pl.BlockSpec(prepared[2].shape, lambda s: (0, 0)),
+        pl.BlockSpec((per_step,) + prepared[3].shape[1:], lambda s: (s, 0, 0)),
+        pl.BlockSpec((per_step,) + prepared[4].shape[1:], lambda s: (s, 0, 0)),
     ]
     in_specs += [] if first else [mixed, stats]
     if last:
@@ -350,7 +360,7 @@
         complete = held == head_size
         if not complete:
             scales = scales + [swap_heads(jnp.concatenate(scales, axis=0), held)]
-        if step == 2:
+        if step == 1:
             prepared = prepare(queries, span_order, block_keep, sources, kv_heads, sizes)
         if complete:
             if rows is None:

time: 43.8 us -> 44.5 us (1.016)
  waiting for transfers between devices: 7.38 us -> 8.19 us
  transfers between devices with their start and end apart: 19 -> 19, of which waited for: 6 -> 6; matrix products, arithmetic and copies ran while one was open for 2% -> 2% of each run, Pallas kernels for 27% -> 26%
where the time goes in v9:
time: 44.5 us; the launch traced here: 44.3 us
  starting transfers between devices  16 us (36%)
  Pallas kernels  15.1 us (34%)
  waiting for transfers between devices  8.19 us (18%)
  local copies, waits for them, and re-layouts  2.59 us (6%)
  other arithmetic  1.7 us (4%)
  between operations  0.75 us (2%)
    pallas_call x3, Pallas kernels, absorb(): pl.pallas_call(functools.partial(absorb_kernel, groups=groups, tokens=tok...  12.5 us
    ppermute x8, starting transfers between devices, around(): return lax.ppermute(block, ('ctx', 'head'), route)  9.25 us
    ppermute x2, waiting for transfers between devices, swap_heads(): lax.ppermute(block, 'head', [(i, i ^ flip) for i in range(head_size)])  5.78 us
    ppermute x2, starting transfers between devices, swap_heads(): lax.ppermute(block, 'head', [(i, i ^ flip) for i in range(head_size)])  4.61 us
    unnamed x6, local copies, waits for them, and re-layouts  2.57 us
    ppermute x9, starting transfers between devices, to_other_core(): lax.ppermute(block, 'ctx', [(i, i ^ 1) for i in range(ctx_size)])  2.1 us
    pallas_call x1, Pallas kernels, prepare(): pl.pallas_call(functools.partial(prepare_kernel, groups=groups, per_step=...  1.54 us
    ppermute x8, waiting for transfers between devices, around(): return lax.ppermute(block, ('ctx', 'head'), route)  1.37 us
  transfers between devices with their start and end apart: 19, of which 6 were waited for; matrix products, arithmetic and copies ran while one was open for 2% of the time, Pallas kernels for 26%

profile of v9, /device:TPU:0, one launch (start us, length us, event | category | flops | bytes accessed | tf_op | source)
XLA Modules:
  0.0 44.3 jit_solution(12693857481659935175)
XLA Ops:
  0.6 1.0 %pad_maximum_fusion.refs_0_.refs_1_ = bf16[128,1024]{1,0:T(8,128)(2,1)S(1)} fusion(bf16[64,1024]{1,0:T(8,128)(2,1)} %param.9, bf16[64,1024]{1,0:T(8,128)(2,1)} %param.8), kind=kLoop, calls=%fused_computation | loop fusion | flops 524288 | bytes 524288 | tf_op jit(solution)/shard_map/concatenate | solution.py:346
  1.6 3.1 %collective-permute-start = (bf16[128,1024]{1,0:T(8,128)(2,1)S(1)}, bf16[128,1024]{1,0:T(8,128)(2,1)S(1)}, u32[]{:S(2)}, u32[]{:S(2)}) collective-permute-start(bf16[128,1024]{1,0:T(8,128)(2,1)S(1)} %pad_maximum_fusion.refs_0_.refs_1_), channel_id=1, source_target_pairs={{0,2},{8,10},{2,4},{10,12},{4,6},{12,14},{6,22},{14,30},{22,20},{3... | collective-permute-start | bytes 786440 | tf_op jit(solution)/shard_map/ppermute | solution.py:325
  4.7 0.0 collective-permute-start.1
  4.7 0.0 collective-permute-start.2
  4.7 0.7 %maximum_bitcast_fusion.refs_0_ = f32[1,4,8]{2,1,0:T(4,128)S(1)} fusion(f32[2,8]{1,0:T(2,128)} %bitcast.4, f32[2,8]{1,0:T(2,128)} %bitcast.5), kind=kLoop, calls=%fused_computation.2 | loop fusion | flops 32 | bytes 256 | tf_op jit(solution)/shard_map/broadcast_in_dim | solution.py:348
  5.4 2.0 %collective-permute-start.3 = (f32[1,4,8]{2,1,0:T(4,128)S(1)}, f32[1,4,8]{2,1,0:T(4,128)S(1)}, u32[]{:S(2)}, u32[]{:S(2)}) collective-permute-start(f32[1,4,8]{2,1,0:T(4,128)S(1)} %maximum_bitcast_fusion.refs_0_), channel_id=1, source_target_pairs={{0,2},{2,0},{4,6},{6,4},{1,3},{3,1},{5,7},{7,5},{8,10},{10,8},{12,... | collective-permute-start | bytes 392 | tf_op jit(solution)/shard_map/ppermute | solution.py:331
  7.4 1.2 %copy-done = bf16[64,8192]{1,0:T(8,128)(2,1)S(1)} copy-done((bf16[64,8192]{1,0:T(8,128)(2,1)S(1)}, bf16[64,8192]{1,0:T(8,128)(2,1)}, u32[]{:S(2)}) %copy-start) | copy-done | bytes 1048600
  8.7 0.7 %copy-done.1 = s32[8,8]{1,0:T(8,128)S(1)} copy-done((s32[8,8]{1,0:T(8,128)S(1)}, s32[8,8]{1,0:T(8,128)}, u32[]{:S(2)}) %copy-start.1) | copy-done | bytes 280
  9.3 0.7 %copy-done.2 = s32[8]{0:T(128)S(1)} copy-done((s32[8]{0:T(128)S(1)}, s32[8]{0:T(128)}, u32[]{:S(2)}) %copy-start.2) | copy-done | bytes 56
  10.0 1.5 %shard_map.86 = (bf16[8,128,512]{2,1,0:T(8,128)(2,1)S(1)}, bf16[128,512]{1,0:T(8,128)(2,1)S(1)}, bf16[1024,128]{1,0:T(8,128)(2,1)S(1)}) custom-call(s32[8]{0:T(128)S(1)} %copy-done.2, s32[8,8]{1,0:T(8,128)S(1)} %copy-done.1, bf16[64,8192]{1,0:T(8,128)(2,1)S(1)} %copy-done), custom_call_target="tpu_custom_call" | custom-call | flops 4194304 | bytes 8388608 | tf_op jit(solution)/shard_map/pallas_call | solution.py:65
  11.5 1.0 %collective-permute-done.3.refs_1_ = f32[1,4,8]{2,1,0:T(4,128)S(1)} collective-permute-done((f32[1,4,8]{2,1,0:T(4,128)S(1)}, f32[1,4,8]{2,1,0:T(4,128)S(1)}, u32[]{:S(2)}, u32[]{:S(2)}) %collective-permute-start.3) | collective-permute-done | bytes 160 | tf_op jit(solution)/shard_map/ppermute | solution.py:331
  12.5 0.0 collective-permute-done.refs_2_.refs_3_
  12.5 0.0 collective-permute-done.1.refs_4_.refs_5_
  12.5 0.0 collective-permute-done.2.refs_6_.refs_7_
  12.5 1.5 %collective-permute-start.4 = (bf16[128,1024]{1,0:T(8,128)(2,1)S(1)}, bf16[128,1024]{1,0:T(8,128)(2,1)S(1)}, u32[]{:S(2)}, u32[]{:S(2)}) collective-permute-start(bf16[128,1024]{1,0:T(8,128)(2,1)S(1)} %collective-permute-done.refs_2_.refs_3_), channel_id=1, source_target_pairs={{0,2},{8,10},{2,4},{10,12},{4,6},{12,14},{6,22},{14,30},{22,20},{3... | collective-permute-start | bytes 786440 | tf_op jit(solution)/shard_map/ppermute | solution.py:325
  14.0 0.6 %collective-permute-start.5 = (bf16[128,1024]{1,0:T(8,128)(2,1)S(1)}, bf16[128,1024]{1,0:T(8,128)(2,1)S(1)}, u32[]{:S(2)}, u32[]{:S(2)}) collective-permute-start(bf16[128,1024]{1,0:T(8,128)(2,1)S(1)} %collective-permute-done.1.refs_4_.refs_5_), channel_id=1, source_target_pairs={{0,16},{8,24},{2,0},{10,8},{4,2},{12,10},{6,4},{14,12},{22,6},{30,... | collective-permute-start | bytes 786440 | tf_op jit(solution)/shard_map/ppermute | solution.py:325
  14.6 0.0 collective-permute-start.6
  14.6 0.5 %collective-permute-start.7 = (bf16[128,1024]{1,0:T(8,128)(2,1)S(1)}, bf16[128,1024]{1,0:T(8,128)(2,1)S(1)}, u32[]{:S(2)}, u32[]{:S(2)}) collective-permute-start(bf16[128,1024]{1,0:T(8,128)(2,1)S(1)} %collective-permute-done.1.refs_4_.refs_5_), channel_id=1, source_target_pairs={{0,8},{8,0},{16,24},{24,16},{1,9},{9,1},{17,25},{25,17},{2,10},{10... | collective-permute-start | bytes 786440 | tf_op jit(solution)/shard_map/ppermute | solution.py:328
  15.1 2.6 %collective-permute-start.8 = (f32[2,4,8]{2,1,0:T(4,128)S(1)}, f32[2,4,8]{2,1,0:T(4,128)S(1)}, u32[]{:S(2)}, u32[]{:S(2)}) collective-permute-start(f32[2,4,8]{2,1,0:T(4,128)S(1)} %pad_maximum_fusion.1), channel_id=1, source_target_pairs={{0,4},{2,6},{4,0},{6,2},{1,5},{3,7},{5,1},{7,3},{8,12},{10,14},{12... | collective-permute-start | bytes 776 | tf_op jit(solution)/shard_map/ppermute | solution.py:331
  17.7 4.8 %collective-permute-done.8.refs_2_ = f32[2,4,8]{2,1,0:T(4,128)S(1)} collective-permute-done((f32[2,4,8]{2,1,0:T(4,128)S(1)}, f32[2,4,8]{2,1,0:T(4,128)S(1)}, u32[]{:S(2)}, u32[]{:S(2)}) %collective-permute-start.8) | collective-permute-done | bytes 288 | tf_op jit(solution)/shard_map/ppermute | solution.py:331
  22.5 0.0 collective-permute-done.4.refs_8_.refs_9_
  22.5 0.0 collective-permute-done.5.refs_10_.refs_11_
  22.5 0.0 collective-permute-done.6.refs_12_.refs_13_
  22.5 0.0 collective-permute-done.7.refs_14_.refs_15_
  22.5 0.1 collective-permute-start.10
  22.6 0.1 collective-permute-start.12
  22.7 0.5 %collective-permute-start.11 = (bf16[128,1024]{1,0:T(8,128)(2,1)S(1)}, bf16[128,1024]{1,0:T(8,128)(2,1)S(1)}, u32[]{:S(2)}, u32[]{:S(2)}) collective-permute-start(bf16[128,1024]{1,0:T(8,128)(2,1)S(1)} %collective-permute-done.4.refs_8_.refs_9_), channel_id=1, source_target_pairs={{0,8},{8,0},{16,24},{24,16},{1,9},{9,1},{17,25},{25,17},{2,10},{10... | collective-permute-start | bytes 786440 | tf_op jit(solution)/shard_map/ppermute | solution.py:328
  23.2 1.9 %collective-permute-start.9 = (bf16[128,1024]{1,0:T(8,128)(2,1)S(1)}, bf16[128,1024]{1,0:T(8,128)(2,1)S(1)}, u32[]{:S(2)}, u32[]{:S(2)}) collective-permute-start(bf16[128,1024]{1,0:T(8,128)(2,1)S(1)} %collective-permute-done.4.refs_8_.refs_9_), channel_id=1, source_target_pairs={{0,2},{8,10},{2,4},{10,12},{4,6},{12,14},{6,22},{14,30},{22,20},{3... | collective-permute-start | bytes 786440 | tf_op jit(solution)/shard_map/ppermute | solution.py:325
  25.1 1.1 %shard_map.87 = (f32[8,16,128]{2,1,0:T(8,128)S(1)}, f32[8,1,1024]{2,1,0:T(1,128)S(1)}) custom-call(f32[1,4,8]{2,1,0:T(4,128)S(1)} %maximum_bitcast_fusion.refs_0_, f32[1,4,8]{2,1,0:T(4,128)S(1)} %collective-permute-done.3.refs_1_, f32[2,4,8]{2,1,0:T(4,128)S(1)} %collective-permute-done.8.refs_2_), custom_call_target="tpu_custom_call" | custom-call | flops 100000000 | bytes 1000000 | tf_op jit(solution)/shard_map/pallas_call | solution.py:133
  26.2 4.7 %shard_map.88 = (f32[8,128,512]{2,1,0:T(8,128)S(1)}, f32[8,2,512]{2,1,0:T(2,128)S(1)}) custom-call(bf16[128,1024]{1,0:T(8,128)(2,1)S(1)} %pad_maximum_fusion.refs_0_.refs_1_, bf16[128,1024]{1,0:T(8,128)(2,1)S(1)} %pad_maximum_fusion.refs_0_.refs_1_, bf16[128,1024]{1,0:T(8,128)(2,1)S(1)} %collective-permute-done.refs_2_.refs_3_, ...), custom_call_target="tpu_custom_call" | custom-call | flops 4294967296 | bytes 8388608 | tf_op jit(solution)/shard_map/pallas_call | solution.py:279
  30.9 0.0 collective-permute-done.10.refs_2_.refs_3_
  31.0 0.0 collective-permute-done.11.refs_4_.refs_5_
  31.0 0.0 collective-permute-done.12.refs_6_.refs_7_
  31.0 0.5 %collective-permute-done.9.refs_0_.refs_1_ = bf16[128,1024]{1,0:T(8,128)(2,1)S(1)} collective-permute-done((bf16[128,1024]{1,0:T(8,128)(2,1)S(1)}, bf16[128,1024]{1,0:T(8,128)(2,1)S(1)}, u32[]{:S(2)}, u32[]{:S(2)}) %collective-permute-start.9) | collective-permute-done | bytes 262176 | tf_op jit(solution)/shard_map/ppermute | solution.py:325
  31.5 0.0 collective-permute-start.15
  31.5 0.5 %collective-permute-start.16 = (bf16[128,1024]{1,0:T(8,128)(2,1)S(1)}, bf16[128,1024]{1,0:T(8,128)(2,1)S(1)}, u32[]{:S(2)}, u32[]{:S(2)}) collective-permute-start(bf16[128,1024]{1,0:T(8,128)(2,1)S(1)} %collective-permute-done.10.refs_2_.refs_3_), channel_id=1, source_target_pairs={{0,8},{8,0},{16,24},{24,16},{1,9},{9,1},{17,25},{25,17},{2,10},{10... | collective-permute-start | bytes 786440 | tf_op jit(solution)/shard_map/ppermute | solution.py:328
  32.0 1.9 %collective-permute-start.13 = (bf16[64,1024]{1,0:T(8,128)(2,1)S(1)}, bf16[64,1024]{1,0:T(8,128)(2,1)S(1)}, u32[]{:S(2)}, u32[]{:S(2)}) collective-permute-start(bf16[64,1024]{1,0:T(8,128)(2,1)S(1)} %slice.6), channel_id=1, source_target_pairs={{0,2},{8,10},{2,4},{10,12},{4,6},{12,14},{6,22},{14,30},{22,20},{3... | collective-permute-start | bytes 393224 | tf_op jit(solution)/shard_map/ppermute | solution.py:325
  33.9 0.2 collective-permute-start.14
  34.1 0.0 collective-permute-done.15.refs_8_.refs_9_
  34.1 0.0 collective-permute-done.16.refs_10_.refs_11_
  34.1 4.1 %shard_map.89 = (f32[8,128,512]{2,1,0:T(8,128)S(1)}, f32[8,2,512]{2,1,0:T(2,128)S(1)}) custom-call(bf16[128,1024]{1,0:T(8,128)(2,1)S(1)} %collective-permute-done.9.refs_0_.refs_1_, bf16[128,1024]{1,0:T(8,128)(2,1)S(1)} %collective-permute-done.9.refs_0_.refs_1_, bf16[128,1024]{1,0:T(8,128)(2,1)S(1)} %collective-permute-done.10.refs_2_.refs_3_, ...), custom_call_target="tpu_custom_call" | custom-call | flops 3221225472 | bytes 8388608 | tf_op jit(solution)/shard_map/pallas_call | solution.py:279
  38.2 0.0 collective-permute-done.13.refs_0_
  38.2 0.9 %collective-permute-done.14.refs_1_ = bf16[64,1024]{1,0:T(8,128)(2,1)S(1)} collective-permute-done((bf16[64,1024]{1,0:T(8,128)(2,1)S(1)}, bf16[64,1024]{1,0:T(8,128)(2,1)S(1)}, u32[]{:S(2)}, u32[]{:S(2)}) %collective-permute-start.14) | collective-permute-done | bytes 131104 | tf_op jit(solution)/shard_map/ppermute | solution.py:325
  39.1 0.0 collective-permute-start.17
  39.1 0.5 %collective-permute-start.18 = (bf16[64,1024]{1,0:T(8,128)(2,1)S(1)}, bf16[64,1024]{1,0:T(8,128)(2,1)S(1)}, u32[]{:S(2)}, u32[]{:S(2)}) collective-permute-start(bf16[64,1024]{1,0:T(8,128)(2,1)S(1)} %collective-permute-done.14.refs_1_), channel_id=1, source_target_pairs={{0,8},{8,0},{16,24},{24,16},{1,9},{9,1},{17,25},{25,17},{2,10},{10... | collective-permute-start | bytes 393224 | tf_op jit(solution)/shard_map/ppermute | solution.py:328
  39.6 0.8 %collective-permute-done.17.refs_2_ = bf16[64,1024]{1,0:T(8,128)(2,1)S(1)} collective-permute-done((bf16[64,1024]{1,0:T(8,128)(2,1)S(1)}, bf16[64,1024]{1,0:T(8,128)(2,1)S(1)}, u32[]{:S(2)}, u32[]{:S(2)}) %collective-permute-start.17) | collective-permute-done | bytes 131104 | tf_op jit(solution)/shard_map/ppermute | solution.py:328
  40.4 0.2 collective-permute-done.18.refs_3_
  40.6 3.7 %shard_map.90 = (bf16[64,8192]{1,0:T(8,128)(2,1)}, f32[64,64]{1,0:T(8,128)}) custom-call(bf16[64,1024]{1,0:T(8,128)(2,1)S(1)} %collective-permute-done.13.refs_0_, bf16[64,1024]{1,0:T(8,128)(2,1)S(1)} %collective-permute-done.14.refs_1_, bf16[64,1024]{1,0:T(8,128)(2,1)S(1)} %collective-permute-done.17.refs_2_, ...), custom_call_target="tpu_custom_call" | custom-call | flops 1073741824 | bytes 8388608 | tf_op jit(solution)/shard_map/pallas_call | solution.py:279
  (6 shorter events, 0.0 us)
Async XLA Ops:
  1.6 10.9 %collective-permute-start = (bf16[128,1024]{1,0:T(8,128)(2,1)S(1)}, bf16[128,1024]{1,0:T(8,128)(2,1)S(1)}, u32[]{:S(2)}, u32[]{:S(2)}) collective-permute-start(bf16[128,1024]{1,0:T(8,128)(2,1)S(1)} %pad_maximum_fusion.refs_0_.refs_1_), channel_id=1, source_target_pairs={{0,2},{8,10},{2,4},{10,12},{4,6},{12,14},{6,22},{14,30},{22,20},{3... | collective-permute-start | bytes 786440 | tf_op jit(solution)/shard_map/ppermute | solution.py:325
  4.7 7.8 %collective-permute-start.1 = (bf16[128,1024]{1,0:T(8,128)(2,1)S(1)}, bf16[128,1024]{1,0:T(8,128)(2,1)S(1)}, u32[]{:S(2)}, u32[]{:S(2)}) collective-permute-start(bf16[128,1024]{1,0:T(8,128)(2,1)S(1)} %pad_maximum_fusion.refs_0_.refs_1_), channel_id=1, source_target_pairs={{0,16},{8,24},{2,0},{10,8},{4,2},{12,10},{6,4},{14,12},{22,6},{30,... | collective-permute-start | bytes 786440 | tf_op jit(solution)/shard_map/ppermute | solution.py:325
  4.7 7.8 %collective-permute-start.2 = (bf16[128,1024]{1,0:T(8,128)(2,1)S(1)}, bf16[128,1024]{1,0:T(8,128)(2,1)S(1)}, u32[]{:S(2)}, u32[]{:S(2)}) collective-permute-start(bf16[128,1024]{1,0:T(8,128)(2,1)S(1)} %pad_maximum_fusion.refs_0_.refs_1_), channel_id=1, source_target_pairs={{0,8},{8,0},{16,24},{24,16},{1,9},{9,1},{17,25},{25,17},{2,10},{10... | collective-permute-start | bytes 786440 | tf_op jit(solution)/shard_map/ppermute | solution.py:328
  5.4 7.1 %collective-permute-start.3 = (f32[1,4,8]{2,1,0:T(4,128)S(1)}, f32[1,4,8]{2,1,0:T(4,128)S(1)}, u32[]{:S(2)}, u32[]{:S(2)}) collective-permute-start(f32[1,4,8]{2,1,0:T(4,128)S(1)} %maximum_bitcast_fusion.refs_0_), channel_id=1, source_target_pairs={{0,2},{2,0},{4,6},{6,4},{1,3},{3,1},{5,7},{7,5},{8,10},{10,8},{12,... | collective-permute-start | bytes 392 | tf_op jit(solution)/shard_map/ppermute | solution.py:331
  7.4 1.2 %copy-start = (bf16[64,8192]{1,0:T(8,128)(2,1)S(1)}, bf16[64,8192]{1,0:T(8,128)(2,1)}, u32[]{:S(2)}) copy-start(bf16[64,8192]{1,0:T(8,128)(2,1)} %q_ref.1) | copy-start | bytes 3145732
  8.7 0.7 %copy-start.1 = (s32[8,8]{1,0:T(8,128)S(1)}, s32[8,8]{1,0:T(8,128)}, u32[]{:S(2)}) copy-start(s32[8,8]{1,0:T(8,128)} %keep_ref.1) | copy-start | bytes 772
  9.3 0.7 %copy-start.2 = (s32[8]{0:T(128)S(1)}, s32[8]{0:T(128)}, u32[]{:S(2)}) copy-start(s32[8]{0:T(128)} %order_ref.1) | copy-start | bytes 100
  12.5 10.0 %collective-permute-start.4 = (bf16[128,1024]{1,0:T(8,128)(2,1)S(1)}, bf16[128,1024]{1,0:T(8,128)(2,1)S(1)}, u32[]{:S(2)}, u32[]{:S(2)}) collective-permute-start(bf16[128,1024]{1,0:T(8,128)(2,1)S(1)} %collective-permute-done.refs_2_.refs_3_), channel_id=1, source_target_pairs={{0,2},{8,10},{2,4},{10,12},{4,6},{12,14},{6,22},{14,30},{22,20},{3... | collective-permute-start | bytes 786440 | tf_op jit(solution)/shard_map/ppermute | solution.py:325
  14.0 8.5 %collective-permute-start.5 = (bf16[128,1024]{1,0:T(8,128)(2,1)S(1)}, bf16[128,1024]{1,0:T(8,128)(2,1)S(1)}, u32[]{:S(2)}, u32[]{:S(2)}) collective-permute-start(bf16[128,1024]{1,0:T(8,128)(2,1)S(1)} %collective-permute-done.1.refs_4_.refs_5_), channel_id=1, source_target_pairs={{0,16},{8,24},{2,0},{10,8},{4,2},{12,10},{6,4},{14,12},{22,6},{30,... | collective-permute-start | bytes 786440 | tf_op jit(solution)/shard_map/ppermute | solution.py:325
  14.6 7.9 %collective-permute-start.6 = (bf16[128,1024]{1,0:T(8,128)(2,1)S(1)}, bf16[128,1024]{1,0:T(8,128)(2,1)S(1)}, u32[]{:S(2)}, u32[]{:S(2)}) collective-permute-start(bf16[128,1024]{1,0:T(8,128)(2,1)S(1)} %collective-permute-done.refs_2_.refs_3_), channel_id=1, source_target_pairs={{0,8},{8,0},{16,24},{24,16},{1,9},{9,1},{17,25},{25,17},{2,10},{10... | collective-permute-start | bytes 786440 | tf_op jit(solution)/shard_map/ppermute | solution.py:328
  14.6 7.9 %collective-permute-start.7 = (bf16[128,1024]{1,0:T(8,128)(2,1)S(1)}, bf16[128,1024]{1,0:T(8,128)(2,1)S(1)}, u32[]{:S(2)}, u32[]{:S(2)}) collective-permute-start(bf16[128,1024]{1,0:T(8,128)(2,1)S(1)} %collective-permute-done.1.refs_4_.refs_5_), channel_id=1, source_target_pairs={{0,8},{8,0},{16,24},{24,16},{1,9},{9,1},{17,25},{25,17},{2,10},{10... | collective-permute-start | bytes 786440 | tf_op jit(solution)/shard_map/ppermute | solution.py:328
  15.1 7.4 %collective-permute-start.8 = (f32[2,4,8]{2,1,0:T(4,128)S(1)}, f32[2,4,8]{2,1,0:T(4,128)S(1)}, u32[]{:S(2)}, u32[]{:S(2)}) collective-permute-start(f32[2,4,8]{2,1,0:T(4,128)S(1)} %pad_maximum_fusion.1), channel_id=1, source_target_pairs={{0,4},{2,6},{4,0},{6,2},{1,5},{3,7},{5,1},{7,3},{8,12},{10,14},{12... | collective-permute-start | bytes 776 | tf_op jit(solution)/shard_map/ppermute | solution.py:331
  22.5 8.4 %collective-permute-start.10 = (bf16[128,1024]{1,0:T(8,128)(2,1)S(1)}, bf16[128,1024]{1,0:T(8,128)(2,1)S(1)}, u32[]{:S(2)}, u32[]{:S(2)}) collective-permute-start(bf16[128,1024]{1,0:T(8,128)(2,1)S(1)} %collective-permute-done.5.refs_10_.refs_11_), channel_id=1, source_target_pairs={{0,16},{8,24},{2,0},{10,8},{4,2},{12,10},{6,4},{14,12},{22,6},{30,... | collective-permute-start | bytes 786440 | tf_op jit(solution)/shard_map/ppermute | solution.py:325
  22.6 8.4 %collective-permute-start.12 = (bf16[128,1024]{1,0:T(8,128)(2,1)S(1)}, bf16[128,1024]{1,0:T(8,128)(2,1)S(1)}, u32[]{:S(2)}, u32[]{:S(2)}) collective-permute-start(bf16[128,1024]{1,0:T(8,128)(2,1)S(1)} %collective-permute-done.5.refs_10_.refs_11_), channel_id=1, source_target_pairs={{0,8},{8,0},{16,24},{24,16},{1,9},{9,1},{17,25},{25,17},{2,10},{10... | collective-permute-start | bytes 786440 | tf_op jit(solution)/shard_map/ppermute | solution.py:328
  22.7 8.3 %collective-permute-start.11 = (bf16[128,1024]{1,0:T(8,128)(2,1)S(1)}, bf16[128,1024]{1,0:T(8,128)(2,1)S(1)}, u32[]{:S(2)}, u32[]{:S(2)}) collective-permute-start(bf16[128,1024]{1,0:T(8,128)(2,1)S(1)} %collective-permute-done.4.refs_8_.refs_9_), channel_id=1, source_target_pairs={{0,8},{8,0},{16,24},{24,16},{1,9},{9,1},{17,25},{25,17},{2,10},{10... | collective-permute-start | bytes 786440 | tf_op jit(solution)/shard_map/ppermute | solution.py:328
  23.2 8.3 %collective-permute-start.9 = (bf16[128,1024]{1,0:T(8,128)(2,1)S(1)}, bf16[128,1024]{1,0:T(8,128)(2,1)S(1)}, u32[]{:S(2)}, u32[]{:S(2)}) collective-permute-start(bf16[128,1024]{1,0:T(8,128)(2,1)S(1)} %collective-permute-done.4.refs_8_.refs_9_), channel_id=1, source_target_pairs={{0,2},{8,10},{2,4},{10,12},{4,6},{12,14},{6,22},{14,30},{22,20},{3... | collective-permute-start | bytes 786440 | tf_op jit(solution)/shard_map/ppermute | solution.py:325
  31.5 2.6 %collective-permute-start.15 = (bf16[128,1024]{1,0:T(8,128)(2,1)S(1)}, bf16[128,1024]{1,0:T(8,128)(2,1)S(1)}, u32[]{:S(2)}, u32[]{:S(2)}) collective-permute-start(bf16[128,1024]{1,0:T(8,128)(2,1)S(1)} %collective-permute-done.9.refs_0_.refs_1_), channel_id=1, source_target_pairs={{0,8},{8,0},{16,24},{24,16},{1,9},{9,1},{17,25},{25,17},{2,10},{10... | collective-permute-start | bytes 786440 | tf_op jit(solution)/shard_map/ppermute | solution.py:328
  31.5 2.6 %collective-permute-start.16 = (bf16[128,1024]{1,0:T(8,128)(2,1)S(1)}, bf16[128,1024]{1,0:T(8,128)(2,1)S(1)}, u32[]{:S(2)}, u32[]{:S(2)}) collective-permute-start(bf16[128,1024]{1,0:T(8,128)(2,1)S(1)} %collective-permute-done.10.refs_2_.refs_3_), channel_id=1, source_target_pairs={{0,8},{8,0},{16,24},{24,16},{1,9},{9,1},{17,25},{25,17},{2,10},{10... | collective-permute-start | bytes 786440 | tf_op jit(solution)/shard_map/ppermute | solution.py:328
  32.0 6.2 %collective-permute-start.13 = (bf16[64,1024]{1,0:T(8,128)(2,1)S(1)}, bf16[64,1024]{1,0:T(8,128)(2,1)S(1)}, u32[]{:S(2)}, u32[]{:S(2)}) collective-permute-start(bf16[64,1024]{1,0:T(8,128)(2,1)S(1)} %slice.6), channel_id=1, source_target_pairs={{0,2},{8,10},{2,4},{10,12},{4,6},{12,14},{6,22},{14,30},{22,20},{3... | collective-permute-start | bytes 393224 | tf_op jit(solution)/shard_map/ppermute | solution.py:325
  33.9 5.1 %collective-permute-start.14 = (bf16[64,1024]{1,0:T(8,128)(2,1)S(1)}, bf16[64,1024]{1,0:T(8,128)(2,1)S(1)}, u32[]{:S(2)}, u32[]{:S(2)}) collective-permute-start(bf16[64,1024]{1,0:T(8,128)(2,1)S(1)} %slice.7), channel_id=1, source_target_pairs={{0,16},{8,24},{2,0},{10,8},{4,2},{12,10},{6,4},{14,12},{22,6},{30,... | collective-permute-start | bytes 393224 | tf_op jit(solution)/shard_map/ppermute | solution.py:325
  39.1 1.3 %collective-permute-start.17 = (bf16[64,1024]{1,0:T(8,128)(2,1)S(1)}, bf16[64,1024]{1,0:T(8,128)(2,1)S(1)}, u32[]{:S(2)}, u32[]{:S(2)}) collective-permute-start(bf16[64,1024]{1,0:T(8,128)(2,1)S(1)} %collective-permute-done.13.refs_0_), channel_id=1, source_target_pairs={{0,8},{8,0},{16,24},{24,16},{1,9},{9,1},{17,25},{25,17},{2,10},{10... | collective-permute-start | bytes 393224 | tf_op jit(solution)/shard_map/ppermute | solution.py:328
  39.1 1.5 %collective-permute-start.18 = (bf16[64,1024]{1,0:T(8,128)(2,1)S(1)}, bf16[64,1024]{1,0:T(8,128)(2,1)S(1)}, u32[]{:S(2)}, u32[]{:S(2)}) collective-permute-start(bf16[64,1024]{1,0:T(8,128)(2,1)S(1)} %collective-permute-done.14.refs_1_), channel_id=1, source_target_pairs={{0,8},{8,0},{16,24},{24,16},{1,9},{9,1},{17,25},{25,17},{2,10},{10... | collective-permute-start | bytes 393224 | tf_op jit(solution)/shard_map/ppermute | solution.py:328

commit v10 on v9

--- a/solution.py
+++ b/solution.py
@@ -175,17 +175,13 @@
             jnp.concatenate([qa_ref[u], hot_ref[...]], axis=0),
             preferred_element_type=jnp.float32,
         )
+    rows = []
     for u in range(per_step):
         g = step * per_step + u
         cols = pl.ds(pl.multiple_of(g * HEAD_WIDTH, HEAD_WIDTH), HEAD_WIDTH)
         factors = [key_scale_ref[u, begin + i : begin + i + 1, :] for i in range(count)]
-        v = jnp.concatenate([value_ref[:, cols] for _, value_ref in pieces], axis=0)
-        v = jnp.transpose(v).astype(jnp.float32)
-        v = v * value_scale_ref[u, :, begin * tokens : (begin + count) * tokens]
-        high = v.astype(jnp.bfloat16)
-        low = (v - high.astype(jnp.float32)).astype(jnp.bfloat16)
-        v = jnp.concatenate([high, low], axis=0)
         tops, totals, fades = [], [], []
+        rows.append((tops, totals, fades))
         for tile in range(groups * tokens // SPAN):
             lanes = slice(tile * SPAN, (tile + 1) * SPAN)
             top = None
@@ -210,6 +206,16 @@
                 total = total + fades[tile] * stats_in[u, 1:2, lanes]
             tops.append(top)
             totals.append(total)
+    for u in range(per_step):
+        g = step * per_step + u
+        cols = pl.ds(pl.multiple_of(g * HEAD_WIDTH, HEAD_WIDTH), HEAD_WIDTH)
+        tops, totals, fades = rows[u]
+        v = jnp.concatenate([value_ref[:, cols] for _, value_ref in pieces], axis=0)
+        v = jnp.transpose(v).astype(jnp.float32)
+        v = v * value_scale_ref[u, :, begin * tokens : (begin + count) * tokens]
+        high = v.astype(jnp.bfloat16)
+        low = (v - high.astype(jnp.float32)).astype(jnp.bfloat16)
+        v = jnp.concatenate([high, low], axis=0)
         both = jnp.dot(v, p_ref[u], preferred_element_type=jnp.float32)
         for tile in range(groups * tokens // SPAN):
             lanes = slice(tile * SPAN, (tile + 1) * SPAN)
@@ -240,7 +246,7 @@
     kv_heads, _, rows = prepared[0].shape
     groups = rows // tokens
     count = len(pieces)
-    per_step = 2 if kv_heads % 2 == 0 else 1
+    per_step = 4 if kv_heads % 4 == 0 else 1
     keys = tokens * count
     width = kv_heads * groups * HEAD_WIDTH
     first = state is None
@@ -296,7 +302,7 @@
             pltpu.VMEM((per_step, keys, rows), jnp.bfloat16),
             pltpu.VMEM((kv_heads * groups, tokens), jnp.float32),
         ],
-        compiler_params=pltpu.CompilerParams(vmem_limit_bytes=32 * 1024 * 1024),
+        compiler_params=pltpu.CompilerParams(vmem_limit_bytes=40 * 1024 * 1024),
         cost_estimate=pl.CostEstimate(
             flops=16 * tokens * width * keys,
             bytes_accessed=16 * tokens * width,
@@ -373,9 +379,14 @@
             if ready:
                 state = absorb((*prepared, *rows), now, done, state, False, tokens)
                 done += ready
-        sent, crossed, scales, prepared, rows, state = lax.optimization_barrier(
-            (sent, crossed, scales, prepared, rows, state)
-        )
+        if step == size // 2 - 1:
+            crossed, sent, scales, prepared, rows, state = lax.optimization_barrier(
+                (crossed, sent, scales, prepared, rows, state)
+            )
+        else:
+            sent, crossed, scales, prepared, rows, state = lax.optimization_barrier(
+                (sent, crossed, scales, prepared, rows, state)
+            )
         fresh = sent
         if step < size // 2:
             forward, backward = fresh[0][0], fresh[1][0]

time: 44.5 us -> 43.5 us (0.978)
  Pallas kernels: 15.1 us -> 13.1 us
  waiting for transfers between devices: 8.19 us -> 9.55 us
  starting transfers between devices: 16 us -> 15.5 us
    pallas_call x3, Pallas kernels: 12.5 us -> 10.5 us  [absorb(): pl.pallas_call(functools.partial(absorb_kernel, groups=groups, tokens=tok...]
    ppermute x8, waiting for transfers between devices: 1.37 us -> 2.74 us  [around(): return lax.ppermute(block, ('ctx', 'head'), route)]
    ppermute x9, starting transfers between devices: 2.1 us -> 1.6 us  [to_other_core(): lax.ppermute(block, 'ctx', [(i, i ^ 1) for i in range(ctx_size)])]
  transfers between devices with their start and end apart: 19 -> 19, of which waited for: 6 -> 6; matrix products, arithmetic and copies ran while one was open for 2% -> 2% of each run, Pallas kernels for 26% -> 24%
where the time goes in v10:
time: 43.5 us; the launch traced here: 43.2 us
  starting transfers between devices  15.5 us (36%)
  Pallas kernels  13.1 us (30%)
  waiting for transfers between devices  9.55 us (22%)
  local copies, waits for them, and re-layouts  2.59 us (6%)
  other arithmetic  1.7 us (4%)
  between operations  0.74 us (2%)
    pallas_call x3, Pallas kernels, absorb(): pl.pallas_call(functools.partial(absorb_kernel, groups=groups, tokens=tok...  10.5 us
    ppermute x8, starting transfers between devices, around(): return lax.ppermute(block, ('ctx', 'head'), route)  9.32 us
    ppermute x2, waiting for transfers between devices, swap_heads(): lax.ppermute(block, 'head', [(i, i ^ flip) for i in range(head_size)])  5.78 us
    ppermute x2, starting transfers between devices, swap_heads(): lax.ppermute(block, 'head', [(i, i ^ flip) for i in range(head_size)])  4.61 us
    ppermute x8, waiting for transfers between devices, around(): return lax.ppermute(block, ('ctx', 'head'), route)  2.74 us
    unnamed x6, local copies, waits for them, and re-layouts  2.57 us
    ppermute x9, starting transfers between devices, to_other_core(): lax.ppermute(block, 'ctx', [(i, i ^ 1) for i in range(ctx_size)])  1.6 us
    pallas_call x1, Pallas kernels, prepare(): pl.pallas_call(functools.partial(prepare_kernel, groups=groups, per_step=...  1.54 us
  transfers between devices with their start and end apart: 19, of which 6 were waited for; matrix products, arithmetic and copies ran while one was open for 2% of the time, Pallas kernels for 24%

profile of v10, /device:TPU:0, one launch (start us, length us, event | category | flops | bytes accessed | tf_op | source)
XLA Modules:
  0.0 43.2 jit_solution(12032583757425830519)
XLA Ops:
  0.6 1.0 %pad_maximum_fusion.refs_0_.refs_1_ = bf16[128,1024]{1,0:T(8,128)(2,1)S(1)} fusion(bf16[64,1024]{1,0:T(8,128)(2,1)} %param.9, bf16[64,1024]{1,0:T(8,128)(2,1)} %param.8), kind=kLoop, calls=%fused_computation | loop fusion | flops 524288 | bytes 524288 | tf_op jit(solution)/shard_map/concatenate | solution.py:352
  1.6 3.1 %collective-permute-start = (bf16[128,1024]{1,0:T(8,128)(2,1)S(1)}, bf16[128,1024]{1,0:T(8,128)(2,1)S(1)}, u32[]{:S(2)}, u32[]{:S(2)}) collective-permute-start(bf16[128,1024]{1,0:T(8,128)(2,1)S(1)} %pad_maximum_fusion.refs_0_.refs_1_), channel_id=1, source_target_pairs={{0,2},{8,10},{2,4},{10,12},{4,6},{12,14},{6,22},{14,30},{22,20},{3... | collective-permute-start | bytes 786440 | tf_op jit(solution)/shard_map/ppermute | solution.py:331
  4.7 0.0 collective-permute-start.1
  4.7 0.0 collective-permute-start.2
  4.7 0.7 %maximum_bitcast_fusion.refs_0_ = f32[1,4,8]{2,1,0:T(4,128)S(1)} fusion(f32[2,8]{1,0:T(2,128)} %bitcast.4, f32[2,8]{1,0:T(2,128)} %bitcast.5), kind=kLoop, calls=%fused_computation.2 | loop fusion | flops 32 | bytes 256 | tf_op jit(solution)/shard_map/broadcast_in_dim | solution.py:354
  5.4 2.0 %collective-permute-start.3 = (f32[1,4,8]{2,1,0:T(4,128)S(1)}, f32[1,4,8]{2,1,0:T(4,128)S(1)}, u32[]{:S(2)}, u32[]{:S(2)}) collective-permute-start(f32[1,4,8]{2,1,0:T(4,128)S(1)} %maximum_bitcast_fusion.refs_0_), channel_id=1, source_target_pairs={{0,2},{2,0},{4,6},{6,4},{1,3},{3,1},{5,7},{7,5},{8,10},{10,8},{12,... | collective-permute-start | bytes 392 | tf_op jit(solution)/shard_map/ppermute | solution.py:337
  7.4 1.2 %copy-done = bf16[64,8192]{1,0:T(8,128)(2,1)S(1)} copy-done((bf16[64,8192]{1,0:T(8,128)(2,1)S(1)}, bf16[64,8192]{1,0:T(8,128)(2,1)}, u32[]{:S(2)}) %copy-start) | copy-done | bytes 1048600
  8.7 0.7 %copy-done.1 = s32[8,8]{1,0:T(8,128)S(1)} copy-done((s32[8,8]{1,0:T(8,128)S(1)}, s32[8,8]{1,0:T(8,128)}, u32[]{:S(2)}) %copy-start.1) | copy-done | bytes 280
  9.3 0.7 %copy-done.2 = s32[8]{0:T(128)S(1)} copy-done((s32[8]{0:T(128)S(1)}, s32[8]{0:T(128)}, u32[]{:S(2)}) %copy-start.2) | copy-done | bytes 56
  10.0 1.5 %shard_map.86 = (bf16[8,128,512]{2,1,0:T(8,128)(2,1)S(1)}, bf16[128,512]{1,0:T(8,128)(2,1)S(1)}, bf16[1024,128]{1,0:T(8,128)(2,1)S(1)}) custom-call(s32[8]{0:T(128)S(1)} %copy-done.2, s32[8,8]{1,0:T(8,128)S(1)} %copy-done.1, bf16[64,8192]{1,0:T(8,128)(2,1)S(1)} %copy-done), custom_call_target="tpu_custom_call" | custom-call | flops 4194304 | bytes 8388608 | tf_op jit(solution)/shard_map/pallas_call | solution.py:65
  11.5 1.0 %collective-permute-done.3.refs_1_ = f32[1,4,8]{2,1,0:T(4,128)S(1)} collective-permute-done((f32[1,4,8]{2,1,0:T(4,128)S(1)}, f32[1,4,8]{2,1,0:T(4,128)S(1)}, u32[]{:S(2)}, u32[]{:S(2)}) %collective-permute-start.3) | collective-permute-done | bytes 160 | tf_op jit(solution)/shard_map/ppermute | solution.py:337
  12.5 0.0 collective-permute-done.refs_2_.refs_3_
  12.5 0.0 collective-permute-done.1.refs_4_.refs_5_
  12.5 0.0 collective-permute-done.2.refs_6_.refs_7_
  12.5 1.5 %collective-permute-start.4 = (bf16[128,1024]{1,0:T(8,128)(2,1)S(1)}, bf16[128,1024]{1,0:T(8,128)(2,1)S(1)}, u32[]{:S(2)}, u32[]{:S(2)}) collective-permute-start(bf16[128,1024]{1,0:T(8,128)(2,1)S(1)} %collective-permute-done.refs_2_.refs_3_), channel_id=1, source_target_pairs={{0,2},{8,10},{2,4},{10,12},{4,6},{12,14},{6,22},{14,30},{22,20},{3... | collective-permute-start | bytes 786440 | tf_op jit(solution)/shard_map/ppermute | solution.py:331
  14.0 0.6 %collective-permute-start.5 = (bf16[128,1024]{1,0:T(8,128)(2,1)S(1)}, bf16[128,1024]{1,0:T(8,128)(2,1)S(1)}, u32[]{:S(2)}, u32[]{:S(2)}) collective-permute-start(bf16[128,1024]{1,0:T(8,128)(2,1)S(1)} %collective-permute-done.1.refs_4_.refs_5_), channel_id=1, source_target_pairs={{0,16},{8,24},{2,0},{10,8},{4,2},{12,10},{6,4},{14,12},{22,6},{30,... | collective-permute-start | bytes 786440 | tf_op jit(solution)/shard_map/ppermute | solution.py:331
  14.6 0.0 collective-permute-start.6
  14.6 0.5 %collective-permute-start.7 = (bf16[128,1024]{1,0:T(8,128)(2,1)S(1)}, bf16[128,1024]{1,0:T(8,128)(2,1)S(1)}, u32[]{:S(2)}, u32[]{:S(2)}) collective-permute-start(bf16[128,1024]{1,0:T(8,128)(2,1)S(1)} %collective-permute-done.1.refs_4_.refs_5_), channel_id=1, source_target_pairs={{0,8},{8,0},{16,24},{24,16},{1,9},{9,1},{17,25},{25,17},{2,10},{10... | collective-permute-start | bytes 786440 | tf_op jit(solution)/shard_map/ppermute | solution.py:334
  15.1 2.6 %collective-permute-start.8 = (f32[2,4,8]{2,1,0:T(4,128)S(1)}, f32[2,4,8]{2,1,0:T(4,128)S(1)}, u32[]{:S(2)}, u32[]{:S(2)}) collective-permute-start(f32[2,4,8]{2,1,0:T(4,128)S(1)} %pad_maximum_fusion.1), channel_id=1, source_target_pairs={{0,4},{2,6},{4,0},{6,2},{1,5},{3,7},{5,1},{7,3},{8,12},{10,14},{12... | collective-permute-start | bytes 776 | tf_op jit(solution)/shard_map/ppermute | solution.py:337
  17.7 4.8 %collective-permute-done.8.refs_2_ = f32[2,4,8]{2,1,0:T(4,128)S(1)} collective-permute-done((f32[2,4,8]{2,1,0:T(4,128)S(1)}, f32[2,4,8]{2,1,0:T(4,128)S(1)}, u32[]{:S(2)}, u32[]{:S(2)}) %collective-permute-start.8) | collective-permute-done | bytes 288 | tf_op jit(solution)/shard_map/ppermute | solution.py:337
  22.5 0.0 collective-permute-done.4.refs_8_.refs_9_
  22.5 0.0 collective-permute-done.5.refs_10_.refs_11_
  22.5 0.0 collective-permute-done.6.refs_12_.refs_13_
  22.5 0.0 collective-permute-done.7.refs_14_.refs_15_
  22.5 0.1 collective-permute-start.10
  22.6 0.1 collective-permute-start.12
  22.7 2.0 %collective-permute-start.11 = (bf16[128,1024]{1,0:T(8,128)(2,1)S(1)}, bf16[128,1024]{1,0:T(8,128)(2,1)S(1)}, u32[]{:S(2)}, u32[]{:S(2)}) collective-permute-start(bf16[128,1024]{1,0:T(8,128)(2,1)S(1)} %collective-permute-done.4.refs_8_.refs_9_), channel_id=1, source_target_pairs={{0,2},{8,10},{2,4},{10,12},{4,6},{12,14},{6,22},{14,30},{22,20},{3... | collective-permute-start | bytes 786440 | tf_op jit(solution)/shard_map/ppermute | solution.py:331
  24.7 0.0 collective-permute-start.9
  24.7 1.1 %shard_map.87 = (f32[8,16,128]{2,1,0:T(8,128)S(1)}, f32[8,1,1024]{2,1,0:T(1,128)S(1)}) custom-call(f32[1,4,8]{2,1,0:T(4,128)S(1)} %maximum_bitcast_fusion.refs_0_, f32[1,4,8]{2,1,0:T(4,128)S(1)} %collective-permute-done.3.refs_1_, f32[2,4,8]{2,1,0:T(4,128)S(1)} %collective-permute-done.8.refs_2_), custom_call_target="tpu_custom_call" | custom-call | flops 100000000 | bytes 1000000 | tf_op jit(solution)/shard_map/pallas_call | solution.py:133
  25.8 4.3 %shard_map.88 = (f32[8,128,512]{2,1,0:T(8,128)S(1)}, f32[8,2,512]{2,1,0:T(2,128)S(1)}) custom-call(bf16[128,1024]{1,0:T(8,128)(2,1)S(1)} %pad_maximum_fusion.refs_0_.refs_1_, bf16[128,1024]{1,0:T(8,128)(2,1)S(1)} %pad_maximum_fusion.refs_0_.refs_1_, bf16[128,1024]{1,0:T(8,128)(2,1)S(1)} %collective-permute-done.refs_2_.refs_3_, ...), custom_call_target="tpu_custom_call" | custom-call | flops 4294967296 | bytes 8388608 | tf_op jit(solution)/shard_map/pallas_call | solution.py:285
  30.1 0.0 collective-permute-done.10.refs_6_.refs_7_
  30.1 1.3 %collective-permute-done.11.refs_0_.refs_1_ = bf16[128,1024]{1,0:T(8,128)(2,1)S(1)} collective-permute-done((bf16[128,1024]{1,0:T(8,128)(2,1)S(1)}, bf16[128,1024]{1,0:T(8,128)(2,1)S(1)}, u32[]{:S(2)}, u32[]{:S(2)}) %collective-permute-start.11) | collective-permute-done | bytes 262176 | tf_op jit(solution)/shard_map/ppermute | solution.py:331
  31.3 0.0 collective-permute-done.12.refs_2_.refs_3_
  31.3 0.0 collective-permute-done.9.refs_4_.refs_5_
  31.3 0.0 collective-permute-start.15
  31.3 0.5 %collective-permute-start.16 = (bf16[128,1024]{1,0:T(8,128)(2,1)S(1)}, bf16[128,1024]{1,0:T(8,128)(2,1)S(1)}, u32[]{:S(2)}, u32[]{:S(2)}) collective-permute-start(bf16[128,1024]{1,0:T(8,128)(2,1)S(1)} %collective-permute-done.12.refs_2_.refs_3_), channel_id=1, source_target_pairs={{0,8},{8,0},{16,24},{24,16},{1,9},{9,1},{17,25},{25,17},{2,10},{10... | collective-permute-start | bytes 786440 | tf_op jit(solution)/shard_map/ppermute | solution.py:334
  31.9 1.8 %collective-permute-start.13 = (bf16[64,1024]{1,0:T(8,128)(2,1)S(1)}, bf16[64,1024]{1,0:T(8,128)(2,1)S(1)}, u32[]{:S(2)}, u32[]{:S(2)}) collective-permute-start(bf16[64,1024]{1,0:T(8,128)(2,1)S(1)} %slice.6), channel_id=1, source_target_pairs={{0,2},{8,10},{2,4},{10,12},{4,6},{12,14},{6,22},{14,30},{22,20},{3... | collective-permute-start | bytes 393224 | tf_op jit(solution)/shard_map/ppermute | solution.py:331
  33.7 0.3 collective-permute-start.14
  34.0 0.0 collective-permute-done.15.refs_8_.refs_9_
  34.0 0.0 collective-permute-done.16.refs_10_.refs_11_
  34.0 3.4 %shard_map.89 = (f32[8,128,512]{2,1,0:T(8,128)S(1)}, f32[8,2,512]{2,1,0:T(2,128)S(1)}) custom-call(bf16[128,1024]{1,0:T(8,128)(2,1)S(1)} %collective-permute-done.11.refs_0_.refs_1_, bf16[128,1024]{1,0:T(8,128)(2,1)S(1)} %collective-permute-done.11.refs_0_.refs_1_, bf16[128,1024]{1,0:T(8,128)(2,1)S(1)} %collective-permute-done.12.refs_2_.refs_3_, ...), custom_call_target="tpu_custom_call" | custom-call | flops 3221225472 | bytes 8388608 | tf_op jit(solution)/shard_map/pallas_call | solution.py:285
  37.4 0.0 collective-permute-done.13.refs_0_
  37.4 1.5 %collective-permute-done.14.refs_1_ = bf16[64,1024]{1,0:T(8,128)(2,1)S(1)} collective-permute-done((bf16[64,1024]{1,0:T(8,128)(2,1)S(1)}, bf16[64,1024]{1,0:T(8,128)(2,1)S(1)}, u32[]{:S(2)}, u32[]{:S(2)}) %collective-permute-start.14) | collective-permute-done | bytes 131104 | tf_op jit(solution)/shard_map/ppermute | solution.py:331
  38.9 0.0 collective-permute-start.17
  38.9 0.5 %collective-permute-start.18 = (bf16[64,1024]{1,0:T(8,128)(2,1)S(1)}, bf16[64,1024]{1,0:T(8,128)(2,1)S(1)}, u32[]{:S(2)}, u32[]{:S(2)}) collective-permute-start(bf16[64,1024]{1,0:T(8,128)(2,1)S(1)} %collective-permute-done.14.refs_1_), channel_id=1, source_target_pairs={{0,8},{8,0},{16,24},{24,16},{1,9},{9,1},{17,25},{25,17},{2,10},{10... | collective-permute-start | bytes 393224 | tf_op jit(solution)/shard_map/ppermute | solution.py:334
  39.4 0.8 %collective-permute-done.17.refs_2_ = bf16[64,1024]{1,0:T(8,128)(2,1)S(1)} collective-permute-done((bf16[64,1024]{1,0:T(8,128)(2,1)S(1)}, bf16[64,1024]{1,0:T(8,128)(2,1)S(1)}, u32[]{:S(2)}, u32[]{:S(2)}) %collective-permute-start.17) | collective-permute-done | bytes 131104 | tf_op jit(solution)/shard_map/ppermute | solution.py:334
  40.2 0.2 collective-permute-done.18.refs_3_
  40.4 2.8 %shard_map.90 = (bf16[64,8192]{1,0:T(8,128)(2,1)}, f32[64,64]{1,0:T(8,128)}) custom-call(bf16[64,1024]{1,0:T(8,128)(2,1)S(1)} %collective-permute-done.13.refs_0_, bf16[64,1024]{1,0:T(8,128)(2,1)S(1)} %collective-permute-done.14.refs_1_, bf16[64,1024]{1,0:T(8,128)(2,1)S(1)} %collective-permute-done.17.refs_2_, ...), custom_call_target="tpu_custom_call" | custom-call | flops 1073741824 | bytes 8388608 | tf_op jit(solution)/shard_map/pallas_call | solution.py:285
  (6 shorter events, 0.0 us)
Async XLA Ops:
  1.6 10.9 %collective-permute-start = (bf16[128,1024]{1,0:T(8,128)(2,1)S(1)}, bf16[128,1024]{1,0:T(8,128)(2,1)S(1)}, u32[]{:S(2)}, u32[]{:S(2)}) collective-permute-start(bf16[128,1024]{1,0:T(8,128)(2,1)S(1)} %pad_maximum_fusion.refs_0_.refs_1_), channel_id=1, source_target_pairs={{0,2},{8,10},{2,4},{10,12},{4,6},{12,14},{6,22},{14,30},{22,20},{3... | collective-permute-start | bytes 786440 | tf_op jit(solution)/shard_map/ppermute | solution.py:331
  4.7 7.8 %collective-permute-start.1 = (bf16[128,1024]{1,0:T(8,128)(2,1)S(1)}, bf16[128,1024]{1,0:T(8,128)(2,1)S(1)}, u32[]{:S(2)}, u32[]{:S(2)}) collective-permute-start(bf16[128,1024]{1,0:T(8,128)(2,1)S(1)} %pad_maximum_fusion.refs_0_.refs_1_), channel_id=1, source_target_pairs={{0,16},{8,24},{2,0},{10,8},{4,2},{12,10},{6,4},{14,12},{22,6},{30,... | collective-permute-start | bytes 786440 | tf_op jit(solution)/shard_map/ppermute | solution.py:331
  4.7 7.8 %collective-permute-start.2 = (bf16[128,1024]{1,0:T(8,128)(2,1)S(1)}, bf16[128,1024]{1,0:T(8,128)(2,1)S(1)}, u32[]{:S(2)}, u32[]{:S(2)}) collective-permute-start(bf16[128,1024]{1,0:T(8,128)(2,1)S(1)} %pad_maximum_fusion.refs_0_.refs_1_), channel_id=1, source_target_pairs={{0,8},{8,0},{16,24},{24,16},{1,9},{9,1},{17,25},{25,17},{2,10},{10... | collective-permute-start | bytes 786440 | tf_op jit(solution)/shard_map/ppermute | solution.py:334
  5.4 7.1 %collective-permute-start.3 = (f32[1,4,8]{2,1,0:T(4,128)S(1)}, f32[1,4,8]{2,1,0:T(4,128)S(1)}, u32[]{:S(2)}, u32[]{:S(2)}) collective-permute-start(f32[1,4,8]{2,1,0:T(4,128)S(1)} %maximum_bitcast_fusion.refs_0_), channel_id=1, source_target_pairs={{0,2},{2,0},{4,6},{6,4},{1,3},{3,1},{5,7},{7,5},{8,10},{10,8},{12,... | collective-permute-start | bytes 392 | tf_op jit(solution)/shard_map/ppermute | solution.py:337
  7.4 1.2 %copy-start = (bf16[64,8192]{1,0:T(8,128)(2,1)S(1)}, bf16[64,8192]{1,0:T(8,128)(2,1)}, u32[]{:S(2)}) copy-start(bf16[64,8192]{1,0:T(8,128)(2,1)} %q_ref.1) | copy-start | bytes 3145732
  8.7 0.7 %copy-start.1 = (s32[8,8]{1,0:T(8,128)S(1)}, s32[8,8]{1,0:T(8,128)}, u32[]{:S(2)}) copy-start(s32[8,8]{1,0:T(8,128)} %keep_ref.1) | copy-start | bytes 772
  9.3 0.7 %copy-start.2 = (s32[8]{0:T(128)S(1)}, s32[8]{0:T(128)}, u32[]{:S(2)}) copy-start(s32[8]{0:T(128)} %order_ref.1) | copy-start | bytes 100
  12.5 10.0 %collective-permute-start.4 = (bf16[128,1024]{1,0:T(8,128)(2,1)S(1)}, bf16[128,1024]{1,0:T(8,128)(2,1)S(1)}, u32[]{:S(2)}, u32[]{:S(2)}) collective-permute-start(bf16[128,1024]{1,0:T(8,128)(2,1)S(1)} %collective-permute-done.refs_2_.refs_3_), channel_id=1, source_target_pairs={{0,2},{8,10},{2,4},{10,12},{4,6},{12,14},{6,22},{14,30},{22,20},{3... | collective-permute-start | bytes 786440 | tf_op jit(solution)/shard_map/ppermute | solution.py:331
  14.0 8.5 %collective-permute-start.5 = (bf16[128,1024]{1,0:T(8,128)(2,1)S(1)}, bf16[128,1024]{1,0:T(8,128)(2,1)S(1)}, u32[]{:S(2)}, u32[]{:S(2)}) collective-permute-start(bf16[128,1024]{1,0:T(8,128)(2,1)S(1)} %collective-permute-done.1.refs_4_.refs_5_), channel_id=1, source_target_pairs={{0,16},{8,24},{2,0},{10,8},{4,2},{12,10},{6,4},{14,12},{22,6},{30,... | collective-permute-start | bytes 786440 | tf_op jit(solution)/shard_map/ppermute | solution.py:331
  14.6 7.9 %collective-permute-start.6 = (bf16[128,1024]{1,0:T(8,128)(2,1)S(1)}, bf16[128,1024]{1,0:T(8,128)(2,1)S(1)}, u32[]{:S(2)}, u32[]{:S(2)}) collective-permute-start(bf16[128,1024]{1,0:T(8,128)(2,1)S(1)} %collective-permute-done.refs_2_.refs_3_), channel_id=1, source_target_pairs={{0,8},{8,0},{16,24},{24,16},{1,9},{9,1},{17,25},{25,17},{2,10},{10... | collective-permute-start | bytes 786440 | tf_op jit(solution)/shard_map/ppermute | solution.py:334
  14.6 7.9 %collective-permute-start.7 = (bf16[128,1024]{1,0:T(8,128)(2,1)S(1)}, bf16[128,1024]{1,0:T(8,128)(2,1)S(1)}, u32[]{:S(2)}, u32[]{:S(2)}) collective-permute-start(bf16[128,1024]{1,0:T(8,128)(2,1)S(1)} %collective-permute-done.1.refs_4_.refs_5_), channel_id=1, source_target_pairs={{0,8},{8,0},{16,24},{24,16},{1,9},{9,1},{17,25},{25,17},{2,10},{10... | collective-permute-start | bytes 786440 | tf_op jit(solution)/shard_map/ppermute | solution.py:334
  15.1 7.4 %collective-permute-start.8 = (f32[2,4,8]{2,1,0:T(4,128)S(1)}, f32[2,4,8]{2,1,0:T(4,128)S(1)}, u32[]{:S(2)}, u32[]{:S(2)}) collective-permute-start(f32[2,4,8]{2,1,0:T(4,128)S(1)} %pad_maximum_fusion.1), channel_id=1, source_target_pairs={{0,4},{2,6},{4,0},{6,2},{1,5},{3,7},{5,1},{7,3},{8,12},{10,14},{12... | collective-permute-start | bytes 776 | tf_op jit(solution)/shard_map/ppermute | solution.py:337
  22.5 7.5 %collective-permute-start.10 = (bf16[128,1024]{1,0:T(8,128)(2,1)S(1)}, bf16[128,1024]{1,0:T(8,128)(2,1)S(1)}, u32[]{:S(2)}, u32[]{:S(2)}) collective-permute-start(bf16[128,1024]{1,0:T(8,128)(2,1)S(1)} %collective-permute-done.5.refs_10_.refs_11_), channel_id=1, source_target_pairs={{0,8},{8,0},{16,24},{24,16},{1,9},{9,1},{17,25},{25,17},{2,10},{10... | collective-permute-start | bytes 786440 | tf_op jit(solution)/shard_map/ppermute | solution.py:334
  22.6 8.7 %collective-permute-start.12 = (bf16[128,1024]{1,0:T(8,128)(2,1)S(1)}, bf16[128,1024]{1,0:T(8,128)(2,1)S(1)}, u32[]{:S(2)}, u32[]{:S(2)}) collective-permute-start(bf16[128,1024]{1,0:T(8,128)(2,1)S(1)} %collective-permute-done.5.refs_10_.refs_11_), channel_id=1, source_target_pairs={{0,16},{8,24},{2,0},{10,8},{4,2},{12,10},{6,4},{14,12},{22,6},{30,... | collective-permute-start | bytes 786440 | tf_op jit(solution)/shard_map/ppermute | solution.py:331
  22.7 8.6 %collective-permute-start.11 = (bf16[128,1024]{1,0:T(8,128)(2,1)S(1)}, bf16[128,1024]{1,0:T(8,128)(2,1)S(1)}, u32[]{:S(2)}, u32[]{:S(2)}) collective-permute-start(bf16[128,1024]{1,0:T(8,128)(2,1)S(1)} %collective-permute-done.4.refs_8_.refs_9_), channel_id=1, source_target_pairs={{0,2},{8,10},{2,4},{10,12},{4,6},{12,14},{6,22},{14,30},{22,20},{3... | collective-permute-start | bytes 786440 | tf_op jit(solution)/shard_map/ppermute | solution.py:331
  24.7 6.6 %collective-permute-start.9 = (bf16[128,1024]{1,0:T(8,128)(2,1)S(1)}, bf16[128,1024]{1,0:T(8,128)(2,1)S(1)}, u32[]{:S(2)}, u32[]{:S(2)}) collective-permute-start(bf16[128,1024]{1,0:T(8,128)(2,1)S(1)} %collective-permute-done.4.refs_8_.refs_9_), channel_id=1, source_target_pairs={{0,8},{8,0},{16,24},{24,16},{1,9},{9,1},{17,25},{25,17},{2,10},{10... | collective-permute-start | bytes 786440 | tf_op jit(solution)/shard_map/ppermute | solution.py:334
  31.3 2.6 %collective-permute-start.15 = (bf16[128,1024]{1,0:T(8,128)(2,1)S(1)}, bf16[128,1024]{1,0:T(8,128)(2,1)S(1)}, u32[]{:S(2)}, u32[]{:S(2)}) collective-permute-start(bf16[128,1024]{1,0:T(8,128)(2,1)S(1)} %collective-permute-done.11.refs_0_.refs_1_), channel_id=1, source_target_pairs={{0,8},{8,0},{16,24},{24,16},{1,9},{9,1},{17,25},{25,17},{2,10},{10... | collective-permute-start | bytes 786440 | tf_op jit(solution)/shard_map/ppermute | solution.py:334
  31.3 2.6 %collective-permute-start.16 = (bf16[128,1024]{1,0:T(8,128)(2,1)S(1)}, bf16[128,1024]{1,0:T(8,128)(2,1)S(1)}, u32[]{:S(2)}, u32[]{:S(2)}) collective-permute-start(bf16[128,1024]{1,0:T(8,128)(2,1)S(1)} %collective-permute-done.12.refs_2_.refs_3_), channel_id=1, source_target_pairs={{0,8},{8,0},{16,24},{24,16},{1,9},{9,1},{17,25},{25,17},{2,10},{10... | collective-permute-start | bytes 786440 | tf_op jit(solution)/shard_map/ppermute | solution.py:334
  31.9 5.5 %collective-permute-start.13 = (bf16[64,1024]{1,0:T(8,128)(2,1)S(1)}, bf16[64,1024]{1,0:T(8,128)(2,1)S(1)}, u32[]{:S(2)}, u32[]{:S(2)}) collective-permute-start(bf16[64,1024]{1,0:T(8,128)(2,1)S(1)} %slice.6), channel_id=1, source_target_pairs={{0,2},{8,10},{2,4},{10,12},{4,6},{12,14},{6,22},{14,30},{22,20},{3... | collective-permute-start | bytes 393224 | tf_op jit(solution)/shard_map/ppermute | solution.py:331
  33.7 5.2 %collective-permute-start.14 = (bf16[64,1024]{1,0:T(8,128)(2,1)S(1)}, bf16[64,1024]{1,0:T(8,128)(2,1)S(1)}, u32[]{:S(2)}, u32[]{:S(2)}) collective-permute-start(bf16[64,1024]{1,0:T(8,128)(2,1)S(1)} %slice.7), channel_id=1, source_target_pairs={{0,16},{8,24},{2,0},{10,8},{4,2},{12,10},{6,4},{14,12},{22,6},{30,... | collective-permute-start | bytes 393224 | tf_op jit(solution)/shard_map/ppermute | solution.py:331
  38.9 1.3 %collective-permute-start.17 = (bf16[64,1024]{1,0:T(8,128)(2,1)S(1)}, bf16[64,1024]{1,0:T(8,128)(2,1)S(1)}, u32[]{:S(2)}, u32[]{:S(2)}) collective-permute-start(bf16[64,1024]{1,0:T(8,128)(2,1)S(1)} %collective-permute-done.13.refs_0_), channel_id=1, source_target_pairs={{0,8},{8,0},{16,24},{24,16},{1,9},{9,1},{17,25},{25,17},{2,10},{10... | collective-permute-start | bytes 393224 | tf_op jit(solution)/shard_map/ppermute | solution.py:334
  38.9 1.5 %collective-permute-start.18 = (bf16[64,1024]{1,0:T(8,128)(2,1)S(1)}, bf16[64,1024]{1,0:T(8,128)(2,1)S(1)}, u32[]{:S(2)}, u32[]{:S(2)}) collective-permute-start(bf16[64,1024]{1,0:T(8,128)(2,1)S(1)} %collective-permute-done.14.refs_1_), channel_id=1, source_target_pairs={{0,8},{8,0},{16,24},{24,16},{1,9},{9,1},{17,25},{25,17},{2,10},{10... | collective-permute-start | bytes 393224 | tf_op jit(solution)/shard_map/ppermute | solution.py:334

commit v11 on v10

--- a/solution.py
+++ b/solution.py
@@ -92,7 +92,7 @@
 
 def scale_rows_kernel(*refs, owners, tokens, kv_local, sources, ctx_size, head_size):
     scale_in = refs[: len(owners)]
-    key_scale_ref, value_scale_ref, scale_ref, scale_sem = refs[len(owners) :]
+    _, key_scale_ref, value_scale_ref, scale_ref, scale_sem = refs[len(owners) :]
     inverse_root = 1.0 / math.sqrt(HEAD_WIDTH)
     head = lax.axis_index("head")
     copies, flip = [], 0
@@ -127,7 +127,7 @@
             value_scale_ref[g, :, tile * SPAN : (tile + 1) * SPAN] = row
 
 
-def scale_rows(scales, sources, tokens, sizes):
+def scale_rows(scales, gate, sources, tokens, sizes):
     kv_local = scales[0].shape[1] // 2
     kv_heads = sizes[1] * kv_local
     return pl.pallas_call(
@@ -140,7 +140,7 @@
             ctx_size=sizes[0],
             head_size=sizes[1],
         ),
-        in_specs=[pl.BlockSpec(memory_space=pl.ANY)] * len(scales),
+        in_specs=[pl.BlockSpec(memory_space=pl.ANY)] * (len(scales) + 1),
         out_specs=[pl.BlockSpec(memory_space=pltpu.VMEM)] * 2,
         out_shape=[
             jax.ShapeDtypeStruct((kv_heads, len(sources), SPAN), jnp.float32),
@@ -154,7 +154,7 @@
         cost_estimate=pl.CostEstimate(
             flops=10**8, bytes_accessed=10**6, transcendentals=0
         ),
-    )(*scales)
+    )(*scales, gate)
 
 
 def absorb_kernel(*refs, groups, tokens, per_step, begin, count, first, last):
@@ -353,7 +353,7 @@
     scale = jnp.concatenate([jnp.transpose(key_scale), jnp.transpose(value_scale)], axis=0)
     scales, pieces, done = [scale[None]], [[block]], 0
     fresh, forward, backward = [[block]], block, block
-    prepared, rows, state = None, None, None
+    prepared, rows, state, gate = None, None, None, span_order
     for step in range(1, size // 2 + 2):
         crossed = [to_other_core(piece) for piece in fresh]
         sent = []
@@ -361,7 +361,7 @@
             forward, backward = around(forward, 1), around(backward, -1)
             sent = [[forward], [backward]]
         elif step == size // 2:
-            sent = [[around(forward[:tokens], 1), around(backward[tokens:], -1)]]
+            sent = [[around(halves[0], 1), around(halves[1], -1)]]
         held = sum(scale.shape[0] for scale in scales)
         complete = held == head_size
         if not complete:
@@ -370,7 +370,7 @@
             prepared = prepare(queries, span_order, block_keep, sources, kv_heads, sizes)
         if complete:
             if rows is None:
-                rows = scale_rows(scales, sources, tokens, sizes)
+                rows = scale_rows(scales, gate, sources, tokens, sizes)
             ready = (len(pieces) - done) // batch * batch if step < size // 2 else 0
             now = pieces[done : done + ready]
             if step == size // 2:
@@ -380,12 +380,17 @@
                 state = absorb((*prepared, *rows), now, done, state, False, tokens)
                 done += ready
         if step == size // 2 - 1:
+            halves = [sent[0][0][:tokens], sent[1][0][tokens:]]
+            crossed, halves, sent, prepared, rows, state = lax.optimization_barrier(
+                (crossed, halves, sent, prepared, rows, state)
+            )
+        elif sum(scale.shape[0] for scale in scales) < head_size:
             crossed, sent, scales, prepared, rows, state = lax.optimization_barrier(
                 (crossed, sent, scales, prepared, rows, state)
             )
         else:
-            sent, crossed, scales, prepared, rows, state = lax.optimization_barrier(
-                (sent, crossed, scales, prepared, rows, state)
+            crossed, sent, gate, prepared, rows, state = lax.optimization_barrier(
+                (crossed, sent, gate, prepared, rows, state)
             )
         fresh = sent
         if step < size // 2:

time: 43.5 us -> 44.1 us (1.014)
  waiting for transfers between devices: 9.55 us -> 11.1 us
  starting transfers between devices: 15.5 us -> 14.6 us
    ppermute x8, waiting for transfers between devices: 2.74 us -> 10.1 us  [around(): return lax.ppermute(block, ('ctx', 'head'), route)]
    ppermute x2, waiting for transfers between devices: 5.78 us -> 0.01 us  [swap_heads(): lax.ppermute(block, 'head', [(i, i ^ flip) for i in range(head_size)])]
    ppermute x2, starting transfers between devices: 4.61 us -> 3.78 us  [swap_heads(): lax.ppermute(block, 'head', [(i, i ^ flip) for i in range(head_size)])]
  transfers between devices with their start and end apart: 19 -> 19, of which waited for: 6 -> 8; matrix products, arithmetic and copies ran while one was open for 2% -> 2% of each run, Pallas kernels for 24% -> 24%
where the time goes in v11:
time: 44.1 us; the launch traced here: 43.8 us
  starting transfers between devices  14.6 us (33%)
  Pallas kernels  13.1 us (30%)
  waiting for transfers between devices  11.1 us (25%)
  local copies, waits for them, and re-layouts  2.58 us (6%)
  other arithmetic  1.7 us (4%)
  between operations  0.74 us (2%)
    pallas_call x3, Pallas kernels, absorb(): pl.pallas_call(functools.partial(absorb_kernel, groups=groups, tokens=tok...  10.5 us
    ppermute x8, waiting for transfers between devices, around(): return lax.ppermute(block, ('ctx', 'head'), route)  10.1 us
    ppermute x8, starting transfers between devices, around(): return lax.ppermute(block, ('ctx', 'head'), route)  9.22 us
    ppermute x2, starting transfers between devices, swap_heads(): lax.ppermute(block, 'head', [(i, i ^ flip) for i in range(head_size)])  3.78 us
    unnamed x6, local copies, waits for them, and re-layouts  2.57 us
    ppermute x9, starting transfers between devices, to_other_core(): lax.ppermute(block, 'ctx', [(i, i ^ 1) for i in range(ctx_size)])  1.58 us
    pallas_call x1, Pallas kernels, prepare(): pl.pallas_call(functools.partial(prepare_kernel, groups=groups, per_step=...  1.54 us
    pallas_call x1, Pallas kernels, scale_rows(): pl.pallas_call(functools.partial(scale_rows_kernel, owners=[scale.shape[0...  1.06 us
  transfers between devices with their start and end apart: 19, of which 8 were waited for; matrix products, arithmetic and copies ran while one was open for 2% of the time, Pallas kernels for 24%

profile of v11, /device:TPU:0, one launch (start us, length us, event | category | flops | bytes accessed | tf_op | source)
XLA Modules:
  0.0 43.8 jit_solution(13316195056353931339)
XLA Ops:
  0.6 1.0 %pad_maximum_fusion.refs_0_.refs_1_ = bf16[128,1024]{1,0:T(8,128)(2,1)S(1)} fusion(bf16[64,1024]{1,0:T(8,128)(2,1)} %param.9, bf16[64,1024]{1,0:T(8,128)(2,1)} %param.8), kind=kLoop, calls=%fused_computation | loop fusion | flops 524288 | bytes 524288 | tf_op jit(solution)/shard_map/concatenate | solution.py:352
  1.6 3.0 %collective-permute-start.2 = (bf16[128,1024]{1,0:T(8,128)(2,1)S(1)}, bf16[128,1024]{1,0:T(8,128)(2,1)S(1)}, u32[]{:S(2)}, u32[]{:S(2)}) collective-permute-start(bf16[128,1024]{1,0:T(8,128)(2,1)S(1)} %pad_maximum_fusion.refs_0_.refs_1_), channel_id=1, source_target_pairs={{0,16},{8,24},{2,0},{10,8},{4,2},{12,10},{6,4},{14,12},{22,6},{30,... | collective-permute-start | bytes 786440 | tf_op jit(solution)/shard_map/ppermute | solution.py:331
  4.6 0.1 collective-permute-start.1
  4.8 0.0 collective-permute-start
  4.8 0.7 %maximum_bitcast_fusion.refs_0_ = f32[1,4,8]{2,1,0:T(4,128)S(1)} fusion(f32[2,8]{1,0:T(2,128)} %bitcast.4, f32[2,8]{1,0:T(2,128)} %bitcast.5), kind=kLoop, calls=%fused_computation.2 | loop fusion | flops 32 | bytes 256 | tf_op jit(solution)/shard_map/broadcast_in_dim | solution.py:354
  5.5 2.0 %collective-permute-start.3 = (f32[1,4,8]{2,1,0:T(4,128)S(1)}, f32[1,4,8]{2,1,0:T(4,128)S(1)}, u32[]{:S(2)}, u32[]{:S(2)}) collective-permute-start(f32[1,4,8]{2,1,0:T(4,128)S(1)} %maximum_bitcast_fusion.refs_0_), channel_id=1, source_target_pairs={{0,2},{2,0},{4,6},{6,4},{1,3},{3,1},{5,7},{7,5},{8,10},{10,8},{12,... | collective-permute-start | bytes 392 | tf_op jit(solution)/shard_map/ppermute | solution.py:337
  7.4 1.2 %copy-done = bf16[64,8192]{1,0:T(8,128)(2,1)S(1)} copy-done((bf16[64,8192]{1,0:T(8,128)(2,1)S(1)}, bf16[64,8192]{1,0:T(8,128)(2,1)}, u32[]{:S(2)}) %copy-start) | copy-done | bytes 1048600
  8.7 0.7 %copy-done.1 = s32[8,8]{1,0:T(8,128)S(1)} copy-done((s32[8,8]{1,0:T(8,128)S(1)}, s32[8,8]{1,0:T(8,128)}, u32[]{:S(2)}) %copy-start.1) | copy-done | bytes 280
  9.3 0.7 %copy-done.2 = s32[8]{0:T(128)S(1)} copy-done((s32[8]{0:T(128)S(1)}, s32[8]{0:T(128)}, u32[]{:S(2)}) %copy-start.2) | copy-done | bytes 56
  10.0 1.5 %shard_map.86 = (bf16[8,128,512]{2,1,0:T(8,128)(2,1)S(1)}, bf16[128,512]{1,0:T(8,128)(2,1)S(1)}, bf16[1024,128]{1,0:T(8,128)(2,1)S(1)}) custom-call(s32[8]{0:T(128)S(1)} %copy-done.2, s32[8,8]{1,0:T(8,128)S(1)} %copy-done.1, bf16[64,8192]{1,0:T(8,128)(2,1)S(1)} %copy-done), custom_call_target="tpu_custom_call" | custom-call | flops 4194304 | bytes 8388608 | tf_op jit(solution)/shard_map/pallas_call | solution.py:65
  11.5 0.0 collective-permute-done.3.refs_1_
  11.6 0.0 collective-permute-done.2.refs_4_.refs_5_
  11.6 0.8 %collective-permute-done.1.refs_2_.refs_3_ = bf16[128,1024]{1,0:T(8,128)(2,1)S(1)} collective-permute-done((bf16[128,1024]{1,0:T(8,128)(2,1)S(1)}, bf16[128,1024]{1,0:T(8,128)(2,1)S(1)}, u32[]{:S(2)}, u32[]{:S(2)}) %collective-permute-start.1) | collective-permute-done | bytes 262176 | tf_op jit(solution)/shard_map/ppermute | solution.py:331
  12.4 0.0 collective-permute-done.refs_6_.refs_7_
  12.4 0.5 %collective-permute-start.6 = (bf16[128,1024]{1,0:T(8,128)(2,1)S(1)}, bf16[128,1024]{1,0:T(8,128)(2,1)S(1)}, u32[]{:S(2)}, u32[]{:S(2)}) collective-permute-start(bf16[128,1024]{1,0:T(8,128)(2,1)S(1)} %collective-permute-done.1.refs_2_.refs_3_), channel_id=1, source_target_pairs={{0,2},{8,10},{2,4},{10,12},{4,6},{12,14},{6,22},{14,30},{22,20},{3... | collective-permute-start | bytes 786440 | tf_op jit(solution)/shard_map/ppermute | solution.py:331
  12.9 0.0 collective-permute-start.4
  12.9 1.5 %collective-permute-start.7 = (bf16[128,1024]{1,0:T(8,128)(2,1)S(1)}, bf16[128,1024]{1,0:T(8,128)(2,1)S(1)}, u32[]{:S(2)}, u32[]{:S(2)}) collective-permute-start(bf16[128,1024]{1,0:T(8,128)(2,1)S(1)} %collective-permute-done.2.refs_4_.refs_5_), channel_id=1, source_target_pairs={{0,16},{8,24},{2,0},{10,8},{4,2},{12,10},{6,4},{14,12},{22,6},{30,... | collective-permute-start | bytes 786440 | tf_op jit(solution)/shard_map/ppermute | solution.py:331
  14.4 0.2 collective-permute-start.5
  14.7 1.8 %collective-permute-start.12 = (f32[2,4,8]{2,1,0:T(4,128)S(1)}, f32[2,4,8]{2,1,0:T(4,128)S(1)}, u32[]{:S(2)}, u32[]{:S(2)}) collective-permute-start(f32[2,4,8]{2,1,0:T(4,128)S(1)} %pad_maximum_fusion.1), channel_id=1, source_target_pairs={{0,4},{2,6},{4,0},{6,2},{1,5},{3,7},{5,1},{7,3},{8,12},{10,14},{12... | collective-permute-start | bytes 776 | tf_op jit(solution)/shard_map/ppermute | solution.py:337
  16.5 3.6 %collective-permute-done.6.refs_8_.refs_9_ = bf16[128,1024]{1,0:T(8,128)(2,1)S(1)} collective-permute-done((bf16[128,1024]{1,0:T(8,128)(2,1)S(1)}, bf16[128,1024]{1,0:T(8,128)(2,1)S(1)}, u32[]{:S(2)}, u32[]{:S(2)}) %collective-permute-start.6) | collective-permute-done | bytes 262176 | tf_op jit(solution)/shard_map/ppermute | solution.py:331
  20.1 0.0 collective-permute-done.4.refs_12_.refs_13_
  20.1 1.7 %collective-permute-done.7.refs_10_.refs_11_ = bf16[128,1024]{1,0:T(8,128)(2,1)S(1)} collective-permute-done((bf16[128,1024]{1,0:T(8,128)(2,1)S(1)}, bf16[128,1024]{1,0:T(8,128)(2,1)S(1)}, u32[]{:S(2)}, u32[]{:S(2)}) %collective-permute-start.7) | collective-permute-done | bytes 262176 | tf_op jit(solution)/shard_map/ppermute | solution.py:331
  21.8 0.0 collective-permute-done.5.refs_14_.refs_15_
  21.8 1.8 %collective-permute-start.10 = (bf16[128,1024]{1,0:T(8,128)(2,1)S(1)}, bf16[128,1024]{1,0:T(8,128)(2,1)S(1)}, u32[]{:S(2)}, u32[]{:S(2)}) collective-permute-start(bf16[128,1024]{1,0:T(8,128)(2,1)S(1)} %collective-permute-done.6.refs_8_.refs_9_), channel_id=1, source_target_pairs={{0,2},{8,10},{2,4},{10,12},{4,6},{12,14},{6,22},{14,30},{22,20},{3... | collective-permute-start | bytes 786440 | tf_op jit(solution)/shard_map/ppermute | solution.py:331
  23.6 0.0 collective-permute-start.8
  23.6 0.2 collective-permute-start.11
  23.8 0.3 collective-permute-start.9
  24.1 0.0 collective-permute-done.12.refs_2_
  24.1 1.1 %shard_map.87 = (f32[8,16,128]{2,1,0:T(8,128)S(1)}, f32[8,1,1024]{2,1,0:T(1,128)S(1)}) custom-call(f32[1,4,8]{2,1,0:T(4,128)S(1)} %maximum_bitcast_fusion.refs_0_, f32[1,4,8]{2,1,0:T(4,128)S(1)} %collective-permute-done.3.refs_1_, f32[2,4,8]{2,1,0:T(4,128)S(1)} %collective-permute-done.12.refs_2_, s32[8]{0:T(128)S(1)} %copy-done.2), custom_call_target="tpu_custom_call" | custom-call | flops 100000000 | bytes 1000000 | tf_op jit(solution)/shard_map/pallas_call | solution.py:133
  25.1 4.3 %shard_map.88 = (f32[8,128,512]{2,1,0:T(8,128)S(1)}, f32[8,2,512]{2,1,0:T(2,128)S(1)}) custom-call(bf16[128,1024]{1,0:T(8,128)(2,1)S(1)} %pad_maximum_fusion.refs_0_.refs_1_, bf16[128,1024]{1,0:T(8,128)(2,1)S(1)} %pad_maximum_fusion.refs_0_.refs_1_, bf16[128,1024]{1,0:T(8,128)(2,1)S(1)} %collective-permute-done.1.refs_2_.refs_3_, ...), custom_call_target="tpu_custom_call" | custom-call | flops 4294967296 | bytes 8388608 | tf_op jit(solution)/shard_map/pallas_call | solution.py:285
  29.4 0.3 collective-permute-done.10.refs_0_.refs_1_
  29.8 2.5 %collective-permute-done.11.refs_2_.refs_3_ = bf16[128,1024]{1,0:T(8,128)(2,1)S(1)} collective-permute-done((bf16[128,1024]{1,0:T(8,128)(2,1)S(1)}, bf16[128,1024]{1,0:T(8,128)(2,1)S(1)}, u32[]{:S(2)}, u32[]{:S(2)}) %collective-permute-start.11) | collective-permute-done | bytes 262176 | tf_op jit(solution)/shard_map/ppermute | solution.py:331
  32.3 0.0 collective-permute-done.8.refs_4_.refs_5_
  32.3 0.0 collective-permute-done.9.refs_6_.refs_7_
  32.3 0.1 collective-permute-start.13
  32.4 0.5 %collective-permute-start.14 = (bf16[128,1024]{1,0:T(8,128)(2,1)S(1)}, bf16[128,1024]{1,0:T(8,128)(2,1)S(1)}, u32[]{:S(2)}, u32[]{:S(2)}) collective-permute-start(bf16[128,1024]{1,0:T(8,128)(2,1)S(1)} %collective-permute-done.11.refs_2_.refs_3_), channel_id=1, source_target_pairs={{0,8},{8,0},{16,24},{24,16},{1,9},{9,1},{17,25},{25,17},{2,10},{10... | collective-permute-start | bytes 786440 | tf_op jit(solution)/shard_map/ppermute | solution.py:334
  32.9 1.4 %collective-permute-start.15 = (bf16[64,1024]{1,0:T(8,128)(2,1)S(1)}, bf16[64,1024]{1,0:T(8,128)(2,1)S(1)}, u32[]{:S(2)}, u32[]{:S(2)}) collective-permute-start(bf16[64,1024]{1,0:T(8,128)(2,1)S(1)} %slice.8), channel_id=1, source_target_pairs={{0,2},{8,10},{2,4},{10,12},{4,6},{12,14},{6,22},{14,30},{22,20},{3... | collective-permute-start | bytes 393224 | tf_op jit(solution)/shard_map/ppermute | solution.py:331
  34.3 0.6 %collective-permute-start.16 = (bf16[64,1024]{1,0:T(8,128)(2,1)S(1)}, bf16[64,1024]{1,0:T(8,128)(2,1)S(1)}, u32[]{:S(2)}, u32[]{:S(2)}) collective-permute-start(bf16[64,1024]{1,0:T(8,128)(2,1)S(1)} %slice.9), channel_id=1, source_target_pairs={{0,16},{8,24},{2,0},{10,8},{4,2},{12,10},{6,4},{14,12},{22,6},{30,... | collective-permute-start | bytes 393224 | tf_op jit(solution)/shard_map/ppermute | solution.py:331
  34.9 0.0 collective-permute-done.13.refs_8_.refs_9_
  34.9 0.0 collective-permute-done.14.refs_10_.refs_11_
  34.9 3.4 %shard_map.89 = (f32[8,128,512]{2,1,0:T(8,128)S(1)}, f32[8,2,512]{2,1,0:T(2,128)S(1)}) custom-call(bf16[128,1024]{1,0:T(8,128)(2,1)S(1)} %collective-permute-done.10.refs_0_.refs_1_, bf16[128,1024]{1,0:T(8,128)(2,1)S(1)} %collective-permute-done.10.refs_0_.refs_1_, bf16[128,1024]{1,0:T(8,128)(2,1)S(1)} %collective-permute-done.11.refs_2_.refs_3_, ...), custom_call_target="tpu_custom_call" | custom-call | flops 3221225472 | bytes 8388608 | tf_op jit(solution)/shard_map/pallas_call | solution.py:285
  38.4 0.0 collective-permute-done.15.refs_0_
  38.4 1.1 %collective-permute-done.16.refs_1_ = bf16[64,1024]{1,0:T(8,128)(2,1)S(1)} collective-permute-done((bf16[64,1024]{1,0:T(8,128)(2,1)S(1)}, bf16[64,1024]{1,0:T(8,128)(2,1)S(1)}, u32[]{:S(2)}, u32[]{:S(2)}) %collective-permute-start.16) | collective-permute-done | bytes 131104 | tf_op jit(solution)/shard_map/ppermute | solution.py:331
  39.5 0.0 collective-permute-start.17
  39.5 0.5 %collective-permute-start.18 = (bf16[64,1024]{1,0:T(8,128)(2,1)S(1)}, bf16[64,1024]{1,0:T(8,128)(2,1)S(1)}, u32[]{:S(2)}, u32[]{:S(2)}) collective-permute-start(bf16[64,1024]{1,0:T(8,128)(2,1)S(1)} %collective-permute-done.16.refs_1_), channel_id=1, source_target_pairs={{0,8},{8,0},{16,24},{24,16},{1,9},{9,1},{17,25},{25,17},{2,10},{10... | collective-permute-start | bytes 393224 | tf_op jit(solution)/shard_map/ppermute | solution.py:334
  40.0 0.8 %collective-permute-done.17.refs_2_ = bf16[64,1024]{1,0:T(8,128)(2,1)S(1)} collective-permute-done((bf16[64,1024]{1,0:T(8,128)(2,1)S(1)}, bf16[64,1024]{1,0:T(8,128)(2,1)S(1)}, u32[]{:S(2)}, u32[]{:S(2)}) %collective-permute-start.17) | collective-permute-done | bytes 131104 | tf_op jit(solution)/shard_map/ppermute | solution.py:334
  40.8 0.2 collective-permute-done.18.refs_3_
  41.0 2.8 %shard_map.90 = (bf16[64,8192]{1,0:T(8,128)(2,1)}, f32[64,64]{1,0:T(8,128)}) custom-call(bf16[64,1024]{1,0:T(8,128)(2,1)S(1)} %collective-permute-done.15.refs_0_, bf16[64,1024]{1,0:T(8,128)(2,1)S(1)} %collective-permute-done.16.refs_1_, bf16[64,1024]{1,0:T(8,128)(2,1)S(1)} %collective-permute-done.17.refs_2_, ...), custom_call_target="tpu_custom_call" | custom-call | flops 1073741824 | bytes 8388608 | tf_op jit(solution)/shard_map/pallas_call | solution.py:285
  (6 shorter events, 0.0 us)
Async XLA Ops:
  1.6 9.9 %collective-permute-start.2 = (bf16[128,1024]{1,0:T(8,128)(2,1)S(1)}, bf16[128,1024]{1,0:T(8,128)(2,1)S(1)}, u32[]{:S(2)}, u32[]{:S(2)}) collective-permute-start(bf16[128,1024]{1,0:T(8,128)(2,1)S(1)} %pad_maximum_fusion.refs_0_.refs_1_), channel_id=1, source_target_pairs={{0,16},{8,24},{2,0},{10,8},{4,2},{12,10},{6,4},{14,12},{22,6},{30,... | collective-permute-start | bytes 786440 | tf_op jit(solution)/shard_map/ppermute | solution.py:331
  4.6 7.8 %collective-permute-start.1 = (bf16[128,1024]{1,0:T(8,128)(2,1)S(1)}, bf16[128,1024]{1,0:T(8,128)(2,1)S(1)}, u32[]{:S(2)}, u32[]{:S(2)}) collective-permute-start(bf16[128,1024]{1,0:T(8,128)(2,1)S(1)} %pad_maximum_fusion.refs_0_.refs_1_), channel_id=1, source_target_pairs={{0,2},{8,10},{2,4},{10,12},{4,6},{12,14},{6,22},{14,30},{22,20},{3... | collective-permute-start | bytes 786440 | tf_op jit(solution)/shard_map/ppermute | solution.py:331
  4.8 7.6 %collective-permute-start = (bf16[128,1024]{1,0:T(8,128)(2,1)S(1)}, bf16[128,1024]{1,0:T(8,128)(2,1)S(1)}, u32[]{:S(2)}, u32[]{:S(2)}) collective-permute-start(bf16[128,1024]{1,0:T(8,128)(2,1)S(1)} %pad_maximum_fusion.refs_0_.refs_1_), channel_id=1, source_target_pairs={{0,8},{8,0},{16,24},{24,16},{1,9},{9,1},{17,25},{25,17},{2,10},{10... | collective-permute-start | bytes 786440 | tf_op jit(solution)/shard_map/ppermute | solution.py:334
  5.5 6.1 %collective-permute-start.3 = (f32[1,4,8]{2,1,0:T(4,128)S(1)}, f32[1,4,8]{2,1,0:T(4,128)S(1)}, u32[]{:S(2)}, u32[]{:S(2)}) collective-permute-start(f32[1,4,8]{2,1,0:T(4,128)S(1)} %maximum_bitcast_fusion.refs_0_), channel_id=1, source_target_pairs={{0,2},{2,0},{4,6},{6,4},{1,3},{3,1},{5,7},{7,5},{8,10},{10,8},{12,... | collective-permute-start | bytes 392 | tf_op jit(solution)/shard_map/ppermute | solution.py:337
  7.4 1.2 %copy-start = (bf16[64,8192]{1,0:T(8,128)(2,1)S(1)}, bf16[64,8192]{1,0:T(8,128)(2,1)}, u32[]{:S(2)}) copy-start(bf16[64,8192]{1,0:T(8,128)(2,1)} %q_ref.1) | copy-start | bytes 3145732
  8.7 0.7 %copy-start.1 = (s32[8,8]{1,0:T(8,128)S(1)}, s32[8,8]{1,0:T(8,128)}, u32[]{:S(2)}) copy-start(s32[8,8]{1,0:T(8,128)} %keep_ref.1) | copy-start | bytes 772
  9.3 0.7 %copy-start.2 = (s32[8]{0:T(128)S(1)}, s32[8]{0:T(128)}, u32[]{:S(2)}) copy-start(s32[8]{0:T(128)} %refs_3_) | copy-start | bytes 100
  12.4 7.7 %collective-permute-start.6 = (bf16[128,1024]{1,0:T(8,128)(2,1)S(1)}, bf16[128,1024]{1,0:T(8,128)(2,1)S(1)}, u32[]{:S(2)}, u32[]{:S(2)}) collective-permute-start(bf16[128,1024]{1,0:T(8,128)(2,1)S(1)} %collective-permute-done.1.refs_2_.refs_3_), channel_id=1, source_target_pairs={{0,2},{8,10},{2,4},{10,12},{4,6},{12,14},{6,22},{14,30},{22,20},{3... | collective-permute-start | bytes 786440 | tf_op jit(solution)/shard_map/ppermute | solution.py:331
  12.9 7.2 %collective-permute-start.4 = (bf16[128,1024]{1,0:T(8,128)(2,1)S(1)}, bf16[128,1024]{1,0:T(8,128)(2,1)S(1)}, u32[]{:S(2)}, u32[]{:S(2)}) collective-permute-start(bf16[128,1024]{1,0:T(8,128)(2,1)S(1)} %collective-permute-done.1.refs_2_.refs_3_), channel_id=1, source_target_pairs={{0,8},{8,0},{16,24},{24,16},{1,9},{9,1},{17,25},{25,17},{2,10},{10... | collective-permute-start | bytes 786440 | tf_op jit(solution)/shard_map/ppermute | solution.py:334
  12.9 8.8 %collective-permute-start.7 = (bf16[128,1024]{1,0:T(8,128)(2,1)S(1)}, bf16[128,1024]{1,0:T(8,128)(2,1)S(1)}, u32[]{:S(2)}, u32[]{:S(2)}) collective-permute-start(bf16[128,1024]{1,0:T(8,128)(2,1)S(1)} %collective-permute-done.2.refs_4_.refs_5_), channel_id=1, source_target_pairs={{0,16},{8,24},{2,0},{10,8},{4,2},{12,10},{6,4},{14,12},{22,6},{30,... | collective-permute-start | bytes 786440 | tf_op jit(solution)/shard_map/ppermute | solution.py:331
  14.4 7.3 %collective-permute-start.5 = (bf16[128,1024]{1,0:T(8,128)(2,1)S(1)}, bf16[128,1024]{1,0:T(8,128)(2,1)S(1)}, u32[]{:S(2)}, u32[]{:S(2)}) collective-permute-start(bf16[128,1024]{1,0:T(8,128)(2,1)S(1)} %collective-permute-done.2.refs_4_.refs_5_), channel_id=1, source_target_pairs={{0,8},{8,0},{16,24},{24,16},{1,9},{9,1},{17,25},{25,17},{2,10},{10... | collective-permute-start | bytes 786440 | tf_op jit(solution)/shard_map/ppermute | solution.py:334
  14.7 9.4 %collective-permute-start.12 = (f32[2,4,8]{2,1,0:T(4,128)S(1)}, f32[2,4,8]{2,1,0:T(4,128)S(1)}, u32[]{:S(2)}, u32[]{:S(2)}) collective-permute-start(f32[2,4,8]{2,1,0:T(4,128)S(1)} %pad_maximum_fusion.1), channel_id=1, source_target_pairs={{0,4},{2,6},{4,0},{6,2},{1,5},{3,7},{5,1},{7,3},{8,12},{10,14},{12... | collective-permute-start | bytes 776 | tf_op jit(solution)/shard_map/ppermute | solution.py:337
  21.8 8.0 %collective-permute-start.10 = (bf16[128,1024]{1,0:T(8,128)(2,1)S(1)}, bf16[128,1024]{1,0:T(8,128)(2,1)S(1)}, u32[]{:S(2)}, u32[]{:S(2)}) collective-permute-start(bf16[128,1024]{1,0:T(8,128)(2,1)S(1)} %collective-permute-done.6.refs_8_.refs_9_), channel_id=1, source_target_pairs={{0,2},{8,10},{2,4},{10,12},{4,6},{12,14},{6,22},{14,30},{22,20},{3... | collective-permute-start | bytes 786440 | tf_op jit(solution)/shard_map/ppermute | solution.py:331
  23.6 8.7 %collective-permute-start.8 = (bf16[128,1024]{1,0:T(8,128)(2,1)S(1)}, bf16[128,1024]{1,0:T(8,128)(2,1)S(1)}, u32[]{:S(2)}, u32[]{:S(2)}) collective-permute-start(bf16[128,1024]{1,0:T(8,128)(2,1)S(1)} %collective-permute-done.6.refs_8_.refs_9_), channel_id=1, source_target_pairs={{0,8},{8,0},{16,24},{24,16},{1,9},{9,1},{17,25},{25,17},{2,10},{10... | collective-permute-start | bytes 786440 | tf_op jit(solution)/shard_map/ppermute | solution.py:334
  23.6 8.7 %collective-permute-start.11 = (bf16[128,1024]{1,0:T(8,128)(2,1)S(1)}, bf16[128,1024]{1,0:T(8,128)(2,1)S(1)}, u32[]{:S(2)}, u32[]{:S(2)}) collective-permute-start(bf16[128,1024]{1,0:T(8,128)(2,1)S(1)} %collective-permute-done.7.refs_10_.refs_11_), channel_id=1, source_target_pairs={{0,16},{8,24},{2,0},{10,8},{4,2},{12,10},{6,4},{14,12},{22,6},{30,... | collective-permute-start | bytes 786440 | tf_op jit(solution)/shard_map/ppermute | solution.py:331
  23.8 8.5 %collective-permute-start.9 = (bf16[128,1024]{1,0:T(8,128)(2,1)S(1)}, bf16[128,1024]{1,0:T(8,128)(2,1)S(1)}, u32[]{:S(2)}, u32[]{:S(2)}) collective-permute-start(bf16[128,1024]{1,0:T(8,128)(2,1)S(1)} %collective-permute-done.7.refs_10_.refs_11_), channel_id=1, source_target_pairs={{0,8},{8,0},{16,24},{24,16},{1,9},{9,1},{17,25},{25,17},{2,10},{10... | collective-permute-start | bytes 786440 | tf_op jit(solution)/shard_map/ppermute | solution.py:334
  32.3 2.6 %collective-permute-start.13 = (bf16[128,1024]{1,0:T(8,128)(2,1)S(1)}, bf16[128,1024]{1,0:T(8,128)(2,1)S(1)}, u32[]{:S(2)}, u32[]{:S(2)}) collective-permute-start(bf16[128,1024]{1,0:T(8,128)(2,1)S(1)} %collective-permute-done.10.refs_0_.refs_1_), channel_id=1, source_target_pairs={{0,8},{8,0},{16,24},{24,16},{1,9},{9,1},{17,25},{25,17},{2,10},{10... | collective-permute-start | bytes 786440 | tf_op jit(solution)/shard_map/ppermute | solution.py:334
  32.4 2.5 %collective-permute-start.14 = (bf16[128,1024]{1,0:T(8,128)(2,1)S(1)}, bf16[128,1024]{1,0:T(8,128)(2,1)S(1)}, u32[]{:S(2)}, u32[]{:S(2)}) collective-permute-start(bf16[128,1024]{1,0:T(8,128)(2,1)S(1)} %collective-permute-done.11.refs_2_.refs_3_), channel_id=1, source_target_pairs={{0,8},{8,0},{16,24},{24,16},{1,9},{9,1},{17,25},{25,17},{2,10},{10... | collective-permute-start | bytes 786440 | tf_op jit(solution)/shard_map/ppermute | solution.py:334
  32.9 5.5 %collective-permute-start.15 = (bf16[64,1024]{1,0:T(8,128)(2,1)S(1)}, bf16[64,1024]{1,0:T(8,128)(2,1)S(1)}, u32[]{:S(2)}, u32[]{:S(2)}) collective-permute-start(bf16[64,1024]{1,0:T(8,128)(2,1)S(1)} %slice.8), channel_id=1, source_target_pairs={{0,2},{8,10},{2,4},{10,12},{4,6},{12,14},{6,22},{14,30},{22,20},{3... | collective-permute-start | bytes 393224 | tf_op jit(solution)/shard_map/ppermute | solution.py:331
  34.3 5.2 %collective-permute-start.16 = (bf16[64,1024]{1,0:T(8,128)(2,1)S(1)}, bf16[64,1024]{1,0:T(8,128)(2,1)S(1)}, u32[]{:S(2)}, u32[]{:S(2)}) collective-permute-start(bf16[64,1024]{1,0:T(8,128)(2,1)S(1)} %slice.9), channel_id=1, source_target_pairs={{0,16},{8,24},{2,0},{10,8},{4,2},{12,10},{6,4},{14,12},{22,6},{30,... | collective-permute-start | bytes 393224 | tf_op jit(solution)/shard_map/ppermute | solution.py:331
  39.5 1.3 %collective-permute-start.17 = (bf16[64,1024]{1,0:T(8,128)(2,1)S(1)}, bf16[64,1024]{1,0:T(8,128)(2,1)S(1)}, u32[]{:S(2)}, u32[]{:S(2)}) collective-permute-start(bf16[64,1024]{1,0:T(8,128)(2,1)S(1)} %collective-permute-done.15.refs_0_), channel_id=1, source_target_pairs={{0,8},{8,0},{16,24},{24,16},{1,9},{9,1},{17,25},{25,17},{2,10},{10... | collective-permute-start | bytes 393224 | tf_op jit(solution)/shard_map/ppermute | solution.py:334
  39.5 1.5 %collective-permute-start.18 = (bf16[64,1024]{1,0:T(8,128)(2,1)S(1)}, bf16[64,1024]{1,0:T(8,128)(2,1)S(1)}, u32[]{:S(2)}, u32[]{:S(2)}) collective-permute-start(bf16[64,1024]{1,0:T(8,128)(2,1)S(1)} %collective-permute-done.16.refs_1_), channel_id=1, source_target_pairs={{0,8},{8,0},{16,24},{24,16},{1,9},{9,1},{17,25},{25,17},{2,10},{10... | collective-permute-start | bytes 393224 | tf_op jit(solution)/shard_map/ppermute | solution.py:334

commit v12 on v11

--- a/solution.py
+++ b/solution.py
@@ -361,7 +361,7 @@
             forward, backward = around(forward, 1), around(backward, -1)
             sent = [[forward], [backward]]
         elif step == size // 2:
-            sent = [[around(halves[0], 1), around(halves[1], -1)]]
+            sent = [[around(forward[:tokens], 1), around(backward[tokens:], -1)]]
         held = sum(scale.shape[0] for scale in scales)
         complete = held == head_size
         if not complete:
@@ -379,18 +379,17 @@
             if ready:
                 state = absorb((*prepared, *rows), now, done, state, False, tokens)
                 done += ready
-        if step == size // 2 - 1:
-            halves = [sent[0][0][:tokens], sent[1][0][tokens:]]
-            crossed, halves, sent, prepared, rows, state = lax.optimization_barrier(
-                (crossed, halves, sent, prepared, rows, state)
+        if sum(scale.shape[0] for scale in scales) < head_size:
+            sent, crossed, scales, prepared, rows, state = lax.optimization_barrier(
+                (sent, crossed, scales, prepared, rows, state)
             )
-        elif sum(scale.shape[0] for scale in scales) < head_size:
-            crossed, sent, scales, prepared, rows, state = lax.optimization_barrier(
-                (crossed, sent, scales, prepared, rows, state)
+        elif step == size // 2 - 1:
+            crossed, sent, prepared, rows, state = lax.optimization_barrier(
+                (crossed, sent, prepared, rows, state)
             )
         else:
-            crossed, sent, gate, prepared, rows, state = lax.optimization_barrier(
-                (crossed, sent, gate, prepared, rows, state)
+            sent, crossed, gate, prepared, rows, state = lax.optimization_barrier(
+                (sent, crossed, gate, prepared, rows, state)
             )
         fresh = sent
         if step < size // 2:

time: 44.1 us -> 42.9 us (0.973)
  waiting for transfers between devices: 11.1 us -> 8.83 us
  starting transfers between devices: 14.6 us -> 15.7 us
    ppermute x8, waiting for transfers between devices: 10.1 us -> 6.82 us  [around(): return lax.ppermute(block, ('ctx', 'head'), route)]
    ppermute x2, waiting for transfers between devices: 0.01 us -> 0.97 us  [swap_heads(): lax.ppermute(block, 'head', [(i, i ^ flip) for i in range(head_size)])]
    ppermute x2, starting transfers between devices: 3.78 us -> 4.61 us  [swap_heads(): lax.ppermute(block, 'head', [(i, i ^ flip) for i in range(head_size)])]
  transfers between devices with their start and end apart: 19 -> 19, of which waited for: 8 -> 7; matrix products, arithmetic and copies ran while one was open for 2% -> 2% of each run, Pallas kernels for 24% -> 24%
where the time goes in v12:
time: 42.9 us; the launch traced here: 42.7 us
  starting transfers between devices  15.7 us (37%)
  Pallas kernels  13.1 us (31%)
  waiting for transfers between devices  8.83 us (21%)
  local copies, waits for them, and re-layouts  2.59 us (6%)
  other arithmetic  1.7 us (4%)
  between operations  0.72 us (2%)
    pallas_call x3, Pallas kernels, absorb(): pl.pallas_call(functools.partial(absorb_kernel, groups=groups, tokens=tok...  10.5 us
    ppermute x8, starting transfers between devices, around(): return lax.ppermute(block, ('ctx', 'head'), route)  9.27 us
    ppermute x8, waiting for transfers between devices, around(): return lax.ppermute(block, ('ctx', 'head'), route)  6.82 us
    ppermute x2, starting transfers between devices, swap_heads(): lax.ppermute(block, 'head', [(i, i ^ flip) for i in range(head_size)])  4.61 us
    unnamed x6, local copies, waits for them, and re-layouts  2.57 us
    ppermute x9, starting transfers between devices, to_other_core(): lax.ppermute(block, 'ctx', [(i, i ^ 1) for i in range(ctx_size)])  1.8 us
    pallas_call x1, Pallas kernels, prepare(): pl.pallas_call(functools.partial(prepare_kernel, groups=groups, per_step=...  1.54 us
    pallas_call x1, Pallas kernels, scale_rows(): pl.pallas_call(functools.partial(scale_rows_kernel, owners=[scale.shape[0...  1.06 us
  transfers between devices with their start and end apart: 19, of which 7 were waited for; matrix products, arithmetic and copies ran while one was open for 2% of the time, Pallas kernels for 24%

profile of v12, /device:TPU:0, one launch (start us, length us, event | category | flops | bytes accessed | tf_op | source)
XLA Modules:
  0.0 42.7 jit_solution(4559491005097251908)
XLA Ops:
  0.6 1.0 %pad_maximum_fusion.refs_0_.refs_1_ = bf16[128,1024]{1,0:T(8,128)(2,1)S(1)} fusion(bf16[64,1024]{1,0:T(8,128)(2,1)} %param.9, bf16[64,1024]{1,0:T(8,128)(2,1)} %param.8), kind=kLoop, calls=%fused_computation | loop fusion | flops 524288 | bytes 524288 | tf_op jit(solution)/shard_map/concatenate | solution.py:352
  1.6 3.1 %collective-permute-start = (bf16[128,1024]{1,0:T(8,128)(2,1)S(1)}, bf16[128,1024]{1,0:T(8,128)(2,1)S(1)}, u32[]{:S(2)}, u32[]{:S(2)}) collective-permute-start(bf16[128,1024]{1,0:T(8,128)(2,1)S(1)} %pad_maximum_fusion.refs_0_.refs_1_), channel_id=1, source_target_pairs={{0,2},{8,10},{2,4},{10,12},{4,6},{12,14},{6,22},{14,30},{22,20},{3... | collective-permute-start | bytes 786440 | tf_op jit(solution)/shard_map/ppermute | solution.py:331
  4.7 0.0 collective-permute-start.1
  4.7 0.0 collective-permute-start.2
  4.7 0.7 %maximum_bitcast_fusion.refs_0_ = f32[1,4,8]{2,1,0:T(4,128)S(1)} fusion(f32[2,8]{1,0:T(2,128)} %bitcast.4, f32[2,8]{1,0:T(2,128)} %bitcast.5), kind=kLoop, calls=%fused_computation.2 | loop fusion | flops 32 | bytes 256 | tf_op jit(solution)/shard_map/broadcast_in_dim | solution.py:354
  5.4 2.0 %collective-permute-start.3 = (f32[1,4,8]{2,1,0:T(4,128)S(1)}, f32[1,4,8]{2,1,0:T(4,128)S(1)}, u32[]{:S(2)}, u32[]{:S(2)}) collective-permute-start(f32[1,4,8]{2,1,0:T(4,128)S(1)} %maximum_bitcast_fusion.refs_0_), channel_id=1, source_target_pairs={{0,2},{2,0},{4,6},{6,4},{1,3},{3,1},{5,7},{7,5},{8,10},{10,8},{12,... | collective-permute-start | bytes 392 | tf_op jit(solution)/shard_map/ppermute | solution.py:337
  7.4 1.2 %copy-done = bf16[64,8192]{1,0:T(8,128)(2,1)S(1)} copy-done((bf16[64,8192]{1,0:T(8,128)(2,1)S(1)}, bf16[64,8192]{1,0:T(8,128)(2,1)}, u32[]{:S(2)}) %copy-start) | copy-done | bytes 1048600
  8.7 0.7 %copy-done.1 = s32[8,8]{1,0:T(8,128)S(1)} copy-done((s32[8,8]{1,0:T(8,128)S(1)}, s32[8,8]{1,0:T(8,128)}, u32[]{:S(2)}) %copy-start.1) | copy-done | bytes 280
  9.3 0.7 %copy-done.2 = s32[8]{0:T(128)S(1)} copy-done((s32[8]{0:T(128)S(1)}, s32[8]{0:T(128)}, u32[]{:S(2)}) %copy-start.2) | copy-done | bytes 56
  10.0 1.5 %shard_map.86 = (bf16[8,128,512]{2,1,0:T(8,128)(2,1)S(1)}, bf16[128,512]{1,0:T(8,128)(2,1)S(1)}, bf16[1024,128]{1,0:T(8,128)(2,1)S(1)}) custom-call(s32[8]{0:T(128)S(1)} %copy-done.2, s32[8,8]{1,0:T(8,128)S(1)} %copy-done.1, bf16[64,8192]{1,0:T(8,128)(2,1)S(1)} %copy-done), custom_call_target="tpu_custom_call" | custom-call | flops 4194304 | bytes 8388608 | tf_op jit(solution)/shard_map/pallas_call | solution.py:65
  11.5 1.0 %collective-permute-done.3.refs_1_ = f32[1,4,8]{2,1,0:T(4,128)S(1)} collective-permute-done((f32[1,4,8]{2,1,0:T(4,128)S(1)}, f32[1,4,8]{2,1,0:T(4,128)S(1)}, u32[]{:S(2)}, u32[]{:S(2)}) %collective-permute-start.3) | collective-permute-done | bytes 160 | tf_op jit(solution)/shard_map/ppermute | solution.py:337
  12.5 0.0 collective-permute-done.refs_2_.refs_3_
  12.5 0.0 collective-permute-done.1.refs_4_.refs_5_
  12.5 0.0 collective-permute-done.2.refs_6_.refs_7_
  12.5 1.5 %collective-permute-start.4 = (bf16[128,1024]{1,0:T(8,128)(2,1)S(1)}, bf16[128,1024]{1,0:T(8,128)(2,1)S(1)}, u32[]{:S(2)}, u32[]{:S(2)}) collective-permute-start(bf16[128,1024]{1,0:T(8,128)(2,1)S(1)} %collective-permute-done.refs_2_.refs_3_), channel_id=1, source_target_pairs={{0,2},{8,10},{2,4},{10,12},{4,6},{12,14},{6,22},{14,30},{22,20},{3... | collective-permute-start | bytes 786440 | tf_op jit(solution)/shard_map/ppermute | solution.py:331
  14.0 0.6 %collective-permute-start.5 = (bf16[128,1024]{1,0:T(8,128)(2,1)S(1)}, bf16[128,1024]{1,0:T(8,128)(2,1)S(1)}, u32[]{:S(2)}, u32[]{:S(2)}) collective-permute-start(bf16[128,1024]{1,0:T(8,128)(2,1)S(1)} %collective-permute-done.1.refs_4_.refs_5_), channel_id=1, source_target_pairs={{0,16},{8,24},{2,0},{10,8},{4,2},{12,10},{6,4},{14,12},{22,6},{30,... | collective-permute-start | bytes 786440 | tf_op jit(solution)/shard_map/ppermute | solution.py:331
  14.6 0.0 collective-permute-start.6
  14.6 0.5 %collective-permute-start.7 = (bf16[128,1024]{1,0:T(8,128)(2,1)S(1)}, bf16[128,1024]{1,0:T(8,128)(2,1)S(1)}, u32[]{:S(2)}, u32[]{:S(2)}) collective-permute-start(bf16[128,1024]{1,0:T(8,128)(2,1)S(1)} %collective-permute-done.1.refs_4_.refs_5_), channel_id=1, source_target_pairs={{0,8},{8,0},{16,24},{24,16},{1,9},{9,1},{17,25},{25,17},{2,10},{10... | collective-permute-start | bytes 786440 | tf_op jit(solution)/shard_map/ppermute | solution.py:334
  15.1 2.6 %collective-permute-start.12 = (f32[2,4,8]{2,1,0:T(4,128)S(1)}, f32[2,4,8]{2,1,0:T(4,128)S(1)}, u32[]{:S(2)}, u32[]{:S(2)}) collective-permute-start(f32[2,4,8]{2,1,0:T(4,128)S(1)} %pad_maximum_fusion.1), channel_id=1, source_target_pairs={{0,4},{2,6},{4,0},{6,2},{1,5},{3,7},{5,1},{7,3},{8,12},{10,14},{12... | collective-permute-start | bytes 776 | tf_op jit(solution)/shard_map/ppermute | solution.py:337
  17.7 2.4 %collective-permute-done.4.refs_8_.refs_9_ = bf16[128,1024]{1,0:T(8,128)(2,1)S(1)} collective-permute-done((bf16[128,1024]{1,0:T(8,128)(2,1)S(1)}, bf16[128,1024]{1,0:T(8,128)(2,1)S(1)}, u32[]{:S(2)}, u32[]{:S(2)}) %collective-permute-start.4) | collective-permute-done | bytes 262176 | tf_op jit(solution)/shard_map/ppermute | solution.py:331
  20.1 1.2 %collective-permute-done.5.refs_10_.refs_11_ = bf16[128,1024]{1,0:T(8,128)(2,1)S(1)} collective-permute-done((bf16[128,1024]{1,0:T(8,128)(2,1)S(1)}, bf16[128,1024]{1,0:T(8,128)(2,1)S(1)}, u32[]{:S(2)}, u32[]{:S(2)}) %collective-permute-start.5) | collective-permute-done | bytes 262176 | tf_op jit(solution)/shard_map/ppermute | solution.py:331
  21.2 0.0 collective-permute-done.6.refs_12_.refs_13_
  21.3 0.0 collective-permute-done.7.refs_14_.refs_15_
  21.3 1.8 %collective-permute-start.10 = (bf16[128,1024]{1,0:T(8,128)(2,1)S(1)}, bf16[128,1024]{1,0:T(8,128)(2,1)S(1)}, u32[]{:S(2)}, u32[]{:S(2)}) collective-permute-start(bf16[128,1024]{1,0:T(8,128)(2,1)S(1)} %collective-permute-done.4.refs_8_.refs_9_), channel_id=1, source_target_pairs={{0,2},{8,10},{2,4},{10,12},{4,6},{12,14},{6,22},{14,30},{22,20},{3... | collective-permute-start | bytes 786440 | tf_op jit(solution)/shard_map/ppermute | solution.py:331
  23.0 0.0 collective-permute-start.8
  23.0 0.2 collective-permute-start.11
  23.3 0.3 collective-permute-start.9
  23.6 0.0 collective-permute-done.12.refs_2_
  23.6 1.1 %shard_map.87 = (f32[8,16,128]{2,1,0:T(8,128)S(1)}, f32[8,1,1024]{2,1,0:T(1,128)S(1)}) custom-call(f32[1,4,8]{2,1,0:T(4,128)S(1)} %maximum_bitcast_fusion.refs_0_, f32[1,4,8]{2,1,0:T(4,128)S(1)} %collective-permute-done.3.refs_1_, f32[2,4,8]{2,1,0:T(4,128)S(1)} %collective-permute-done.12.refs_2_, s32[8]{0:T(128)S(1)} %copy-done.2), custom_call_target="tpu_custom_call" | custom-call | flops 100000000 | bytes 1000000 | tf_op jit(solution)/shard_map/pallas_call | solution.py:133
  24.6 4.3 %shard_map.88 = (f32[8,128,512]{2,1,0:T(8,128)S(1)}, f32[8,2,512]{2,1,0:T(2,128)S(1)}) custom-call(bf16[128,1024]{1,0:T(8,128)(2,1)S(1)} %pad_maximum_fusion.refs_0_.refs_1_, bf16[128,1024]{1,0:T(8,128)(2,1)S(1)} %pad_maximum_fusion.refs_0_.refs_1_, bf16[128,1024]{1,0:T(8,128)(2,1)S(1)} %collective-permute-done.refs_2_.refs_3_, ...), custom_call_target="tpu_custom_call" | custom-call | flops 4294967296 | bytes 8388608 | tf_op jit(solution)/shard_map/pallas_call | solution.py:285
  28.9 0.0 collective-permute-done.10.refs_0_.refs_1_
  28.9 2.8 %collective-permute-done.11.refs_2_.refs_3_ = bf16[128,1024]{1,0:T(8,128)(2,1)S(1)} collective-permute-done((bf16[128,1024]{1,0:T(8,128)(2,1)S(1)}, bf16[128,1024]{1,0:T(8,128)(2,1)S(1)}, u32[]{:S(2)}, u32[]{:S(2)}) %collective-permute-start.11) | collective-permute-done | bytes 262176 | tf_op jit(solution)/shard_map/ppermute | solution.py:331
  31.8 0.0 collective-permute-done.8.refs_4_.refs_5_
  31.8 0.0 collective-permute-done.9.refs_6_.refs_7_
  31.8 0.0 collective-permute-start.15
  31.8 0.5 %collective-permute-start.16 = (bf16[128,1024]{1,0:T(8,128)(2,1)S(1)}, bf16[128,1024]{1,0:T(8,128)(2,1)S(1)}, u32[]{:S(2)}, u32[]{:S(2)}) collective-permute-start(bf16[128,1024]{1,0:T(8,128)(2,1)S(1)} %collective-permute-done.11.refs_2_.refs_3_), channel_id=1, source_target_pairs={{0,8},{8,0},{16,24},{24,16},{1,9},{9,1},{17,25},{25,17},{2,10},{10... | collective-permute-start | bytes 786440 | tf_op jit(solution)/shard_map/ppermute | solution.py:334
  32.3 0.8 %collective-permute-start.13 = (bf16[64,1024]{1,0:T(8,128)(2,1)S(1)}, bf16[64,1024]{1,0:T(8,128)(2,1)S(1)}, u32[]{:S(2)}, u32[]{:S(2)}) collective-permute-start(bf16[64,1024]{1,0:T(8,128)(2,1)S(1)} %slice.6), channel_id=1, source_target_pairs={{0,2},{8,10},{2,4},{10,12},{4,6},{12,14},{6,22},{14,30},{22,20},{3... | collective-permute-start | bytes 393224 | tf_op jit(solution)/shard_map/ppermute | solution.py:331
  33.1 1.3 %collective-permute-start.14 = (bf16[64,1024]{1,0:T(8,128)(2,1)S(1)}, bf16[64,1024]{1,0:T(8,128)(2,1)S(1)}, u32[]{:S(2)}, u32[]{:S(2)}) collective-permute-start(bf16[64,1024]{1,0:T(8,128)(2,1)S(1)} %slice.7), channel_id=1, source_target_pairs={{0,16},{8,24},{2,0},{10,8},{4,2},{12,10},{6,4},{14,12},{22,6},{30,... | collective-permute-start | bytes 393224 | tf_op jit(solution)/shard_map/ppermute | solution.py:331
  34.4 0.0 collective-permute-done.15.refs_8_.refs_9_
  34.4 0.0 collective-permute-done.16.refs_10_.refs_11_
  34.4 3.4 %shard_map.89 = (f32[8,128,512]{2,1,0:T(8,128)S(1)}, f32[8,2,512]{2,1,0:T(2,128)S(1)}) custom-call(bf16[128,1024]{1,0:T(8,128)(2,1)S(1)} %collective-permute-done.10.refs_0_.refs_1_, bf16[128,1024]{1,0:T(8,128)(2,1)S(1)} %collective-permute-done.10.refs_0_.refs_1_, bf16[128,1024]{1,0:T(8,128)(2,1)S(1)} %collective-permute-done.11.refs_2_.refs_3_, ...), custom_call_target="tpu_custom_call" | custom-call | flops 3221225472 | bytes 8388608 | tf_op jit(solution)/shard_map/pallas_call | solution.py:285
  37.9 0.0 collective-permute-done.13.refs_0_
  37.9 0.4 collective-permute-done.14.refs_1_
  38.3 0.0 collective-permute-start.17
  38.3 0.5 %collective-permute-start.18 = (bf16[64,1024]{1,0:T(8,128)(2,1)S(1)}, bf16[64,1024]{1,0:T(8,128)(2,1)S(1)}, u32[]{:S(2)}, u32[]{:S(2)}) collective-permute-start(bf16[64,1024]{1,0:T(8,128)(2,1)S(1)} %collective-permute-done.14.refs_1_), channel_id=1, source_target_pairs={{0,8},{8,0},{16,24},{24,16},{1,9},{9,1},{17,25},{25,17},{2,10},{10... | collective-permute-start | bytes 393224 | tf_op jit(solution)/shard_map/ppermute | solution.py:334
  38.8 0.8 %collective-permute-done.17.refs_2_ = bf16[64,1024]{1,0:T(8,128)(2,1)S(1)} collective-permute-done((bf16[64,1024]{1,0:T(8,128)(2,1)S(1)}, bf16[64,1024]{1,0:T(8,128)(2,1)S(1)}, u32[]{:S(2)}, u32[]{:S(2)}) %collective-permute-start.17) | collective-permute-done | bytes 131104 | tf_op jit(solution)/shard_map/ppermute | solution.py:334
  39.6 0.2 collective-permute-done.18.refs_3_
  39.8 2.8 %shard_map.90 = (bf16[64,8192]{1,0:T(8,128)(2,1)}, f32[64,64]{1,0:T(8,128)}) custom-call(bf16[64,1024]{1,0:T(8,128)(2,1)S(1)} %collective-permute-done.13.refs_0_, bf16[64,1024]{1,0:T(8,128)(2,1)S(1)} %collective-permute-done.14.refs_1_, bf16[64,1024]{1,0:T(8,128)(2,1)S(1)} %collective-permute-done.17.refs_2_, ...), custom_call_target="tpu_custom_call" | custom-call | flops 1073741824 | bytes 8388608 | tf_op jit(solution)/shard_map/pallas_call | solution.py:285
  (6 shorter events, 0.0 us)
Async XLA Ops:
  1.6 10.9 %collective-permute-start = (bf16[128,1024]{1,0:T(8,128)(2,1)S(1)}, bf16[128,1024]{1,0:T(8,128)(2,1)S(1)}, u32[]{:S(2)}, u32[]{:S(2)}) collective-permute-start(bf16[128,1024]{1,0:T(8,128)(2,1)S(1)} %pad_maximum_fusion.refs_0_.refs_1_), channel_id=1, source_target_pairs={{0,2},{8,10},{2,4},{10,12},{4,6},{12,14},{6,22},{14,30},{22,20},{3... | collective-permute-start | bytes 786440 | tf_op jit(solution)/shard_map/ppermute | solution.py:331
  4.7 7.8 %collective-permute-start.1 = (bf16[128,1024]{1,0:T(8,128)(2,1)S(1)}, bf16[128,1024]{1,0:T(8,128)(2,1)S(1)}, u32[]{:S(2)}, u32[]{:S(2)}) collective-permute-start(bf16[128,1024]{1,0:T(8,128)(2,1)S(1)} %pad_maximum_fusion.refs_0_.refs_1_), channel_id=1, source_target_pairs={{0,16},{8,24},{2,0},{10,8},{4,2},{12,10},{6,4},{14,12},{22,6},{30,... | collective-permute-start | bytes 786440 | tf_op jit(solution)/shard_map/ppermute | solution.py:331
  4.7 7.8 %collective-permute-start.2 = (bf16[128,1024]{1,0:T(8,128)(2,1)S(1)}, bf16[128,1024]{1,0:T(8,128)(2,1)S(1)}, u32[]{:S(2)}, u32[]{:S(2)}) collective-permute-start(bf16[128,1024]{1,0:T(8,128)(2,1)S(1)} %pad_maximum_fusion.refs_0_.refs_1_), channel_id=1, source_target_pairs={{0,8},{8,0},{16,24},{24,16},{1,9},{9,1},{17,25},{25,17},{2,10},{10... | collective-permute-start | bytes 786440 | tf_op jit(solution)/shard_map/ppermute | solution.py:334
  5.4 7.1 %collective-permute-start.3 = (f32[1,4,8]{2,1,0:T(4,128)S(1)}, f32[1,4,8]{2,1,0:T(4,128)S(1)}, u32[]{:S(2)}, u32[]{:S(2)}) collective-permute-start(f32[1,4,8]{2,1,0:T(4,128)S(1)} %maximum_bitcast_fusion.refs_0_), channel_id=1, source_target_pairs={{0,2},{2,0},{4,6},{6,4},{1,3},{3,1},{5,7},{7,5},{8,10},{10,8},{12,... | collective-permute-start | bytes 392 | tf_op jit(solution)/shard_map/ppermute | solution.py:337
  7.4 1.2 %copy-start = (bf16[64,8192]{1,0:T(8,128)(2,1)S(1)}, bf16[64,8192]{1,0:T(8,128)(2,1)}, u32[]{:S(2)}) copy-start(bf16[64,8192]{1,0:T(8,128)(2,1)} %q_ref.1) | copy-start | bytes 3145732
  8.7 0.7 %copy-start.1 = (s32[8,8]{1,0:T(8,128)S(1)}, s32[8,8]{1,0:T(8,128)}, u32[]{:S(2)}) copy-start(s32[8,8]{1,0:T(8,128)} %keep_ref.1) | copy-start | bytes 772
  9.3 0.7 %copy-start.2 = (s32[8]{0:T(128)S(1)}, s32[8]{0:T(128)}, u32[]{:S(2)}) copy-start(s32[8]{0:T(128)} %refs_3_) | copy-start | bytes 100
  12.5 7.6 %collective-permute-start.4 = (bf16[128,1024]{1,0:T(8,128)(2,1)S(1)}, bf16[128,1024]{1,0:T(8,128)(2,1)S(1)}, u32[]{:S(2)}, u32[]{:S(2)}) collective-permute-start(bf16[128,1024]{1,0:T(8,128)(2,1)S(1)} %collective-permute-done.refs_2_.refs_3_), channel_id=1, source_target_pairs={{0,2},{8,10},{2,4},{10,12},{4,6},{12,14},{6,22},{14,30},{22,20},{3... | collective-permute-start | bytes 786440 | tf_op jit(solution)/shard_map/ppermute | solution.py:331
  14.0 7.2 %collective-permute-start.5 = (bf16[128,1024]{1,0:T(8,128)(2,1)S(1)}, bf16[128,1024]{1,0:T(8,128)(2,1)S(1)}, u32[]{:S(2)}, u32[]{:S(2)}) collective-permute-start(bf16[128,1024]{1,0:T(8,128)(2,1)S(1)} %collective-permute-done.1.refs_4_.refs_5_), channel_id=1, source_target_pairs={{0,16},{8,24},{2,0},{10,8},{4,2},{12,10},{6,4},{14,12},{22,6},{30,... | collective-permute-start | bytes 786440 | tf_op jit(solution)/shard_map/ppermute | solution.py:331
  14.6 6.7 %collective-permute-start.6 = (bf16[128,1024]{1,0:T(8,128)(2,1)S(1)}, bf16[128,1024]{1,0:T(8,128)(2,1)S(1)}, u32[]{:S(2)}, u32[]{:S(2)}) collective-permute-start(bf16[128,1024]{1,0:T(8,128)(2,1)S(1)} %collective-permute-done.refs_2_.refs_3_), channel_id=1, source_target_pairs={{0,8},{8,0},{16,24},{24,16},{1,9},{9,1},{17,25},{25,17},{2,10},{10... | collective-permute-start | bytes 786440 | tf_op jit(solution)/shard_map/ppermute | solution.py:334
  14.6 6.7 %collective-permute-start.7 = (bf16[128,1024]{1,0:T(8,128)(2,1)S(1)}, bf16[128,1024]{1,0:T(8,128)(2,1)S(1)}, u32[]{:S(2)}, u32[]{:S(2)}) collective-permute-start(bf16[128,1024]{1,0:T(8,128)(2,1)S(1)} %collective-permute-done.1.refs_4_.refs_5_), channel_id=1, source_target_pairs={{0,8},{8,0},{16,24},{24,16},{1,9},{9,1},{17,25},{25,17},{2,10},{10... | collective-permute-start | bytes 786440 | tf_op jit(solution)/shard_map/ppermute | solution.py:334
  15.1 8.4 %collective-permute-start.12 = (f32[2,4,8]{2,1,0:T(4,128)S(1)}, f32[2,4,8]{2,1,0:T(4,128)S(1)}, u32[]{:S(2)}, u32[]{:S(2)}) collective-permute-start(f32[2,4,8]{2,1,0:T(4,128)S(1)} %pad_maximum_fusion.1), channel_id=1, source_target_pairs={{0,4},{2,6},{4,0},{6,2},{1,5},{3,7},{5,1},{7,3},{8,12},{10,14},{12... | collective-permute-start | bytes 776 | tf_op jit(solution)/shard_map/ppermute | solution.py:337
  21.3 7.7 %collective-permute-start.10 = (bf16[128,1024]{1,0:T(8,128)(2,1)S(1)}, bf16[128,1024]{1,0:T(8,128)(2,1)S(1)}, u32[]{:S(2)}, u32[]{:S(2)}) collective-permute-start(bf16[128,1024]{1,0:T(8,128)(2,1)S(1)} %collective-permute-done.4.refs_8_.refs_9_), channel_id=1, source_target_pairs={{0,2},{8,10},{2,4},{10,12},{4,6},{12,14},{6,22},{14,30},{22,20},{3... | collective-permute-start | bytes 786440 | tf_op jit(solution)/shard_map/ppermute | solution.py:331
  23.0 8.7 %collective-permute-start.8 = (bf16[128,1024]{1,0:T(8,128)(2,1)S(1)}, bf16[128,1024]{1,0:T(8,128)(2,1)S(1)}, u32[]{:S(2)}, u32[]{:S(2)}) collective-permute-start(bf16[128,1024]{1,0:T(8,128)(2,1)S(1)} %collective-permute-done.4.refs_8_.refs_9_), channel_id=1, source_target_pairs={{0,8},{8,0},{16,24},{24,16},{1,9},{9,1},{17,25},{25,17},{2,10},{10... | collective-permute-start | bytes 786440 | tf_op jit(solution)/shard_map/ppermute | solution.py:334
  23.0 8.7 %collective-permute-start.11 = (bf16[128,1024]{1,0:T(8,128)(2,1)S(1)}, bf16[128,1024]{1,0:T(8,128)(2,1)S(1)}, u32[]{:S(2)}, u32[]{:S(2)}) collective-permute-start(bf16[128,1024]{1,0:T(8,128)(2,1)S(1)} %collective-permute-done.5.refs_10_.refs_11_), channel_id=1, source_target_pairs={{0,16},{8,24},{2,0},{10,8},{4,2},{12,10},{6,4},{14,12},{22,6},{30,... | collective-permute-start | bytes 786440 | tf_op jit(solution)/shard_map/ppermute | solution.py:331
  23.3 8.5 %collective-permute-start.9 = (bf16[128,1024]{1,0:T(8,128)(2,1)S(1)}, bf16[128,1024]{1,0:T(8,128)(2,1)S(1)}, u32[]{:S(2)}, u32[]{:S(2)}) collective-permute-start(bf16[128,1024]{1,0:T(8,128)(2,1)S(1)} %collective-permute-done.5.refs_10_.refs_11_), channel_id=1, source_target_pairs={{0,8},{8,0},{16,24},{24,16},{1,9},{9,1},{17,25},{25,17},{2,10},{10... | collective-permute-start | bytes 786440 | tf_op jit(solution)/shard_map/ppermute | solution.py:334
  31.8 2.6 %collective-permute-start.15 = (bf16[128,1024]{1,0:T(8,128)(2,1)S(1)}, bf16[128,1024]{1,0:T(8,128)(2,1)S(1)}, u32[]{:S(2)}, u32[]{:S(2)}) collective-permute-start(bf16[128,1024]{1,0:T(8,128)(2,1)S(1)} %collective-permute-done.10.refs_0_.refs_1_), channel_id=1, source_target_pairs={{0,8},{8,0},{16,24},{24,16},{1,9},{9,1},{17,25},{25,17},{2,10},{10... | collective-permute-start | bytes 786440 | tf_op jit(solution)/shard_map/ppermute | solution.py:334
  31.8 2.6 %collective-permute-start.16 = (bf16[128,1024]{1,0:T(8,128)(2,1)S(1)}, bf16[128,1024]{1,0:T(8,128)(2,1)S(1)}, u32[]{:S(2)}, u32[]{:S(2)}) collective-permute-start(bf16[128,1024]{1,0:T(8,128)(2,1)S(1)} %collective-permute-done.11.refs_2_.refs_3_), channel_id=1, source_target_pairs={{0,8},{8,0},{16,24},{24,16},{1,9},{9,1},{17,25},{25,17},{2,10},{10... | collective-permute-start | bytes 786440 | tf_op jit(solution)/shard_map/ppermute | solution.py:334
  32.3 5.5 %collective-permute-start.13 = (bf16[64,1024]{1,0:T(8,128)(2,1)S(1)}, bf16[64,1024]{1,0:T(8,128)(2,1)S(1)}, u32[]{:S(2)}, u32[]{:S(2)}) collective-permute-start(bf16[64,1024]{1,0:T(8,128)(2,1)S(1)} %slice.6), channel_id=1, source_target_pairs={{0,2},{8,10},{2,4},{10,12},{4,6},{12,14},{6,22},{14,30},{22,20},{3... | collective-permute-start | bytes 393224 | tf_op jit(solution)/shard_map/ppermute | solution.py:331
  33.1 5.2 %collective-permute-start.14 = (bf16[64,1024]{1,0:T(8,128)(2,1)S(1)}, bf16[64,1024]{1,0:T(8,128)(2,1)S(1)}, u32[]{:S(2)}, u32[]{:S(2)}) collective-permute-start(bf16[64,1024]{1,0:T(8,128)(2,1)S(1)} %slice.7), channel_id=1, source_target_pairs={{0,16},{8,24},{2,0},{10,8},{4,2},{12,10},{6,4},{14,12},{22,6},{30,... | collective-permute-start | bytes 393224 | tf_op jit(solution)/shard_map/ppermute | solution.py:331
  38.3 1.3 %collective-permute-start.17 = (bf16[64,1024]{1,0:T(8,128)(2,1)S(1)}, bf16[64,1024]{1,0:T(8,128)(2,1)S(1)}, u32[]{:S(2)}, u32[]{:S(2)}) collective-permute-start(bf16[64,1024]{1,0:T(8,128)(2,1)S(1)} %collective-permute-done.13.refs_0_), channel_id=1, source_target_pairs={{0,8},{8,0},{16,24},{24,16},{1,9},{9,1},{17,25},{25,17},{2,10},{10... | collective-permute-start | bytes 393224 | tf_op jit(solution)/shard_map/ppermute | solution.py:334
  38.3 1.5 %collective-permute-start.18 = (bf16[64,1024]{1,0:T(8,128)(2,1)S(1)}, bf16[64,1024]{1,0:T(8,128)(2,1)S(1)}, u32[]{:S(2)}, u32[]{:S(2)}) collective-permute-start(bf16[64,1024]{1,0:T(8,128)(2,1)S(1)} %collective-permute-done.14.refs_1_), channel_id=1, source_target_pairs={{0,8},{8,0},{16,24},{24,16},{1,9},{9,1},{17,25},{25,17},{2,10},{10... | collective-permute-start | bytes 393224 | tf_op jit(solution)/shard_map/ppermute | solution.py:334

commit v13 on v12

--- a/solution.py
+++ b/solution.py
@@ -247,6 +247,7 @@
     groups = rows // tokens
     count = len(pieces)
     per_step = 4 if kv_heads % 4 == 0 else 1
+    per_step = per_step if last else kv_heads
     keys = tokens * count
     width = kv_heads * groups * HEAD_WIDTH
     first = state is None
@@ -302,7 +303,7 @@
             pltpu.VMEM((per_step, keys, rows), jnp.bfloat16),
             pltpu.VMEM((kv_heads * groups, tokens), jnp.float32),
         ],
-        compiler_params=pltpu.CompilerParams(vmem_limit_bytes=40 * 1024 * 1024),
+        compiler_params=pltpu.CompilerParams(vmem_limit_bytes=44 * 1024 * 1024),
         cost_estimate=pl.CostEstimate(
             flops=16 * tokens * width * keys,
             bytes_accessed=16 * tokens * width,

time: 42.9 us -> 42.9 us (level)
  Pallas kernels: 13.1 us -> 12.5 us
  waiting for transfers between devices: 8.83 us -> 9.43 us
    ppermute x8, waiting for transfers between devices: 6.82 us -> 7.42 us  [around(): return lax.ppermute(block, ('ctx', 'head'), route)]
    pallas_call x3, Pallas kernels: 10.5 us -> 9.95 us  [absorb(): pl.pallas_call(functools.partial(absorb_kernel, groups=groups, tokens=tok...]
  transfers between devices with their start and end apart: 19 -> 19, of which waited for: 7 -> 8; matrix products, arithmetic and copies ran while one was open for 2% -> 2% of each run, Pallas kernels for 24% -> 23%
where the time goes in v13:
time: 42.9 us; the launch traced here: 42.7 us
  starting transfers between devices  15.7 us (37%)
  Pallas kernels  12.5 us (29%)
  waiting for transfers between devices  9.43 us (22%)
  local copies, waits for them, and re-layouts  2.59 us (6%)
  other arithmetic  1.7 us (4%)
  between operations  0.72 us (2%)
    pallas_call x3, Pallas kernels, absorb(): pl.pallas_call(functools.partial(absorb_kernel, groups=groups, tokens=tok...  9.95 us
    ppermute x8, starting transfers between devices, around(): return lax.ppermute(block, ('ctx', 'head'), route)  9.27 us
    ppermute x8, waiting for transfers between devices, around(): return lax.ppermute(block, ('ctx', 'head'), route)  7.42 us
    ppermute x2, starting transfers between devices, swap_heads(): lax.ppermute(block, 'head', [(i, i ^ flip) for i in range(head_size)])  4.61 us
    unnamed x6, local copies, waits for them, and re-layouts  2.57 us
    ppermute x9, starting transfers between devices, to_other_core(): lax.ppermute(block, 'ctx', [(i, i ^ 1) for i in range(ctx_size)])  1.8 us
    pallas_call x1, Pallas kernels, prepare(): pl.pallas_call(functools.partial(prepare_kernel, groups=groups, per_step=...  1.54 us
    pallas_call x1, Pallas kernels, scale_rows(): pl.pallas_call(functools.partial(scale_rows_kernel, owners=[scale.shape[0...  1.06 us
  transfers between devices with their start and end apart: 19, of which 8 were waited for; matrix products, arithmetic and copies ran while one was open for 2% of the time, Pallas kernels for 23%

profile of v13, /device:TPU:0, one launch (start us, length us, event | category | flops | bytes accessed | tf_op | source)
XLA Modules:
  0.0 42.7 jit_solution(14194523198764624013)
XLA Ops:
  0.6 1.0 %pad_maximum_fusion.refs_0_.refs_1_ = bf16[128,1024]{1,0:T(8,128)(2,1)S(1)} fusion(bf16[64,1024]{1,0:T(8,128)(2,1)} %param.9, bf16[64,1024]{1,0:T(8,128)(2,1)} %param.8), kind=kLoop, calls=%fused_computation | loop fusion | flops 524288 | bytes 524288 | tf_op jit(solution)/shard_map/concatenate | solution.py:353
  1.6 3.1 %collective-permute-start = (bf16[128,1024]{1,0:T(8,128)(2,1)S(1)}, bf16[128,1024]{1,0:T(8,128)(2,1)S(1)}, u32[]{:S(2)}, u32[]{:S(2)}) collective-permute-start(bf16[128,1024]{1,0:T(8,128)(2,1)S(1)} %pad_maximum_fusion.refs_0_.refs_1_), channel_id=1, source_target_pairs={{0,2},{8,10},{2,4},{10,12},{4,6},{12,14},{6,22},{14,30},{22,20},{3... | collective-permute-start | bytes 786440 | tf_op jit(solution)/shard_map/ppermute | solution.py:332
  4.7 0.0 collective-permute-start.1
  4.7 0.0 collective-permute-start.2
  4.7 0.7 %maximum_bitcast_fusion.refs_0_ = f32[1,4,8]{2,1,0:T(4,128)S(1)} fusion(f32[2,8]{1,0:T(2,128)} %bitcast.4, f32[2,8]{1,0:T(2,128)} %bitcast.5), kind=kLoop, calls=%fused_computation.2 | loop fusion | flops 32 | bytes 256 | tf_op jit(solution)/shard_map/broadcast_in_dim | solution.py:355
  5.4 2.0 %collective-permute-start.3 = (f32[1,4,8]{2,1,0:T(4,128)S(1)}, f32[1,4,8]{2,1,0:T(4,128)S(1)}, u32[]{:S(2)}, u32[]{:S(2)}) collective-permute-start(f32[1,4,8]{2,1,0:T(4,128)S(1)} %maximum_bitcast_fusion.refs_0_), channel_id=1, source_target_pairs={{0,2},{2,0},{4,6},{6,4},{1,3},{3,1},{5,7},{7,5},{8,10},{10,8},{12,... | collective-permute-start | bytes 392 | tf_op jit(solution)/shard_map/ppermute | solution.py:338
  7.4 1.2 %copy-done = bf16[64,8192]{1,0:T(8,128)(2,1)S(1)} copy-done((bf16[64,8192]{1,0:T(8,128)(2,1)S(1)}, bf16[64,8192]{1,0:T(8,128)(2,1)}, u32[]{:S(2)}) %copy-start) | copy-done | bytes 1048600
  8.7 0.7 %copy-done.1 = s32[8,8]{1,0:T(8,128)S(1)} copy-done((s32[8,8]{1,0:T(8,128)S(1)}, s32[8,8]{1,0:T(8,128)}, u32[]{:S(2)}) %copy-start.1) | copy-done | bytes 280
  9.3 0.7 %copy-done.2 = s32[8]{0:T(128)S(1)} copy-done((s32[8]{0:T(128)S(1)}, s32[8]{0:T(128)}, u32[]{:S(2)}) %copy-start.2) | copy-done | bytes 56
  10.0 1.5 %shard_map.86 = (bf16[8,128,512]{2,1,0:T(8,128)(2,1)S(1)}, bf16[128,512]{1,0:T(8,128)(2,1)S(1)}, bf16[1024,128]{1,0:T(8,128)(2,1)S(1)}) custom-call(s32[8]{0:T(128)S(1)} %copy-done.2, s32[8,8]{1,0:T(8,128)S(1)} %copy-done.1, bf16[64,8192]{1,0:T(8,128)(2,1)S(1)} %copy-done), custom_call_target="tpu_custom_call" | custom-call | flops 4194304 | bytes 8388608 | tf_op jit(solution)/shard_map/pallas_call | solution.py:65
  11.5 1.0 %collective-permute-done.3.refs_1_ = f32[1,4,8]{2,1,0:T(4,128)S(1)} collective-permute-done((f32[1,4,8]{2,1,0:T(4,128)S(1)}, f32[1,4,8]{2,1,0:T(4,128)S(1)}, u32[]{:S(2)}, u32[]{:S(2)}) %collective-permute-start.3) | collective-permute-done | bytes 160 | tf_op jit(solution)/shard_map/ppermute | solution.py:338
  12.5 0.0 collective-permute-done.refs_2_.refs_3_
  12.5 0.0 collective-permute-done.1.refs_4_.refs_5_
  12.5 0.0 collective-permute-done.2.refs_6_.refs_7_
  12.5 1.5 %collective-permute-start.4 = (bf16[128,1024]{1,0:T(8,128)(2,1)S(1)}, bf16[128,1024]{1,0:T(8,128)(2,1)S(1)}, u32[]{:S(2)}, u32[]{:S(2)}) collective-permute-start(bf16[128,1024]{1,0:T(8,128)(2,1)S(1)} %collective-permute-done.refs_2_.refs_3_), channel_id=1, source_target_pairs={{0,2},{8,10},{2,4},{10,12},{4,6},{12,14},{6,22},{14,30},{22,20},{3... | collective-permute-start | bytes 786440 | tf_op jit(solution)/shard_map/ppermute | solution.py:332
  14.0 0.6 %collective-permute-start.5 = (bf16[128,1024]{1,0:T(8,128)(2,1)S(1)}, bf16[128,1024]{1,0:T(8,128)(2,1)S(1)}, u32[]{:S(2)}, u32[]{:S(2)}) collective-permute-start(bf16[128,1024]{1,0:T(8,128)(2,1)S(1)} %collective-permute-done.1.refs_4_.refs_5_), channel_id=1, source_target_pairs={{0,16},{8,24},{2,0},{10,8},{4,2},{12,10},{6,4},{14,12},{22,6},{30,... | collective-permute-start | bytes 786440 | tf_op jit(solution)/shard_map/ppermute | solution.py:332
  14.6 0.0 collective-permute-start.6
  14.6 0.5 %collective-permute-start.7 = (bf16[128,1024]{1,0:T(8,128)(2,1)S(1)}, bf16[128,1024]{1,0:T(8,128)(2,1)S(1)}, u32[]{:S(2)}, u32[]{:S(2)}) collective-permute-start(bf16[128,1024]{1,0:T(8,128)(2,1)S(1)} %collective-permute-done.1.refs_4_.refs_5_), channel_id=1, source_target_pairs={{0,8},{8,0},{16,24},{24,16},{1,9},{9,1},{17,25},{25,17},{2,10},{10... | collective-permute-start | bytes 786440 | tf_op jit(solution)/shard_map/ppermute | solution.py:335
  15.1 2.6 %collective-permute-start.12 = (f32[2,4,8]{2,1,0:T(4,128)S(1)}, f32[2,4,8]{2,1,0:T(4,128)S(1)}, u32[]{:S(2)}, u32[]{:S(2)}) collective-permute-start(f32[2,4,8]{2,1,0:T(4,128)S(1)} %pad_maximum_fusion.1), channel_id=1, source_target_pairs={{0,4},{2,6},{4,0},{6,2},{1,5},{3,7},{5,1},{7,3},{8,12},{10,14},{12... | collective-permute-start | bytes 776 | tf_op jit(solution)/shard_map/ppermute | solution.py:338
  17.7 2.4 %collective-permute-done.4.refs_8_.refs_9_ = bf16[128,1024]{1,0:T(8,128)(2,1)S(1)} collective-permute-done((bf16[128,1024]{1,0:T(8,128)(2,1)S(1)}, bf16[128,1024]{1,0:T(8,128)(2,1)S(1)}, u32[]{:S(2)}, u32[]{:S(2)}) %collective-permute-start.4) | collective-permute-done | bytes 262176 | tf_op jit(solution)/shard_map/ppermute | solution.py:332
  20.1 1.2 %collective-permute-done.5.refs_10_.refs_11_ = bf16[128,1024]{1,0:T(8,128)(2,1)S(1)} collective-permute-done((bf16[128,1024]{1,0:T(8,128)(2,1)S(1)}, bf16[128,1024]{1,0:T(8,128)(2,1)S(1)}, u32[]{:S(2)}, u32[]{:S(2)}) %collective-permute-start.5) | collective-permute-done | bytes 262176 | tf_op jit(solution)/shard_map/ppermute | solution.py:332
  21.2 0.0 collective-permute-done.6.refs_12_.refs_13_
  21.3 0.0 collective-permute-done.7.refs_14_.refs_15_
  21.3 1.8 %collective-permute-start.10 = (bf16[128,1024]{1,0:T(8,128)(2,1)S(1)}, bf16[128,1024]{1,0:T(8,128)(2,1)S(1)}, u32[]{:S(2)}, u32[]{:S(2)}) collective-permute-start(bf16[128,1024]{1,0:T(8,128)(2,1)S(1)} %collective-permute-done.4.refs_8_.refs_9_), channel_id=1, source_target_pairs={{0,2},{8,10},{2,4},{10,12},{4,6},{12,14},{6,22},{14,30},{22,20},{3... | collective-permute-start | bytes 786440 | tf_op jit(solution)/shard_map/ppermute | solution.py:332
  23.0 0.0 collective-permute-start.8
  23.0 0.2 collective-permute-start.11
  23.3 0.3 collective-permute-start.9
  23.6 0.0 collective-permute-done.12.refs_2_
  23.6 1.1 %shard_map.87 = (f32[8,16,128]{2,1,0:T(8,128)S(1)}, f32[8,1,1024]{2,1,0:T(1,128)S(1)}) custom-call(f32[1,4,8]{2,1,0:T(4,128)S(1)} %maximum_bitcast_fusion.refs_0_, f32[1,4,8]{2,1,0:T(4,128)S(1)} %collective-permute-done.3.refs_1_, f32[2,4,8]{2,1,0:T(4,128)S(1)} %collective-permute-done.12.refs_2_, s32[8]{0:T(128)S(1)} %copy-done.2), custom_call_target="tpu_custom_call" | custom-call | flops 100000000 | bytes 1000000 | tf_op jit(solution)/shard_map/pallas_call | solution.py:133
  24.6 4.0 %shard_map.88 = (f32[8,128,512]{2,1,0:T(8,128)S(1)}, f32[8,2,512]{2,1,0:T(2,128)S(1)}) custom-call(bf16[128,1024]{1,0:T(8,128)(2,1)S(1)} %pad_maximum_fusion.refs_0_.refs_1_, bf16[128,1024]{1,0:T(8,128)(2,1)S(1)} %pad_maximum_fusion.refs_0_.refs_1_, bf16[128,1024]{1,0:T(8,128)(2,1)S(1)} %collective-permute-done.refs_2_.refs_3_, ...), custom_call_target="tpu_custom_call" | custom-call | flops 4294967296 | bytes 8388608 | tf_op jit(solution)/shard_map/pallas_call | solution.py:286
  28.6 0.0 collective-permute-done.10.refs_0_.refs_1_
  28.6 3.1 %collective-permute-done.11.refs_2_.refs_3_ = bf16[128,1024]{1,0:T(8,128)(2,1)S(1)} collective-permute-done((bf16[128,1024]{1,0:T(8,128)(2,1)S(1)}, bf16[128,1024]{1,0:T(8,128)(2,1)S(1)}, u32[]{:S(2)}, u32[]{:S(2)}) %collective-permute-start.11) | collective-permute-done | bytes 262176 | tf_op jit(solution)/shard_map/ppermute | solution.py:332
  31.8 0.0 collective-permute-done.8.refs_4_.refs_5_
  31.8 0.0 collective-permute-done.9.refs_6_.refs_7_
  31.8 0.0 collective-permute-start.15
  31.8 0.5 %collective-permute-start.16 = (bf16[128,1024]{1,0:T(8,128)(2,1)S(1)}, bf16[128,1024]{1,0:T(8,128)(2,1)S(1)}, u32[]{:S(2)}, u32[]{:S(2)}) collective-permute-start(bf16[128,1024]{1,0:T(8,128)(2,1)S(1)} %collective-permute-done.11.refs_2_.refs_3_), channel_id=1, source_target_pairs={{0,8},{8,0},{16,24},{24,16},{1,9},{9,1},{17,25},{25,17},{2,10},{10... | collective-permute-start | bytes 786440 | tf_op jit(solution)/shard_map/ppermute | solution.py:335
  32.3 0.8 %collective-permute-start.13 = (bf16[64,1024]{1,0:T(8,128)(2,1)S(1)}, bf16[64,1024]{1,0:T(8,128)(2,1)S(1)}, u32[]{:S(2)}, u32[]{:S(2)}) collective-permute-start(bf16[64,1024]{1,0:T(8,128)(2,1)S(1)} %slice.6), channel_id=1, source_target_pairs={{0,2},{8,10},{2,4},{10,12},{4,6},{12,14},{6,22},{14,30},{22,20},{3... | collective-permute-start | bytes 393224 | tf_op jit(solution)/shard_map/ppermute | solution.py:332
  33.1 1.3 %collective-permute-start.14 = (bf16[64,1024]{1,0:T(8,128)(2,1)S(1)}, bf16[64,1024]{1,0:T(8,128)(2,1)S(1)}, u32[]{:S(2)}, u32[]{:S(2)}) collective-permute-start(bf16[64,1024]{1,0:T(8,128)(2,1)S(1)} %slice.7), channel_id=1, source_target_pairs={{0,16},{8,24},{2,0},{10,8},{4,2},{12,10},{6,4},{14,12},{22,6},{30,... | collective-permute-start | bytes 393224 | tf_op jit(solution)/shard_map/ppermute | solution.py:332
  34.4 0.0 collective-permute-done.15.refs_8_.refs_9_
  34.4 0.0 collective-permute-done.16.refs_10_.refs_11_
  34.4 3.1 %shard_map.89 = (f32[8,128,512]{2,1,0:T(8,128)S(1)}, f32[8,2,512]{2,1,0:T(2,128)S(1)}) custom-call(bf16[128,1024]{1,0:T(8,128)(2,1)S(1)} %collective-permute-done.10.refs_0_.refs_1_, bf16[128,1024]{1,0:T(8,128)(2,1)S(1)} %collective-permute-done.10.refs_0_.refs_1_, bf16[128,1024]{1,0:T(8,128)(2,1)S(1)} %collective-permute-done.11.refs_2_.refs_3_, ...), custom_call_target="tpu_custom_call" | custom-call | flops 3221225472 | bytes 8388608 | tf_op jit(solution)/shard_map/pallas_call | solution.py:286
  37.5 0.3 collective-permute-done.13.refs_0_
  37.8 0.4 %collective-permute-done.14.refs_1_ = bf16[64,1024]{1,0:T(8,128)(2,1)S(1)} collective-permute-done((bf16[64,1024]{1,0:T(8,128)(2,1)S(1)}, bf16[64,1024]{1,0:T(8,128)(2,1)S(1)}, u32[]{:S(2)}, u32[]{:S(2)}) %collective-permute-start.14) | collective-permute-done | bytes 131104 | tf_op jit(solution)/shard_map/ppermute | solution.py:332
  38.3 0.0 collective-permute-start.17
  38.3 0.5 %collective-permute-start.18 = (bf16[64,1024]{1,0:T(8,128)(2,1)S(1)}, bf16[64,1024]{1,0:T(8,128)(2,1)S(1)}, u32[]{:S(2)}, u32[]{:S(2)}) collective-permute-start(bf16[64,1024]{1,0:T(8,128)(2,1)S(1)} %collective-permute-done.14.refs_1_), channel_id=1, source_target_pairs={{0,8},{8,0},{16,24},{24,16},{1,9},{9,1},{17,25},{25,17},{2,10},{10... | collective-permute-start | bytes 393224 | tf_op jit(solution)/shard_map/ppermute | solution.py:335
  38.8 0.8 %collective-permute-done.17.refs_2_ = bf16[64,1024]{1,0:T(8,128)(2,1)S(1)} collective-permute-done((bf16[64,1024]{1,0:T(8,128)(2,1)S(1)}, bf16[64,1024]{1,0:T(8,128)(2,1)S(1)}, u32[]{:S(2)}, u32[]{:S(2)}) %collective-permute-start.17) | collective-permute-done | bytes 131104 | tf_op jit(solution)/shard_map/ppermute | solution.py:335
  39.6 0.2 collective-permute-done.18.refs_3_
  39.8 2.8 %shard_map.90 = (bf16[64,8192]{1,0:T(8,128)(2,1)}, f32[64,64]{1,0:T(8,128)}) custom-call(bf16[64,1024]{1,0:T(8,128)(2,1)S(1)} %collective-permute-done.13.refs_0_, bf16[64,1024]{1,0:T(8,128)(2,1)S(1)} %collective-permute-done.14.refs_1_, bf16[64,1024]{1,0:T(8,128)(2,1)S(1)} %collective-permute-done.17.refs_2_, ...), custom_call_target="tpu_custom_call" | custom-call | flops 1073741824 | bytes 8388608 | tf_op jit(solution)/shard_map/pallas_call | solution.py:286
  (6 shorter events, 0.0 us)
Async XLA Ops:
  1.6 10.9 %collective-permute-start = (bf16[128,1024]{1,0:T(8,128)(2,1)S(1)}, bf16[128,1024]{1,0:T(8,128)(2,1)S(1)}, u32[]{:S(2)}, u32[]{:S(2)}) collective-permute-start(bf16[128,1024]{1,0:T(8,128)(2,1)S(1)} %pad_maximum_fusion.refs_0_.refs_1_), channel_id=1, source_target_pairs={{0,2},{8,10},{2,4},{10,12},{4,6},{12,14},{6,22},{14,30},{22,20},{3... | collective-permute-start | bytes 786440 | tf_op jit(solution)/shard_map/ppermute | solution.py:332
  4.7 7.8 %collective-permute-start.1 = (bf16[128,1024]{1,0:T(8,128)(2,1)S(1)}, bf16[128,1024]{1,0:T(8,128)(2,1)S(1)}, u32[]{:S(2)}, u32[]{:S(2)}) collective-permute-start(bf16[128,1024]{1,0:T(8,128)(2,1)S(1)} %pad_maximum_fusion.refs_0_.refs_1_), channel_id=1, source_target_pairs={{0,16},{8,24},{2,0},{10,8},{4,2},{12,10},{6,4},{14,12},{22,6},{30,... | collective-permute-start | bytes 786440 | tf_op jit(solution)/shard_map/ppermute | solution.py:332
  4.7 7.8 %collective-permute-start.2 = (bf16[128,1024]{1,0:T(8,128)(2,1)S(1)}, bf16[128,1024]{1,0:T(8,128)(2,1)S(1)}, u32[]{:S(2)}, u32[]{:S(2)}) collective-permute-start(bf16[128,1024]{1,0:T(8,128)(2,1)S(1)} %pad_maximum_fusion.refs_0_.refs_1_), channel_id=1, source_target_pairs={{0,8},{8,0},{16,24},{24,16},{1,9},{9,1},{17,25},{25,17},{2,10},{10... | collective-permute-start | bytes 786440 | tf_op jit(solution)/shard_map/ppermute | solution.py:335
  5.4 7.1 %collective-permute-start.3 = (f32[1,4,8]{2,1,0:T(4,128)S(1)}, f32[1,4,8]{2,1,0:T(4,128)S(1)}, u32[]{:S(2)}, u32[]{:S(2)}) collective-permute-start(f32[1,4,8]{2,1,0:T(4,128)S(1)} %maximum_bitcast_fusion.refs_0_), channel_id=1, source_target_pairs={{0,2},{2,0},{4,6},{6,4},{1,3},{3,1},{5,7},{7,5},{8,10},{10,8},{12,... | collective-permute-start | bytes 392 | tf_op jit(solution)/shard_map/ppermute | solution.py:338
  7.4 1.2 %copy-start = (bf16[64,8192]{1,0:T(8,128)(2,1)S(1)}, bf16[64,8192]{1,0:T(8,128)(2,1)}, u32[]{:S(2)}) copy-start(bf16[64,8192]{1,0:T(8,128)(2,1)} %q_ref.1) | copy-start | bytes 3145732
  8.7 0.7 %copy-start.1 = (s32[8,8]{1,0:T(8,128)S(1)}, s32[8,8]{1,0:T(8,128)}, u32[]{:S(2)}) copy-start(s32[8,8]{1,0:T(8,128)} %keep_ref.1) | copy-start | bytes 772
  9.3 0.7 %copy-start.2 = (s32[8]{0:T(128)S(1)}, s32[8]{0:T(128)}, u32[]{:S(2)}) copy-start(s32[8]{0:T(128)} %refs_3_) | copy-start | bytes 100
  12.5 7.6 %collective-permute-start.4 = (bf16[128,1024]{1,0:T(8,128)(2,1)S(1)}, bf16[128,1024]{1,0:T(8,128)(2,1)S(1)}, u32[]{:S(2)}, u32[]{:S(2)}) collective-permute-start(bf16[128,1024]{1,0:T(8,128)(2,1)S(1)} %collective-permute-done.refs_2_.refs_3_), channel_id=1, source_target_pairs={{0,2},{8,10},{2,4},{10,12},{4,6},{12,14},{6,22},{14,30},{22,20},{3... | collective-permute-start | bytes 786440 | tf_op jit(solution)/shard_map/ppermute | solution.py:332
  14.0 7.2 %collective-permute-start.5 = (bf16[128,1024]{1,0:T(8,128)(2,1)S(1)}, bf16[128,1024]{1,0:T(8,128)(2,1)S(1)}, u32[]{:S(2)}, u32[]{:S(2)}) collective-permute-start(bf16[128,1024]{1,0:T(8,128)(2,1)S(1)} %collective-permute-done.1.refs_4_.refs_5_), channel_id=1, source_target_pairs={{0,16},{8,24},{2,0},{10,8},{4,2},{12,10},{6,4},{14,12},{22,6},{30,... | collective-permute-start | bytes 786440 | tf_op jit(solution)/shard_map/ppermute | solution.py:332
  14.6 6.7 %collective-permute-start.6 = (bf16[128,1024]{1,0:T(8,128)(2,1)S(1)}, bf16[128,1024]{1,0:T(8,128)(2,1)S(1)}, u32[]{:S(2)}, u32[]{:S(2)}) collective-permute-start(bf16[128,1024]{1,0:T(8,128)(2,1)S(1)} %collective-permute-done.refs_2_.refs_3_), channel_id=1, source_target_pairs={{0,8},{8,0},{16,24},{24,16},{1,9},{9,1},{17,25},{25,17},{2,10},{10... | collective-permute-start | bytes 786440 | tf_op jit(solution)/shard_map/ppermute | solution.py:335
  14.6 6.7 %collective-permute-start.7 = (bf16[128,1024]{1,0:T(8,128)(2,1)S(1)}, bf16[128,1024]{1,0:T(8,128)(2,1)S(1)}, u32[]{:S(2)}, u32[]{:S(2)}) collective-permute-start(bf16[128,1024]{1,0:T(8,128)(2,1)S(1)} %collective-permute-done.1.refs_4_.refs_5_), channel_id=1, source_target_pairs={{0,8},{8,0},{16,24},{24,16},{1,9},{9,1},{17,25},{25,17},{2,10},{10... | collective-permute-start | bytes 786440 | tf_op jit(solution)/shard_map/ppermute | solution.py:335
  15.1 8.4 %collective-permute-start.12 = (f32[2,4,8]{2,1,0:T(4,128)S(1)}, f32[2,4,8]{2,1,0:T(4,128)S(1)}, u32[]{:S(2)}, u32[]{:S(2)}) collective-permute-start(f32[2,4,8]{2,1,0:T(4,128)S(1)} %pad_maximum_fusion.1), channel_id=1, source_target_pairs={{0,4},{2,6},{4,0},{6,2},{1,5},{3,7},{5,1},{7,3},{8,12},{10,14},{12... | collective-permute-start | bytes 776 | tf_op jit(solution)/shard_map/ppermute | solution.py:338
  21.3 7.4 %collective-permute-start.10 = (bf16[128,1024]{1,0:T(8,128)(2,1)S(1)}, bf16[128,1024]{1,0:T(8,128)(2,1)S(1)}, u32[]{:S(2)}, u32[]{:S(2)}) collective-permute-start(bf16[128,1024]{1,0:T(8,128)(2,1)S(1)} %collective-permute-done.4.refs_8_.refs_9_), channel_id=1, source_target_pairs={{0,2},{8,10},{2,4},{10,12},{4,6},{12,14},{6,22},{14,30},{22,20},{3... | collective-permute-start | bytes 786440 | tf_op jit(solution)/shard_map/ppermute | solution.py:332
  23.0 8.7 %collective-permute-start.8 = (bf16[128,1024]{1,0:T(8,128)(2,1)S(1)}, bf16[128,1024]{1,0:T(8,128)(2,1)S(1)}, u32[]{:S(2)}, u32[]{:S(2)}) collective-permute-start(bf16[128,1024]{1,0:T(8,128)(2,1)S(1)} %collective-permute-done.4.refs_8_.refs_9_), channel_id=1, source_target_pairs={{0,8},{8,0},{16,24},{24,16},{1,9},{9,1},{17,25},{25,17},{2,10},{10... | collective-permute-start | bytes 786440 | tf_op jit(solution)/shard_map/ppermute | solution.py:335
  23.0 8.7 %collective-permute-start.11 = (bf16[128,1024]{1,0:T(8,128)(2,1)S(1)}, bf16[128,1024]{1,0:T(8,128)(2,1)S(1)}, u32[]{:S(2)}, u32[]{:S(2)}) collective-permute-start(bf16[128,1024]{1,0:T(8,128)(2,1)S(1)} %collective-permute-done.5.refs_10_.refs_11_), channel_id=1, source_target_pairs={{0,16},{8,24},{2,0},{10,8},{4,2},{12,10},{6,4},{14,12},{22,6},{30,... | collective-permute-start | bytes 786440 | tf_op jit(solution)/shard_map/ppermute | solution.py:332
  23.3 8.5 %collective-permute-start.9 = (bf16[128,1024]{1,0:T(8,128)(2,1)S(1)}, bf16[128,1024]{1,0:T(8,128)(2,1)S(1)}, u32[]{:S(2)}, u32[]{:S(2)}) collective-permute-start(bf16[128,1024]{1,0:T(8,128)(2,1)S(1)} %collective-permute-done.5.refs_10_.refs_11_), channel_id=1, source_target_pairs={{0,8},{8,0},{16,24},{24,16},{1,9},{9,1},{17,25},{25,17},{2,10},{10... | collective-permute-start | bytes 786440 | tf_op jit(solution)/shard_map/ppermute | solution.py:335
  31.8 2.6 %collective-permute-start.15 = (bf16[128,1024]{1,0:T(8,128)(2,1)S(1)}, bf16[128,1024]{1,0:T(8,128)(2,1)S(1)}, u32[]{:S(2)}, u32[]{:S(2)}) collective-permute-start(bf16[128,1024]{1,0:T(8,128)(2,1)S(1)} %collective-permute-done.10.refs_0_.refs_1_), channel_id=1, source_target_pairs={{0,8},{8,0},{16,24},{24,16},{1,9},{9,1},{17,25},{25,17},{2,10},{10... | collective-permute-start | bytes 786440 | tf_op jit(solution)/shard_map/ppermute | solution.py:335
  31.8 2.6 %collective-permute-start.16 = (bf16[128,1024]{1,0:T(8,128)(2,1)S(1)}, bf16[128,1024]{1,0:T(8,128)(2,1)S(1)}, u32[]{:S(2)}, u32[]{:S(2)}) collective-permute-start(bf16[128,1024]{1,0:T(8,128)(2,1)S(1)} %collective-permute-done.11.refs_2_.refs_3_), channel_id=1, source_target_pairs={{0,8},{8,0},{16,24},{24,16},{1,9},{9,1},{17,25},{25,17},{2,10},{10... | collective-permute-start | bytes 786440 | tf_op jit(solution)/shard_map/ppermute | solution.py:335
  32.3 5.5 %collective-permute-start.13 = (bf16[64,1024]{1,0:T(8,128)(2,1)S(1)}, bf16[64,1024]{1,0:T(8,128)(2,1)S(1)}, u32[]{:S(2)}, u32[]{:S(2)}) collective-permute-start(bf16[64,1024]{1,0:T(8,128)(2,1)S(1)} %slice.6), channel_id=1, source_target_pairs={{0,2},{8,10},{2,4},{10,12},{4,6},{12,14},{6,22},{14,30},{22,20},{3... | collective-permute-start | bytes 393224 | tf_op jit(solution)/shard_map/ppermute | solution.py:332
  33.1 5.2 %collective-permute-start.14 = (bf16[64,1024]{1,0:T(8,128)(2,1)S(1)}, bf16[64,1024]{1,0:T(8,128)(2,1)S(1)}, u32[]{:S(2)}, u32[]{:S(2)}) collective-permute-start(bf16[64,1024]{1,0:T(8,128)(2,1)S(1)} %slice.7), channel_id=1, source_target_pairs={{0,16},{8,24},{2,0},{10,8},{4,2},{12,10},{6,4},{14,12},{22,6},{30,... | collective-permute-start | bytes 393224 | tf_op jit(solution)/shard_map/ppermute | solution.py:332
  38.3 1.3 %collective-permute-start.17 = (bf16[64,1024]{1,0:T(8,128)(2,1)S(1)}, bf16[64,1024]{1,0:T(8,128)(2,1)S(1)}, u32[]{:S(2)}, u32[]{:S(2)}) collective-permute-start(bf16[64,1024]{1,0:T(8,128)(2,1)S(1)} %collective-permute-done.13.refs_0_), channel_id=1, source_target_pairs={{0,8},{8,0},{16,24},{24,16},{1,9},{9,1},{17,25},{25,17},{2,10},{10... | collective-permute-start | bytes 393224 | tf_op jit(solution)/shard_map/ppermute | solution.py:335
  38.3 1.5 %collective-permute-start.18 = (bf16[64,1024]{1,0:T(8,128)(2,1)S(1)}, bf16[64,1024]{1,0:T(8,128)(2,1)S(1)}, u32[]{:S(2)}, u32[]{:S(2)}) collective-permute-start(bf16[64,1024]{1,0:T(8,128)(2,1)S(1)} %collective-permute-done.14.refs_1_), channel_id=1, source_target_pairs={{0,8},{8,0},{16,24},{24,16},{1,9},{9,1},{17,25},{25,17},{2,10},{10... | collective-permute-start | bytes 393224 | tf_op jit(solution)/shard_map/ppermute | solution.py:335
